TPU v7x, 32 devices: a whole 2x2x4 slice. The times are simulated.
32 devices in a mesh: decade: 2 (over x), row: 8 (over z, y), col: 2 (over core).
Axes of the slice: x: 2, y: 2, z: 4, core: 2. Of those that a mesh axis runs over, the one named last changes fastest.
Arguments:
- counts: int32 [144, 256, 256], P(('decade', 'row')), parts along dimension 0, may hold values from 0 to 96, as said below
- block_pairs: int32 [16, 9, 3], P('decade'), parts along dimension 0, may hold values from 0 to 15, as said below
- sketch: bfloat16 [16, 4096, 256], P(None, ('decade', 'row'), 'col'), parts along dimension 1, may hold values from -6 to 6
Outputs:
- basis: float32 [16, 4096, 256], P(None, ('decade', 'row'), 'col'), parts along dimension 1
There are 2 independent parts, one for each index of `decade`. A program takes and returns all parts, laid end to end along the dimension named above; each array names one. Nothing has to cross between parts.
Inputs may be any that keep to these rules, and one draw needn't show every extreme that they name: Counts of each stored block, in row group r's range of rows of counts. `block_pairs`: i < j, both within 0 to 15. The first 8 stored blocks of a row group name every row group once as g; the last 1 name 1 row groups a second time, the same 1 group for every row group, each with another i than the first time; so no row group stores more than 2 blocks against one group, and no unordered pair of blocks is stored twice.
All inputs are finite; a program needn't handle non-finite values.
Results may differ from a plain program's by a relative error of at most 0.014.
Values may be sent and summed in bfloat16 or wider, within the bound.
No kernel may reach another device: no remote copies, remote signals or barrier semaphores. Data moves between devices by JAX's collectives and lax.ppermute only.
A program may use at most 128 MiB of HBM per device.

v0:
```python
import jax
import jax.numpy as jnp
from jax import lax
from jax.sharding import PartitionSpec as P

CAP = 2


highest = lax.Precision.HIGHEST


def slot_ranks(dest_all):
    stored = dest_all.shape[1]
    same_dest = dest_all[:, :, None] == dest_all[:, None, :]
    earlier = jnp.arange(stored)[None, :] < jnp.arange(stored)[:, None]
    return jnp.sum(same_dest & earlier[None], axis=2)


def body(counts, block_pairs, sketch):
    groups = lax.axis_size("row")
    my_row = lax.axis_index("row")
    my_col = lax.axis_index("col")
    local_blocks, block_rows, half_cols = sketch.shape
    width = half_cols * lax.axis_size("col")
    vocab = local_blocks * block_rows * groups
    slots = groups * CAP
    dest_all = block_pairs[:, :, 1]
    ranks_all = slot_ranks(dest_all)
    mine = lax.dynamic_index_in_dim(block_pairs, my_row, 0, keepdims=False)
    row_block = mine[:, 0]
    dest_group = mine[:, 1]
    col_block = mine[:, 2]
    my_ranks = lax.dynamic_index_in_dim(ranks_all, my_row, 0, keepdims=False)
    my_slots = dest_group * CAP + my_ranks
    select = (dest_all[:, None, :] == my_row) & (
        ranks_all[:, None, :] == jnp.arange(CAP)[None, :, None]
    )
    incoming_block = jnp.sum(jnp.where(select, block_pairs[:, None, :, 2], 0), axis=2).reshape(
        slots
    )
    incoming_live = jnp.any(select, axis=2).reshape(slots)
    count_float = counts.astype(jnp.float32)
    flat_ids = jnp.arange(local_blocks * groups)[:, None]
    row_target = row_block * groups + my_row
    col_target = col_block * groups + dest_group
    partial_margin = jnp.dot(
        (flat_ids == row_target[None, :]).astype(jnp.float32),
        jnp.sum(count_float, axis=2),
        precision=highest,
        preferred_element_type=jnp.float32,
    )
    partial_margin = partial_margin + jnp.dot(
        (flat_ids == col_target[None, :]).astype(jnp.float32),
        jnp.sum(count_float, axis=1),
        precision=highest,
        preferred_element_type=jnp.float32,
    )
    margins = lax.psum(partial_margin, "row")
    log_margin = jnp.log(margins)
    log_total = jnp.log(jnp.sum(margins))
    scores = (
        jnp.log(count_float)
        + log_total
        - jnp.take(log_margin, row_target, axis=0)[:, :, None]
        - jnp.take(log_margin, col_target, axis=0)[:, None, :]
    )
    ppmi_blocks = jnp.where(counts > 0, jnp.maximum(scores, 0.0), 0.0).astype(jnp.bfloat16)
    place_out = (jnp.arange(slots)[:, None] == my_slots[None, :]).astype(jnp.bfloat16)
    gather_own = (jnp.arange(local_blocks)[:, None] == row_block[None, :]).astype(jnp.bfloat16)
    gather_in = (
        (jnp.arange(local_blocks)[:, None] == incoming_block[None, :]) & incoming_live[None, :]
    ).astype(jnp.bfloat16)
    mirror_send = jnp.einsum(
        "ts,sab->tab", place_out, ppmi_blocks, preferred_element_type=jnp.float32
    ).astype(jnp.bfloat16)
    mirror_send = mirror_send.reshape(groups, CAP, block_rows, block_rows)
    mirrored = lax.all_to_all(mirror_send, "row", split_axis=0, concat_axis=0, tiled=True).reshape(
        slots, block_rows, block_rows
    )

    def apply_matrix(source):
        transposed = jnp.einsum(
            "sab,sah->sbh",
            ppmi_blocks,
            jnp.take(source, row_block, axis=0),
            preferred_element_type=jnp.float32,
        ).astype(jnp.bfloat16)
        part_send = jnp.einsum(
            "ts,sbh->tbh", place_out, transposed, preferred_element_type=jnp.float32
        ).astype(jnp.bfloat16)
        part_send = part_send.reshape(groups, CAP, block_rows, half_cols)
        answered = jnp.einsum(
            "tab,tbh->tah",
            mirrored,
            jnp.take(source, incoming_block, axis=0),
            preferred_element_type=jnp.float32,
        ).astype(jnp.bfloat16)
        answered = answered.reshape(groups, CAP, block_rows, half_cols)
        returned, arrived = (
            lax.all_to_all(answered, "row", split_axis=0, concat_axis=0, tiled=True),
            lax.all_to_all(part_send, "row", split_axis=0, concat_axis=0, tiled=True),
        )
        forward = jnp.take(returned.reshape(slots, block_rows, half_cols), my_slots, axis=0)
        result = jnp.einsum("ls,sah->lah", gather_own, forward, preferred_element_type=jnp.float32)
        return result + jnp.einsum(
            "lt,tah->lah",
            gather_in,
            arrived.reshape(slots, block_rows, half_cols),
            preferred_element_type=jnp.float32,
        )

    def orthonormal(result):
        flat_rows = result.reshape(local_blocks * block_rows, half_cols)
        full_rows = lax.all_gather(flat_rows, "col", axis=1, tiled=True)
        product = jnp.dot(
            full_rows.T, full_rows, precision=highest, preferred_element_type=jnp.float32
        )
        gram = lax.psum(product, "row")
        lower_factor = jnp.linalg.cholesky(gram / vocab)
        inverse_factor = jax.scipy.linalg.solve_triangular(
            lower_factor, jnp.eye(width, dtype=jnp.float32), lower=True
        ).T
        own_cols = lax.dynamic_slice_in_dim(inverse_factor, my_col * half_cols, half_cols, 1)
        basis_rows = jnp.dot(
            full_rows, own_cols, precision=highest, preferred_element_type=jnp.float32
        )
        return basis_rows.reshape(local_blocks, block_rows, half_cols)

    first_basis = orthonormal(apply_matrix(sketch)).astype(jnp.bfloat16)
    return orthonormal(apply_matrix(first_basis))


def solution(mesh):
    placed = (
        P(("decade", "row"), None, None),
        P("decade", None, None),
        P(None, ("decade", "row"), "col"),
    )
    return jax.shard_map(
        body,
        mesh=mesh,
        in_specs=placed,
        out_specs=P(None, ("decade", "row"), "col"),
        check_vma=False,
    )
```

profile of v0, /device:TPU:0, one launch (start us, length us, event | category | flops | bytes accessed | tf_op | source)
XLA Modules:
  0.0 630.5 jit_solution(6085992849553704183)
XLA Ops:
  8.8 2.1 convert_reduce_fusion
  12.1 72.4 %all-reduce.5.cloned.1.call-done = f32[128,256]{1,0:T(8,128)} async-done(((f32[128,256]{1,0:T(8,128)}), f32[128,256]{1,0:T(8,128)}) %all-reduce.5.cloned.1.call-update) | async-done | bytes 131088 | tf_op jit(solution)/shard_map/psum | solution.py:58
  88.0 3.2 select_convert_fusion
  91.2 2.2 fusion.2
  93.4 4.1 reshape.134
  97.5 4.3 copy.66
  101.8 4.3 all-to-all-start
  108.0 1.8 copy.74
  109.8 43.1 %all-to-all-done = bf16[8,2,256,256]{3,1,2,0:T(2,128)(2,1)} async-done(((bf16[8,2,256,256]{3,1,2,0:T(2,128)(2,1)}), bf16[8,2,256,256]{3,1,2,0:T(2,128)(2,1)}, u32[]{:S(2)}, u32[]{:S(2)}) %all-to-all-start) | async-done | bytes 2097184 | tf_op jit(solution)/shard_map/all_to_all | solution.py:77
  152.9 3.6 all-to-all-start.2
  157.6 1.7 gather_fusion.2
  159.3 2.0 copy.67
  162.6 1.7 convolution_convert_fusion.4
  164.4 18.1 %all-to-all-done.2 = bf16[8,2,256,128]{3,1,2,0:T(2,128)(2,1)S(1)} async-done(((bf16[8,2,256,128]{3,1,2,0:T(2,128)(2,1)}), bf16[8,2,256,128]{3,1,2,0:T(2,128)(2,1)S(1)}, u32[]{:S(2)}, u32[]{:S(2)}) %all-to-all-start.2) | async-done | bytes 1048608 | tf_op jit(solution)/shard_map/all_to_all | solution.py:101
  182.4 4.2 all-to-all-start.1
  187.1 1.7 copy.75
  188.8 23.5 %all-to-all-done.1 = bf16[8,2,256,128]{3,2,1,0:T(8,128)(2,1)} async-done(((bf16[8,2,256,128]{3,2,1,0:T(8,128)(2,1)}), bf16[8,2,256,128]{3,2,1,0:T(8,128)(2,1)}, u32[]{:S(2)}, u32[]{:S(2)}) %all-to-all-start.1) | async-done | bytes 1048608 | tf_op jit(solution)/shard_map/all_to_all | solution.py:100
  212.3 1.9 gather_fusion.3
  215.9 2.0 copy.76
  218.2 11.6 %all-gather.3.cloned.1.call-done = f32[4096,256]{1,0:T(8,128)} async-done(((f32[4096,128]{1,0:T(8,128)}), f32[4096,256]{1,0:T(8,128)}) %all-gather.3.cloned.1.call-update) | async-done | bytes 4194320 | tf_op jit(solution)/shard_map/all_gather | solution.py:114
  229.8 10.9 %fusion.81 = f32[256,256]{0,1:T(8,128)} fusion(f32[4096,256]{1,0:T(8,128)} %all-gather.3.cloned.1.call-done), kind=kOutput, calls=%fused_computation.172 | convolution fusion | flops 3221225472 | bytes 4456448 | tf_op jit(solution)/shard_map/dot_general | solution.py:115
  240.8 71.9 %all-reduce.7.cloned.1.call-done = f32[256,256]{0,1:T(8,128)} async-done(((f32[256,256]{0,1:T(8,128)}), f32[256,256]{0,1:T(8,128)}) %all-reduce.7.cloned.1.call-update) | async-done | bytes 262160 | tf_op jit(solution)/shard_map/psum | solution.py:118
  314.7 11.7 %cholesky.130 = f32[128,128]{1,0:T(8,128)S(1)} custom-call(f32[128,128]{1,0:T(8,128)S(1)} %cholesky.194), custom_call_target="Cholesky" | custom-call | tf_op jit(solution)/shard_map/jit(cholesky)/cholesky | solution.py:119
  326.5 9.8 %custom-call.13 = f32[1,128,128]{1,2,0:T(8,128)S(1)} custom-call(f32[1,128,128]{2,1,0:T(8,128)S(1)} %get-tuple-element.67), custom_call_target="InvertDiagBlocksLowerTriangular" | custom-call | tf_op jit(solution)/shard_map/jit(cholesky)/cholesky | solution.py:119
  336.8 11.7 %cholesky.147 = f32[128,128]{1,0:T(8,128)S(1)} custom-call(f32[128,128]{1,0:T(8,128)S(1)} %convolution_subtract_fusion.3), custom_call_target="Cholesky" | custom-call | tf_op jit(solution)/shard_map/jit(cholesky)/cholesky | solution.py:119
  351.1 12.6 %while.4 = (s32[]{:T(128)}, f32[256,256]{1,0:T(8,128)S(1)}, s32[2,2]{1,0:T(2,128)S(1)}, f32[2,128,128]{2,1,0:T(8,128)S(1)}, s32[]{:T(128)}) while((s32[]{:T(128)}, f32[256,256]{1,0:T(8,128)S(1)}, s32[2,2]{1,0:T(2,128)S(1)}, f32[2,128,128]{2,1,0:T(8,128)S(1)}, s32[]{:T(128)}) %tuple.61), condition=%wide.while_cond, body=%wide.while_body.sunk | while | flops 2 | bytes 131181 | solution.py:120
  364.2 19.7 %custom-call.14 = f32[2,128,128]{1,2,0:T(8,128)S(1)} custom-call(f32[2,128,128]{2,1,0:T(8,128)S(1)} %get-tuple-element.24), custom_call_target="InvertDiagBlocksLowerTriangular" | custom-call | tf_op jit(solution)/shard_map/jit(_solve_triangular)/triangular_solve | solution.py:120
  384.8 5.6 convolution_convert_fusion
  390.4 1.7 gather_fusion.5
  392.1 3.7 convolution_convert_fusion.2
  395.8 4.4 all-to-all-start.3
  401.6 1.6 convolution_convert_fusion.5
  403.8 1.8 copy.82
  405.6 19.0 %all-to-all-done.3 = bf16[8,2,256,128]{3,2,1,0:T(8,128)(2,1)} async-done(((bf16[8,2,256,128]{3,2,1,0:T(8,128)(2,1)}), bf16[8,2,256,128]{3,2,1,0:T(8,128)(2,1)}, u32[]{:S(2)}, u32[]{:S(2)}) %all-to-all-start.3) | async-done | bytes 1048608 | tf_op jit(solution)/shard_map/all_to_all | solution.py:100
  424.6 4.2 all-to-all-start.4
  428.9 1.9 gather_fusion.6
  431.4 22.9 %all-to-all-done.4 = bf16[8,2,256,128]{3,1,2,0:T(2,128)(2,1)} async-done(((bf16[8,2,256,128]{3,1,2,0:T(2,128)(2,1)}), bf16[8,2,256,128]{3,1,2,0:T(2,128)(2,1)}, u32[]{:S(2)}, u32[]{:S(2)}) %all-to-all-start.4) | async-done | bytes 1048608 | tf_op jit(solution)/shard_map/all_to_all | solution.py:101
  454.3 1.9 copy.83
  456.7 2.0 copy.84
  458.9 11.7 %all-gather.5.cloned.1.call-done = f32[4096,256]{1,0:T(8,128)} async-done(((f32[4096,128]{1,0:T(8,128)}), f32[4096,256]{1,0:T(8,128)}) %all-gather.5.cloned.1.call-update) | async-done | bytes 4194320 | tf_op jit(solution)/shard_map/all_gather | solution.py:114
  470.6 10.9 %fusion.82 = f32[256,256]{0,1:T(8,128)} fusion(f32[4096,256]{1,0:T(8,128)} %all-gather.5.cloned.1.call-done), kind=kOutput, calls=%fused_computation.173 | convolution fusion | flops 3221225472 | bytes 4456448 | tf_op jit(solution)/shard_map/dot_general | solution.py:115
  481.5 71.9 %all-reduce.9.cloned.1.call-done = f32[256,256]{0,1:T(8,128)} async-done(((f32[256,256]{0,1:T(8,128)}), f32[256,256]{0,1:T(8,128)}) %all-reduce.9.cloned.1.call-update) | async-done | bytes 262160 | tf_op jit(solution)/shard_map/psum | solution.py:118
  555.5 11.7 %cholesky.164 = f32[128,128]{1,0:T(8,128)S(1)} custom-call(f32[128,128]{1,0:T(8,128)S(1)} %cholesky.197), custom_call_target="Cholesky" | custom-call | tf_op jit(solution)/shard_map/jit(cholesky)/cholesky | solution.py:119
  567.3 10.0 %custom-call.15 = f32[1,128,128]{1,2,0:T(8,128)S(1)} custom-call(f32[1,128,128]{2,1,0:T(8,128)S(1)} %get-tuple-element.63), custom_call_target="InvertDiagBlocksLowerTriangular" | custom-call | tf_op jit(solution)/shard_map/jit(cholesky)/cholesky | solution.py:119
  577.8 11.7 %cholesky.181 = f32[128,128]{1,0:T(8,128)S(1)} custom-call(f32[128,128]{1,0:T(8,128)S(1)} %convolution_subtract_fusion.2), custom_call_target="Cholesky" | custom-call | tf_op jit(solution)/shard_map/jit(cholesky)/cholesky | solution.py:119
  592.1 3.8 while.5
  595.9 19.7 %custom-call.16 = f32[2,128,128]{1,2,0:T(8,128)S(1)} custom-call(f32[2,128,128]{2,1,0:T(8,128)S(1)} %get-tuple-element.25), custom_call_target="InvertDiagBlocksLowerTriangular" | custom-call | tf_op jit(solution)/shard_map/jit(_solve_triangular)/triangular_solve | solution.py:120
  616.5 7.0 %fusion.27 = f32[4096,128]{1,0:T(8,128)} fusion(f32[4096,256]{1,0:T(8,128)} %all-gather.5.cloned.1.call-done, s32[]{:T(128)S(6)} %select_n.44, f32[128,256]{1,0:T(8,128)S(1)} %fusion.31, f32[128,256]{1,0:T(8,128)S(1)} %fusion.36), kind=kOutput, calls=%fused_computation.66 | convolution fusion | flops 1610645504 | bytes 6553604 | tf_op jit(solution)/shard_map/dot_general | solution.py:124
  (135 shorter events, 33.7 us)
Async XLA Ops:
  6.5 99.7 %copy-start = (bf16[16,256,128]{2,1,0:T(8,128)(2,1)S(1)}, bf16[16,256,128]{2,1,0:T(8,128)(2,1)}, u32[]{:S(2)}) copy-start(bf16[16,256,128]{2,1,0:T(8,128)(2,1)} %param.14) | copy-start | bytes 3145732
  6.5 78.0 %all-reduce.5.cloned.1.call-start = ((), (), s32[]{:S(2)}) async-start(), calls=%async_computation.5 | async-start | bytes 262144 | tf_op jit(solution)/shard_map/psum | solution.py:58
  8.1 206.3 %copy-start.10 = (s32[9]{0:T(128)}, s32[9]{0:T(128)S(1)}, u32[]{:S(2)}) copy-start(s32[9]{0:T(128)S(1)} %get-tuple-element.76) | copy-start | bytes 112
  8.8 98.1 %copy-start.8 = (pred[9]{0:T(512)(128)(4,1)}, pred[9]{0:T(512)(128)(4,1)S(1)}, u32[]{:S(2)}) copy-start(pred[9]{0:T(512)(128)(4,1)S(1)} %get-tuple-element.46) | copy-start | bytes 31
  8.8 205.4 %copy-start.6 = (pred[9]{0:T(512)(128)(4,1)}, pred[9]{0:T(512)(128)(4,1)S(1)}, u32[]{:S(2)}) copy-start(pred[9]{0:T(512)(128)(4,1)S(1)} %get-tuple-element.72) | copy-start | bytes 31
  101.8 51.1 %all-to-all-start = ((bf16[8,2,256,256]{3,1,2,0:T(2,128)(2,1)}), bf16[8,2,256,256]{3,1,2,0:T(2,128)(2,1)}, u32[]{:S(2)}, u32[]{:S(2)}) async-start(bf16[8,2,256,256]{3,1,2,0:T(2,128)(2,1)} %copy.66), calls=%async_computation | async-start | bytes 4194304 | tf_op jit(solution)/shard_map/all_to_all | solution.py:77
  152.9 29.5 %all-to-all-start.2 = ((bf16[8,2,256,128]{3,1,2,0:T(2,128)(2,1)}), bf16[8,2,256,128]{3,1,2,0:T(2,128)(2,1)S(1)}, u32[]{:S(2)}, u32[]{:S(2)}) async-start(bf16[8,2,256,128]{3,1,2,0:T(2,128)(2,1)} %copy.74), calls=%async_computation.2 | async-start | bytes 2097152 | tf_op jit(solution)/shard_map/all_to_all | solution.py:101
  157.6 57.3 %copy-start.4 = (s32[16]{0:T(128)}, s32[16]{0:T(128)S(1)}, u32[]{:S(2)}) copy-start(s32[16]{0:T(128)S(1)} %reshape.136) | copy-start | bytes 196
  159.3 2.0 copy-start.16
  159.3 3.4 copy-start.3
  161.3 1.3 copy-start.2
  182.4 29.9 %all-to-all-start.1 = ((bf16[8,2,256,128]{3,2,1,0:T(8,128)(2,1)}), bf16[8,2,256,128]{3,2,1,0:T(8,128)(2,1)}, u32[]{:S(2)}, u32[]{:S(2)}) async-start(bf16[8,2,256,128]{3,2,1,0:T(8,128)(2,1)} %bitcast.141), calls=%async_computation.1 | async-start | bytes 2097152 | tf_op jit(solution)/shard_map/all_to_all | solution.py:100
  186.7 43.1 %all-gather.3.cloned.1.call-start = ((), (), s32[]{:S(2)}) async-start(), calls=%async_computation.6 | async-start | bytes 6291456 | tf_op jit(solution)/shard_map/all_gather | solution.py:114
  187.1 27.8 %copy-start.12 = (pred[16]{0:T(512)(128)(4,1)}, pred[16]{0:T(512)(128)(4,1)S(1)}, u32[]{:S(2)}) copy-start(pred[16]{0:T(512)(128)(4,1)S(1)} %and.44) | copy-start | bytes 52
  214.2 1.2 copy-start.1
  217.9 94.8 %all-reduce.7.cloned.1.call-start = ((), (), s32[]{:S(2)}) async-start(), calls=%async_computation.7 | async-start | bytes 524288 | tf_op jit(solution)/shard_map/psum | solution.py:118
  363.7 0.5 copy-start.14
  395.8 5.9 copy-start.9
  395.8 28.8 %all-to-all-start.3 = ((bf16[8,2,256,128]{3,2,1,0:T(8,128)(2,1)}), bf16[8,2,256,128]{3,2,1,0:T(8,128)(2,1)}, u32[]{:S(2)}, u32[]{:S(2)}) async-start(bf16[8,2,256,128]{3,2,1,0:T(8,128)(2,1)} %bitcast.142), calls=%async_computation.3 | async-start | bytes 2097152 | tf_op jit(solution)/shard_map/all_to_all | solution.py:100
  405.6 25.2 %copy-start.7 = (pred[9]{0:T(512)(128)(4,1)S(1)}, pred[9]{0:T(512)(128)(4,1)}, u32[]{:S(2)}) copy-start(pred[9]{0:T(512)(128)(4,1)} %copy-done.6) | copy-start | bytes 31
  405.6 25.3 %copy-start.11 = (s32[9]{0:T(128)S(1)}, s32[9]{0:T(128)}, u32[]{:S(2)}) copy-start(s32[9]{0:T(128)} %copy-done.10) | copy-start | bytes 112
  424.6 29.7 %all-to-all-start.4 = ((bf16[8,2,256,128]{3,1,2,0:T(2,128)(2,1)}), bf16[8,2,256,128]{3,1,2,0:T(2,128)(2,1)}, u32[]{:S(2)}, u32[]{:S(2)}) async-start(bf16[8,2,256,128]{3,1,2,0:T(2,128)(2,1)} %copy.82), calls=%async_computation.4 | async-start | bytes 2097152 | tf_op jit(solution)/shard_map/all_to_all | solution.py:101
  428.8 41.8 %all-gather.5.cloned.1.call-start = ((), (), s32[]{:S(2)}) async-start(), calls=%async_computation.8 | async-start | bytes 6291456 | tf_op jit(solution)/shard_map/all_gather | solution.py:114
  430.9 25.3 %copy-start.5 = (s32[16]{0:T(128)S(1)}, s32[16]{0:T(128)}, u32[]{:S(2)}) copy-start(s32[16]{0:T(128)} %copy-done.4) | copy-start | bytes 196
  430.9 25.3 %copy-start.13 = (pred[16]{0:T(512)(128)(4,1)S(1)}, pred[16]{0:T(512)(128)(4,1)}, u32[]{:S(2)}) copy-start(pred[16]{0:T(512)(128)(4,1)} %copy-done.12) | copy-start | bytes 52
  458.7 94.7 %all-reduce.9.cloned.1.call-start = ((), (), s32[]{:S(2)}) async-start(), calls=%async_computation.9 | async-start | bytes 524288 | tf_op jit(solution)/shard_map/psum | solution.py:118
  481.5 110.6 %copy-start.15 = (s32[2,2]{1,0:T(2,128)S(1)}, s32[2,2]{1,0:T(2,128)}, u32[]{:S(2)}) copy-start(s32[2,2]{1,0:T(2,128)} %copy-done.14) | copy-start | bytes 52
Sparse Core Ops, SparseCore 0:
  12.1 72.3 all-reduce.4
  218.0 11.7 all-gather.2
  240.8 71.7 all-reduce.6
  458.8 11.7 all-gather.4
  481.6 71.7 all-reduce.8
where the time goes:
time: 640 us; the launch traced here: 630 us
  waiting for transfers between devices  366 us (57%)
  other arithmetic  121 us (19%)
  matrix products  50.7 us (8%)
  local copies, waits for them, and re-layouts  44.4 us (7%)
  starting transfers between devices  21.4 us (3%)
  between operations  17.3 us (3%)
  loops' own time  9.04 us (1%)
    psum x2, waiting for transfers between devices, orthonormal(): gram = lax.psum(product, 'row')  144 us
    psum x1, waiting for transfers between devices, body(): margins = lax.psum(partial_margin, 'row')  72.4 us
    another operation x14, other arithmetic, orthonormal(): lower_factor = jnp.linalg.cholesky(gram / vocab)  69.3 us
    all_to_all x1, waiting for transfers between devices, body(): lax.all_to_all(mirror_send, 'row', split_axis=0, concat_axis=0, tiled=True)  43.1 us
    all_to_all x2, waiting for transfers between devices, apply_matrix(): lax.all_to_all(answered, 'row', split_axis=0, concat_axis=0, tiled=True)  42.5 us
    all_to_all x2, waiting for transfers between devices, apply_matrix(): lax.all_to_all(part_send, 'row', split_axis=0, concat_axis=0, tiled=True)  40.9 us
    another operation x5, other arithmetic, orthonormal(): jax.scipy.linalg.solve_triangular(lower_factor, jnp.eye(width, dtype=jnp....  39.4 us
    all_gather x2, waiting for transfers between devices, orthonormal(): full_rows = lax.all_gather(flat_rows, 'col', axis=1, tiled=True)  23.3 us
  transfers between devices with their start and end apart: 10, of which 10 were waited for; matrix products, arithmetic and copies ran while one was open for 3% of the time, Pallas kernels for 0%

commit v1 on v0

v1 whole, which is shorter than its diff:
```python
import jax
import jax.numpy as jnp
from jax import lax
from jax.experimental import pallas as pl
from jax.experimental.pallas import tpu as pltpu
from jax.sharding import PartitionSpec as P

CAP = 2
MIB = 1 << 20
HIGHEST = lax.Precision.HIGHEST
VMEM = pl.BlockSpec(memory_space=pltpu.VMEM)
SMEM = pl.BlockSpec(memory_space=pltpu.SMEM)


def contract(a, b, a_dim, b_dim, precision=None):
    return lax.dot_general(
        a,
        b,
        (((a_dim,), (b_dim,)), ((), ())),
        precision=precision,
        preferred_element_type=jnp.float32,
    )


def call(kernel, out_shape, in_specs, scratch=(), flops=0, vmem=40):
    return pl.pallas_call(
        kernel,
        out_shape=out_shape,
        in_specs=in_specs,
        out_specs=jax.tree.map(lambda _: VMEM, out_shape),
        scratch_shapes=list(scratch),
        compiler_params=pltpu.CompilerParams(vmem_limit_bytes=vmem * MIB),
        cost_estimate=pl.CostEstimate(flops=flops, bytes_accessed=4 * MIB, transcendentals=0),
    )


def sums_kernel(counts_ref, sums_ref):
    nnz, rows, cols = counts_ref.shape
    ones = jnp.ones((8, cols), jnp.bfloat16)
    for s in range(nnz):
        block = counts_ref[s].astype(jnp.bfloat16)
        sums_ref[pl.ds(s, 1), :] = contract(ones, block, 1, 1)[0:1, :]
        sums_ref[pl.ds(nnz + s, 1), :] = contract(ones, block, 1, 0)[0:1, :]


def source_kernel(me_ref, pairs_ref, answer_ref, sketch_ref, send_ref, own_ref, turned):
    groups = send_ref.shape[0]
    nnz = own_ref.shape[0]
    me = me_ref[0]

    @pl.loop(0, sketch_ref.shape[0])
    def _(i):
        turned[i] = sketch_ref[i].T

    gather_blocks(me, groups, nnz, pairs_ref, answer_ref, turned, send_ref)

    @pl.loop(0, nnz)
    def _(s):
        own_ref[s] = turned[pairs_ref[me, s, 0]]


def gather_blocks(me, groups, nnz, pairs_ref, answer_ref, blocks, send_ref):
    @pl.loop(0, groups)
    def _(r):
        send_ref[r, 0] = blocks[answer_ref[0, r]]

        @pl.when(answer_ref[1, r] >= 0)
        def _():
            send_ref[r, 1] = blocks[answer_ref[1, r]]


def first_kernel(
    me_ref, pairs_ref, sums_ref, match_ref, counts_ref, recv_ref, own_ref,
    ppmi_ref, forward_ref, send_ref, cols_log,
):
    nnz = counts_ref.shape[0]
    groups = recv_ref.shape[0]
    me = me_ref[0]
    sums = sums_ref[...]
    high = jnp.floor(sums * (1.0 / 256.0))
    low = sums - high * 256.0
    match = match_ref[...]
    margins = 256.0 * contract(match, high.astype(jnp.bfloat16), 1, 0) + contract(
        match, low.astype(jnp.bfloat16), 1, 0
    )
    log_total = jnp.log(jnp.sum(sums))
    log_margin = jnp.log(margins)
    cols_log[...] = log_margin
    padded = jnp.concatenate(
        [log_margin, jnp.zeros((128 - log_margin.shape[0] % 128, log_margin.shape[1]), jnp.float32)],
        axis=0,
    )
    row_log = padded.T
    for s in range(nnz):
        counts = counts_ref[s]
        scores = (
            jnp.log(counts.astype(jnp.float32))
            + log_total
            - row_log[:, s : s + 1]
            - cols_log[pl.ds(nnz + s, 1), :]
        )
        ppmi = jnp.where(counts > 0, jnp.maximum(scores, 0.0), 0.0).astype(jnp.bfloat16)
        ppmi_ref[s] = ppmi
        group, rank = pairs_ref[me, s, 1], int(s >= groups)
        forward_ref[s] = contract(recv_ref[group, rank], ppmi, 1, 1).astype(jnp.bfloat16)
        send_ref[group, rank] = contract(own_ref[s], ppmi, 1, 0).astype(jnp.bfloat16)


def result_kernel(
    me_ref, pairs_ref, answer_ref, forward_ref, arrived_ref, other_forward_ref, other_arrived_ref,
    result_ref, gram_ref,
):
    nnz = forward_ref.shape[0]
    groups = arrived_ref.shape[0]
    blocks, half = result_ref.shape[1:3]
    me, my_col = me_ref[0], me_ref[1]
    result_ref[...] = jnp.zeros_like(result_ref)

    def add(side, forward, arrived):
        @pl.loop(0, nnz)
        def _(s):
            i = pairs_ref[me, s, 0]
            result_ref[side, i] += forward[s].astype(jnp.float32)

        @pl.loop(0, groups)
        def _(r):
            j = answer_ref[0, r]
            result_ref[side, j] += arrived[r, 0].astype(jnp.float32)
            k = answer_ref[1, r]

            @pl.when(k >= 0)
            def _():
                result_ref[side, k] += arrived[r, 1].astype(jnp.float32)

    add(my_col, forward_ref, arrived_ref)
    add(1 - my_col, other_forward_ref, other_arrived_ref)
    gram_ref[...] = jnp.zeros_like(gram_ref)

    @pl.loop(0, blocks // 2)
    def _(n):
        i = n + my_col * (blocks // 2)
        low, high = result_ref[0, i], result_ref[1, i]
        gram_ref[0] += contract(low, low, 1, 1, HIGHEST)
        gram_ref[1] += contract(high, low, 1, 1, HIGHEST)
        gram_ref[2] += contract(high, high, 1, 1, HIGHEST)


def inverse_factor(block):
    size = block.shape[0]
    tiles = size // 8
    full = (8, size)
    lane = lax.broadcasted_iota(jnp.int32, full, 1)
    sub = lax.broadcasted_iota(jnp.int32, full, 0)
    left = [block[8 * t : 8 * t + 8, :] for t in range(tiles)]
    right = [(lane == sub + 8 * t).astype(jnp.float32) for t in range(tiles)]
    for j in range(tiles):
        cols = [jnp.broadcast_to(left[j][:, 8 * j + k : 8 * j + k + 1], full) for k in range(8)]
        pivot = [
            [jnp.broadcast_to(cols[k][i : i + 1, :], full) for k in range(i + 1)] for i in range(8)
        ]
        row_l = [jnp.broadcast_to(left[j][i : i + 1, :], full) for i in range(8)]
        row_r = [jnp.broadcast_to(right[j][i : i + 1, :], full) for i in range(8)]
        scale = []
        for k in range(8):
            scale.append(lax.rsqrt(pivot[k][k]))
            for i in range(k + 1, 8):
                pivot[i][k] = pivot[i][k] * scale[k]
            for i in range(k + 1, 8):
                for m in range(k + 1, i + 1):
                    pivot[i][m] = pivot[i][m] - pivot[i][k] * pivot[m][k]
            row_l[k] = row_l[k] * scale[k]
            row_r[k] = row_r[k] * scale[k]
            for i in range(k + 1, 8):
                row_l[i] = row_l[i] - pivot[i][k] * row_l[k]
                row_r[i] = row_r[i] - pivot[i][k] * row_r[k]
        done = row_r[0]
        for i in range(1, 8):
            done = jnp.where(sub == i, row_r[i], done)
        right[j] = done
        if j < tiles - 1:
            for k in range(7, -1, -1):
                row_l[k] = row_l[k] * scale[k]
                row_r[k] = row_r[k] * scale[k]
                for i in range(k):
                    row_l[i] = row_l[i] - pivot[k][i] * row_l[k]
                    row_r[i] = row_r[i] - pivot[k][i] * row_r[k]
            for t in range(j + 1, tiles):
                cur = left[t]
                new_l, new_r = cur, right[t]
                for k in range(8):
                    col = jnp.broadcast_to(cur[:, 8 * j + k : 8 * j + k + 1], full)
                    new_l = new_l - col * row_l[k]
                    new_r = new_r - col * row_r[k]
                left[t], right[t] = new_l, new_r
    return jnp.concatenate(right, axis=0)


def invert(gram_ref, vocab, inverse):
    low = inverse_factor(gram_ref[0] * vocab)
    across = contract(gram_ref[1] * vocab, low, 1, 1, HIGHEST)
    high = inverse_factor(gram_ref[2] * vocab - contract(across, across, 1, 1, HIGHEST))
    inverse[0, 0] = low
    inverse[0, 1] = jnp.zeros_like(low)
    inverse[1, 0] = -contract(high, contract(across, low, 1, 0, HIGHEST), 1, 0, HIGHEST)
    inverse[1, 1] = high


def normal_block(inverse, result_ref, my_col, i):
    return contract(inverse[my_col, 0], result_ref[0, i], 1, 0, HIGHEST) + contract(
        inverse[my_col, 1], result_ref[1, i], 1, 0, HIGHEST
    )


def second_kernel(
    inv_vocab, me_ref, pairs_ref, answer_ref, gram_ref, result_ref, ppmi_ref,
    x_send_ref, send_ref, inverse, normal,
):
    nnz = ppmi_ref.shape[0]
    groups = send_ref.shape[0]
    me, my_col = me_ref[0], me_ref[1]
    invert(gram_ref, inv_vocab, inverse)

    @pl.loop(0, normal.shape[0])
    def _(i):
        normal[i] = normal_block(inverse, result_ref, my_col, i).astype(jnp.bfloat16)

    gather_blocks(me, groups, nnz, pairs_ref, answer_ref, normal, x_send_ref)

    for s in range(nnz):
        group, rank = pairs_ref[me, s, 1], int(s >= groups)
        own = normal[pairs_ref[me, s, 0]]
        send_ref[group, rank] = contract(own, ppmi_ref[s], 1, 0).astype(jnp.bfloat16)


def forward_kernel(me_ref, pairs_ref, recv_ref, ppmi_ref, forward_ref):
    groups = recv_ref.shape[0]
    me = me_ref[0]
    for s in range(ppmi_ref.shape[0]):
        group, rank = pairs_ref[me, s, 1], int(s >= groups)
        forward_ref[s] = contract(recv_ref[group, rank], ppmi_ref[s], 1, 1).astype(jnp.bfloat16)


def final_kernel(inv_vocab, me_ref, gram_ref, result_ref, out_ref, inverse):
    my_col = me_ref[1]
    invert(gram_ref, inv_vocab, inverse)

    @pl.loop(0, out_ref.shape[0])
    def _(i):
        out_ref[i] = normal_block(inverse, result_ref, my_col, i).T


def body(counts, block_pairs, sketch):
    groups = lax.axis_size("row")
    cols = lax.axis_size("col")
    me = lax.axis_index("row")
    my_col = lax.axis_index("col")
    nnz, rows, _ = counts.shape
    blocks, _, half = sketch.shape
    vocab = blocks * rows * groups
    f32, bf16 = jnp.float32, jnp.bfloat16
    shape = jax.ShapeDtypeStruct

    place = jnp.stack([me, my_col]).astype(jnp.int32)
    hit = block_pairs[:, :, 1] == me
    late = jnp.arange(nnz)[None, :] >= groups
    first_answer = jnp.sum(jnp.where(hit & ~late, block_pairs[:, :, 2], 0), axis=1)
    more_answer = jnp.sum(jnp.where(hit & late, block_pairs[:, :, 2] + 1, 0), axis=1) - 1
    answer = jnp.stack([first_answer, more_answer]).astype(jnp.int32)

    owner = jnp.arange(groups)[:, None]
    row_ids = block_pairs[:, :, 0] * groups + owner
    col_ids = block_pairs[:, :, 2] * groups + block_pairs[:, :, 1]
    depth = -(-2 * nnz // 8) * 8
    no_id = jnp.full((groups, depth - 2 * nnz), -1, jnp.int32)
    all_ids = jnp.concatenate([row_ids, col_ids, no_id], axis=1)
    my_ids = lax.dynamic_index_in_dim(all_ids, me, 0, keepdims=False)
    match = (my_ids[:, None] == all_ids.reshape(-1)[None, :]).astype(bf16)

    def swap(x):
        return lax.ppermute(x, "col", [(0, 1), (1, 0)])

    def exchange(x):
        return lax.all_to_all(x, "row", split_axis=0, concat_axis=0, tiled=True)

    def exchange_all(x):
        return lax.all_to_all(x, ("row", "col"), split_axis=0, concat_axis=0, tiled=True)

    def reduce_gram(part):
        ranks = groups * cols
        pieces = part.reshape(ranks, 3 * half // ranks, half)
        mine = jnp.sum(exchange_all(pieces), axis=0)
        every = exchange_all(jnp.broadcast_to(mine[None], pieces.shape))
        return every.reshape(3, half, half)

    sums = call(sums_kernel, shape((depth, rows), f32), [VMEM])(counts)
    sums_all = exchange(jnp.broadcast_to(sums[None], (groups, depth, rows)))

    x_send, own = call(
        source_kernel,
        (shape((groups, CAP, half, rows), bf16), shape((nnz, half, rows), bf16)),
        [SMEM, SMEM, SMEM, VMEM],
        [pltpu.VMEM((blocks, half, rows), bf16)],
    )(place, block_pairs, answer, sketch)
    x_recv = exchange(x_send)

    live = (jnp.arange(depth) < 2 * nnz)[None, :, None]
    sums_live = jnp.where(live, sums_all, 0.0).reshape(groups * depth, rows)
    ppmi, forward, send = call(
        first_kernel,
        (
            shape((nnz, rows, rows), bf16),
            shape((nnz, half, rows), bf16),
            shape((groups, CAP, half, rows), bf16),
        ),
        [SMEM, SMEM, VMEM, VMEM, VMEM, VMEM, VMEM],
        [pltpu.VMEM((depth, rows), f32)],
    )(place, block_pairs, sums_live, match, counts, x_recv, own)

    def finish(forward, send):
        other_forward = swap(forward)
        arrived = exchange(send)
        other_arrived = swap(arrived)
        result, gram = call(
            result_kernel,
            (shape((2, blocks, half, rows), f32), shape((3, half, half), f32)),
            [SMEM, SMEM, SMEM, VMEM, VMEM, VMEM, VMEM],
        )(place, block_pairs, answer, forward, arrived, other_forward, other_arrived)
        return result, reduce_gram(gram)

    result, gram = finish(forward, send)

    def second(*refs):
        second_kernel(1.0 / vocab, *refs)

    x_send, send = call(
        second,
        (shape((groups, CAP, half, rows), bf16), shape((groups, CAP, half, rows), bf16)),
        [SMEM, SMEM, SMEM, VMEM, VMEM, VMEM],
        [pltpu.VMEM((2, 2, half, half), f32), pltpu.VMEM((blocks, half, rows), bf16)],
    )(place, block_pairs, answer, gram, result, ppmi)
    x_recv = exchange(x_send)
    forward = call(
        forward_kernel,
        shape((nnz, half, rows), bf16),
        [SMEM, SMEM, VMEM, VMEM],
    )(place, block_pairs, x_recv, ppmi)
    result, gram = finish(forward, send)

    def final(*refs):
        final_kernel(1.0 / vocab, *refs)

    return call(
        final,
        shape((blocks, rows, half), f32),
        [SMEM, VMEM, VMEM],
        [pltpu.VMEM((2, 2, half, half), f32)],
    )(place, gram, result)


def solution(mesh):
    placed = (
        P(("decade", "row"), None, None),
        P("decade", None, None),
        P(None, ("decade", "row"), "col"),
    )
    return jax.shard_map(
        body,
        mesh=mesh,
        in_specs=placed,
        out_specs=P(None, ("decade", "row"), "col"),
        check_vma=False,
    )
```

time: 640 us -> 259 us (0.40); the launches traced: 630 us -> 258 us
  waiting for transfers between devices: 366 us -> 56.6 us
  other arithmetic: 121 us -> 2.12 us
  blocking collectives: 0 us -> 106 us
  Pallas kernels: 0 us -> 60 us
  matrix products: 50.7 us -> 0 us
  local copies, waits for them, and re-layouts: 44.4 us -> 18.4 us
  between operations: 17.3 us -> 0.2 us
  loops' own time: 9.04 us -> 0 us
    psum x3 -> x0, waiting for transfers between devices: 216 us -> none  [the longest x2 144 us: orthonormal(): gram = lax.psum(product, 'row')]
    another operation x19 -> x2, other arithmetic: 109 us -> 0.09 us  [the longest x1 0.08 us: body(): place = jnp.stack([me, my_col]).astype(jnp.int32)]
    all_to_all x0 -> x6, blocking collectives: none -> 106 us  [the longest x2 57.5 us: exchange(): return lax.all_to_all(x, 'row', split_axis=0, concat_axis=0, tiled=True)]
    all_to_all x5 -> x3, waiting for transfers between devices: 127 us -> 51.6 us  [exchange(): return lax.all_to_all(x, 'row', split_axis=0, concat_axis=0, tiled=True)]
    pallas_call x0 -> x8, Pallas kernels: none -> 60 us  [the longest x1 19.6 us: body(): call(final, shape((blocks, rows, half), f32), [SMEM, VMEM, VMEM], [pltpu....]
    dot_general x17 -> x0, matrix products: 48 us -> none  [the longest x2 21.8 us: orthonormal(): jnp.dot(full_rows.T, full_rows, precision=highest, preferred_element_type...]
    all_gather x2 -> x0, waiting for transfers between devices: 23.3 us -> none  [orthonormal(): full_rows = lax.all_gather(flat_rows, 'col', axis=1, tiled=True)]
    unnamed x35 -> x45, local copies, waits for them, and re-layouts: 2.47 us -> 17.5 us
  transfers between devices with their start and end apart: 10 -> 7, of which waited for: 10 -> 5; matrix products, arithmetic and copies ran while one was open for 3% -> 1% of each run, Pallas kernels for 0% -> 2%
where the time goes in v1:
time: 259 us; the launch traced here: 258 us
  blocking collectives  106 us (41%)
  Pallas kernels  60 us (23%)
  waiting for transfers between devices  56.6 us (22%)
  local copies, waits for them, and re-layouts  18.4 us (7%)
  starting transfers between devices  15.2 us (6%)
    all_to_all x2, blocking collectives, exchange(): return lax.all_to_all(x, 'row', split_axis=0, concat_axis=0, tiled=True)  57.5 us
    all_to_all x3, waiting for transfers between devices, exchange(): return lax.all_to_all(x, 'row', split_axis=0, concat_axis=0, tiled=True)  51.6 us
    all_to_all x4, blocking collectives, exchange_all(): lax.all_to_all(x, ('row', 'col'), split_axis=0, concat_axis=0, tiled=True)  48.4 us
    pallas_call x1, Pallas kernels, body(): call(final, shape((blocks, rows, half), f32), [SMEM, VMEM, VMEM], [pltpu....  19.6 us
    pallas_call x1, Pallas kernels, body(): call(second, (shape((groups, CAP, half, rows), bf16), shape((groups, CAP,...  18.8 us
    unnamed x45, local copies, waits for them, and re-layouts  17.5 us
    all_to_all x3, starting transfers between devices, exchange(): return lax.all_to_all(x, 'row', split_axis=0, concat_axis=0, tiled=True)  14.6 us
    pallas_call x2, Pallas kernels, finish(): call(result_kernel, (shape((2, blocks, half, rows), f32), shape((3, half,...  12.8 us
  transfers between devices with their start and end apart: 7, of which 5 were waited for; matrix products, arithmetic and copies ran while one was open for 1% of the time, Pallas kernels for 2%

profile of v1, /device:TPU:0, one launch (start us, length us, event | category | flops | bytes accessed | tf_op | source)
XLA Modules:
  0.0 258.5 jit_solution(651313284465196882)
XLA Ops:
  0.0 1.7 copy-done
  1.7 0.6 shard_map.37
  2.3 0.7 broadcast_in_dim.44
  3.0 7.4 %all-to-all-start = ((f32[8,24,256]{2,1,0:T(8,128)}), f32[8,24,256]{2,1,0:T(8,128)}, u32[]{:S(2)}, u32[]{:S(2)}) async-start(f32[8,24,256]{2,1,0:T(8,128)} %broadcast_in_dim.44), calls=%async_computation | async-start | bytes 393216 | tf_op jit(solution)/shard_map/all_to_all | solution.py:283
  10.4 0.1 bitcast_add_fusion
  10.5 0.1 pad_add_fusion.1.me_ref.refs_0_
  10.6 0.1 copy.9.pairs_ref.refs_1_
  10.8 3.0 %shard_map.38 = (bf16[8,2,128,256]{3,2,1,0:T(8,128)(2,1)S(1)}, bf16[9,128,256]{2,1,0:T(8,128)(2,1)S(1)}) custom-call(s32[2]{0:T(128)S(1)} %pad_add_fusion.1.me_ref.refs_0_, s32[8,9,3]{2,1,0:T(8,128)S(1)} %copy.9.pairs_ref.refs_1_, s32[2,8]{1,0:T(2,128)S(1)} %pad_add_fusion.answer_ref.refs_2_, bf16[16,256,128]{2,1,0:T(8,128)(2,1)S(1)} %copy-done.12), custom_call_target="tpu_custom_call" | custom-call | bytes 4194304 | tf_op jit(solution)/shard_map/pallas_call | solution.py:298
  13.8 0.0 copy-start.13
  13.8 1.0 copy-done.13
  14.8 0.8 copy-done.16
  15.6 2.8 %all-to-all-done = f32[8,24,256]{2,1,0:T(8,128)} async-done(((f32[8,24,256]{2,1,0:T(8,128)}), f32[8,24,256]{2,1,0:T(8,128)}, u32[]{:S(2)}, u32[]{:S(2)}) %all-to-all-start) | async-done | bytes 196640 | tf_op jit(solution)/shard_map/all_to_all | solution.py:283
  18.4 3.6 %all-to-all-start.1 = ((bf16[8,2,128,256]{3,2,1,0:T(8,128)(2,1)}), bf16[8,2,128,256]{3,2,1,0:T(8,128)(2,1)S(1)}, u32[]{:S(2)}, u32[]{:S(2)}) async-start(bf16[8,2,128,256]{3,2,1,0:T(8,128)(2,1)} %copy-done.13), calls=%async_computation.1 | async-start | bytes 2097152 | tf_op jit(solution)/shard_map/all_to_all | solution.py:283
  22.0 0.1 pad.2.clone
  22.1 0.1 add_add_fusion
  22.2 0.1 eq.27
  22.3 0.1 compare_convert_fusion.match_ref
  22.3 1.7 broadcast_select_fusion
  24.0 23.2 %all-to-all-done.1.recv_ref = bf16[8,2,128,256]{3,2,1,0:T(8,128)(2,1)S(1)} async-done(((bf16[8,2,128,256]{3,2,1,0:T(8,128)(2,1)}), bf16[8,2,128,256]{3,2,1,0:T(8,128)(2,1)S(1)}, u32[]{:S(2)}, u32[]{:S(2)}) %all-to-all-start.1) | async-done | bytes 1048608 | tf_op jit(solution)/shard_map/all_to_all | solution.py:283
  47.3 1.0 copy-done.6
  48.3 1.2 copy-done.7
  49.5 0.8 copy-done.9
  50.3 0.9 copy-done.15
  51.2 1.1 copy-done.17
  52.3 0.6 copy-done.19
  52.9 3.1 %shard_map.39 = (bf16[9,256,256]{2,1,0:T(8,128)(2,1)S(1)}, bf16[9,128,256]{2,1,0:T(8,128)(2,1)S(1)}, bf16[8,2,128,256]{3,2,1,0:T(8,128)(2,1)S(1)}) custom-call(s32[2]{0:T(128)S(1)} %copy-done.19, s32[8,9,3]{2,1,0:T(8,128)S(1)} %copy-done.9, f32[192,256]{1,0:T(8,128)S(1)} %bitcast.31, bf16[24,192]{1,0:T(8,128)(2,1)S(1)} %compare_convert_fusion.match_ref, ...), custom_call_target="tpu_custom_call" | custom-call | bytes 4194304 | tf_op jit(solution)/shard_map/pallas_call | solution.py:308
  56.0 29.1 %all_to_all.45.arrived_ref = bf16[8,2,128,256]{3,2,1,0:T(8,128)(2,1)S(1)} all-to-all(bf16[8,2,128,256]{3,2,1,0:T(8,128)(2,1)S(1)} %get-tuple-element.19), channel_id=1, replica_groups=mesh['decade'=2,'row'=8,'col'=2] {'row'}, dimensions={0} | all-to-all | bytes 2097152 | tf_op jit(solution)/shard_map/all_to_all | solution.py:283
  85.1 0.5 collective-permute-start
  85.6 3.0 %collective-permute-done.other_forward_ref = bf16[9,128,256]{2,1,0:T(8,128)(2,1)S(1)} collective-permute-done((bf16[9,128,256]{2,1,0:T(8,128)(2,1)S(1)}, bf16[9,128,256]{2,1,0:T(8,128)(2,1)S(1)}, u32[]{:S(2)}, u32[]{:S(2)}) %collective-permute-start) | collective-permute-done | bytes 589856 | tf_op jit(solution)/shard_map/ppermute | solution.py:280
  88.6 6.4 %shard_map.40 = (f32[2,16,128,256]{3,2,1,0:T(8,128)S(1)}, f32[3,128,128]{2,1,0:T(8,128)S(1)}) custom-call(s32[2]{0:T(128)S(1)} %copy-done.19, s32[8,9,3]{2,1,0:T(8,128)S(1)} %copy-done.10, s32[2,8]{1,0:T(2,128)S(1)} %pad_add_fusion.answer_ref.refs_2_, bf16[9,128,256]{2,1,0:T(8,128)(2,1)S(1)} %get-tuple-element.18.forward_ref, ...), custom_call_target="tpu_custom_call" | custom-call | bytes 4194304 | tf_op jit(solution)/shard_map/pallas_call | solution.py:323
  95.0 1.9 copy-done.2
  96.9 12.7 %all_to_all.46 = f32[16,24,128]{2,1,0:T(8,128)S(1)} all-to-all(f32[16,24,128]{2,1,0:T(8,128)S(1)} %bitcast.33), channel_id=1, replica_groups=mesh['decade'=2,'row'=8,'col'=2] {'row','col'}, dimensions={0} | all-to-all | bytes 393216 | tf_op jit(solution)/shard_map/all_to_all | solution.py:286
  109.7 11.6 %all_to_all.47 = f32[16,24,128]{2,1,0:T(8,128)S(1)} all-to-all(f32[16,24,128]{2,1,0:T(8,128)S(1)} %broadcast_in_dim.47), channel_id=1, replica_groups=mesh['decade'=2,'row'=8,'col'=2] {'row','col'}, dimensions={0} | all-to-all | bytes 393216 | tf_op jit(solution)/shard_map/all_to_all | solution.py:286
  121.3 2.2 copy-done.3
  123.5 18.8 %shard_map.41 = (bf16[8,2,128,256]{3,2,1,0:T(8,128)(2,1)S(1)}, bf16[8,2,128,256]{3,2,1,0:T(8,128)(2,1)S(1)}) custom-call(s32[2]{0:T(128)S(1)} %copy-done.20, s32[8,9,3]{2,1,0:T(8,128)S(1)} %copy-done.11, s32[2,8]{1,0:T(2,128)S(1)} %pad_add_fusion.answer_ref.refs_2_, f32[3,128,128]{2,1,0:T(8,128)S(1)} %bitcast.29, f32[2,16,128,256]{3,2,1,0:T(8,128)S(1)} %copy-done.3, ...), custom_call_target="tpu_custom_call" | custom-call | bytes 4194304 | tf_op jit(solution)/shard_map/pallas_call | solution.py:335
  142.3 28.4 %all_to_all.48.arrived_ref = bf16[8,2,128,256]{3,2,1,0:T(8,128)(2,1)S(1)} all-to-all(bf16[8,2,128,256]{3,2,1,0:T(8,128)(2,1)S(1)} %get-tuple-element.24), channel_id=1, replica_groups=mesh['decade'=2,'row'=8,'col'=2] {'row'}, dimensions={0} | all-to-all | bytes 2097152 | tf_op jit(solution)/shard_map/all_to_all | solution.py:283
  170.7 3.6 %all-to-all-start.5 = ((bf16[8,2,128,256]{3,2,1,0:T(8,128)(2,1)}), bf16[8,2,128,256]{3,2,1,0:T(8,128)(2,1)S(1)}, u32[]{:S(2)}, u32[]{:S(2)}) async-start(bf16[8,2,128,256]{3,2,1,0:T(8,128)(2,1)} %copy-done.14), calls=%async_computation.5 | async-start | bytes 2097152 | tf_op jit(solution)/shard_map/all_to_all | solution.py:283
  174.4 0.0 collective-permute-start.3
  174.4 25.6 %all-to-all-done.5.recv_ref = bf16[8,2,128,256]{3,2,1,0:T(8,128)(2,1)S(1)} async-done(((bf16[8,2,128,256]{3,2,1,0:T(8,128)(2,1)}), bf16[8,2,128,256]{3,2,1,0:T(8,128)(2,1)S(1)}, u32[]{:S(2)}, u32[]{:S(2)}) %all-to-all-start.5) | async-done | bytes 1048608 | tf_op jit(solution)/shard_map/all_to_all | solution.py:283
  200.0 2.1 shard_map.42.forward_ref
  202.1 0.1 collective-permute-start.2
  202.2 2.0 collective-permute-done.2.other_forward_ref
  204.2 6.4 %shard_map.43 = (f32[2,16,128,256]{3,2,1,0:T(8,128)S(1)}, f32[3,128,128]{2,1,0:T(8,128)S(1)}) custom-call(s32[2]{0:T(128)S(1)} %copy-done.20, s32[8,9,3]{2,1,0:T(8,128)S(1)} %copy-done.11, s32[2,8]{1,0:T(2,128)S(1)} %pad_add_fusion.answer_ref.refs_2_, bf16[9,128,256]{2,1,0:T(8,128)(2,1)S(1)} %shard_map.42.forward_ref, ...), custom_call_target="tpu_custom_call" | custom-call | bytes 4194304 | tf_op jit(solution)/shard_map/pallas_call | solution.py:323
  210.6 1.9 copy-done.4
  212.5 12.5 %all_to_all.49 = f32[16,24,128]{2,1,0:T(8,128)S(1)} all-to-all(f32[16,24,128]{2,1,0:T(8,128)S(1)} %bitcast.32), channel_id=1, replica_groups=mesh['decade'=2,'row'=8,'col'=2] {'row','col'}, dimensions={0} | all-to-all | bytes 393216 | tf_op jit(solution)/shard_map/all_to_all | solution.py:286
  225.1 11.6 %all_to_all.50 = f32[16,24,128]{2,1,0:T(8,128)S(1)} all-to-all(f32[16,24,128]{2,1,0:T(8,128)S(1)} %broadcast_in_dim.48), channel_id=1, replica_groups=mesh['decade'=2,'row'=8,'col'=2] {'row','col'}, dimensions={0} | all-to-all | bytes 393216 | tf_op jit(solution)/shard_map/all_to_all | solution.py:286
  236.7 2.2 copy-done.5
  238.9 19.6 %shard_map.44 = f32[16,256,128]{2,1,0:T(8,128)} custom-call(s32[2]{0:T(128)S(1)} %copy-done.20, f32[3,128,128]{2,1,0:T(8,128)S(1)} %bitcast.30, f32[2,16,128,256]{3,2,1,0:T(8,128)S(1)} %copy-done.5), custom_call_target="tpu_custom_call" | custom-call | bytes 4194304 | tf_op jit(solution)/shard_map/pallas_call | solution.py:352
  (43 shorter events, 0.2 us)
Async XLA Ops:
  0.0 1.7 copy-start
  1.7 8.7 %copy-start.21 = (s32[8,9,3]{1,0,2:T(8,128)S(1)}, s32[8,9,3]{1,0,2:T(8,128)}, u32[]{:S(2)}) copy-start(s32[8,9,3]{1,0,2:T(8,128)} %param.4) | copy-start | bytes 2596
  1.7 9.1 %copy-start.12 = (bf16[16,256,128]{2,1,0:T(8,128)(2,1)S(1)}, bf16[16,256,128]{2,1,0:T(8,128)(2,1)}, u32[]{:S(2)}) copy-start(bf16[16,256,128]{2,1,0:T(8,128)(2,1)} %sketch_ref.1) | copy-start | bytes 3145732
  2.2 46.0 %copy-start.1 = (s32[9,256,256]{2,1,0:T(8,128)S(1)}, s32[9,256,256]{2,1,0:T(8,128)}, u32[]{:S(2)}) copy-start(s32[9,256,256]{2,1,0:T(8,128)} %counts_ref.3) | copy-start | bytes 7077892
  3.0 15.5 %all-to-all-start = ((f32[8,24,256]{2,1,0:T(8,128)}), f32[8,24,256]{2,1,0:T(8,128)}, u32[]{:S(2)}, u32[]{:S(2)}) async-start(f32[8,24,256]{2,1,0:T(8,128)} %broadcast_in_dim.44), calls=%async_computation | async-start | bytes 393216 | tf_op jit(solution)/shard_map/all_to_all | solution.py:283
  10.6 37.6 %copy-start.18 = (s32[2]{0:T(128)}, s32[2]{0:T(128)S(1)}, u32[]{:S(2)}) copy-start(s32[2]{0:T(128)S(1)} %pad_add_fusion.1.me_ref.refs_0_) | copy-start | bytes 28
  10.8 7.7 %copy-start.8 = (s32[8,9,3]{2,1,0:T(8,128)}, s32[8,9,3]{2,1,0:T(8,128)S(1)}, u32[]{:S(2)}) copy-start(s32[8,9,3]{2,1,0:T(8,128)S(1)} %copy.9.pairs_ref.refs_1_) | copy-start | bytes 2596
  13.8 1.0 copy-start.13
  14.8 0.8 copy-start.16
  18.4 28.8 %all-to-all-start.1 = ((bf16[8,2,128,256]{3,2,1,0:T(8,128)(2,1)}), bf16[8,2,128,256]{3,2,1,0:T(8,128)(2,1)S(1)}, u32[]{:S(2)}, u32[]{:S(2)}) async-start(bf16[8,2,128,256]{3,2,1,0:T(8,128)(2,1)} %copy-done.13), calls=%async_computation.1 | async-start | bytes 2097152 | tf_op jit(solution)/shard_map/all_to_all | solution.py:283
  47.3 1.0 copy-start.6
  48.2 1.2 copy-start.7
  49.5 0.8 copy-start.9
  50.3 0.9 copy-start.15
  51.2 1.1 copy-start.17
  52.3 0.6 copy-start.19
  52.9 35.7 %copy-start.10 = (s32[8,9,3]{2,1,0:T(8,128)S(1)}, s32[8,9,3]{2,1,0:T(8,128)}, u32[]{:S(2)}) copy-start(s32[8,9,3]{2,1,0:T(8,128)} %copy-done.8) | copy-start | bytes 2596
  85.0 36.3 %copy-start.11 = (s32[8,9,3]{2,1,0:T(8,128)S(1)}, s32[8,9,3]{2,1,0:T(8,128)}, u32[]{:S(2)}) copy-start(s32[8,9,3]{2,1,0:T(8,128)} %copy-done.8) | copy-start | bytes 2596
  85.0 36.3 %copy-start.20 = (s32[2]{0:T(128)S(1)}, s32[2]{0:T(128)}, u32[]{:S(2)}) copy-start(s32[2]{0:T(128)} %copy-done.18) | copy-start | bytes 28
  85.0 3.5 %collective-permute-start.1 = (bf16[8,2,128,256]{3,2,1,0:T(8,128)(2,1)S(1)}, bf16[8,2,128,256]{3,2,1,0:T(8,128)(2,1)S(1)}, u32[]{:S(2)}, u32[]{:S(2)}) collective-permute-start(bf16[8,2,128,256]{3,2,1,0:T(8,128)(2,1)S(1)} %all_to_all.45.arrived_ref), channel_id=1, source_target_pairs={{0,1},{1,0},{2,3},{3,2},{4,5},{5,4},{6,7},{7,6},{8,9},{9,8},{10,11... | collective-permute-start | bytes 3145736 | tf_op jit(solution)/shard_map/ppermute | solution.py:280
  85.1 3.5 %collective-permute-start = (bf16[9,128,256]{2,1,0:T(8,128)(2,1)S(1)}, bf16[9,128,256]{2,1,0:T(8,128)(2,1)S(1)}, u32[]{:S(2)}, u32[]{:S(2)}) collective-permute-start(bf16[9,128,256]{2,1,0:T(8,128)(2,1)S(1)} %get-tuple-element.18.forward_ref), channel_id=1, source_target_pairs={{0,1},{1,0},{2,3},{3,2},{4,5},{5,4},{6,7},{7,6},{8,9},{9,8},{10,11... | collective-permute-start | bytes 1769480 | tf_op jit(solution)/shard_map/ppermute | solution.py:280
  95.0 2.0 copy-start.2
  121.3 2.2 copy-start.3
  142.3 28.4 %copy-start.14 = (bf16[8,2,128,256]{3,2,1,0:T(8,128)(2,1)}, bf16[8,2,128,256]{3,2,1,0:T(8,128)(2,1)S(1)}, u32[]{:S(2)}) copy-start(bf16[8,2,128,256]{3,2,1,0:T(8,128)(2,1)S(1)} %get-tuple-element.23) | copy-start | bytes 3145732
  170.7 29.2 %all-to-all-start.5 = ((bf16[8,2,128,256]{3,2,1,0:T(8,128)(2,1)}), bf16[8,2,128,256]{3,2,1,0:T(8,128)(2,1)S(1)}, u32[]{:S(2)}, u32[]{:S(2)}) async-start(bf16[8,2,128,256]{3,2,1,0:T(8,128)(2,1)} %copy-done.14), calls=%async_computation.5 | async-start | bytes 2097152 | tf_op jit(solution)/shard_map/all_to_all | solution.py:283
  174.4 29.8 %collective-permute-start.3 = (bf16[8,2,128,256]{3,2,1,0:T(8,128)(2,1)S(1)}, bf16[8,2,128,256]{3,2,1,0:T(8,128)(2,1)}, u32[]{:S(2)}, u32[]{:S(2)}) collective-permute-start(bf16[8,2,128,256]{3,2,1,0:T(8,128)(2,1)S(1)} %all_to_all.48.arrived_ref), channel_id=1, source_target_pairs={{0,1},{1,0},{2,3},{3,2},{4,5},{5,4},{6,7},{7,6},{8,9},{9,8},{10,11... | collective-permute-start | bytes 3145736 | tf_op jit(solution)/shard_map/ppermute | solution.py:280
  202.1 2.1 collective-permute-start.2
  210.6 2.0 copy-start.4
  236.7 2.2 copy-start.5

commit v2 on v0

v2 whole, which is shorter than its diff:
```python
import jax
import jax.numpy as jnp
from jax import lax
from jax.experimental import pallas as pl
from jax.experimental.pallas import tpu as pltpu
from jax.sharding import PartitionSpec as P

MIB = 1 << 20
HIGHEST = lax.Precision.HIGHEST
VMEM = pl.BlockSpec(memory_space=pltpu.VMEM)
SMEM = pl.BlockSpec(memory_space=pltpu.SMEM)
ANY = pl.BlockSpec(memory_space=pl.ANY)
shape = jax.ShapeDtypeStruct
f32, bf16, i32 = jnp.float32, jnp.bfloat16, jnp.int32


def contract(a, b, a_dim, b_dim, precision=None):
    return lax.dot_general(
        a,
        b,
        (((a_dim,), (b_dim,)), ((), ())),
        precision=precision,
        preferred_element_type=f32,
    )


def call(kernel, out_shape, in_specs, out_specs=None, scratch=(), flops=0, vmem=32):
    if out_specs is None:
        out_specs = jax.tree.map(lambda _: VMEM, out_shape)
    return pl.pallas_call(
        kernel,
        out_shape=out_shape,
        in_specs=in_specs,
        out_specs=out_specs,
        scratch_shapes=list(scratch),
        compiler_params=pltpu.CompilerParams(vmem_limit_bytes=vmem * MIB),
        cost_estimate=pl.CostEstimate(flops=flops, bytes_accessed=4 * MIB, transcendentals=0),
    )


class Table:
    def __init__(self, groups, nnz):
        self.groups, self.nnz, self.hot = groups, nnz, nnz - groups
        self.main_j = 0
        self.my_s = self.main_j + groups
        self.hot_j = self.my_s + groups
        self.row_i = self.hot_j + groups * self.hot
        self.hot_k = self.row_i + nnz
        self.me = self.hot_k + self.hot
        self.col = self.me + 1

    def build(self, block_pairs, me, my_col):
        groups = self.groups
        peers = me ^ jnp.arange(groups)
        theirs = jnp.take(block_pairs, peers, axis=0)
        mine = theirs[0]
        hit = theirs[:, :, 1] == me
        main_j = jnp.sum(jnp.where(hit[:, :groups], theirs[:, :groups, 2], 0), axis=1)
        my_s = jnp.sum(
            jnp.where(mine[None, :groups, 1] == peers[:, None], jnp.arange(groups)[None, :], 0),
            axis=1,
        )
        hot_j = jnp.where(hit[:, groups:], theirs[:, groups:, 2], -1).reshape(-1)
        hot_k = (mine[groups:, 1] ^ me) & ~1
        parts = [main_j, my_s, hot_j, mine[:, 0], hot_k, jnp.stack([me, my_col])]
        return jnp.concatenate([p.astype(i32) for p in parts]), theirs


def sums_kernel(counts_ref, sums_ref):
    nnz, rows, cols = counts_ref.shape
    ones = jnp.ones((8, cols), bf16)
    sums_ref[...] = jnp.zeros_like(sums_ref)
    for s in range(nnz):
        block = counts_ref[s].astype(bf16)
        sums_ref[pl.ds(s, 1), :] = contract(ones, block, 1, 1)[0:1, :]
        sums_ref[pl.ds(nnz + s, 1), :] = contract(ones, block, 1, 0)[0:1, :]


def gather_blocks(t, tab, blocks, main, hot):
    for k in range(t.groups):
        main[k][...] = blocks[tab[t.main_j + k]]
        for m in range(t.hot):
            j = tab[t.hot_j + k * t.hot + m]

            @pl.when(j >= 0)
            def _():
                hot[k][m] = blocks[j]


def products(t, tab, blocks, ppmi, main, hot):
    def product(s):
        return contract(blocks[tab[t.row_i + s]], ppmi[s], 1, 0).astype(bf16)

    for k in range(t.groups):
        main[k][...] = product(tab[t.my_s + k])
    for m in range(t.hot):
        hot[m] = product(t.groups + m)


def make_source_kernel(t):
    def kernel(tab, sketch_ref, turned, *outs):
        main, hot = outs[: t.groups], outs[t.groups :]

        @pl.loop(0, sketch_ref.shape[0])
        def _(i):
            turned[i] = sketch_ref[i].T

        gather_blocks(t, tab, turned, main, hot)

    return kernel


def make_ppmi_kernel(t):
    def kernel(tab, match_ref, counts_ref, turned, *refs):
        sums_refs = refs[: t.groups]
        ppmi_ref, hot = refs[t.groups : t.groups + 2]
        main = refs[t.groups + 2 : 2 * t.groups + 2]
        cols_log = refs[-1]
        sums = jnp.concatenate([ref[...] for ref in sums_refs], axis=0)
        high = jnp.floor(sums * (1.0 / 256.0))
        low = sums - high * 256.0
        match = match_ref[...]
        margins = 256.0 * contract(match, high.astype(bf16), 1, 0) + contract(
            match, low.astype(bf16), 1, 0
        )
        log_total = jnp.log(jnp.sum(sums))
        log_margin = jnp.log(margins)
        cols_log[...] = log_margin
        fill = 128 - log_margin.shape[0] % 128
        row_log = jnp.concatenate(
            [log_margin, jnp.zeros((fill, log_margin.shape[1]), f32)], axis=0
        ).T
        for s in range(t.nnz):
            counts = counts_ref[s]
            scores = (
                jnp.log(counts.astype(f32))
                + log_total
                - row_log[:, s : s + 1]
                - cols_log[pl.ds(t.nnz + s, 1), :]
            )
            ppmi_ref[s] = jnp.where(counts > 0, jnp.maximum(scores, 0.0), 0.0).astype(bf16)
        products(t, tab, turned, ppmi_ref, main, hot)

    return kernel


def make_forward_kernel(t):
    def kernel(tab, ppmi_ref, *refs):
        main, hot = refs[: t.groups], refs[t.groups : t.groups + t.groups // 2]
        forward, picked = refs[-2:]
        for k in range(t.groups):
            s = tab[t.my_s + k]
            forward[s] = contract(main[k][...], ppmi_ref[s], 1, 1).astype(bf16)
        for m in range(t.hot):
            for n in range(t.groups // 2):

                @pl.when(tab[t.hot_k + m] == 2 * n)
                def _():
                    picked[...] = hot[n][m]

            s = t.groups + m
            forward[s] = contract(picked[...], ppmi_ref[s], 1, 1).astype(bf16)

    return kernel


def make_result_kernel(t):
    def kernel(tab, forward, *refs):
        main, hot = refs[: t.groups], refs[t.groups : 2 * t.groups]
        result = refs[-1]
        result[...] = jnp.zeros_like(result)
        for s in range(t.nnz):
            result[tab[t.row_i + s]] += forward[s].astype(f32)
        for k in range(t.groups):
            result[tab[t.main_j + k]] += main[k][...].astype(f32)
            for m in range(t.hot):
                j = tab[t.hot_j + k * t.hot + m]

                @pl.when(j >= 0)
                def _():
                    result[j] += hot[k][m].astype(f32)

    return kernel


def make_gram_kernel(t, chunk):
    def kernel(tab, own, other, *refs):
        outs, gram = refs[: t.groups], refs[-1]
        blocks, half, _ = own.shape
        me, my_col = tab[t.me], tab[t.col]
        gram[...] = jnp.zeros_like(gram)
        cut = half // 2

        @pl.loop(0, blocks)
        def _(i):
            mine = own[i]
            gram[pl.ds(0, half), :] += contract(mine, mine, 1, 1, HIGHEST)

            @pl.when(my_col == 0)
            def _():
                gram[pl.ds(half, cut), :] += contract(
                    other[i, pl.ds(0, cut), :], mine, 1, 1, HIGHEST
                )

            @pl.when(my_col == 1)
            def _():
                gram[pl.ds(half, cut), :] += contract(
                    own[i, pl.ds(cut, cut), :], other[i], 1, 1, HIGHEST
                )

        for k in range(t.groups):
            start = pl.multiple_of((me ^ k) * chunk, 8)
            outs[k][...] = gram[pl.ds(start, chunk), :]

    return kernel


def inverse_factor(block):
    size = block.shape[0]
    tiles = size // 8
    full = (8, size)
    lane = lax.broadcasted_iota(i32, full, 1)
    sub = lax.broadcasted_iota(i32, full, 0)
    left = [block[8 * t : 8 * t + 8, :] for t in range(tiles)]
    right = [(lane == sub + 8 * t).astype(f32) for t in range(tiles)]
    for j in range(tiles):
        cols = [jnp.broadcast_to(left[j][:, 8 * j + k : 8 * j + k + 1], full) for k in range(8)]
        pivot = [
            [jnp.broadcast_to(cols[k][i : i + 1, :], full) for k in range(i + 1)] for i in range(8)
        ]
        row_l = [jnp.broadcast_to(left[j][i : i + 1, :], full) for i in range(8)]
        row_r = [jnp.broadcast_to(right[j][i : i + 1, :], full) for i in range(8)]
        scale = []
        for k in range(8):
            scale.append(lax.rsqrt(pivot[k][k]))
            for i in range(k + 1, 8):
                pivot[i][k] = pivot[i][k] * scale[k]
            for i in range(k + 1, 8):
                for m in range(k + 1, i + 1):
                    pivot[i][m] = pivot[i][m] - pivot[i][k] * pivot[m][k]
            row_l[k] = row_l[k] * scale[k]
            row_r[k] = row_r[k] * scale[k]
            for i in range(k + 1, 8):
                row_l[i] = row_l[i] - pivot[i][k] * row_l[k]
                row_r[i] = row_r[i] - pivot[i][k] * row_r[k]
        done = row_r[0]
        for i in range(1, 8):
            done = jnp.where(sub == i, row_r[i], done)
        right[j] = done
        if j < tiles - 1:
            for k in range(7, -1, -1):
                row_l[k] = row_l[k] * scale[k]
                row_r[k] = row_r[k] * scale[k]
                for i in range(k):
                    row_l[i] = row_l[i] - pivot[k][i] * row_l[k]
                    row_r[i] = row_r[i] - pivot[k][i] * row_r[k]
            for t in range(j + 1, tiles):
                cur = left[t]
                new_l, new_r = cur, right[t]
                for k in range(8):
                    col = jnp.broadcast_to(cur[:, 8 * j + k : 8 * j + k + 1], full)
                    new_l = new_l - col * row_l[k]
                    new_r = new_r - col * row_r[k]
                left[t], right[t] = new_l, new_r
    return jnp.concatenate(right, axis=0)


def invert(t, tab, own, other, gram, inverse, scale):
    chunk, half = own[0].shape
    me, my_col = tab[t.me], tab[t.col]
    for k in range(t.groups):
        rows = pl.ds(pl.multiple_of((me ^ k) * chunk, 8), chunk)
        gram[my_col, rows, :] = own[k][...] * scale
        gram[1 - my_col, rows, :] = other[k][...] * scale
    cut = half // 2
    low = inverse_factor(gram[0, pl.ds(0, half), :])
    lower = jnp.concatenate([gram[0, pl.ds(half, cut), :], gram[1, pl.ds(half, cut), :]], axis=0)
    across = contract(lower, low, 1, 1, HIGHEST)
    high = inverse_factor(
        gram[1, pl.ds(0, half), :] - contract(across, across, 1, 1, HIGHEST)
    )
    inverse[0, 0] = low
    inverse[0, 1] = jnp.zeros_like(low)
    inverse[1, 0] = -contract(high, contract(across, low, 1, 0, HIGHEST), 1, 0, HIGHEST)
    inverse[1, 1] = high


def normal_block(inverse, mine, other, my_col, i):
    return contract(inverse[my_col, my_col], mine[i], 1, 0, HIGHEST) + contract(
        inverse[my_col, 1 - my_col], other[i], 1, 0, HIGHEST
    )


def start_copies(pairs, sems):
    copies = [pltpu.make_async_copy(a, b, sems.at[n]) for n, (a, b) in enumerate(pairs)]
    for copy in copies:
        copy.start()
    return copies


def make_second_kernel(t, scale):
    def kernel(tab, *refs):
        g = t.groups
        own_g, other_g = refs[:g], refs[g : 2 * g]
        mine_hbm, other_hbm, ppmi_hbm = refs[2 * g : 2 * g + 3]
        outs = refs[2 * g + 3 : 5 * g + 4]
        x_main, x_hot, t_main, t_hot = outs[:g], outs[g : 2 * g], outs[2 * g : 3 * g], outs[3 * g]
        gram, inverse, normal, mine, other, ppmi, sems = refs[5 * g + 4 :]
        copies = start_copies([(mine_hbm, mine), (other_hbm, other), (ppmi_hbm, ppmi)], sems)
        invert(t, tab, own_g, other_g, gram, inverse, scale)
        my_col = tab[t.col]
        for copy in copies:
            copy.wait()

        @pl.loop(0, normal.shape[0])
        def _(i):
            normal[i] = normal_block(inverse, mine, other, my_col, i).astype(bf16)

        gather_blocks(t, tab, normal, x_main, x_hot)
        products(t, tab, normal, ppmi, t_main, t_hot)

    return kernel


def make_final_kernel(t, scale):
    def kernel(tab, *refs):
        g = t.groups
        own_g, other_g = refs[:g], refs[g : 2 * g]
        mine_hbm, other_hbm, out_ref, gram, inverse, mine, other, sems = refs[2 * g :]
        copies = start_copies([(mine_hbm, mine), (other_hbm, other)], sems)
        invert(t, tab, own_g, other_g, gram, inverse, scale)
        my_col = tab[t.col]
        for copy in copies:
            copy.wait()

        @pl.loop(0, out_ref.shape[0])
        def _(i):
            out_ref[i] = normal_block(inverse, mine, other, my_col, i).T

    return kernel


def body(counts, block_pairs, sketch):
    groups = lax.axis_size("row")
    me = lax.axis_index("row")
    my_col = lax.axis_index("col")
    nnz, rows, _ = counts.shape
    blocks, _, half = sketch.shape
    vocab = blocks * rows * groups
    t = Table(groups, nnz)
    hot = t.hot
    chunk = -(-(half + half // 2) // (8 * groups)) * 8
    depth = -(-2 * nnz // 8) * 8

    def peer(x, k):
        return lax.ppermute(x, "row", [(r, r ^ k) for r in range(groups)])

    def swap(x):
        return lax.ppermute(x, "col", [(0, 1), (1, 0)])

    far_first = sorted(range(1, groups), reverse=True)

    def exchange(parts):
        got = {0: parts[0]}
        for k in far_first:
            got[k] = peer(parts[k], k)
        return [got[k] for k in range(groups)]

    def spread(part):
        return exchange([part] * groups)

    def spread_hot(part):
        got = {0: part}
        for k in far_first:
            if k % 2 == 0:
                got[k] = peer(part, k)
        for k in range(0, groups, 2):
            got[k + 1] = peer(got[k], 1)
        return [got[k] for k in range(groups)]

    def scatter_hot(parts, live):
        passed = {k: peer(parts[k + 1], 1) for k in range(0, groups, 2)}
        out = []
        for k in range(0, groups, 2):
            part = jnp.where(live[k][:, None, None], parts[k], passed[k])
            out.append(peer(part, k) if k else part)
        return out

    main_shapes = [shape((half, rows), bf16)] * groups
    hot_shape = shape((hot, half, rows), bf16)
    ppmi_shape = shape((nnz, rows, rows), bf16)
    result_shape = shape((blocks, half, rows), f32)

    sums = call(sums_kernel, shape((depth, rows), f32), [VMEM])(counts)
    sums_all = spread(sums)
    tab, theirs = t.build(block_pairs, me, my_col)
    hot_live = (tab[t.hot_j : t.hot_j + groups * hot] >= 0).reshape(groups, hot)

    source = call(
        make_source_kernel(t),
        [shape((blocks, half, rows), bf16)] + main_shapes + [hot_shape] * groups,
        [SMEM, VMEM],
    )(tab, sketch)
    turned = source[0]
    x_main = exchange(source[1 : 1 + groups])
    x_hot = scatter_hot(source[1 + groups :], hot_live)

    owner = (me ^ jnp.arange(groups))[:, None]
    row_ids = theirs[:, :, 0] * groups + owner
    col_ids = theirs[:, :, 2] * groups + theirs[:, :, 1]
    no_id = jnp.full((groups, depth - 2 * nnz), -1, i32)
    ids = jnp.concatenate([row_ids, col_ids, no_id], axis=1)
    match = (ids[0][:, None] == ids.reshape(-1)[None, :]).astype(bf16)

    found = call(
        make_ppmi_kernel(t),
        [ppmi_shape, hot_shape] + main_shapes,
        [SMEM] + [VMEM] * (3 + groups),
        scratch=[pltpu.VMEM((depth, rows), f32)],
    )(tab, match, counts, turned, *sums_all)
    ppmi, t_hot, t_main = found[0], found[1], found[2:]

    def finish(x_main, x_hot, t_main, t_hot):
        t_main = exchange(t_main)
        t_hot = spread_hot(t_hot)
        forward = call(
            make_forward_kernel(t),
            shape((nnz, half, rows), bf16),
            [SMEM] + [VMEM] * (1 + groups + groups // 2),
            scratch=[pltpu.VMEM((half, rows), bf16)],
        )(tab, ppmi, *x_main, *x_hot)
        result = call(
            make_result_kernel(t),
            result_shape,
            [SMEM] + [VMEM] * (1 + 2 * groups),
        )(tab, forward, *t_main, *t_hot)
        other = swap(result)
        part = call(
            make_gram_kernel(t, chunk),
            [shape((chunk, half), f32)] * groups,
            [SMEM, VMEM, VMEM],
            scratch=[pltpu.VMEM((groups * chunk, half), f32)],
        )(tab, result, other)
        gram = spread(sum(exchange(part)[1:], part[0]))
        return result, other, gram, [swap(x) for x in gram]

    gram_scratch = [
        pltpu.VMEM((2, groups * chunk, half), f32),
        pltpu.VMEM((2, 2, half, half), f32),
    ]
    result_scratch = [pltpu.VMEM((blocks, half, rows), f32)] * 2
    result, other, gram, other_gram = finish(x_main, x_hot, t_main, t_hot)
    second = call(
        make_second_kernel(t, 1.0 / vocab),
        main_shapes + [hot_shape] * groups + main_shapes + [hot_shape],
        [SMEM] + [VMEM] * (2 * groups) + [ANY] * 3,
        scratch=gram_scratch
        + [pltpu.VMEM((blocks, half, rows), bf16)]
        + result_scratch
        + [pltpu.VMEM((nnz, rows, rows), bf16), pltpu.SemaphoreType.DMA((3,))],
    )(tab, *gram, *other_gram, result, other, ppmi)
    x_main = exchange(second[:groups])
    x_hot = scatter_hot(second[groups : 2 * groups], hot_live)
    result, other, gram, other_gram = finish(
        x_main, x_hot, second[2 * groups : 3 * groups], second[3 * groups]
    )
    return call(
        make_final_kernel(t, 1.0 / vocab),
        shape((blocks, rows, half), f32),
        [SMEM] + [VMEM] * (2 * groups) + [ANY] * 2,
        scratch=gram_scratch + result_scratch + [pltpu.SemaphoreType.DMA((2,))],
    )(tab, *gram, *other_gram, result, other)


def solution(mesh):
    placed = (
        P(("decade", "row"), None, None),
        P("decade", None, None),
        P(None, ("decade", "row"), "col"),
    )
    return jax.shard_map(
        body,
        mesh=mesh,
        in_specs=placed,
        out_specs=P(None, ("decade", "row"), "col"),
        check_vma=False,
    )
```

time: 640 us -> 254 us (0.40); the launches traced: 630 us -> 254 us
  waiting for transfers between devices: 366 us -> 37.9 us
  starting transfers between devices: 21.4 us -> 139 us
  other arithmetic: 121 us -> 5.96 us
  Pallas kernels: 0 us -> 65.5 us
  matrix products: 50.7 us -> 0 us
  local copies, waits for them, and re-layouts: 44.4 us -> 5.01 us
  between operations: 17.3 us -> 1.2 us
  loops' own time: 9.04 us -> 0 us
    psum x3 -> x0, waiting for transfers between devices: 216 us -> none  [the longest x2 144 us: orthonormal(): gram = lax.psum(product, 'row')]
    ppermute x0 -> x109, starting transfers between devices: none -> 139 us  [the longest x91 135 us: peer(): return lax.ppermute(x, 'row', [(r, r ^ k) for r in range(groups)])]
    all_to_all x5 -> x0, waiting for transfers between devices: 127 us -> none  [the longest x1 43.1 us: body(): lax.all_to_all(mirror_send, 'row', split_axis=0, concat_axis=0, tiled=True)]
    another operation x19 -> x0, other arithmetic: 109 us -> none  [the longest x14 69.3 us: orthonormal(): lower_factor = jnp.linalg.cholesky(gram / vocab)]
    pallas_call x0 -> x11, Pallas kernels: none -> 65.5 us  [the longest x1 19.9 us: body(): call(make_final_kernel(t, 1.0 / vocab), shape((blocks, rows, half), f32),...]
    dot_general x17 -> x0, matrix products: 48 us -> none  [the longest x2 21.8 us: orthonormal(): jnp.dot(full_rows.T, full_rows, precision=highest, preferred_element_type...]
    ppermute x0 -> x109, waiting for transfers between devices: none -> 37.9 us  [the longest x91 27.4 us: peer(): return lax.ppermute(x, 'row', [(r, r ^ k) for r in range(groups)])]
    all_gather x2 -> x0, waiting for transfers between devices: 23.3 us -> none  [orthonormal(): full_rows = lax.all_gather(flat_rows, 'col', axis=1, tiled=True)]
  transfers between devices with their start and end apart: 10 -> 109, of which waited for: 10 -> 27; matrix products, arithmetic and copies ran while one was open for 3% -> 3% of each run, Pallas kernels for 0% -> 2%
where the time goes in v2:
time: 254 us
  starting transfers between devices  139 us (55%)
  Pallas kernels  65.5 us (26%)
  waiting for transfers between devices  37.9 us (15%)
  other arithmetic  5.96 us (2%)
  local copies, waits for them, and re-layouts  5.01 us (2%)
    ppermute x91, starting transfers between devices, peer(): return lax.ppermute(x, 'row', [(r, r ^ k) for r in range(groups)])  135 us
    ppermute x91, waiting for transfers between devices, peer(): return lax.ppermute(x, 'row', [(r, r ^ k) for r in range(groups)])  27.4 us
    pallas_call x1, Pallas kernels, body(): call(make_final_kernel(t, 1.0 / vocab), shape((blocks, rows, half), f32),...  19.9 us
    pallas_call x2, Pallas kernels, finish(): call(make_gram_kernel(t, chunk), [shape((chunk, half), f32)] * groups, [S...  18.6 us
    pallas_call x1, Pallas kernels, body(): call(make_second_kernel(t, 1.0 / vocab), main_shapes + [hot_shape] * grou...  18.4 us
    ppermute x18, waiting for transfers between devices, swap(): return lax.ppermute(x, 'col', [(0, 1), (1, 0)])  10.5 us
    select_n x8, other arithmetic, scatter_hot(): part = jnp.where(live[k][:, None, None], parts[k], passed[k])  5.26 us
  transfers between devices with their start and end apart: 109, of which 27 were waited for; matrix products, arithmetic and copies ran while one was open for 3% of the time, Pallas kernels for 2%

profile of v2, /device:TPU:0, one launch (start us, length us, event | category | flops | bytes accessed | tf_op | source)
XLA Modules:
  0.0 254.3 jit_solution(17155611163934845919)
XLA Ops:
  2.3 6.0 %collective-permute-start.6 = (f32[24,256]{1,0:T(8,128)S(1)}, f32[24,256]{1,0:T(8,128)S(1)}, u32[]{:S(2)}, u32[]{:S(2)}) collective-permute-start(f32[24,256]{1,0:T(8,128)S(1)} %shard_map.38.refs_0_), channel_id=1, source_target_pairs={{0,14},{2,12},{4,10},{6,8},{8,6},{10,4},{12,2},{14,0},{1,15},{3,13... | collective-permute-start | bytes 73736 | tf_op jit(solution)/shard_map/ppermute | solution.py:356
  9.3 2.0 collective-permute-start.3
  11.3 2.3 collective-permute-start.2
  18.9 1.7 shard_map.37
  24.2 2.4 collective-permute-start.10
  28.7 1.9 shard_map.39
  31.2 3.7 %collective-permute-start.12 = (bf16[128,256]{1,0:T(8,128)(2,1)S(1)}, bf16[128,256]{1,0:T(8,128)(2,1)S(1)}, u32[]{:S(2)}, u32[]{:S(2)}) collective-permute-start(bf16[128,256]{1,0:T(8,128)(2,1)S(1)} %get-tuple-element.81), channel_id=1, source_target_pairs={{0,12},{2,14},{4,8},{6,10},{8,4},{10,6},{12,0},{14,2},{1,13},{3,15... | collective-permute-start | bytes 196616 | tf_op jit(solution)/shard_map/ppermute | solution.py:356
  42.0 3.5 %collective-permute-start.23 = (bf16[128,256]{1,0:T(8,128)(2,1)S(1)}, bf16[128,256]{1,0:T(8,128)(2,1)S(1)}, u32[]{:S(2)}, u32[]{:S(2)}) collective-permute-start(bf16[128,256]{1,0:T(8,128)(2,1)S(1)} %get-tuple-element.94), channel_id=1, source_target_pairs={{0,6},{2,4},{4,2},{6,0},{8,14},{10,12},{12,10},{14,8},{1,7},{3,5},... | collective-permute-start | bytes 196616 | tf_op jit(solution)/shard_map/ppermute | solution.py:356
  46.1 2.4 collective-permute-start.33
  55.2 3.5 %collective-permute-done.25.refs_5_ = bf16[128,256]{1,0:T(8,128)(2,1)S(1)} collective-permute-done((bf16[128,256]{1,0:T(8,128)(2,1)S(1)}, bf16[128,256]{1,0:T(8,128)(2,1)S(1)}, u32[]{:S(2)}, u32[]{:S(2)}) %collective-permute-start.25) | collective-permute-done | bytes 65568 | tf_op jit(solution)/shard_map/ppermute | solution.py:356
  59.3 3.5 %collective-permute-start.18 = (bf16[1,128,256]{2,1,0:T(8,128)(2,1)S(1)}, bf16[1,128,256]{2,1,0:T(8,128)(2,1)S(1)}, u32[]{:S(2)}, u32[]{:S(2)}) collective-permute-start(bf16[1,128,256]{2,1,0:T(8,128)(2,1)S(1)} %broadcast_select_fusion.3), channel_id=1, source_target_pairs={{0,8},{2,10},{4,12},{6,14},{8,0},{10,2},{12,4},{14,6},{1,9},{3,11}... | collective-permute-start | bytes 196616 | tf_op jit(solution)/shard_map/ppermute | solution.py:356
  62.8 2.4 collective-permute-start.20
  66.0 2.1 collective-permute-start.27
  75.7 4.1 %collective-permute-done.35.other.refs_17_ = f32[16,128,256]{2,1,0:T(8,128)S(1)} collective-permute-done((f32[16,128,256]{2,1,0:T(8,128)S(1)}, f32[16,128,256]{2,1,0:T(8,128)S(1)}, u32[]{:S(2)}, u32[]{:S(2)}) %collective-permute-start.35) | collective-permute-done | bytes 2097184 | tf_op jit(solution)/shard_map/ppermute | solution.py:359
  79.8 9.3 %shard_map.42 = (f32[24,128]{1,0:T(8,128)S(1)}, f32[24,128]{1,0:T(8,128)S(1)}, f32[24,128]{1,0:T(8,128)S(1)}, f32[24,128]{1,0:T(8,128)S(1)}, f32[24,128]{1,0:T(8...) custom-call(s32[36]{0:T(128)S(1)} %concatenate.6.tab, ...), custom_call_target="tpu_custom_call" | custom-call | bytes 4194304 | tf_op jit(solution)/shard_map/pallas_call | solution.py:438
  90.3 2.4 collective-permute-start.38
  93.6 2.5 collective-permute-start.40
  96.2 2.1 collective-permute-start.41
  98.2 2.1 collective-permute-start.42
  101.6 3.0 %collective-permute-done.42 = f32[24,128]{1,0:T(8,128)S(1)} collective-permute-done((f32[24,128]{1,0:T(8,128)S(1)}, f32[24,128]{1,0:T(8,128)S(1)}, u32[]{:S(2)}, u32[]{:S(2)}) %collective-permute-start.42) | collective-permute-done | bytes 12320 | tf_op jit(solution)/shard_map/ppermute | solution.py:356
  104.7 2.1 collective-permute-start.49
  106.9 2.4 collective-permute-start.48
  109.3 3.1 %collective-permute-start.46 = (f32[24,128]{1,0:T(8,128)S(1)}, f32[24,128]{1,0:T(8,128)S(1)}, u32[]{:S(2)}, u32[]{:S(2)}) collective-permute-start(f32[24,128]{1,0:T(8,128)S(1)} %add_add_fusion.1.refs_0_), channel_id=1, source_target_pairs={{0,8},{2,10},{4,12},{6,14},{8,0},{10,2},{12,4},{14,6},{1,9},{3,11}... | collective-permute-start | bytes 36872 | tf_op jit(solution)/shard_map/ppermute | solution.py:356
  112.5 2.7 %collective-permute-start.44 = (f32[24,128]{1,0:T(8,128)S(1)}, f32[24,128]{1,0:T(8,128)S(1)}, u32[]{:S(2)}, u32[]{:S(2)}) collective-permute-start(f32[24,128]{1,0:T(8,128)S(1)} %add_add_fusion.1.refs_0_), channel_id=1, source_target_pairs={{0,4},{2,6},{4,0},{6,2},{8,12},{10,14},{12,8},{14,10},{1,5},{3,7},... | collective-permute-start | bytes 36872 | tf_op jit(solution)/shard_map/ppermute | solution.py:356
  120.6 18.4 %shard_map.43 = (bf16[128,256]{1,0:T(8,128)(2,1)S(1)}, bf16[128,256]{1,0:T(8,128)(2,1)S(1)}, bf16[128,256]{1,0:T(8,128)(2,1)S(1)}, bf16[128,256]{1,0:T(8,128)(2,...) custom-call(s32[36]{0:T(128)S(1)} %concatenate.6.tab, ...), custom_call_target="tpu_custom_call" | custom-call | bytes 4194304 | tf_op jit(solution)/shard_map/pallas_call | solution.py:453
  140.0 2.5 collective-permute-start.60
  143.7 3.2 %collective-permute-start.62 = (bf16[128,256]{1,0:T(8,128)(2,1)S(1)}, bf16[128,256]{1,0:T(8,128)(2,1)S(1)}, u32[]{:S(2)}, u32[]{:S(2)}) collective-permute-start(bf16[128,256]{1,0:T(8,128)(2,1)S(1)} %get-tuple-element.113), channel_id=1, source_target_pairs={{0,10},{2,8},{4,14},{6,12},{8,2},{10,0},{12,6},{14,4},{1,11},{3,9}... | collective-permute-start | bytes 196616 | tf_op jit(solution)/shard_map/ppermute | solution.py:356
  148.3 2.6 %collective-permute-start.64 = (bf16[128,256]{1,0:T(8,128)(2,1)S(1)}, bf16[128,256]{1,0:T(8,128)(2,1)S(1)}, u32[]{:S(2)}, u32[]{:S(2)}) collective-permute-start(bf16[128,256]{1,0:T(8,128)(2,1)S(1)} %get-tuple-element.115), channel_id=1, source_target_pairs={{0,14},{2,12},{4,10},{6,8},{8,6},{10,4},{12,2},{14,0},{1,15},{3,13... | collective-permute-start | bytes 196616 | tf_op jit(solution)/shard_map/ppermute | solution.py:356
  158.5 1.8 collective-permute-start.75
  161.0 2.0 collective-permute-start.84
  163.0 2.4 collective-permute-start.80
  166.3 2.0 collective-permute-start.77
  168.9 5.7 %collective-permute-done.76.refs_5_ = bf16[128,256]{1,0:T(8,128)(2,1)S(1)} collective-permute-done((bf16[128,256]{1,0:T(8,128)(2,1)S(1)}, bf16[128,256]{1,0:T(8,128)(2,1)S(1)}, u32[]{:S(2)}, u32[]{:S(2)}) %collective-permute-start.76) | collective-permute-done | bytes 65568 | tf_op jit(solution)/shard_map/ppermute | solution.py:356
  174.7 2.4 collective-permute-start.69
  177.0 2.0 collective-permute-start.71
  180.2 2.1 collective-permute-start.78
  189.7 4.1 %collective-permute-done.86.other.refs_17_ = f32[16,128,256]{2,1,0:T(8,128)S(1)} collective-permute-done((f32[16,128,256]{2,1,0:T(8,128)S(1)}, f32[16,128,256]{2,1,0:T(8,128)S(1)}, u32[]{:S(2)}, u32[]{:S(2)}) %collective-permute-start.86) | collective-permute-done | bytes 2097184 | tf_op jit(solution)/shard_map/ppermute | solution.py:359
  193.8 9.3 %shard_map.46 = (f32[24,128]{1,0:T(8,128)S(1)}, f32[24,128]{1,0:T(8,128)S(1)}, f32[24,128]{1,0:T(8,128)S(1)}, f32[24,128]{1,0:T(8,128)S(1)}, f32[24,128]{1,0:T(8...) custom-call(s32[36]{0:T(128)S(1)} %concatenate.6.tab, ...), custom_call_target="tpu_custom_call" | custom-call | bytes 4194304 | tf_op jit(solution)/shard_map/pallas_call | solution.py:438
  204.5 2.2 collective-permute-start.89
  207.4 2.8 %collective-permute-start.91 = (f32[24,128]{1,0:T(8,128)S(1)}, f32[24,128]{1,0:T(8,128)S(1)}, u32[]{:S(2)}, u32[]{:S(2)}) collective-permute-start(f32[24,128]{1,0:T(8,128)S(1)} %get-tuple-element.138), channel_id=1, source_target_pairs={{0,10},{2,8},{4,14},{6,12},{8,2},{10,0},{12,6},{14,4},{1,11},{3,9}... | collective-permute-start | bytes 36872 | tf_op jit(solution)/shard_map/ppermute | solution.py:356
  210.1 2.1 collective-permute-start.92
  212.3 2.1 collective-permute-start.93
  215.7 2.9 %collective-permute-done.93 = f32[24,128]{1,0:T(8,128)S(1)} collective-permute-done((f32[24,128]{1,0:T(8,128)S(1)}, f32[24,128]{1,0:T(8,128)S(1)}, u32[]{:S(2)}, u32[]{:S(2)}) %collective-permute-start.93) | collective-permute-done | bytes 12320 | tf_op jit(solution)/shard_map/ppermute | solution.py:356
  218.7 2.2 collective-permute-start.100
  220.9 2.1 collective-permute-start.99
  223.0 3.4 %collective-permute-start.97 = (f32[24,128]{1,0:T(8,128)S(1)}, f32[24,128]{1,0:T(8,128)S(1)}, u32[]{:S(2)}, u32[]{:S(2)}) collective-permute-start(f32[24,128]{1,0:T(8,128)S(1)} %add_add_fusion.refs_0_), channel_id=1, source_target_pairs={{0,8},{2,10},{4,12},{6,14},{8,0},{10,2},{12,4},{14,6},{1,9},{3,11}... | collective-permute-start | bytes 36872 | tf_op jit(solution)/shard_map/ppermute | solution.py:356
  226.5 2.4 collective-permute-start.95
  234.3 19.9 %shard_map.47 = f32[16,256,128]{2,1,0:T(8,128)} custom-call(s32[36]{0:T(128)S(1)} %concatenate.6.tab, f32[24,128]{1,0:T(8,128)S(1)} %add_add_fusion.refs_0_, f32[24,128]{1,0:T(8,128)S(1)} %collective-permute-done.94.refs_1_, f32[24,128]{1,0:T(8,128)S(1)} %collective-permute-done.95.refs_2_, f32[24,128]{1,0:T(8,128)S(1)} %collective-permute-done.96.refs_3_, ...), custom_call_target="tpu_custom_call" | custom-call | bytes 4194304 | tf_op jit(solution)/shard_map/pallas_call | solution.py:467
  (224 shorter events, 77.2 us)
Async XLA Ops:
  2.3 12.7 %collective-permute-start.6 = (f32[24,256]{1,0:T(8,128)S(1)}, f32[24,256]{1,0:T(8,128)S(1)}, u32[]{:S(2)}, u32[]{:S(2)}) collective-permute-start(f32[24,256]{1,0:T(8,128)S(1)} %shard_map.38.refs_0_), channel_id=1, source_target_pairs={{0,14},{2,12},{4,10},{6,8},{8,6},{10,4},{12,2},{14,0},{1,15},{3,13... | collective-permute-start | bytes 73736 | tf_op jit(solution)/shard_map/ppermute | solution.py:356
  8.5 12.1 %collective-permute-start.4 = (f32[24,256]{1,0:T(8,128)S(1)}, f32[24,256]{1,0:T(8,128)S(1)}, u32[]{:S(2)}, u32[]{:S(2)}) collective-permute-start(f32[24,256]{1,0:T(8,128)S(1)} %shard_map.38.refs_0_), channel_id=1, source_target_pairs={{0,10},{2,8},{4,14},{6,12},{8,2},{10,0},{12,6},{14,4},{1,11},{3,9}... | collective-permute-start | bytes 73736 | tf_op jit(solution)/shard_map/ppermute | solution.py:356
  9.3 13.1 %collective-permute-start.3 = (f32[24,256]{1,0:T(8,128)S(1)}, f32[24,256]{1,0:T(8,128)S(1)}, u32[]{:S(2)}, u32[]{:S(2)}) collective-permute-start(f32[24,256]{1,0:T(8,128)S(1)} %shard_map.38.refs_0_), channel_id=1, source_target_pairs={{0,8},{2,10},{4,12},{6,14},{8,0},{10,2},{12,4},{14,6},{1,9},{3,11}... | collective-permute-start | bytes 73736 | tf_op jit(solution)/shard_map/ppermute | solution.py:356
  11.3 12.3 %collective-permute-start.2 = (f32[24,256]{1,0:T(8,128)S(1)}, f32[24,256]{1,0:T(8,128)S(1)}, u32[]{:S(2)}, u32[]{:S(2)}) collective-permute-start(f32[24,256]{1,0:T(8,128)S(1)} %shard_map.38.refs_0_), channel_id=1, source_target_pairs={{0,6},{2,4},{4,2},{6,0},{8,14},{10,12},{12,10},{14,8},{1,7},{3,5},... | collective-permute-start | bytes 73736 | tf_op jit(solution)/shard_map/ppermute | solution.py:356
  14.9 9.3 %collective-permute-start.1 = (f32[24,256]{1,0:T(8,128)S(1)}, f32[24,256]{1,0:T(8,128)S(1)}, u32[]{:S(2)}, u32[]{:S(2)}) collective-permute-start(f32[24,256]{1,0:T(8,128)S(1)} %shard_map.38.refs_0_), channel_id=1, source_target_pairs={{0,4},{2,6},{4,0},{6,2},{8,12},{10,14},{12,8},{14,10},{1,5},{3,7},... | collective-permute-start | bytes 73736 | tf_op jit(solution)/shard_map/ppermute | solution.py:356
  15.8 10.8 %collective-permute-start = (f32[24,256]{1,0:T(8,128)S(1)}, f32[24,256]{1,0:T(8,128)S(1)}, u32[]{:S(2)}, u32[]{:S(2)}) collective-permute-start(f32[24,256]{1,0:T(8,128)S(1)} %shard_map.38.refs_0_), channel_id=1, source_target_pairs={{0,2},{2,0},{4,6},{6,4},{8,10},{10,8},{12,14},{14,12},{1,3},{3,1},... | collective-permute-start | bytes 73736 | tf_op jit(solution)/shard_map/ppermute | solution.py:356
  20.6 9.9 %collective-permute-start.7 = (bf16[128,256]{1,0:T(8,128)(2,1)S(1)}, bf16[128,256]{1,0:T(8,128)(2,1)S(1)}, u32[]{:S(2)}, u32[]{:S(2)}) collective-permute-start(bf16[128,256]{1,0:T(8,128)(2,1)S(1)} %get-tuple-element.76), channel_id=1, source_target_pairs={{0,2},{2,0},{4,6},{6,4},{8,10},{10,8},{12,14},{14,12},{1,3},{3,1},... | collective-permute-start | bytes 196616 | tf_op jit(solution)/shard_map/ppermute | solution.py:356
  22.3 8.9 %collective-permute-start.8 = (bf16[128,256]{1,0:T(8,128)(2,1)S(1)}, bf16[128,256]{1,0:T(8,128)(2,1)S(1)}, u32[]{:S(2)}, u32[]{:S(2)}) collective-permute-start(bf16[128,256]{1,0:T(8,128)(2,1)S(1)} %get-tuple-element.77), channel_id=1, source_target_pairs={{0,4},{2,6},{4,0},{6,2},{8,12},{10,14},{12,8},{14,10},{1,5},{3,7},... | collective-permute-start | bytes 196616 | tf_op jit(solution)/shard_map/ppermute | solution.py:356
  23.6 11.4 %collective-permute-start.9 = (bf16[128,256]{1,0:T(8,128)(2,1)S(1)}, bf16[128,256]{1,0:T(8,128)(2,1)S(1)}, u32[]{:S(2)}, u32[]{:S(2)}) collective-permute-start(bf16[128,256]{1,0:T(8,128)(2,1)S(1)} %get-tuple-element.78), channel_id=1, source_target_pairs={{0,6},{2,4},{4,2},{6,0},{8,14},{10,12},{12,10},{14,8},{1,7},{3,5},... | collective-permute-start | bytes 196616 | tf_op jit(solution)/shard_map/ppermute | solution.py:356
  24.2 11.9 %collective-permute-start.10 = (bf16[128,256]{1,0:T(8,128)(2,1)S(1)}, bf16[128,256]{1,0:T(8,128)(2,1)S(1)}, u32[]{:S(2)}, u32[]{:S(2)}) collective-permute-start(bf16[128,256]{1,0:T(8,128)(2,1)S(1)} %get-tuple-element.79), channel_id=1, source_target_pairs={{0,8},{2,10},{4,12},{6,14},{8,0},{10,2},{12,4},{14,6},{1,9},{3,11}... | collective-permute-start | bytes 196616 | tf_op jit(solution)/shard_map/ppermute | solution.py:356
  26.6 9.9 %collective-permute-start.15 = (bf16[1,128,256]{2,1,0:T(8,128)(2,1)S(1)}, bf16[1,128,256]{2,1,0:T(8,128)(2,1)S(1)}, u32[]{:S(2)}, u32[]{:S(2)}) collective-permute-start(bf16[1,128,256]{2,1,0:T(8,128)(2,1)S(1)} %get-tuple-element.86), channel_id=1, source_target_pairs={{0,2},{2,0},{4,6},{6,4},{8,10},{10,8},{12,14},{14,12},{1,3},{3,1},... | collective-permute-start | bytes 196616 | tf_op jit(solution)/shard_map/ppermute | solution.py:356
  30.6 8.2 %collective-permute-start.11 = (bf16[128,256]{1,0:T(8,128)(2,1)S(1)}, bf16[128,256]{1,0:T(8,128)(2,1)S(1)}, u32[]{:S(2)}, u32[]{:S(2)}) collective-permute-start(bf16[128,256]{1,0:T(8,128)(2,1)S(1)} %get-tuple-element.80), channel_id=1, source_target_pairs={{0,10},{2,8},{4,14},{6,12},{8,2},{10,0},{12,6},{14,4},{1,11},{3,9}... | collective-permute-start | bytes 196616 | tf_op jit(solution)/shard_map/ppermute | solution.py:356
  31.2 8.1 %collective-permute-start.12 = (bf16[128,256]{1,0:T(8,128)(2,1)S(1)}, bf16[128,256]{1,0:T(8,128)(2,1)S(1)}, u32[]{:S(2)}, u32[]{:S(2)}) collective-permute-start(bf16[128,256]{1,0:T(8,128)(2,1)S(1)} %get-tuple-element.81), channel_id=1, source_target_pairs={{0,12},{2,14},{4,8},{6,10},{8,4},{10,6},{12,0},{14,2},{1,13},{3,15... | collective-permute-start | bytes 196616 | tf_op jit(solution)/shard_map/ppermute | solution.py:356
  36.5 9.0 %collective-permute-start.17 = (bf16[1,128,256]{2,1,0:T(8,128)(2,1)S(1)}, bf16[1,128,256]{2,1,0:T(8,128)(2,1)S(1)}, u32[]{:S(2)}, u32[]{:S(2)}) collective-permute-start(bf16[1,128,256]{2,1,0:T(8,128)(2,1)S(1)} %get-tuple-element.88), channel_id=1, source_target_pairs={{0,2},{2,0},{4,6},{6,4},{8,10},{10,8},{12,14},{14,12},{1,3},{3,1},... | collective-permute-start | bytes 196616 | tf_op jit(solution)/shard_map/ppermute | solution.py:356
  39.3 9.2 %collective-permute-start.21 = (bf16[128,256]{1,0:T(8,128)(2,1)S(1)}, bf16[128,256]{1,0:T(8,128)(2,1)S(1)}, u32[]{:S(2)}, u32[]{:S(2)}) collective-permute-start(bf16[128,256]{1,0:T(8,128)(2,1)S(1)} %get-tuple-element.92), channel_id=1, source_target_pairs={{0,2},{2,0},{4,6},{6,4},{8,10},{10,8},{12,14},{14,12},{1,3},{3,1},... | collective-permute-start | bytes 196616 | tf_op jit(solution)/shard_map/ppermute | solution.py:356
  42.0 8.5 %collective-permute-start.23 = (bf16[128,256]{1,0:T(8,128)(2,1)S(1)}, bf16[128,256]{1,0:T(8,128)(2,1)S(1)}, u32[]{:S(2)}, u32[]{:S(2)}) collective-permute-start(bf16[128,256]{1,0:T(8,128)(2,1)S(1)} %get-tuple-element.94), channel_id=1, source_target_pairs={{0,6},{2,4},{4,2},{6,0},{8,14},{10,12},{12,10},{14,8},{1,7},{3,5},... | collective-permute-start | bytes 196616 | tf_op jit(solution)/shard_map/ppermute | solution.py:356
  45.5 7.8 %collective-permute-start.24 = (bf16[128,256]{1,0:T(8,128)(2,1)S(1)}, bf16[128,256]{1,0:T(8,128)(2,1)S(1)}, u32[]{:S(2)}, u32[]{:S(2)}) collective-permute-start(bf16[128,256]{1,0:T(8,128)(2,1)S(1)} %get-tuple-element.95), channel_id=1, source_target_pairs={{0,8},{2,10},{4,12},{6,14},{8,0},{10,2},{12,4},{14,6},{1,9},{3,11}... | collective-permute-start | bytes 196616 | tf_op jit(solution)/shard_map/ppermute | solution.py:356
  46.1 16.7 %collective-permute-start.33 = (bf16[1,128,256]{2,1,0:T(8,128)(2,1)S(1)}, bf16[1,128,256]{2,1,0:T(8,128)(2,1)S(1)}, u32[]{:S(2)}, u32[]{:S(2)}) collective-permute-start(bf16[1,128,256]{2,1,0:T(8,128)(2,1)S(1)} %get-tuple-element.99.refs_8_), channel_id=1, source_target_pairs={{0,12},{2,14},{4,8},{6,10},{8,4},{10,6},{12,0},{14,2},{1,13},{3,15... | collective-permute-start | bytes 196616 | tf_op jit(solution)/shard_map/ppermute | solution.py:356
  48.5 16.7 %collective-permute-start.31 = (bf16[1,128,256]{2,1,0:T(8,128)(2,1)S(1)}, bf16[1,128,256]{2,1,0:T(8,128)(2,1)S(1)}, u32[]{:S(2)}, u32[]{:S(2)}) collective-permute-start(bf16[1,128,256]{2,1,0:T(8,128)(2,1)S(1)} %get-tuple-element.99.refs_8_), channel_id=1, source_target_pairs={{0,8},{2,10},{4,12},{6,14},{8,0},{10,2},{12,4},{14,6},{1,9},{3,11}... | collective-permute-start | bytes 196616 | tf_op jit(solution)/shard_map/ppermute | solution.py:356
  49.3 16.8 %collective-permute-start.29 = (bf16[1,128,256]{2,1,0:T(8,128)(2,1)S(1)}, bf16[1,128,256]{2,1,0:T(8,128)(2,1)S(1)}, u32[]{:S(2)}, u32[]{:S(2)}) collective-permute-start(bf16[1,128,256]{2,1,0:T(8,128)(2,1)S(1)} %get-tuple-element.99.refs_8_), channel_id=1, source_target_pairs={{0,4},{2,6},{4,0},{6,2},{8,12},{10,14},{12,8},{14,10},{1,5},{3,7},... | collective-permute-start | bytes 196616 | tf_op jit(solution)/shard_map/ppermute | solution.py:356
  50.6 8.2 %collective-permute-start.25 = (bf16[128,256]{1,0:T(8,128)(2,1)S(1)}, bf16[128,256]{1,0:T(8,128)(2,1)S(1)}, u32[]{:S(2)}, u32[]{:S(2)}) collective-permute-start(bf16[128,256]{1,0:T(8,128)(2,1)S(1)} %get-tuple-element.96), channel_id=1, source_target_pairs={{0,10},{2,8},{4,14},{6,12},{8,2},{10,0},{12,6},{14,4},{1,11},{3,9}... | collective-permute-start | bytes 196616 | tf_op jit(solution)/shard_map/ppermute | solution.py:356
  58.7 9.4 %collective-permute-start.16 = (bf16[1,128,256]{2,1,0:T(8,128)(2,1)S(1)}, bf16[1,128,256]{2,1,0:T(8,128)(2,1)S(1)}, u32[]{:S(2)}, u32[]{:S(2)}) collective-permute-start(bf16[1,128,256]{2,1,0:T(8,128)(2,1)S(1)} %broadcast_select_fusion.5), channel_id=1, source_target_pairs={{0,4},{2,6},{4,0},{6,2},{8,12},{10,14},{12,8},{14,10},{1,5},{3,7},... | collective-permute-start | bytes 196616 | tf_op jit(solution)/shard_map/ppermute | solution.py:356
  59.3 9.6 %collective-permute-start.18 = (bf16[1,128,256]{2,1,0:T(8,128)(2,1)S(1)}, bf16[1,128,256]{2,1,0:T(8,128)(2,1)S(1)}, u32[]{:S(2)}, u32[]{:S(2)}) collective-permute-start(bf16[1,128,256]{2,1,0:T(8,128)(2,1)S(1)} %broadcast_select_fusion.3), channel_id=1, source_target_pairs={{0,8},{2,10},{4,12},{6,14},{8,0},{10,2},{12,4},{14,6},{1,9},{3,11}... | collective-permute-start | bytes 196616 | tf_op jit(solution)/shard_map/ppermute | solution.py:356
  65.2 7.9 %collective-permute-start.28 = (bf16[1,128,256]{2,1,0:T(8,128)(2,1)S(1)}, bf16[1,128,256]{2,1,0:T(8,128)(2,1)S(1)}, u32[]{:S(2)}, u32[]{:S(2)}) collective-permute-start(bf16[1,128,256]{2,1,0:T(8,128)(2,1)S(1)} %get-tuple-element.99.refs_8_), channel_id=1, source_target_pairs={{0,2},{2,0},{4,6},{6,4},{8,10},{10,8},{12,14},{14,12},{1,3},{3,1},... | collective-permute-start | bytes 196616 | tf_op jit(solution)/shard_map/ppermute | solution.py:356
  90.3 7.9 %collective-permute-start.37 = (f32[24,128]{1,0:T(8,128)S(1)}, f32[24,128]{1,0:T(8,128)S(1)}, u32[]{:S(2)}, u32[]{:S(2)}) collective-permute-start(f32[24,128]{1,0:T(8,128)S(1)} %get-tuple-element.102), channel_id=1, source_target_pairs={{0,4},{2,6},{4,0},{6,2},{8,12},{10,14},{12,8},{14,10},{1,5},{3,7},... | collective-permute-start | bytes 36872 | tf_op jit(solution)/shard_map/ppermute | solution.py:356
  90.3 10.0 %collective-permute-start.38 = (f32[24,128]{1,0:T(8,128)S(1)}, f32[24,128]{1,0:T(8,128)S(1)}, u32[]{:S(2)}, u32[]{:S(2)}) collective-permute-start(f32[24,128]{1,0:T(8,128)S(1)} %get-tuple-element.103), channel_id=1, source_target_pairs={{0,6},{2,4},{4,2},{6,0},{8,14},{10,12},{12,10},{14,8},{1,7},{3,5},... | collective-permute-start | bytes 36872 | tf_op jit(solution)/shard_map/ppermute | solution.py:356
  104.7 7.8 %collective-permute-start.50 = (f32[24,128]{1,0:T(8,128)S(1)}, f32[24,128]{1,0:T(8,128)S(1)}, u32[]{:S(2)}, u32[]{:S(2)}) collective-permute-start(f32[24,128]{1,0:T(8,128)S(1)} %add_add_fusion.1.refs_0_), channel_id=1, source_target_pairs={{0,1},{1,0},{2,3},{3,2},{4,5},{5,4},{6,7},{7,6},{8,9},{9,8},{10,11... | collective-permute-start | bytes 36872 | tf_op jit(solution)/shard_map/ppermute | solution.py:359
  104.7 7.7 %collective-permute-start.49 = (f32[24,128]{1,0:T(8,128)S(1)}, f32[24,128]{1,0:T(8,128)S(1)}, u32[]{:S(2)}, u32[]{:S(2)}) collective-permute-start(f32[24,128]{1,0:T(8,128)S(1)} %add_add_fusion.1.refs_0_), channel_id=1, source_target_pairs={{0,14},{2,12},{4,10},{6,8},{8,6},{10,4},{12,2},{14,0},{1,15},{3,13... | collective-permute-start | bytes 36872 | tf_op jit(solution)/shard_map/ppermute | solution.py:356
  106.9 8.3 %collective-permute-start.48 = (f32[24,128]{1,0:T(8,128)S(1)}, f32[24,128]{1,0:T(8,128)S(1)}, u32[]{:S(2)}, u32[]{:S(2)}) collective-permute-start(f32[24,128]{1,0:T(8,128)S(1)} %add_add_fusion.1.refs_0_), channel_id=1, source_target_pairs={{0,12},{2,14},{4,8},{6,10},{8,4},{10,6},{12,0},{14,2},{1,13},{3,15... | collective-permute-start | bytes 36872 | tf_op jit(solution)/shard_map/ppermute | solution.py:356
  140.0 8.4 %collective-permute-start.60 = (bf16[128,256]{1,0:T(8,128)(2,1)S(1)}, bf16[128,256]{1,0:T(8,128)(2,1)S(1)}, u32[]{:S(2)}, u32[]{:S(2)}) collective-permute-start(bf16[128,256]{1,0:T(8,128)(2,1)S(1)} %get-tuple-element.111), channel_id=1, source_target_pairs={{0,6},{2,4},{4,2},{6,0},{8,14},{10,12},{12,10},{14,8},{1,7},{3,5},... | collective-permute-start | bytes 196616 | tf_op jit(solution)/shard_map/ppermute | solution.py:356
  142.5 8.4 %collective-permute-start.61 = (bf16[128,256]{1,0:T(8,128)(2,1)S(1)}, bf16[128,256]{1,0:T(8,128)(2,1)S(1)}, u32[]{:S(2)}, u32[]{:S(2)}) collective-permute-start(bf16[128,256]{1,0:T(8,128)(2,1)S(1)} %get-tuple-element.112), channel_id=1, source_target_pairs={{0,8},{2,10},{4,12},{6,14},{8,0},{10,2},{12,4},{14,6},{1,9},{3,11}... | collective-permute-start | bytes 196616 | tf_op jit(solution)/shard_map/ppermute | solution.py:356
  142.6 9.6 %collective-permute-start.66 = (bf16[1,128,256]{2,1,0:T(8,128)(2,1)S(1)}, bf16[1,128,256]{2,1,0:T(8,128)(2,1)S(1)}, u32[]{:S(2)}, u32[]{:S(2)}) collective-permute-start(bf16[1,128,256]{2,1,0:T(8,128)(2,1)S(1)} %get-tuple-element.119), channel_id=1, source_target_pairs={{0,2},{2,0},{4,6},{6,4},{8,10},{10,8},{12,14},{14,12},{1,3},{3,1},... | collective-permute-start | bytes 196616 | tf_op jit(solution)/shard_map/ppermute | solution.py:356
  143.7 10.1 %collective-permute-start.62 = (bf16[128,256]{1,0:T(8,128)(2,1)S(1)}, bf16[128,256]{1,0:T(8,128)(2,1)S(1)}, u32[]{:S(2)}, u32[]{:S(2)}) collective-permute-start(bf16[128,256]{1,0:T(8,128)(2,1)S(1)} %get-tuple-element.113), channel_id=1, source_target_pairs={{0,10},{2,8},{4,14},{6,12},{8,2},{10,0},{12,6},{14,4},{1,11},{3,9}... | collective-permute-start | bytes 196616 | tf_op jit(solution)/shard_map/ppermute | solution.py:356
  146.9 8.2 %collective-permute-start.63 = (bf16[128,256]{1,0:T(8,128)(2,1)S(1)}, bf16[128,256]{1,0:T(8,128)(2,1)S(1)}, u32[]{:S(2)}, u32[]{:S(2)}) collective-permute-start(bf16[128,256]{1,0:T(8,128)(2,1)S(1)} %get-tuple-element.114), channel_id=1, source_target_pairs={{0,12},{2,14},{4,8},{6,10},{8,4},{10,6},{12,0},{14,2},{1,13},{3,15... | collective-permute-start | bytes 196616 | tf_op jit(solution)/shard_map/ppermute | solution.py:356
  155.0 7.9 %collective-permute-start.72 = (bf16[128,256]{1,0:T(8,128)(2,1)S(1)}, bf16[128,256]{1,0:T(8,128)(2,1)S(1)}, u32[]{:S(2)}, u32[]{:S(2)}) collective-permute-start(bf16[128,256]{1,0:T(8,128)(2,1)S(1)} %get-tuple-element.125), channel_id=1, source_target_pairs={{0,2},{2,0},{4,6},{6,4},{8,10},{10,8},{12,14},{14,12},{1,3},{3,1},... | collective-permute-start | bytes 196616 | tf_op jit(solution)/shard_map/ppermute | solution.py:356
  157.3 8.1 %collective-permute-start.74 = (bf16[128,256]{1,0:T(8,128)(2,1)S(1)}, bf16[128,256]{1,0:T(8,128)(2,1)S(1)}, u32[]{:S(2)}, u32[]{:S(2)}) collective-permute-start(bf16[128,256]{1,0:T(8,128)(2,1)S(1)} %get-tuple-element.127), channel_id=1, source_target_pairs={{0,6},{2,4},{4,2},{6,0},{8,14},{10,12},{12,10},{14,8},{1,7},{3,5},... | collective-permute-start | bytes 196616 | tf_op jit(solution)/shard_map/ppermute | solution.py:356
  161.0 16.1 %collective-permute-start.84 = (bf16[1,128,256]{2,1,0:T(8,128)(2,1)S(1)}, bf16[1,128,256]{2,1,0:T(8,128)(2,1)S(1)}, u32[]{:S(2)}, u32[]{:S(2)}) collective-permute-start(bf16[1,128,256]{2,1,0:T(8,128)(2,1)S(1)} %get-tuple-element.132.refs_8_), channel_id=1, source_target_pairs={{0,12},{2,14},{4,8},{6,10},{8,4},{10,6},{12,0},{14,2},{1,13},{3,15... | collective-permute-start | bytes 196616 | tf_op jit(solution)/shard_map/ppermute | solution.py:356
  163.0 16.1 %collective-permute-start.82 = (bf16[1,128,256]{2,1,0:T(8,128)(2,1)S(1)}, bf16[1,128,256]{2,1,0:T(8,128)(2,1)S(1)}, u32[]{:S(2)}, u32[]{:S(2)}) collective-permute-start(bf16[1,128,256]{2,1,0:T(8,128)(2,1)S(1)} %get-tuple-element.132.refs_8_), channel_id=1, source_target_pairs={{0,8},{2,10},{4,12},{6,14},{8,0},{10,2},{12,4},{14,6},{1,9},{3,11}... | collective-permute-start | bytes 196616 | tf_op jit(solution)/shard_map/ppermute | solution.py:356
  163.0 17.3 %collective-permute-start.80 = (bf16[1,128,256]{2,1,0:T(8,128)(2,1)S(1)}, bf16[1,128,256]{2,1,0:T(8,128)(2,1)S(1)}, u32[]{:S(2)}, u32[]{:S(2)}) collective-permute-start(bf16[1,128,256]{2,1,0:T(8,128)(2,1)S(1)} %get-tuple-element.132.refs_8_), channel_id=1, source_target_pairs={{0,4},{2,6},{4,0},{6,2},{8,12},{10,14},{12,8},{14,10},{1,5},{3,7},... | collective-permute-start | bytes 196616 | tf_op jit(solution)/shard_map/ppermute | solution.py:356
  165.4 9.2 %collective-permute-start.76 = (bf16[128,256]{1,0:T(8,128)(2,1)S(1)}, bf16[128,256]{1,0:T(8,128)(2,1)S(1)}, u32[]{:S(2)}, u32[]{:S(2)}) collective-permute-start(bf16[128,256]{1,0:T(8,128)(2,1)S(1)} %get-tuple-element.129), channel_id=1, source_target_pairs={{0,10},{2,8},{4,14},{6,12},{8,2},{10,0},{12,6},{14,4},{1,11},{3,9}... | collective-permute-start | bytes 196616 | tf_op jit(solution)/shard_map/ppermute | solution.py:356
  166.3 8.4 %collective-permute-start.77 = (bf16[128,256]{1,0:T(8,128)(2,1)S(1)}, bf16[128,256]{1,0:T(8,128)(2,1)S(1)}, u32[]{:S(2)}, u32[]{:S(2)}) collective-permute-start(bf16[128,256]{1,0:T(8,128)(2,1)S(1)} %get-tuple-element.130), channel_id=1, source_target_pairs={{0,12},{2,14},{4,8},{6,10},{8,4},{10,6},{12,0},{14,2},{1,13},{3,15... | collective-permute-start | bytes 196616 | tf_op jit(solution)/shard_map/ppermute | solution.py:356
  174.7 8.8 %collective-permute-start.69 = (bf16[1,128,256]{2,1,0:T(8,128)(2,1)S(1)}, bf16[1,128,256]{2,1,0:T(8,128)(2,1)S(1)}, u32[]{:S(2)}, u32[]{:S(2)}) collective-permute-start(bf16[1,128,256]{2,1,0:T(8,128)(2,1)S(1)} %broadcast_select_fusion.2), channel_id=1, source_target_pairs={{0,8},{2,10},{4,12},{6,14},{8,0},{10,2},{12,4},{14,6},{1,9},{3,11}... | collective-permute-start | bytes 196616 | tf_op jit(solution)/shard_map/ppermute | solution.py:356
  179.0 8.4 %collective-permute-start.79 = (bf16[1,128,256]{2,1,0:T(8,128)(2,1)S(1)}, bf16[1,128,256]{2,1,0:T(8,128)(2,1)S(1)}, u32[]{:S(2)}, u32[]{:S(2)}) collective-permute-start(bf16[1,128,256]{2,1,0:T(8,128)(2,1)S(1)} %get-tuple-element.132.refs_8_), channel_id=1, source_target_pairs={{0,2},{2,0},{4,6},{6,4},{8,10},{10,8},{12,14},{14,12},{1,3},{3,1},... | collective-permute-start | bytes 196616 | tf_op jit(solution)/shard_map/ppermute | solution.py:356
  204.3 8.0 %collective-permute-start.88 = (f32[24,128]{1,0:T(8,128)S(1)}, f32[24,128]{1,0:T(8,128)S(1)}, u32[]{:S(2)}, u32[]{:S(2)}) collective-permute-start(f32[24,128]{1,0:T(8,128)S(1)} %get-tuple-element.135), channel_id=1, source_target_pairs={{0,4},{2,6},{4,0},{6,2},{8,12},{10,14},{12,8},{14,10},{1,5},{3,7},... | collective-permute-start | bytes 36872 | tf_op jit(solution)/shard_map/ppermute | solution.py:356
  204.5 9.8 %collective-permute-start.89 = (f32[24,128]{1,0:T(8,128)S(1)}, f32[24,128]{1,0:T(8,128)S(1)}, u32[]{:S(2)}, u32[]{:S(2)}) collective-permute-start(f32[24,128]{1,0:T(8,128)S(1)} %get-tuple-element.136), channel_id=1, source_target_pairs={{0,6},{2,4},{4,2},{6,0},{8,14},{10,12},{12,10},{14,8},{1,7},{3,5},... | collective-permute-start | bytes 36872 | tf_op jit(solution)/shard_map/ppermute | solution.py:356
  218.7 7.8 %collective-permute-start.101 = (f32[24,128]{1,0:T(8,128)S(1)}, f32[24,128]{1,0:T(8,128)S(1)}, u32[]{:S(2)}, u32[]{:S(2)}) collective-permute-start(f32[24,128]{1,0:T(8,128)S(1)} %add_add_fusion.refs_0_), channel_id=1, source_target_pairs={{0,1},{1,0},{2,3},{3,2},{4,5},{5,4},{6,7},{7,6},{8,9},{9,8},{10,11... | collective-permute-start | bytes 36872 | tf_op jit(solution)/shard_map/ppermute | solution.py:359
  218.7 7.7 %collective-permute-start.100 = (f32[24,128]{1,0:T(8,128)S(1)}, f32[24,128]{1,0:T(8,128)S(1)}, u32[]{:S(2)}, u32[]{:S(2)}) collective-permute-start(f32[24,128]{1,0:T(8,128)S(1)} %add_add_fusion.refs_0_), channel_id=1, source_target_pairs={{0,14},{2,12},{4,10},{6,8},{8,6},{10,4},{12,2},{14,0},{1,15},{3,13... | collective-permute-start | bytes 36872 | tf_op jit(solution)/shard_map/ppermute | solution.py:356
  220.9 8.0 %collective-permute-start.99 = (f32[24,128]{1,0:T(8,128)S(1)}, f32[24,128]{1,0:T(8,128)S(1)}, u32[]{:S(2)}, u32[]{:S(2)}) collective-permute-start(f32[24,128]{1,0:T(8,128)S(1)} %add_add_fusion.refs_0_), channel_id=1, source_target_pairs={{0,12},{2,14},{4,8},{6,10},{8,4},{10,6},{12,0},{14,2},{1,13},{3,15... | collective-permute-start | bytes 36872 | tf_op jit(solution)/shard_map/ppermute | solution.py:356
  (65 other events, 360.4 us)

commit v3 on v2

v3 whole, which is shorter than its diff:
```python
import jax
import jax.numpy as jnp
from jax import lax
from jax.experimental import pallas as pl
from jax.experimental.pallas import tpu as pltpu
from jax.sharding import PartitionSpec as P

MIB = 1 << 20
HIGHEST = lax.Precision.HIGHEST
VMEM = pl.BlockSpec(memory_space=pltpu.VMEM)
SMEM = pl.BlockSpec(memory_space=pltpu.SMEM)
ANY = pl.BlockSpec(memory_space=pl.ANY)
shape = jax.ShapeDtypeStruct
f32, bf16, i32 = jnp.float32, jnp.bfloat16, jnp.int32


def contract(a, b, a_dim, b_dim, precision=None):
    return lax.dot_general(
        a,
        b,
        (((a_dim,), (b_dim,)), ((), ())),
        precision=precision,
        preferred_element_type=f32,
    )


def call(kernel, out_shape, in_specs, out_specs=None, scratch=(), flops=0, vmem=32):
    if out_specs is None:
        out_specs = jax.tree.map(lambda _: VMEM, out_shape)
    return pl.pallas_call(
        kernel,
        out_shape=out_shape,
        in_specs=in_specs,
        out_specs=out_specs,
        scratch_shapes=list(scratch),
        compiler_params=pltpu.CompilerParams(vmem_limit_bytes=vmem * MIB),
        cost_estimate=pl.CostEstimate(flops=flops, bytes_accessed=4 * MIB, transcendentals=0),
    )


class Table:
    def __init__(self, groups, nnz):
        self.groups, self.nnz, self.hot = groups, nnz, nnz - groups
        self.main_j = 0
        self.hot_j = self.main_j + groups
        self.row_i = self.hot_j + groups * self.hot
        self.dest = self.row_i + nnz
        self.col = self.dest + nnz

    def build(self, block_pairs, me, my_col):
        groups = self.groups
        mine = lax.dynamic_index_in_dim(block_pairs, me, 0, keepdims=False)
        main = block_pairs[:, :groups]
        main_j = jnp.sum(jnp.where(main[:, :, 1] == me, main[:, :, 2], 0), axis=1)
        late = jnp.take(block_pairs[:, groups:], me ^ jnp.arange(groups), axis=0)
        hot_j = jnp.where(late[:, :, 1] == me, late[:, :, 2], -1).reshape(-1)
        parts = [main_j, hot_j, mine[:, 0], mine[:, 1], my_col[None]]
        return jnp.concatenate([p.astype(i32) for p in parts]), late[:, :, 1] ^ me


def sums_kernel(counts_ref, sums_ref):
    nnz, rows, cols = counts_ref.shape
    ones = jnp.ones((8, cols), bf16)
    sums_ref[0] = jnp.zeros(sums_ref.shape[1:], f32)
    for s in range(nnz):
        block = counts_ref[s].astype(bf16)
        sums_ref[0, pl.ds(s, 1), :] = contract(ones, block, 1, 1)[0:1, :]
        sums_ref[0, pl.ds(nnz + s, 1), :] = contract(ones, block, 1, 0)[0:1, :]
    for r in range(1, sums_ref.shape[0]):
        sums_ref[r] = sums_ref[0]


def gather_main(t, tab, blocks, send):
    for r in range(t.groups):
        send[r, 1] = blocks[tab[t.main_j + r]]


def gather_hot(t, tab, blocks, near, far):
    for k in range(t.groups):
        for m in range(t.hot):
            j = tab[t.hot_j + k * t.hot + m]

            @pl.when(j >= 0)
            def _():
                (far if k % 2 else near)[k // 2, m] = blocks[j]


def products(t, tab, blocks, ppmi, send, hot):
    for s in range(t.nnz):
        value = contract(blocks[tab[t.row_i + s]], ppmi[s], 1, 0).astype(bf16)
        if s < t.groups:
            send[tab[t.dest + s], 0] = value
        else:
            hot[0, s - t.groups] = value


def make_source_kernel(t):
    def kernel(tab, sketch_ref, turned, near, far):
        @pl.loop(0, sketch_ref.shape[0])
        def _(i):
            turned[i] = sketch_ref[i].T

        gather_hot(t, tab, turned, near, far)

    return kernel


def make_ppmi_kernel(t):
    def kernel(tab, match_ref, counts_ref, turned, sums_ref, ppmi_ref, send, hot, cols_log):
        sums = jnp.concatenate([sums_ref[r] for r in range(t.groups)], axis=0)
        high = jnp.floor(sums * (1.0 / 256.0))
        low = sums - high * 256.0
        match = match_ref[...]
        margins = 256.0 * contract(match, high.astype(bf16), 1, 0) + contract(
            match, low.astype(bf16), 1, 0
        )
        log_total = jnp.log(jnp.sum(sums))
        log_margin = jnp.log(margins)
        cols_log[...] = log_margin
        fill = 128 - log_margin.shape[0] % 128
        row_log = jnp.concatenate(
            [log_margin, jnp.zeros((fill, log_margin.shape[1]), f32)], axis=0
        ).T
        for s in range(t.nnz):
            counts = counts_ref[s]
            scores = (
                jnp.log(counts.astype(f32))
                + log_total
                - row_log[:, s : s + 1]
                - cols_log[pl.ds(t.nnz + s, 1), :]
            )
            ppmi_ref[s] = jnp.where(counts > 0, jnp.maximum(scores, 0.0), 0.0).astype(bf16)
        gather_main(t, tab, turned, send)
        products(t, tab, turned, ppmi_ref, send, hot)

    return kernel


def make_result_kernel(t, order):
    def kernel(tab, ppmi_ref, got, hot_x, hot_a, hot_b, result):
        result[...] = jnp.zeros_like(result)
        for s in range(t.nnz):
            block = got[tab[t.dest + s], 1] if s < t.groups else hot_x[0, s - t.groups]
            forward = contract(block, ppmi_ref[s], 1, 1).astype(bf16)
            result[tab[t.row_i + s]] += forward.astype(f32)
        for r in range(t.groups):
            result[tab[t.main_j + r]] += got[r, 0].astype(f32)
        for n, k in enumerate(order):
            ref, place = (hot_a, n) if n < t.groups // 2 else (hot_b, n - t.groups // 2)
            for m in range(t.hot):
                j = tab[t.hot_j + k * t.hot + m]

                @pl.when(j >= 0)
                def _():
                    result[j] += ref[place, m].astype(f32)

    return kernel


def split(x):
    high = x.astype(bf16)
    rest = x - high.astype(f32)
    mid = rest.astype(bf16)
    return high, mid, (rest - mid.astype(f32)).astype(bf16)


def lanes(ref, start, count, rows=None):
    picked = [ref[start + n] if rows is None else ref[start + n, rows, :] for n in range(count)]
    return jnp.concatenate(picked, axis=1)


def own_gram_kernel(own, gram):
    blocks, half, _ = own.shape
    step = 4
    square = jnp.zeros((half, half), f32)
    skew = jnp.zeros((half, half), f32)
    for i in range(0, blocks, step):
        high, mid, low = split(lanes(own, i, step))
        stack = contract(jnp.concatenate([high, mid, low], axis=0), high, 1, 1)
        square += stack[0:half] + contract(mid, mid, 1, 1)
        skew += stack[half : 2 * half] + stack[2 * half :]
    gram[...] = square + (skew + skew.T)


def make_cross_gram_kernel(t):
    def kernel(tab, own, other, square, gram):
        blocks, half, _ = own.shape
        cut = half // 2
        step = 4
        gram[pl.ds(0, half), :] = square[...]

        def cross(left, rows, right):
            total = jnp.zeros((cut, half), f32)
            for i in range(0, blocks, step):
                high, mid, low = split(lanes(left, i, step, rows))
                r_high, r_mid, r_low = split(lanes(right, i, step))
                by_high = contract(jnp.concatenate([high, mid, low], axis=0), r_high, 1, 1)
                by_mid = contract(jnp.concatenate([high, mid], axis=0), r_mid, 1, 1)
                small = by_high[2 * cut :] + by_mid[cut:] + contract(high, r_low, 1, 1)
                total += by_high[:cut] + (by_high[cut : 2 * cut] + by_mid[:cut] + small)
            gram[pl.ds(half, cut), :] = total

        @pl.when(tab[t.col] == 0)
        def _():
            cross(other, pl.ds(0, cut), own)

        @pl.when(tab[t.col] == 1)
        def _():
            cross(own, pl.ds(cut, cut), other)

    return kernel


def inverse_factor(block):
    size = block.shape[0]
    tiles = size // 8
    full = (8, size)
    lane = lax.broadcasted_iota(i32, full, 1)
    sub = lax.broadcasted_iota(i32, full, 0)
    left = [block[8 * t : 8 * t + 8, :] for t in range(tiles)]
    right = [(lane == sub + 8 * t).astype(f32) for t in range(tiles)]
    for j in range(tiles):
        cols = [jnp.broadcast_to(left[j][:, 8 * j + k : 8 * j + k + 1], full) for k in range(8)]
        pivot = [
            [jnp.broadcast_to(cols[k][i : i + 1, :], full) for k in range(i + 1)] for i in range(8)
        ]
        row_l = [jnp.broadcast_to(left[j][i : i + 1, :], full) for i in range(8)]
        row_r = [jnp.broadcast_to(right[j][i : i + 1, :], full) for i in range(8)]
        scale = []
        for k in range(8):
            scale.append(lax.rsqrt(pivot[k][k]))
            for i in range(k + 1, 8):
                pivot[i][k] = pivot[i][k] * scale[k]
            for i in range(k + 1, 8):
                for m in range(k + 1, i + 1):
                    pivot[i][m] = pivot[i][m] - pivot[i][k] * pivot[m][k]
            row_l[k] = row_l[k] * scale[k]
            row_r[k] = row_r[k] * scale[k]
            for i in range(k + 1, 8):
                row_l[i] = row_l[i] - pivot[i][k] * row_l[k]
                row_r[i] = row_r[i] - pivot[i][k] * row_r[k]
        done = row_r[0]
        for i in range(1, 8):
            done = jnp.where(sub == i, row_r[i], done)
        right[j] = done
        if j < tiles - 1:
            for k in range(7, -1, -1):
                row_l[k] = row_l[k] * scale[k]
                row_r[k] = row_r[k] * scale[k]
                for i in range(k):
                    row_l[i] = row_l[i] - pivot[k][i] * row_l[k]
                    row_r[i] = row_r[i] - pivot[k][i] * row_r[k]
            for t in range(j + 1, tiles):
                cur = left[t]
                new_l, new_r = cur, right[t]
                for k in range(8):
                    col = jnp.broadcast_to(cur[:, 8 * j + k : 8 * j + k + 1], full)
                    new_l = new_l - col * row_l[k]
                    new_r = new_r - col * row_r[k]
                left[t], right[t] = new_l, new_r
    return jnp.concatenate(right, axis=0)


def invert(t, tab, own, other, gram, inverse, scale):
    half = own.shape[1]
    cut = half // 2
    my_col = tab[t.col]
    gram[my_col] = own[...] * scale
    gram[1 - my_col] = other[...] * scale
    low = inverse_factor(gram[0, pl.ds(0, half), :])
    lower = jnp.concatenate([gram[0, pl.ds(half, cut), :], gram[1, pl.ds(half, cut), :]], axis=0)
    across = contract(lower, low, 1, 1, HIGHEST)
    high = inverse_factor(
        gram[1, pl.ds(0, half), :] - contract(across, across, 1, 1, HIGHEST)
    )
    inverse[0, 0] = low
    inverse[0, 1] = jnp.zeros_like(low)
    inverse[1, 0] = -contract(high, contract(across, low, 1, 0, HIGHEST), 1, 0, HIGHEST)
    inverse[1, 1] = high


def normal_blocks(t, tab, inverse, mine, other, store):
    my_col = tab[t.col]
    half = mine.shape[1]
    factor = jnp.concatenate([inverse[my_col, my_col], inverse[my_col, 1 - my_col]], axis=1)
    high, mid, low = split(factor)
    three = jnp.concatenate([high, mid, low], axis=0)
    two = jnp.concatenate([high, mid], axis=0)

    @pl.loop(0, mine.shape[0])
    def _(i):
        y_high, y_mid, y_low = split(jnp.concatenate([mine[i], other[i]], axis=0))
        by_high = contract(three, y_high, 1, 0)
        by_mid = contract(two, y_mid, 1, 0)
        small = by_high[2 * half :] + by_mid[half:] + contract(high, y_low, 1, 0)
        store(i, by_high[:half] + (by_high[half : 2 * half] + by_mid[:half] + small))


def start_copies(pairs, sems):
    copies = [pltpu.make_async_copy(a, b, sems.at[n]) for n, (a, b) in enumerate(pairs)]
    for copy in copies:
        copy.start()
    return copies


def make_second_kernel(t, scale):
    def kernel(
        tab, own_g, other_g, mine_hbm, other_hbm, ppmi_hbm, send, near, far, hot,
        gram, inverse, normal, mine, other, ppmi, sems,
    ):
        copies = start_copies([(mine_hbm, mine), (other_hbm, other), (ppmi_hbm, ppmi)], sems)
        invert(t, tab, own_g, other_g, gram, inverse, scale)
        for copy in copies:
            copy.wait()

        def store(i, value):
            normal[i] = value.astype(bf16)

        normal_blocks(t, tab, inverse, mine, other, store)
        gather_main(t, tab, normal, send)
        gather_hot(t, tab, normal, near, far)
        products(t, tab, normal, ppmi, send, hot)

    return kernel


def make_final_kernel(t, scale):
    def kernel(tab, own_g, other_g, mine_hbm, other_hbm, out, gram, inverse, mine, other, sems):
        copies = start_copies([(mine_hbm, mine), (other_hbm, other)], sems)
        invert(t, tab, own_g, other_g, gram, inverse, scale)
        for copy in copies:
            copy.wait()

        def store(i, value):
            out[i] = value.T

        normal_blocks(t, tab, inverse, mine, other, store)

    return kernel


def body(counts, block_pairs, sketch):
    groups = lax.axis_size("row")
    me = lax.axis_index("row")
    my_col = lax.axis_index("col")
    nnz, rows, _ = counts.shape
    blocks, _, half = sketch.shape
    vocab = blocks * rows * groups
    t = Table(groups, nnz)
    hot = t.hot
    depth = -(-2 * nnz // 8) * 8
    bits = [1 << b for b in range(groups.bit_length() - 1)]

    def peer(x, k):
        return lax.ppermute(x, "row", [(r, r ^ k) for r in range(groups)])

    def swap(x):
        return lax.ppermute(x, "col", [(0, 1), (1, 0)])

    def exchange(x):
        return lax.all_to_all(x, "row", split_axis=0, concat_axis=0, tiled=True)

    def add_up(x):
        for bit in bits:
            x = x + peer(x, bit)
        return x

    def spread_hot(part):
        for bit in bits[:0:-1]:
            part = jnp.concatenate([part, peer(part, bit)], axis=0)
        return part, peer(part, bits[0])

    hot_order = [0]
    for bit in bits[::-1]:
        hot_order += [k ^ bit for k in hot_order]

    def scatter_hot(near, far, towards):
        for bit in bits:
            got = peer(far, bit)
            towards = towards[::2]
            stay = (towards & bit) == 0
            part = jnp.where(stay[:, :, None, None], near, got)
            near, far = part[::2], part[1::2]
        return part

    send_shape = shape((groups, 2, half, rows), bf16)
    hot_shape = shape((1, hot, half, rows), bf16)
    side_shape = shape((groups // 2, hot, half, rows), bf16)
    ppmi_shape = shape((nnz, rows, rows), bf16)
    result_shape = shape((blocks, half, rows), f32)

    sums = call(sums_kernel, shape((groups, depth, rows), f32), [VMEM])(counts)
    sums_all = exchange(sums)
    tab, towards = t.build(block_pairs, me, my_col)
    turned, near, far = call(
        make_source_kernel(t),
        [shape((blocks, half, rows), bf16), side_shape, side_shape],
        [SMEM, VMEM],
    )(tab, sketch)
    hot_x = scatter_hot(near, far, towards)

    row_ids = block_pairs[:, :, 0] * groups + jnp.arange(groups)[:, None]
    col_ids = block_pairs[:, :, 2] * groups + block_pairs[:, :, 1]
    no_id = jnp.full((groups, depth - 2 * nnz), -1, i32)
    ids = jnp.concatenate([row_ids, col_ids, no_id], axis=1)
    my_ids = lax.dynamic_index_in_dim(ids, me, 0, keepdims=False)
    match = (my_ids[:, None] == ids.reshape(-1)[None, :]).astype(bf16)

    ppmi, send, hot_t = call(
        make_ppmi_kernel(t),
        [ppmi_shape, send_shape, hot_shape],
        [SMEM] + [VMEM] * 4,
        scratch=[pltpu.VMEM((depth, rows), f32)],
    )(tab, match, counts, turned, sums_all)

    def finish(send, hot_x, hot_t):
        got = exchange(send)
        hot_a, hot_b = spread_hot(hot_t)
        result = call(
            make_result_kernel(t, hot_order),
            result_shape,
            [SMEM] + [VMEM] * 5,
        )(tab, ppmi, got, hot_x, hot_a, hot_b)
        other = swap(result)
        square = call(own_gram_kernel, shape((half, half), f32), [VMEM])(result)
        gram = call(
            make_cross_gram_kernel(t),
            shape((half + half // 2, half), f32),
            [SMEM] + [VMEM] * 3,
        )(tab, result, other, square)
        gram = add_up(gram)
        return result, other, gram, swap(gram)

    gram_scratch = [
        pltpu.VMEM((2, half + half // 2, half), f32),
        pltpu.VMEM((2, 2, half, half), f32),
    ]
    result_scratch = [pltpu.VMEM((blocks, half, rows), f32)] * 2
    result, other, gram, other_gram = finish(send, hot_x, hot_t)
    send, near, far, hot_t = call(
        make_second_kernel(t, 1.0 / vocab),
        [send_shape, side_shape, side_shape, hot_shape],
        [SMEM] + [VMEM] * 2 + [ANY] * 3,
        scratch=gram_scratch
        + [pltpu.VMEM((blocks, half, rows), bf16)]
        + result_scratch
        + [pltpu.VMEM((nnz, rows, rows), bf16), pltpu.SemaphoreType.DMA((3,))],
    )(tab, gram, other_gram, result, other, ppmi)
    hot_x = scatter_hot(near, far, towards)
    result, other, gram, other_gram = finish(send, hot_x, hot_t)
    return call(
        make_final_kernel(t, 1.0 / vocab),
        shape((blocks, rows, half), f32),
        [SMEM] + [VMEM] * 2 + [ANY] * 2,
        scratch=gram_scratch + result_scratch + [pltpu.SemaphoreType.DMA((2,))],
    )(tab, gram, other_gram, result, other)


def solution(mesh):
    placed = (
        P(("decade", "row"), None, None),
        P("decade", None, None),
        P(None, ("decade", "row"), "col"),
    )
    return jax.shard_map(
        body,
        mesh=mesh,
        in_specs=placed,
        out_specs=P(None, ("decade", "row"), "col"),
        check_vma=False,
    )
```

time: 254 us -> 203 us (0.80)
  starting transfers between devices: 139 us -> 43 us
  waiting for transfers between devices: 37.9 us -> 97.5 us
  Pallas kernels: 65.5 us -> 50.3 us
  other arithmetic: 5.96 us -> 1.39 us
  local copies, waits for them, and re-layouts: 5.01 us -> 9.47 us
    ppermute x91 -> x18, starting transfers between devices: 135 us -> 25.1 us  [peer(): return lax.ppermute(x, 'row', [(r, r ^ k) for r in range(groups)])]
    ppermute x91 -> x18, waiting for transfers between devices: 27.4 us -> 88.7 us  [peer(): return lax.ppermute(x, 'row', [(r, r ^ k) for r in range(groups)])]
    all_to_all x0 -> x3, starting transfers between devices: none -> 17.6 us  [exchange(): return lax.all_to_all(x, 'row', split_axis=0, concat_axis=0, tiled=True)]
    pallas_call x10, Pallas kernels: 45.6 us -> 31.9 us  [the longest x1 17.6 us: body(): call(make_second_kernel(t, 1.0 / vocab), [send_shape, side_shape, side_sh...]
    unnamed x9 -> x33, local copies, waits for them, and re-layouts: 2.92 us -> 8.13 us
    select_n x11 -> x8, other arithmetic: 5.52 us -> 0.38 us  [the longest x6 0.37 us: scatter_hot(): part = jnp.where(stay[:, :, None, None], near, got)]
    ppermute x18 -> x4, starting transfers between devices: 3.48 us -> 0.28 us  [swap(): return lax.ppermute(x, 'col', [(0, 1), (1, 0)])]
    ppermute x18 -> x4, waiting for transfers between devices: 10.5 us -> 8.19 us  [swap(): return lax.ppermute(x, 'col', [(0, 1), (1, 0)])]
  transfers between devices with their start and end apart: 109 -> 25, of which waited for: 27 -> 19; matrix products, arithmetic and copies ran while one was open for 3% -> 1% of each run, Pallas kernels for 2% -> 2%
where the time goes in v3:
time: 203 us; the launch traced here: 202 us
  waiting for transfers between devices  97.5 us (48%)
  Pallas kernels  50.3 us (25%)
  starting transfers between devices  43 us (21%)
  local copies, waits for them, and re-layouts  9.47 us (5%)
    ppermute x18, waiting for transfers between devices, peer(): return lax.ppermute(x, 'row', [(r, r ^ k) for r in range(groups)])  88.7 us
    ppermute x18, starting transfers between devices, peer(): return lax.ppermute(x, 'row', [(r, r ^ k) for r in range(groups)])  25.1 us
    pallas_call x1, Pallas kernels, body(): call(make_final_kernel(t, 1.0 / vocab), shape((blocks, rows, half), f32),...  18.4 us
    all_to_all x3, starting transfers between devices, exchange(): return lax.all_to_all(x, 'row', split_axis=0, concat_axis=0, tiled=True)  17.6 us
    pallas_call x1, Pallas kernels, body(): call(make_second_kernel(t, 1.0 / vocab), [send_shape, side_shape, side_sh...  17.6 us
    ppermute x4, waiting for transfers between devices, swap(): return lax.ppermute(x, 'col', [(0, 1), (1, 0)])  8.19 us
    unnamed x33, local copies, waits for them, and re-layouts  8.13 us
  transfers between devices with their start and end apart: 25, of which 19 were waited for; matrix products, arithmetic and copies ran while one was open for 1% of the time, Pallas kernels for 2%

profile of v3, /device:TPU:0, one launch (start us, length us, event | category | flops | bytes accessed | tf_op | source)
XLA Modules:
  0.0 202.3 jit_solution(12986921736910294629)
XLA Ops:
  0.0 1.7 copy-done
  1.7 1.3 shard_map.38
  3.0 7.3 %all-to-all-start = ((f32[8,24,256]{2,1,0:T(8,128)}), f32[8,24,256]{2,1,0:T(8,128)}, u32[]{:S(2)}, u32[]{:S(2)}) async-start(f32[8,24,256]{2,1,0:T(8,128)} %shard_map.38), calls=%async_computation | async-start | bytes 393216 | tf_op jit(solution)/shard_map/all_to_all | solution.py:361
  12.2 1.2 copy-done.4
  13.5 1.7 shard_map.37
  15.2 1.0 copy-done.2
  18.3 1.2 copy-done.3
  19.5 2.1 %shard_map.39 = (bf16[9,256,256]{2,1,0:T(8,128)(2,1)S(1)}, bf16[8,2,128,256]{3,2,1,0:T(8,128)(2,1)S(1)}, bf16[1,1,128,256]{3,2,1,0:T(8,128)(2,1)S(1)}) custom-call(s32[35]{0:T(128)S(1)} %concatenate.20.tab, bf16[24,192]{1,0:T(8,128)(2,1)S(1)} %compare_convert_fusion.match_ref, s32[9,256,256]{2,1,0:T(8,128)S(1)} %copy-done.1, ...), custom_call_target="tpu_custom_call" | custom-call | bytes 4194304 | tf_op jit(solution)/shard_map/pallas_call | solution.py:409
  21.7 1.0 copy-done.5
  23.3 5.5 %all-to-all-start.1 = ((bf16[8,2,128,256]{3,2,1,0:T(8,128)(2,1)}), bf16[8,2,128,256]{3,2,1,0:T(8,128)(2,1)S(1)}, u32[]{:S(2)}, u32[]{:S(2)}) async-start(bf16[8,2,128,256]{3,2,1,0:T(8,128)(2,1)} %copy-done.5), calls=%async_computation.1 | async-start | bytes 2097152 | tf_op jit(solution)/shard_map/all_to_all | solution.py:361
  28.8 2.0 collective-permute-start
  31.0 15.0 %collective-permute-done = bf16[4,1,128,256]{3,2,1,0:T(8,128)(2,1)S(1)} collective-permute-done((bf16[4,1,128,256]{3,2,1,0:T(8,128)(2,1)S(1)}, bf16[4,1,128,256]{3,2,1,0:T(8,128)(2,1)S(1)}, u32[]{:S(2)}, u32[]{:S(2)}) %collective-permute-start) | collective-permute-done | bytes 262176 | tf_op jit(solution)/shard_map/ppermute | solution.py:355
  46.2 5.2 %collective-permute-start.3 = (bf16[1,1,128,256]{3,2,1,0:T(8,128)(2,1)S(1)}, bf16[1,1,128,256]{3,2,1,0:T(8,128)(2,1)S(1)}, u32[]{:S(2)}, u32[]{:S(2)}) collective-permute-start(bf16[1,1,128,256]{3,2,1,0:T(8,128)(2,1)S(1)} %copy-done.7), channel_id=1, source_target_pairs={{0,8},{2,10},{4,12},{6,14},{8,0},{10,2},{12,4},{14,6},{1,9},{3,11}... | collective-permute-start | bytes 196616 | tf_op jit(solution)/shard_map/ppermute | solution.py:355
  51.5 5.7 %collective-permute-done.3 = bf16[1,1,128,256]{3,2,1,0:T(8,128)(2,1)S(1)} collective-permute-done((bf16[1,1,128,256]{3,2,1,0:T(8,128)(2,1)S(1)}, bf16[1,1,128,256]{3,2,1,0:T(8,128)(2,1)S(1)}, u32[]{:S(2)}, u32[]{:S(2)}) %collective-permute-start.3) | collective-permute-done | bytes 65568 | tf_op jit(solution)/shard_map/ppermute | solution.py:355
  57.3 1.6 collective-permute-start.2
  59.0 3.9 %collective-permute-done.4 = bf16[2,1,128,256]{3,2,1,0:T(8,128)(2,1)S(1)} collective-permute-done((bf16[2,1,128,256]{3,2,1,0:T(8,128)(2,1)S(1)}, bf16[2,1,128,256]{3,2,1,0:T(8,128)(2,1)S(1)}, u32[]{:S(2)}, u32[]{:S(2)}) %collective-permute-start.4) | collective-permute-done | bytes 131104 | tf_op jit(solution)/shard_map/ppermute | solution.py:355
  62.9 1.2 collective-permute-start.5
  64.1 5.2 %collective-permute-done.5.hot_b = bf16[4,1,128,256]{3,2,1,0:T(8,128)(2,1)S(1)} collective-permute-done((bf16[4,1,128,256]{3,2,1,0:T(8,128)(2,1)S(1)}, bf16[4,1,128,256]{3,2,1,0:T(8,128)(2,1)S(1)}, u32[]{:S(2)}, u32[]{:S(2)}) %collective-permute-start.5) | collective-permute-done | bytes 262176 | tf_op jit(solution)/shard_map/ppermute | solution.py:355
  69.3 1.3 shard_map.40.own.mine_hbm
  70.7 1.3 shard_map.41.square
  72.0 2.8 %collective-permute-done.6.other.other_hbm = f32[16,128,256]{2,1,0:T(8,128)S(1)} collective-permute-done((f32[16,128,256]{2,1,0:T(8,128)S(1)}, f32[16,128,256]{2,1,0:T(8,128)S(1)}, u32[]{:S(2)}, u32[]{:S(2)}) %collective-permute-start.6) | collective-permute-done | bytes 2097184 | tf_op jit(solution)/shard_map/ppermute | solution.py:358
  74.8 1.9 shard_map.42
  76.8 1.3 collective-permute-start.7
  78.1 3.6 %collective-permute-done.7 = f32[192,128]{1,0:T(8,128)S(1)} collective-permute-done((f32[192,128]{1,0:T(8,128)S(1)}, f32[192,128]{1,0:T(8,128)S(1)}, u32[]{:S(2)}, u32[]{:S(2)}) %collective-permute-start.7) | collective-permute-done | bytes 98336 | tf_op jit(solution)/shard_map/ppermute | solution.py:355
  81.8 4.6 %collective-permute-done.8 = f32[192,128]{1,0:T(8,128)S(1)} collective-permute-done((f32[192,128]{1,0:T(8,128)S(1)}, f32[192,128]{1,0:T(8,128)S(1)}, u32[]{:S(2)}, u32[]{:S(2)}) %collective-permute-start.8) | collective-permute-done | bytes 98336 | tf_op jit(solution)/shard_map/ppermute | solution.py:355
  86.4 1.6 collective-permute-start.9
  87.9 5.1 %collective-permute-done.9 = f32[192,128]{1,0:T(8,128)S(1)} collective-permute-done((f32[192,128]{1,0:T(8,128)S(1)}, f32[192,128]{1,0:T(8,128)S(1)}, u32[]{:S(2)}, u32[]{:S(2)}) %collective-permute-start.9) | collective-permute-done | bytes 98336 | tf_op jit(solution)/shard_map/ppermute | solution.py:355
  93.1 1.3 collective-permute-done.10.other_g
  94.4 17.6 %shard_map.43 = (bf16[8,2,128,256]{3,2,1,0:T(8,128)(2,1)}, bf16[4,1,128,256]{3,2,1,0:T(8,128)(2,1)S(1)}, bf16[4,1,128,256]{3,2,1,0:T(8,128)(2,1)S(1)}, bf16[1,1,128,256]{3,2,1,0:T(8,128)(2,1)S(1)}) custom-call(s32[35]{0:T(128)S(1)} %concatenate.20.tab, f32[192,128]{1,0:T(8,128)S(1)} %add.62.own_g, f32[192,128]{1,0:T(8,128)S(1)} %collective-permute-done.10.other_g, ...), custom_call_target="tpu_custom_call" | custom-call | bytes 4194304 | tf_op jit(solution)/shard_map/pallas_call | solution.py:440
  112.0 4.9 %all-to-all-start.2 = ((bf16[8,2,128,256]{3,2,1,0:T(8,128)(2,1)}), bf16[8,2,128,256]{3,2,1,0:T(8,128)(2,1)S(1)}, u32[]{:S(2)}, u32[]{:S(2)}) async-start(bf16[8,2,128,256]{3,2,1,0:T(8,128)(2,1)} %get-tuple-element.21), calls=%async_computation.2 | async-start | bytes 2097152 | tf_op jit(solution)/shard_map/all_to_all | solution.py:361
  116.9 2.0 collective-permute-start.11
  118.9 2.4 %collective-permute-start.14 = (bf16[1,1,128,256]{3,2,1,0:T(8,128)(2,1)S(1)}, bf16[1,1,128,256]{3,2,1,0:T(8,128)(2,1)S(1)}, u32[]{:S(2)}, u32[]{:S(2)}) collective-permute-start(bf16[1,1,128,256]{3,2,1,0:T(8,128)(2,1)S(1)} %get-tuple-element.24), channel_id=1, source_target_pairs={{0,8},{2,10},{4,12},{6,14},{8,0},{10,2},{12,4},{14,6},{1,9},{3,11}... | collective-permute-start | bytes 196616 | tf_op jit(solution)/shard_map/ppermute | solution.py:355
  121.3 13.4 %collective-permute-done.11 = bf16[4,1,128,256]{3,2,1,0:T(8,128)(2,1)S(1)} collective-permute-done((bf16[4,1,128,256]{3,2,1,0:T(8,128)(2,1)S(1)}, bf16[4,1,128,256]{3,2,1,0:T(8,128)(2,1)S(1)}, u32[]{:S(2)}, u32[]{:S(2)}) %collective-permute-start.11) | collective-permute-done | bytes 262176 | tf_op jit(solution)/shard_map/ppermute | solution.py:355
  134.8 1.4 collective-permute-start.12
  136.2 9.6 %collective-permute-done.14 = bf16[1,1,128,256]{3,2,1,0:T(8,128)(2,1)S(1)} collective-permute-done((bf16[1,1,128,256]{3,2,1,0:T(8,128)(2,1)S(1)}, bf16[1,1,128,256]{3,2,1,0:T(8,128)(2,1)S(1)}, u32[]{:S(2)}, u32[]{:S(2)}) %collective-permute-start.14) | collective-permute-done | bytes 65568 | tf_op jit(solution)/shard_map/ppermute | solution.py:355
  146.0 2.5 %collective-permute-start.13 = (bf16[1,1,128,256]{3,2,1,0:T(8,128)(2,1)S(1)}, bf16[1,1,128,256]{3,2,1,0:T(8,128)(2,1)S(1)}, u32[]{:S(2)}, u32[]{:S(2)}) collective-permute-start(bf16[1,1,128,256]{3,2,1,0:T(8,128)(2,1)S(1)} %slice.101), channel_id=1, source_target_pairs={{0,8},{2,10},{4,12},{6,14},{8,0},{10,2},{12,4},{14,6},{1,9},{3,11}... | collective-permute-start | bytes 196616 | tf_op jit(solution)/shard_map/ppermute | solution.py:355
  148.5 3.7 %collective-permute-done.15 = bf16[2,1,128,256]{3,2,1,0:T(8,128)(2,1)S(1)} collective-permute-done((bf16[2,1,128,256]{3,2,1,0:T(8,128)(2,1)S(1)}, bf16[2,1,128,256]{3,2,1,0:T(8,128)(2,1)S(1)}, u32[]{:S(2)}, u32[]{:S(2)}) %collective-permute-start.15) | collective-permute-done | bytes 131104 | tf_op jit(solution)/shard_map/ppermute | solution.py:355
  153.1 5.5 %collective-permute-done.16.hot_b = bf16[4,1,128,256]{3,2,1,0:T(8,128)(2,1)S(1)} collective-permute-done((bf16[4,1,128,256]{3,2,1,0:T(8,128)(2,1)S(1)}, bf16[4,1,128,256]{3,2,1,0:T(8,128)(2,1)S(1)}, u32[]{:S(2)}, u32[]{:S(2)}) %collective-permute-start.16) | collective-permute-done | bytes 262176 | tf_op jit(solution)/shard_map/ppermute | solution.py:355
  158.7 1.3 shard_map.44.own.mine_hbm
  160.0 1.3 shard_map.45.square
  161.4 2.8 %collective-permute-done.17.other.other_hbm = f32[16,128,256]{2,1,0:T(8,128)S(1)} collective-permute-done((f32[16,128,256]{2,1,0:T(8,128)S(1)}, f32[16,128,256]{2,1,0:T(8,128)S(1)}, u32[]{:S(2)}, u32[]{:S(2)}) %collective-permute-start.17) | collective-permute-done | bytes 2097184 | tf_op jit(solution)/shard_map/ppermute | solution.py:358
  164.2 2.0 shard_map.46
  167.1 4.0 %collective-permute-done.18 = f32[192,128]{1,0:T(8,128)S(1)} collective-permute-done((f32[192,128]{1,0:T(8,128)S(1)}, f32[192,128]{1,0:T(8,128)S(1)}, u32[]{:S(2)}, u32[]{:S(2)}) %collective-permute-start.18) | collective-permute-done | bytes 98336 | tf_op jit(solution)/shard_map/ppermute | solution.py:355
  171.6 4.2 %collective-permute-done.19 = f32[192,128]{1,0:T(8,128)S(1)} collective-permute-done((f32[192,128]{1,0:T(8,128)S(1)}, f32[192,128]{1,0:T(8,128)S(1)}, u32[]{:S(2)}, u32[]{:S(2)}) %collective-permute-start.19) | collective-permute-done | bytes 98336 | tf_op jit(solution)/shard_map/ppermute | solution.py:355
  175.8 1.3 collective-permute-start.20
  177.0 5.2 %collective-permute-done.20 = f32[192,128]{1,0:T(8,128)S(1)} collective-permute-done((f32[192,128]{1,0:T(8,128)S(1)}, f32[192,128]{1,0:T(8,128)S(1)}, u32[]{:S(2)}, u32[]{:S(2)}) %collective-permute-start.20) | collective-permute-done | bytes 98336 | tf_op jit(solution)/shard_map/ppermute | solution.py:355
  182.4 1.3 collective-permute-done.21.other_g
  183.7 18.4 %shard_map.47 = f32[16,256,128]{2,1,0:T(8,128)} custom-call(s32[35]{0:T(128)S(1)} %concatenate.20.tab, f32[192,128]{1,0:T(8,128)S(1)} %add.65.own_g, f32[192,128]{1,0:T(8,128)S(1)} %collective-permute-done.21.other_g, f32[16,128,256]{2,1,0:T(8,128)S(1)} %shard_map.44.own.mine_hbm, f32[16,128,256]{2,1,0:T(8,128)S(1)} %collective-permute-done.17.other.other_hbm), custom_call_target="tpu_custom_call" | custom-call | bytes 4194304 | tf_op jit(solution)/shard_map/pallas_call | solution.py:451
  (91 shorter events, 8.4 us)
Async XLA Ops:
  0.0 1.7 copy-start
  1.7 8.6 %copy-start.12 = (s32[8,9,3]{1,0,2:T(8,128)S(1)}, s32[8,9,3]{1,0,2:T(8,128)}, u32[]{:S(2)}) copy-start(s32[8,9,3]{1,0,2:T(8,128)} %param.4) | copy-start | bytes 2596
  1.7 16.6 %copy-start.1 = (s32[9,256,256]{2,1,0:T(8,128)S(1)}, s32[9,256,256]{2,1,0:T(8,128)}, u32[]{:S(2)}) copy-start(s32[9,256,256]{2,1,0:T(8,128)} %counts_ref.3) | copy-start | bytes 7077892
  3.0 15.3 %all-to-all-start = ((f32[8,24,256]{2,1,0:T(8,128)}), f32[8,24,256]{2,1,0:T(8,128)}, u32[]{:S(2)}, u32[]{:S(2)}) async-start(f32[8,24,256]{2,1,0:T(8,128)} %shard_map.38), calls=%async_computation | async-start | bytes 393216 | tf_op jit(solution)/shard_map/all_to_all | solution.py:361
  12.2 1.2 copy-start.4
  15.2 1.0 copy-start.2
  16.2 0.7 copy-start.8
  16.9 0.7 copy-start.10
  18.3 1.2 copy-start.3
  21.7 1.0 copy-start.5
  22.7 0.6 copy-start.6
  23.3 5.5 %copy-start.11 = (bf16[4,1,128,256]{3,2,1,0:T(8,128)(2,1)S(1)}, bf16[4,1,128,256]{3,2,1,0:T(8,128)(2,1)}, u32[]{:S(2)}) copy-start(bf16[4,1,128,256]{3,2,1,0:T(8,128)(2,1)} %copy-done.10) | copy-start | bytes 786436
  23.3 7.5 %copy-start.13 = (s32[8,1]{0,1:T(1,128)S(1)}, s32[8,1]{0,1:T(1,128)}, u32[]{:S(2)}) copy-start(s32[8,1]{0,1:T(1,128)} %get-tuple-element.25) | copy-start | bytes 100
  23.3 22.7 %copy-start.9 = (bf16[4,1,128,256]{3,2,1,0:T(8,128)(2,1)S(1)}, bf16[4,1,128,256]{3,2,1,0:T(8,128)(2,1)}, u32[]{:S(2)}) copy-start(bf16[4,1,128,256]{3,2,1,0:T(8,128)(2,1)} %copy-done.8) | copy-start | bytes 786436
  23.3 22.9 %copy-start.7 = (bf16[1,1,128,256]{3,2,1,0:T(8,128)(2,1)S(1)}, bf16[1,1,128,256]{3,2,1,0:T(8,128)(2,1)}, u32[]{:S(2)}) copy-start(bf16[1,1,128,256]{3,2,1,0:T(8,128)(2,1)} %copy-done.6) | copy-start | bytes 196612
  23.3 46.0 %all-to-all-start.1 = ((bf16[8,2,128,256]{3,2,1,0:T(8,128)(2,1)}), bf16[8,2,128,256]{3,2,1,0:T(8,128)(2,1)S(1)}, u32[]{:S(2)}, u32[]{:S(2)}) async-start(bf16[8,2,128,256]{3,2,1,0:T(8,128)(2,1)} %copy-done.5), calls=%async_computation.1 | async-start | bytes 2097152 | tf_op jit(solution)/shard_map/all_to_all | solution.py:361
  28.8 17.2 %collective-permute-start = (bf16[4,1,128,256]{3,2,1,0:T(8,128)(2,1)S(1)}, bf16[4,1,128,256]{3,2,1,0:T(8,128)(2,1)S(1)}, u32[]{:S(2)}, u32[]{:S(2)}) collective-permute-start(bf16[4,1,128,256]{3,2,1,0:T(8,128)(2,1)S(1)} %copy-done.11), channel_id=1, source_target_pairs={{0,2},{2,0},{4,6},{6,4},{8,10},{10,8},{12,14},{14,12},{1,3},{3,1},... | collective-permute-start | bytes 786440 | tf_op jit(solution)/shard_map/ppermute | solution.py:355
  46.1 11.1 %collective-permute-start.1 = (bf16[2,1,128,256]{3,2,1,0:T(8,128)(2,1)S(1)}, bf16[2,1,128,256]{3,2,1,0:T(8,128)(2,1)S(1)}, u32[]{:S(2)}, u32[]{:S(2)}) collective-permute-start(bf16[2,1,128,256]{3,2,1,0:T(8,128)(2,1)S(1)} %slice.89), channel_id=1, source_target_pairs={{0,4},{2,6},{4,0},{6,2},{8,12},{10,14},{12,8},{14,10},{1,5},{3,7},... | collective-permute-start | bytes 393224 | tf_op jit(solution)/shard_map/ppermute | solution.py:355
  46.2 10.9 %collective-permute-start.3 = (bf16[1,1,128,256]{3,2,1,0:T(8,128)(2,1)S(1)}, bf16[1,1,128,256]{3,2,1,0:T(8,128)(2,1)S(1)}, u32[]{:S(2)}, u32[]{:S(2)}) collective-permute-start(bf16[1,1,128,256]{3,2,1,0:T(8,128)(2,1)S(1)} %copy-done.7), channel_id=1, source_target_pairs={{0,8},{2,10},{4,12},{6,14},{8,0},{10,2},{12,4},{14,6},{1,9},{3,11}... | collective-permute-start | bytes 196616 | tf_op jit(solution)/shard_map/ppermute | solution.py:355
  57.1 5.7 %collective-permute-start.4 = (bf16[2,1,128,256]{3,2,1,0:T(8,128)(2,1)S(1)}, bf16[2,1,128,256]{3,2,1,0:T(8,128)(2,1)S(1)}, u32[]{:S(2)}, u32[]{:S(2)}) collective-permute-start(bf16[2,1,128,256]{3,2,1,0:T(8,128)(2,1)S(1)} %pad_maximum_fusion), channel_id=1, source_target_pairs={{0,4},{2,6},{4,0},{6,2},{8,12},{10,14},{12,8},{14,10},{1,5},{3,7},... | collective-permute-start | bytes 393224 | tf_op jit(solution)/shard_map/ppermute | solution.py:355
  57.3 6.8 %collective-permute-start.2 = (bf16[1,1,128,256]{3,2,1,0:T(8,128)(2,1)S(1)}, bf16[1,1,128,256]{3,2,1,0:T(8,128)(2,1)S(1)}, u32[]{:S(2)}, u32[]{:S(2)}) collective-permute-start(bf16[1,1,128,256]{3,2,1,0:T(8,128)(2,1)S(1)} %slice.99), channel_id=1, source_target_pairs={{0,8},{2,10},{4,12},{6,14},{8,0},{10,2},{12,4},{14,6},{1,9},{3,11}... | collective-permute-start | bytes 196616 | tf_op jit(solution)/shard_map/ppermute | solution.py:355
  62.9 6.4 %collective-permute-start.5 = (bf16[4,1,128,256]{3,2,1,0:T(8,128)(2,1)S(1)}, bf16[4,1,128,256]{3,2,1,0:T(8,128)(2,1)S(1)}, u32[]{:S(2)}, u32[]{:S(2)}) collective-permute-start(bf16[4,1,128,256]{3,2,1,0:T(8,128)(2,1)S(1)} %constant_dynamic-update-slice_fusion.hot_a), channel_id=1, source_target_pairs={{0,2},{2,0},{4,6},{6,4},{8,10},{10,8},{12,14},{14,12},{1,3},{3,1},... | collective-permute-start | bytes 786440 | tf_op jit(solution)/shard_map/ppermute | solution.py:355
  70.6 4.2 %collective-permute-start.6 = (f32[16,128,256]{2,1,0:T(8,128)S(1)}, f32[16,128,256]{2,1,0:T(8,128)S(1)}, u32[]{:S(2)}, u32[]{:S(2)}) collective-permute-start(f32[16,128,256]{2,1,0:T(8,128)S(1)} %shard_map.40.own.mine_hbm), channel_id=1, source_target_pairs={{0,1},{1,0},{2,3},{3,2},{4,5},{5,4},{6,7},{7,6},{8,9},{9,8},{10,11... | collective-permute-start | bytes 6291464 | tf_op jit(solution)/shard_map/ppermute | solution.py:358
  76.8 4.9 %collective-permute-start.7 = (f32[192,128]{1,0:T(8,128)S(1)}, f32[192,128]{1,0:T(8,128)S(1)}, u32[]{:S(2)}, u32[]{:S(2)}) collective-permute-start(f32[192,128]{1,0:T(8,128)S(1)} %shard_map.42), channel_id=1, source_target_pairs={{0,2},{2,0},{4,6},{6,4},{8,10},{10,8},{12,14},{14,12},{1,3},{3,1},... | collective-permute-start | bytes 294920 | tf_op jit(solution)/shard_map/ppermute | solution.py:355
  81.7 4.7 %collective-permute-start.8 = (f32[192,128]{1,0:T(8,128)S(1)}, f32[192,128]{1,0:T(8,128)S(1)}, u32[]{:S(2)}, u32[]{:S(2)}) collective-permute-start(f32[192,128]{1,0:T(8,128)S(1)} %add.60), channel_id=1, source_target_pairs={{0,4},{2,6},{4,0},{6,2},{8,12},{10,14},{12,8},{14,10},{1,5},{3,7},... | collective-permute-start | bytes 294920 | tf_op jit(solution)/shard_map/ppermute | solution.py:355
  86.4 6.6 %collective-permute-start.9 = (f32[192,128]{1,0:T(8,128)S(1)}, f32[192,128]{1,0:T(8,128)S(1)}, u32[]{:S(2)}, u32[]{:S(2)}) collective-permute-start(f32[192,128]{1,0:T(8,128)S(1)} %add.61), channel_id=1, source_target_pairs={{0,8},{2,10},{4,12},{6,14},{8,0},{10,2},{12,4},{14,6},{1,9},{3,11}... | collective-permute-start | bytes 294920 | tf_op jit(solution)/shard_map/ppermute | solution.py:355
  93.0 1.4 collective-permute-start.10
  112.0 46.6 %all-to-all-start.2 = ((bf16[8,2,128,256]{3,2,1,0:T(8,128)(2,1)}), bf16[8,2,128,256]{3,2,1,0:T(8,128)(2,1)S(1)}, u32[]{:S(2)}, u32[]{:S(2)}) async-start(bf16[8,2,128,256]{3,2,1,0:T(8,128)(2,1)} %get-tuple-element.21), calls=%async_computation.2 | async-start | bytes 2097152 | tf_op jit(solution)/shard_map/all_to_all | solution.py:361
  116.9 17.8 %collective-permute-start.11 = (bf16[4,1,128,256]{3,2,1,0:T(8,128)(2,1)S(1)}, bf16[4,1,128,256]{3,2,1,0:T(8,128)(2,1)S(1)}, u32[]{:S(2)}, u32[]{:S(2)}) collective-permute-start(bf16[4,1,128,256]{3,2,1,0:T(8,128)(2,1)S(1)} %get-tuple-element.23), channel_id=1, source_target_pairs={{0,2},{2,0},{4,6},{6,4},{8,10},{10,8},{12,14},{14,12},{1,3},{3,1},... | collective-permute-start | bytes 786440 | tf_op jit(solution)/shard_map/ppermute | solution.py:355
  118.9 26.9 %collective-permute-start.14 = (bf16[1,1,128,256]{3,2,1,0:T(8,128)(2,1)S(1)}, bf16[1,1,128,256]{3,2,1,0:T(8,128)(2,1)S(1)}, u32[]{:S(2)}, u32[]{:S(2)}) collective-permute-start(bf16[1,1,128,256]{3,2,1,0:T(8,128)(2,1)S(1)} %get-tuple-element.24), channel_id=1, source_target_pairs={{0,8},{2,10},{4,12},{6,14},{8,0},{10,2},{12,4},{14,6},{1,9},{3,11}... | collective-permute-start | bytes 196616 | tf_op jit(solution)/shard_map/ppermute | solution.py:355
  134.8 11.1 %collective-permute-start.12 = (bf16[2,1,128,256]{3,2,1,0:T(8,128)(2,1)S(1)}, bf16[2,1,128,256]{3,2,1,0:T(8,128)(2,1)S(1)}, u32[]{:S(2)}, u32[]{:S(2)}) collective-permute-start(bf16[2,1,128,256]{3,2,1,0:T(8,128)(2,1)S(1)} %slice.93), channel_id=1, source_target_pairs={{0,4},{2,6},{4,0},{6,2},{8,12},{10,14},{12,8},{14,10},{1,5},{3,7},... | collective-permute-start | bytes 393224 | tf_op jit(solution)/shard_map/ppermute | solution.py:355
  145.8 6.4 %collective-permute-start.15 = (bf16[2,1,128,256]{3,2,1,0:T(8,128)(2,1)S(1)}, bf16[2,1,128,256]{3,2,1,0:T(8,128)(2,1)S(1)}, u32[]{:S(2)}, u32[]{:S(2)}) collective-permute-start(bf16[2,1,128,256]{3,2,1,0:T(8,128)(2,1)S(1)} %pad_maximum_fusion.1), channel_id=1, source_target_pairs={{0,4},{2,6},{4,0},{6,2},{8,12},{10,14},{12,8},{14,10},{1,5},{3,7},... | collective-permute-start | bytes 393224 | tf_op jit(solution)/shard_map/ppermute | solution.py:355
  146.0 7.1 %collective-permute-start.13 = (bf16[1,1,128,256]{3,2,1,0:T(8,128)(2,1)S(1)}, bf16[1,1,128,256]{3,2,1,0:T(8,128)(2,1)S(1)}, u32[]{:S(2)}, u32[]{:S(2)}) collective-permute-start(bf16[1,1,128,256]{3,2,1,0:T(8,128)(2,1)S(1)} %slice.101), channel_id=1, source_target_pairs={{0,8},{2,10},{4,12},{6,14},{8,0},{10,2},{12,4},{14,6},{1,9},{3,11}... | collective-permute-start | bytes 196616 | tf_op jit(solution)/shard_map/ppermute | solution.py:355
  152.2 6.4 %collective-permute-start.16 = (bf16[4,1,128,256]{3,2,1,0:T(8,128)(2,1)S(1)}, bf16[4,1,128,256]{3,2,1,0:T(8,128)(2,1)S(1)}, u32[]{:S(2)}, u32[]{:S(2)}) collective-permute-start(bf16[4,1,128,256]{3,2,1,0:T(8,128)(2,1)S(1)} %constant_dynamic-update-slice_fusion.3.hot_a), channel_id=1, source_target_pairs={{0,2},{2,0},{4,6},{6,4},{8,10},{10,8},{12,14},{14,12},{1,3},{3,1},... | collective-permute-start | bytes 786440 | tf_op jit(solution)/shard_map/ppermute | solution.py:355
  160.0 4.2 %collective-permute-start.17 = (f32[16,128,256]{2,1,0:T(8,128)S(1)}, f32[16,128,256]{2,1,0:T(8,128)S(1)}, u32[]{:S(2)}, u32[]{:S(2)}) collective-permute-start(f32[16,128,256]{2,1,0:T(8,128)S(1)} %shard_map.44.own.mine_hbm), channel_id=1, source_target_pairs={{0,1},{1,0},{2,3},{3,2},{4,5},{5,4},{6,7},{7,6},{8,9},{9,8},{10,11... | collective-permute-start | bytes 6291464 | tf_op jit(solution)/shard_map/ppermute | solution.py:358
  166.1 4.9 %collective-permute-start.18 = (f32[192,128]{1,0:T(8,128)S(1)}, f32[192,128]{1,0:T(8,128)S(1)}, u32[]{:S(2)}, u32[]{:S(2)}) collective-permute-start(f32[192,128]{1,0:T(8,128)S(1)} %shard_map.46), channel_id=1, source_target_pairs={{0,2},{2,0},{4,6},{6,4},{8,10},{10,8},{12,14},{14,12},{1,3},{3,1},... | collective-permute-start | bytes 294920 | tf_op jit(solution)/shard_map/ppermute | solution.py:355
  171.1 4.7 %collective-permute-start.19 = (f32[192,128]{1,0:T(8,128)S(1)}, f32[192,128]{1,0:T(8,128)S(1)}, u32[]{:S(2)}, u32[]{:S(2)}) collective-permute-start(f32[192,128]{1,0:T(8,128)S(1)} %add.63), channel_id=1, source_target_pairs={{0,4},{2,6},{4,0},{6,2},{8,12},{10,14},{12,8},{14,10},{1,5},{3,7},... | collective-permute-start | bytes 294920 | tf_op jit(solution)/shard_map/ppermute | solution.py:355
  175.8 6.5 %collective-permute-start.20 = (f32[192,128]{1,0:T(8,128)S(1)}, f32[192,128]{1,0:T(8,128)S(1)}, u32[]{:S(2)}, u32[]{:S(2)}) collective-permute-start(f32[192,128]{1,0:T(8,128)S(1)} %add.64), channel_id=1, source_target_pairs={{0,8},{2,10},{4,12},{6,14},{8,0},{10,2},{12,4},{14,6},{1,9},{3,11}... | collective-permute-start | bytes 294920 | tf_op jit(solution)/shard_map/ppermute | solution.py:355
  182.3 1.4 collective-permute-start.21

commit v4 on v3

--- a/solution.py
+++ b/solution.py
@@ -70,11 +70,6 @@
         sums_ref[r] = sums_ref[0]
 
 
-def gather_main(t, tab, blocks, send):
-    for r in range(t.groups):
-        send[r, 1] = blocks[tab[t.main_j + r]]
-
-
 def gather_hot(t, tab, blocks, near, far):
     for k in range(t.groups):
         for m in range(t.hot):
@@ -85,13 +80,23 @@
                 (far if k % 2 else near)[k // 2, m] = blocks[j]
 
 
-def products(t, tab, blocks, ppmi, send, hot):
-    for s in range(t.nnz):
-        value = contract(blocks[tab[t.row_i + s]], ppmi[s], 1, 0).astype(bf16)
-        if s < t.groups:
-            send[tab[t.dest + s], 0] = value
-        else:
-            hot[0, s - t.groups] = value
+def product(t, tab, blocks, ppmi, s):
+    return contract(blocks[tab[t.row_i + s]], ppmi[s], 1, 0).astype(bf16)
+
+
+def hot_products(t, tab, blocks, ppmi, hot):
+    for m in range(t.hot):
+        hot[0, m] = product(t, tab, blocks, ppmi, t.groups + m)
+
+
+def make_main_kernel(t):
+    def kernel(tab, blocks, ppmi, send):
+        for r in range(t.groups):
+            send[r, 1] = blocks[tab[t.main_j + r]]
+        for s in range(t.groups):
+            send[tab[t.dest + s], 0] = product(t, tab, blocks, ppmi, s)
+
+    return kernel
 
 
 def make_source_kernel(t):
@@ -106,7 +111,7 @@
 
 
 def make_ppmi_kernel(t):
-    def kernel(tab, match_ref, counts_ref, turned, sums_ref, ppmi_ref, send, hot, cols_log):
+    def kernel(tab, match_ref, counts_ref, turned, sums_ref, ppmi_ref, hot, cols_log):
         sums = jnp.concatenate([sums_ref[r] for r in range(t.groups)], axis=0)
         high = jnp.floor(sums * (1.0 / 256.0))
         low = sums - high * 256.0
@@ -130,8 +135,7 @@
                 - cols_log[pl.ds(t.nnz + s, 1), :]
             )
             ppmi_ref[s] = jnp.where(counts > 0, jnp.maximum(scores, 0.0), 0.0).astype(bf16)
-        gather_main(t, tab, turned, send)
-        products(t, tab, turned, ppmi_ref, send, hot)
+        hot_products(t, tab, turned, ppmi_ref, hot)
 
     return kernel
 
@@ -211,54 +215,86 @@
     return kernel
 
 
+def pivot_rows(left, right, base):
+    full = left.shape
+    cols = [jnp.broadcast_to(left[:, base + k : base + k + 1], full) for k in range(8)]
+    piv = [[jnp.broadcast_to(cols[k][i : i + 1, :], full) for k in range(i + 1)] for i in range(8)]
+    rows = [
+        [jnp.broadcast_to(side[i : i + 1, :], full) for side in (left, right)] for i in range(8)
+    ]
+    scale = []
+    for k in range(0, 8, 2):
+        a, b, c = piv[k][k], piv[k + 1][k], piv[k + 1][k + 1]
+        det = a * c - b * b
+        root, det_root = lax.rsqrt(a), lax.rsqrt(det)
+        both = det_root * root
+        scale += [root, det_root * (a * root)]
+        piv[k + 1][k] = b * root
+        for i in range(k + 2, 8):
+            p, q = piv[i][k], piv[i][k + 1]
+            piv[i][k] = p * root
+            piv[i][k + 1] = (a * q - b * p) * both
+        for i in range(k + 2, 8):
+            for m in range(k + 2, i + 1):
+                piv[i][m] = piv[i][m] - (
+                    piv[i][k] * piv[m][k] + piv[i][k + 1] * piv[m][k + 1]
+                )
+        for side in range(2):
+            first = rows[k][side] * root
+            second = (rows[k + 1][side] - piv[k + 1][k] * first) * scale[k + 1]
+            rows[k][side], rows[k + 1][side] = first, second
+            for i in range(k + 2, 8):
+                rows[i][side] = rows[i][side] - (piv[i][k] * first + piv[i][k + 1] * second)
+    solved = [list(row) for row in rows]
+    for k in range(7, -1, -1):
+        for side in range(2):
+            solved[k][side] = solved[k][side] * scale[k]
+            for i in range(k):
+                solved[i][side] = solved[i][side] - piv[k][i] * solved[k][side]
+    return rows, solved
+
+
 def inverse_factor(block):
     size = block.shape[0]
     tiles = size // 8
+    panel = 4
     full = (8, size)
     lane = lax.broadcasted_iota(i32, full, 1)
     sub = lax.broadcasted_iota(i32, full, 0)
-    left = [block[8 * t : 8 * t + 8, :] for t in range(tiles)]
-    right = [(lane == sub + 8 * t).astype(f32) for t in range(tiles)]
-    for j in range(tiles):
-        cols = [jnp.broadcast_to(left[j][:, 8 * j + k : 8 * j + k + 1], full) for k in range(8)]
-        pivot = [
-            [jnp.broadcast_to(cols[k][i : i + 1, :], full) for k in range(i + 1)] for i in range(8)
-        ]
-        row_l = [jnp.broadcast_to(left[j][i : i + 1, :], full) for i in range(8)]
-        row_r = [jnp.broadcast_to(right[j][i : i + 1, :], full) for i in range(8)]
-        scale = []
-        for k in range(8):
-            scale.append(lax.rsqrt(pivot[k][k]))
-            for i in range(k + 1, 8):
-                pivot[i][k] = pivot[i][k] * scale[k]
-            for i in range(k + 1, 8):
-                for m in range(k + 1, i + 1):
-                    pivot[i][m] = pivot[i][m] - pivot[i][k] * pivot[m][k]
-            row_l[k] = row_l[k] * scale[k]
-            row_r[k] = row_r[k] * scale[k]
-            for i in range(k + 1, 8):
-                row_l[i] = row_l[i] - pivot[i][k] * row_l[k]
-                row_r[i] = row_r[i] - pivot[i][k] * row_r[k]
-        done = row_r[0]
-        for i in range(1, 8):
-            done = jnp.where(sub == i, row_r[i], done)
-        right[j] = done
-        if j < tiles - 1:
-            for k in range(7, -1, -1):
-                row_l[k] = row_l[k] * scale[k]
-                row_r[k] = row_r[k] * scale[k]
-                for i in range(k):
-                    row_l[i] = row_l[i] - pivot[k][i] * row_l[k]
-                    row_r[i] = row_r[i] - pivot[k][i] * row_r[k]
-            for t in range(j + 1, tiles):
-                cur = left[t]
-                new_l, new_r = cur, right[t]
+    sides = [
+        [block[8 * t : 8 * t + 8, :], (lane == sub + 8 * t).astype(f32)] for t in range(tiles)
+    ]
+    for first in range(0, tiles, panel):
+        last = first + panel
+        for j in range(first, last):
+            rows, solved = pivot_rows(*sides[j], 8 * j)
+            for t in range(j + 1, last):
+                old = sides[t][0]
+                new = list(sides[t])
                 for k in range(8):
-                    col = jnp.broadcast_to(cur[:, 8 * j + k : 8 * j + k + 1], full)
-                    new_l = new_l - col * row_l[k]
-                    new_r = new_r - col * row_r[k]
-                left[t], right[t] = new_l, new_r
-    return jnp.concatenate(right, axis=0)
+                    col = jnp.broadcast_to(old[:, 8 * j + k : 8 * j + k + 1], full)
+                    new = [new[n] - col * solved[k][n] for n in range(2)]
+                sides[t] = new
+            for n in range(2):
+                done = rows[0][n]
+                for i in range(1, 8):
+                    done = jnp.where(sub == i, rows[i][n], done)
+                sides[j][n] = done
+        if last < tiles:
+            left = jnp.concatenate([sides[t][0] for t in range(first, last)], axis=0)
+            right = jnp.concatenate([sides[t][1] for t in range(first, last)], axis=0)
+            high, mid, low = split(left)
+            r_high, r_mid, r_low = split(jnp.concatenate([left, right], axis=1))
+            change = contract(
+                jnp.concatenate([high, high, mid, mid, high, low], axis=0),
+                jnp.concatenate([r_high, r_mid, r_high, r_mid, r_low, r_high], axis=0),
+                0,
+                0,
+            )
+            for t in range(last, tiles):
+                part = change[8 * t : 8 * t + 8, :]
+                sides[t] = [sides[t][0] - part[:, :size], sides[t][1] - part[:, size:]]
+    return jnp.concatenate([side[1] for side in sides], axis=0)
 
 
 def invert(t, tab, own, other, gram, inverse, scale):
@@ -305,8 +341,8 @@
 
 def make_second_kernel(t, scale):
     def kernel(
-        tab, own_g, other_g, mine_hbm, other_hbm, ppmi_hbm, send, near, far, hot,
-        gram, inverse, normal, mine, other, ppmi, sems,
+        tab, own_g, other_g, mine_hbm, other_hbm, ppmi_hbm, normal, near, far, hot,
+        gram, inverse, mine, other, ppmi, sems,
     ):
         copies = start_copies([(mine_hbm, mine), (other_hbm, other), (ppmi_hbm, ppmi)], sems)
         invert(t, tab, own_g, other_g, gram, inverse, scale)
@@ -317,9 +353,8 @@
             normal[i] = value.astype(bf16)
 
         normal_blocks(t, tab, inverse, mine, other, store)
-        gather_main(t, tab, normal, send)
         gather_hot(t, tab, normal, near, far)
-        products(t, tab, normal, ppmi, send, hot)
+        hot_products(t, tab, normal, ppmi, hot)
 
     return kernel
 
@@ -365,8 +400,9 @@
             x = x + peer(x, bit)
         return x
 
-    def spread_hot(part):
-        for bit in bits[:0:-1]:
+    def spread_hot(part, got):
+        part = jnp.concatenate([part, got], axis=0)
+        for bit in bits[-2:0:-1]:
             part = jnp.concatenate([part, peer(part, bit)], axis=0)
         return part, peer(part, bits[0])
 
@@ -374,9 +410,10 @@
     for bit in bits[::-1]:
         hot_order += [k ^ bit for k in hot_order]
 
-    def scatter_hot(near, far, towards):
+    def scatter_hot(near, far, got, towards):
         for bit in bits:
-            got = peer(far, bit)
+            if bit > 1:
+                got = peer(far, bit)
             towards = towards[::2]
             stay = (towards & bit) == 0
             part = jnp.where(stay[:, :, None, None], near, got)
@@ -397,7 +434,6 @@
         [shape((blocks, half, rows), bf16), side_shape, side_shape],
         [SMEM, VMEM],
     )(tab, sketch)
-    hot_x = scatter_hot(near, far, towards)
 
     row_ids = block_pairs[:, :, 0] * groups + jnp.arange(groups)[:, None]
     col_ids = block_pairs[:, :, 2] * groups + block_pairs[:, :, 1]
@@ -406,16 +442,21 @@
     my_ids = lax.dynamic_index_in_dim(ids, me, 0, keepdims=False)
     match = (my_ids[:, None] == ids.reshape(-1)[None, :]).astype(bf16)
 
-    ppmi, send, hot_t = call(
+    ppmi, hot_t = call(
         make_ppmi_kernel(t),
-        [ppmi_shape, send_shape, hot_shape],
+        [ppmi_shape, hot_shape],
         [SMEM] + [VMEM] * 4,
         scratch=[pltpu.VMEM((depth, rows), f32)],
     )(tab, match, counts, turned, sums_all)
 
-    def finish(send, hot_x, hot_t):
+    def finish(source, near, far, hot_t):
+        send = call(make_main_kernel(t), send_shape, [SMEM, VMEM, VMEM])(tab, source, ppmi)
+        send, x_step, t_step = lax.optimization_barrier(
+            (send, peer(far, bits[0]), peer(hot_t, bits[-1]))
+        )
         got = exchange(send)
-        hot_a, hot_b = spread_hot(hot_t)
+        hot_x = scatter_hot(near, far, x_step, towards)
+        hot_a, hot_b = spread_hot(hot_t, t_step)
         result = call(
             make_result_kernel(t, hot_order),
             result_shape,
@@ -436,18 +477,16 @@
         pltpu.VMEM((2, 2, half, half), f32),
     ]
     result_scratch = [pltpu.VMEM((blocks, half, rows), f32)] * 2
-    result, other, gram, other_gram = finish(send, hot_x, hot_t)
-    send, near, far, hot_t = call(
+    result, other, gram, other_gram = finish(turned, near, far, hot_t)
+    normal, near, far, hot_t = call(
         make_second_kernel(t, 1.0 / vocab),
-        [send_shape, side_shape, side_shape, hot_shape],
+        [shape((blocks, half, rows), bf16), side_shape, side_shape, hot_shape],
         [SMEM] + [VMEM] * 2 + [ANY] * 3,
         scratch=gram_scratch
-        + [pltpu.VMEM((blocks, half, rows), bf16)]
         + result_scratch
         + [pltpu.VMEM((nnz, rows, rows), bf16), pltpu.SemaphoreType.DMA((3,))],
     )(tab, gram, other_gram, result, other, ppmi)
-    hot_x = scatter_hot(near, far, towards)
-    result, other, gram, other_gram = finish(send, hot_x, hot_t)
+    result, other, gram, other_gram = finish(normal, near, far, hot_t)
     return call(
         make_final_kernel(t, 1.0 / vocab),
         shape((blocks, rows, half), f32),

time: 203 us -> 191 us (0.941)
  waiting for transfers between devices: 97.5 us -> 83.3 us
  starting transfers between devices: 43 us -> 46.5 us
    ppermute x18, waiting for transfers between devices: 88.7 us -> 75.1 us  [peer(): return lax.ppermute(x, 'row', [(r, r ^ k) for r in range(groups)])]
    ppermute x18, starting transfers between devices: 25.1 us -> 30.2 us  [peer(): return lax.ppermute(x, 'row', [(r, r ^ k) for r in range(groups)])]
    pallas_call x1, Pallas kernels: 18.4 us -> 16.4 us  [body(): call(make_final_kernel(t, 1.0 / vocab), shape((blocks, rows, half), f32),...]
    unnamed x33 -> x31, local copies, waits for them, and re-layouts: 8.13 us -> 7.42 us
    pallas_call x2 -> x4, Pallas kernels: 19.8 us -> 19.7 us  [the longest x1 14.4 us: body(): call(make_second_kernel(t, 1.0 / vocab), [shape((blocks, half, rows), bf1...]
  transfers between devices with their start and end apart: 25 -> 25, of which waited for: 19 -> 19; matrix products, arithmetic and copies ran while one was open for 1% -> 2% of each run, Pallas kernels for 2% -> 5%
where the time goes in v4:
time: 191 us; the launch traced here: 190 us
  waiting for transfers between devices  83.3 us (44%)
  Pallas kernels  48.9 us (26%)
  starting transfers between devices  46.5 us (24%)
  local copies, waits for them, and re-layouts  8.76 us (5%)
  other arithmetic  2.28 us (1%)
    ppermute x18, waiting for transfers between devices, peer(): return lax.ppermute(x, 'row', [(r, r ^ k) for r in range(groups)])  75.1 us
    ppermute x18, starting transfers between devices, peer(): return lax.ppermute(x, 'row', [(r, r ^ k) for r in range(groups)])  30.2 us
    pallas_call x1, Pallas kernels, body(): call(make_final_kernel(t, 1.0 / vocab), shape((blocks, rows, half), f32),...  16.4 us
    all_to_all x3, starting transfers between devices, exchange(): return lax.all_to_all(x, 'row', split_axis=0, concat_axis=0, tiled=True)  16.1 us
    pallas_call x1, Pallas kernels, body(): call(make_second_kernel(t, 1.0 / vocab), [shape((blocks, half, rows), bf1...  14.4 us
    ppermute x4, waiting for transfers between devices, swap(): return lax.ppermute(x, 'col', [(0, 1), (1, 0)])  8.14 us
    unnamed x31, local copies, waits for them, and re-layouts  7.42 us
    pallas_call x2, Pallas kernels, finish(): call(make_cross_gram_kernel(t), shape((half + half // 2, half), f32), [SM...  3.91 us
  transfers between devices with their start and end apart: 25, of which 19 were waited for; matrix products, arithmetic and copies ran while one was open for 2% of the time, Pallas kernels for 5%

profile of v4, /device:TPU:0, one launch (start us, length us, event | category | flops | bytes accessed | tf_op | source)
XLA Modules:
  0.0 190.4 jit_solution(6710405448707325571)
XLA Ops:
  0.0 1.7 copy-done
  1.7 1.3 shard_map.38
  2.9 7.3 %all-to-all-start = ((f32[8,24,256]{2,1,0:T(8,128)}), f32[8,24,256]{2,1,0:T(8,128)S(1)}, u32[]{:S(2)}, u32[]{:S(2)}) async-start(f32[8,24,256]{2,1,0:T(8,128)} %shard_map.38), calls=%async_computation | async-start | bytes 393216 | tf_op jit(solution)/shard_map/all_to_all | solution.py:396
  13.1 2.4 %shard_map.37 = (bf16[16,128,256]{2,1,0:T(8,128)(2,1)S(1)}, bf16[4,1,128,256]{3,2,1,0:T(8,128)(2,1)S(1)}, bf16[4,1,128,256]{3,2,1,0:T(8,128)(2,1)}) custom-call(s32[35]{0:T(128)S(1)} %concatenate.20.tab, bf16[16,256,128]{2,1,0:T(8,128)(2,1)S(1)} %copy-done.4), custom_call_target="tpu_custom_call" | custom-call | bytes 4194304 | tf_op jit(solution)/shard_map/pallas_call | solution.py:432
  17.2 2.0 %collective-permute-start = (bf16[4,1,128,256]{3,2,1,0:T(8,128)(2,1)}, bf16[4,1,128,256]{3,2,1,0:T(8,128)(2,1)}, u32[]{:S(2)}, u32[]{:S(2)}) collective-permute-start(bf16[4,1,128,256]{3,2,1,0:T(8,128)(2,1)} %get-tuple-element.22), channel_id=1, source_target_pairs={{0,2},{2,0},{4,6},{6,4},{8,10},{10,8},{12,14},{14,12},{1,3},{3,1},... | collective-permute-start | bytes 786440 | tf_op jit(solution)/shard_map/ppermute | solution.py:390
  22.4 1.6 shard_map.39
  24.0 2.4 %collective-permute-start.1 = (bf16[1,1,128,256]{3,2,1,0:T(8,128)(2,1)S(1)}, bf16[1,1,128,256]{3,2,1,0:T(8,128)(2,1)S(1)}, u32[]{:S(2)}, u32[]{:S(2)}) collective-permute-start(bf16[1,1,128,256]{3,2,1,0:T(8,128)(2,1)S(1)} %get-tuple-element.23), channel_id=1, source_target_pairs={{0,8},{2,10},{4,12},{6,14},{8,0},{10,2},{12,4},{14,6},{1,9},{3,11}... | collective-permute-start | bytes 196616 | tf_op jit(solution)/shard_map/ppermute | solution.py:390
  26.4 1.8 shard_map.40
  29.2 5.2 %all-to-all-start.1 = ((bf16[8,2,128,256]{3,2,1,0:T(8,128)(2,1)}), bf16[8,2,128,256]{3,2,1,0:T(8,128)(2,1)S(1)}, u32[]{:S(2)}, u32[]{:S(2)}) async-start(bf16[8,2,128,256]{3,2,1,0:T(8,128)(2,1)} %shard_map.40), calls=%async_computation.1 | async-start | bytes 2097152 | tf_op jit(solution)/shard_map/all_to_all | solution.py:396
  35.8 2.1 %collective-permute-start.2 = (bf16[2,1,128,256]{3,2,1,0:T(8,128)(2,1)S(1)}, bf16[2,1,128,256]{3,2,1,0:T(8,128)(2,1)S(1)}, u32[]{:S(2)}, u32[]{:S(2)}) collective-permute-start(bf16[2,1,128,256]{3,2,1,0:T(8,128)(2,1)S(1)} %slice.89), channel_id=1, source_target_pairs={{0,4},{2,6},{4,0},{6,2},{8,12},{10,14},{12,8},{14,10},{1,5},{3,7},... | collective-permute-start | bytes 393224 | tf_op jit(solution)/shard_map/ppermute | solution.py:390
  38.0 16.3 %collective-permute-done.2 = bf16[2,1,128,256]{3,2,1,0:T(8,128)(2,1)S(1)} collective-permute-done((bf16[2,1,128,256]{3,2,1,0:T(8,128)(2,1)S(1)}, bf16[2,1,128,256]{3,2,1,0:T(8,128)(2,1)S(1)}, u32[]{:S(2)}, u32[]{:S(2)}) %collective-permute-start.2) | collective-permute-done | bytes 131104 | tf_op jit(solution)/shard_map/ppermute | solution.py:390
  54.3 5.0 %collective-permute-start.3 = (bf16[1,1,128,256]{3,2,1,0:T(8,128)(2,1)S(1)}, bf16[1,1,128,256]{3,2,1,0:T(8,128)(2,1)S(1)}, u32[]{:S(2)}, u32[]{:S(2)}) collective-permute-start(bf16[1,1,128,256]{3,2,1,0:T(8,128)(2,1)S(1)} %slice.99), channel_id=1, source_target_pairs={{0,8},{2,10},{4,12},{6,14},{8,0},{10,2},{12,4},{14,6},{1,9},{3,11}... | collective-permute-start | bytes 196616 | tf_op jit(solution)/shard_map/ppermute | solution.py:390
  59.4 1.4 collective-permute-start.5
  60.9 1.3 collective-permute-done.3
  62.2 3.6 %collective-permute-done.5.hot_b = bf16[4,1,128,256]{3,2,1,0:T(8,128)(2,1)S(1)} collective-permute-done((bf16[4,1,128,256]{3,2,1,0:T(8,128)(2,1)S(1)}, bf16[4,1,128,256]{3,2,1,0:T(8,128)(2,1)S(1)}, u32[]{:S(2)}, u32[]{:S(2)}) %collective-permute-start.5) | collective-permute-done | bytes 262176 | tf_op jit(solution)/shard_map/ppermute | solution.py:390
  65.8 1.3 shard_map.41.own.mine_hbm
  67.2 1.4 shard_map.42.square
  68.6 2.8 %collective-permute-done.6.other.other_hbm = f32[16,128,256]{2,1,0:T(8,128)S(1)} collective-permute-done((f32[16,128,256]{2,1,0:T(8,128)S(1)}, f32[16,128,256]{2,1,0:T(8,128)S(1)}, u32[]{:S(2)}, u32[]{:S(2)}) %collective-permute-start.6) | collective-permute-done | bytes 2097184 | tf_op jit(solution)/shard_map/ppermute | solution.py:393
  71.4 1.9 %shard_map.43 = f32[192,128]{1,0:T(8,128)S(1)} custom-call(s32[35]{0:T(128)S(1)} %concatenate.20.tab, f32[16,128,256]{2,1,0:T(8,128)S(1)} %shard_map.41.own.mine_hbm, f32[16,128,256]{2,1,0:T(8,128)S(1)} %collective-permute-done.6.other.other_hbm, f32[128,128]{1,0:T(8,128)S(1)} %shard_map.42.square), custom_call_target="tpu_custom_call" | custom-call | bytes 4194304 | tf_op jit(solution)/shard_map/pallas_call | solution.py:467
  73.3 1.4 collective-permute-start.7
  74.7 3.5 %collective-permute-done.7 = f32[192,128]{1,0:T(8,128)S(1)} collective-permute-done((f32[192,128]{1,0:T(8,128)S(1)}, f32[192,128]{1,0:T(8,128)S(1)}, u32[]{:S(2)}, u32[]{:S(2)}) %collective-permute-start.7) | collective-permute-done | bytes 98336 | tf_op jit(solution)/shard_map/ppermute | solution.py:390
  78.3 4.6 %collective-permute-done.8 = f32[192,128]{1,0:T(8,128)S(1)} collective-permute-done((f32[192,128]{1,0:T(8,128)S(1)}, f32[192,128]{1,0:T(8,128)S(1)}, u32[]{:S(2)}, u32[]{:S(2)}) %collective-permute-start.8) | collective-permute-done | bytes 98336 | tf_op jit(solution)/shard_map/ppermute | solution.py:390
  82.9 1.4 collective-permute-start.9
  84.3 4.7 %collective-permute-done.9 = f32[192,128]{1,0:T(8,128)S(1)} collective-permute-done((f32[192,128]{1,0:T(8,128)S(1)}, f32[192,128]{1,0:T(8,128)S(1)}, u32[]{:S(2)}, u32[]{:S(2)}) %collective-permute-start.9) | collective-permute-done | bytes 98336 | tf_op jit(solution)/shard_map/ppermute | solution.py:390
  89.1 1.3 collective-permute-done.10.other_g
  90.4 14.4 %shard_map.44 = (bf16[16,128,256]{2,1,0:T(8,128)(2,1)S(1)}, bf16[4,1,128,256]{3,2,1,0:T(8,128)(2,1)S(1)}, bf16[4,1,128,256]{3,2,1,0:T(8,128)(2,1)S(1)}, bf16[1,1,128,256]{3,2,1,0:T(8,128)(2,1)S(1)}) custom-call(s32[35]{0:T(128)S(1)} %concatenate.20.tab, f32[192,128]{1,0:T(8,128)S(1)} %add.62.own_g, f32[192,128]{1,0:T(8,128)S(1)} %collective-permute-done.10.other_g, ...), custom_call_target="tpu_custom_call" | custom-call | bytes 4194304 | tf_op jit(solution)/shard_map/pallas_call | solution.py:481
  104.8 1.4 collective-permute-start.11
  107.0 1.8 shard_map.45
  108.8 2.9 %collective-permute-done.12 = bf16[1,1,128,256]{3,2,1,0:T(8,128)(2,1)S(1)} collective-permute-done((bf16[1,1,128,256]{3,2,1,0:T(8,128)(2,1)S(1)}, bf16[1,1,128,256]{3,2,1,0:T(8,128)(2,1)S(1)}, u32[]{:S(2)}, u32[]{:S(2)}) %collective-permute-start.12) | collective-permute-done | bytes 65568 | tf_op jit(solution)/shard_map/ppermute | solution.py:390
  111.7 1.5 collective-permute-done.11
  113.3 3.6 %all-to-all-start.2 = ((bf16[8,2,128,256]{3,2,1,0:T(8,128)(2,1)}), bf16[8,2,128,256]{3,2,1,0:T(8,128)(2,1)S(1)}, u32[]{:S(2)}, u32[]{:S(2)}) async-start(bf16[8,2,128,256]{3,2,1,0:T(8,128)(2,1)} %shard_map.45), calls=%async_computation.2 | async-start | bytes 2097152 | tf_op jit(solution)/shard_map/all_to_all | solution.py:396
  117.0 2.0 %collective-permute-start.13 = (bf16[2,1,128,256]{3,2,1,0:T(8,128)(2,1)S(1)}, bf16[2,1,128,256]{3,2,1,0:T(8,128)(2,1)S(1)}, u32[]{:S(2)}, u32[]{:S(2)}) collective-permute-start(bf16[2,1,128,256]{3,2,1,0:T(8,128)(2,1)S(1)} %slice.93), channel_id=1, source_target_pairs={{0,4},{2,6},{4,0},{6,2},{8,12},{10,14},{12,8},{14,10},{1,5},{3,7},... | collective-permute-start | bytes 393224 | tf_op jit(solution)/shard_map/ppermute | solution.py:390
  119.1 18.6 %collective-permute-done.13 = bf16[2,1,128,256]{3,2,1,0:T(8,128)(2,1)S(1)} collective-permute-done((bf16[2,1,128,256]{3,2,1,0:T(8,128)(2,1)S(1)}, bf16[2,1,128,256]{3,2,1,0:T(8,128)(2,1)S(1)}, u32[]{:S(2)}, u32[]{:S(2)}) %collective-permute-start.13) | collective-permute-done | bytes 131104 | tf_op jit(solution)/shard_map/ppermute | solution.py:390
  137.9 4.9 %collective-permute-start.14 = (bf16[1,1,128,256]{3,2,1,0:T(8,128)(2,1)S(1)}, bf16[1,1,128,256]{3,2,1,0:T(8,128)(2,1)S(1)}, u32[]{:S(2)}, u32[]{:S(2)}) collective-permute-start(bf16[1,1,128,256]{3,2,1,0:T(8,128)(2,1)S(1)} %slice.101), channel_id=1, source_target_pairs={{0,8},{2,10},{4,12},{6,14},{8,0},{10,2},{12,4},{14,6},{1,9},{3,11}... | collective-permute-start | bytes 196616 | tf_op jit(solution)/shard_map/ppermute | solution.py:390
  142.8 1.5 collective-permute-start.16
  144.3 1.4 collective-permute-done.14
  145.7 3.5 %collective-permute-done.16.hot_b = bf16[4,1,128,256]{3,2,1,0:T(8,128)(2,1)S(1)} collective-permute-done((bf16[4,1,128,256]{3,2,1,0:T(8,128)(2,1)S(1)}, bf16[4,1,128,256]{3,2,1,0:T(8,128)(2,1)S(1)}, u32[]{:S(2)}, u32[]{:S(2)}) %collective-permute-start.16) | collective-permute-done | bytes 262176 | tf_op jit(solution)/shard_map/ppermute | solution.py:390
  149.2 1.3 shard_map.46.own.mine_hbm
  150.6 1.4 shard_map.47.square
  152.0 2.8 %collective-permute-done.17.other.other_hbm = f32[16,128,256]{2,1,0:T(8,128)S(1)} collective-permute-done((f32[16,128,256]{2,1,0:T(8,128)S(1)}, f32[16,128,256]{2,1,0:T(8,128)S(1)}, u32[]{:S(2)}, u32[]{:S(2)}) %collective-permute-start.17) | collective-permute-done | bytes 2097184 | tf_op jit(solution)/shard_map/ppermute | solution.py:393
  154.7 2.0 %shard_map.48 = f32[192,128]{1,0:T(8,128)S(1)} custom-call(s32[35]{0:T(128)S(1)} %concatenate.20.tab, f32[16,128,256]{2,1,0:T(8,128)S(1)} %shard_map.46.own.mine_hbm, f32[16,128,256]{2,1,0:T(8,128)S(1)} %collective-permute-done.17.other.other_hbm, f32[128,128]{1,0:T(8,128)S(1)} %shard_map.47.square), custom_call_target="tpu_custom_call" | custom-call | bytes 4194304 | tf_op jit(solution)/shard_map/pallas_call | solution.py:467
  156.7 1.5 collective-permute-start.18
  158.3 3.4 %collective-permute-done.18 = f32[192,128]{1,0:T(8,128)S(1)} collective-permute-done((f32[192,128]{1,0:T(8,128)S(1)}, f32[192,128]{1,0:T(8,128)S(1)}, u32[]{:S(2)}, u32[]{:S(2)}) %collective-permute-start.18) | collective-permute-done | bytes 98336 | tf_op jit(solution)/shard_map/ppermute | solution.py:390
  161.7 4.6 %collective-permute-done.19 = f32[192,128]{1,0:T(8,128)S(1)} collective-permute-done((f32[192,128]{1,0:T(8,128)S(1)}, f32[192,128]{1,0:T(8,128)S(1)}, u32[]{:S(2)}, u32[]{:S(2)}) %collective-permute-start.19) | collective-permute-done | bytes 98336 | tf_op jit(solution)/shard_map/ppermute | solution.py:390
  166.3 1.8 collective-permute-start.20
  168.2 4.2 %collective-permute-done.20 = f32[192,128]{1,0:T(8,128)S(1)} collective-permute-done((f32[192,128]{1,0:T(8,128)S(1)}, f32[192,128]{1,0:T(8,128)S(1)}, u32[]{:S(2)}, u32[]{:S(2)}) %collective-permute-start.20) | collective-permute-done | bytes 98336 | tf_op jit(solution)/shard_map/ppermute | solution.py:390
  172.5 1.3 collective-permute-done.21.other_g
  173.8 16.4 %shard_map.49 = f32[16,256,128]{2,1,0:T(8,128)} custom-call(s32[35]{0:T(128)S(1)} %concatenate.20.tab, f32[192,128]{1,0:T(8,128)S(1)} %add.65.own_g, f32[192,128]{1,0:T(8,128)S(1)} %collective-permute-done.21.other_g, f32[16,128,256]{2,1,0:T(8,128)S(1)} %shard_map.46.own.mine_hbm, f32[16,128,256]{2,1,0:T(8,128)S(1)} %collective-permute-done.17.other.other_hbm), custom_call_target="tpu_custom_call" | custom-call | bytes 4194304 | tf_op jit(solution)/shard_map/pallas_call | solution.py:490
  (91 shorter events, 11.8 us)
Async XLA Ops:
  0.0 1.7 copy-start
  1.7 8.6 %copy-start.11 = (s32[8,9,3]{1,0,2:T(8,128)S(1)}, s32[8,9,3]{1,0,2:T(8,128)}, u32[]{:S(2)}) copy-start(s32[8,9,3]{1,0,2:T(8,128)} %param.4) | copy-start | bytes 2596
  1.7 18.6 %copy-start.1 = (s32[9,256,256]{2,1,0:T(8,128)S(1)}, s32[9,256,256]{2,1,0:T(8,128)}, u32[]{:S(2)}) copy-start(s32[9,256,256]{2,1,0:T(8,128)} %counts_ref.3) | copy-start | bytes 7077892
  2.9 16.6 %all-to-all-start = ((f32[8,24,256]{2,1,0:T(8,128)}), f32[8,24,256]{2,1,0:T(8,128)S(1)}, u32[]{:S(2)}, u32[]{:S(2)}) async-start(f32[8,24,256]{2,1,0:T(8,128)} %shard_map.38), calls=%async_computation | async-start | bytes 393216 | tf_op jit(solution)/shard_map/all_to_all | solution.py:396
  11.9 1.2 copy-start.4
  15.6 1.0 copy-start.2
  16.5 0.7 copy-start.9
  17.2 11.0 %collective-permute-start = (bf16[4,1,128,256]{3,2,1,0:T(8,128)(2,1)}, bf16[4,1,128,256]{3,2,1,0:T(8,128)(2,1)}, u32[]{:S(2)}, u32[]{:S(2)}) collective-permute-start(bf16[4,1,128,256]{3,2,1,0:T(8,128)(2,1)} %get-tuple-element.22), channel_id=1, source_target_pairs={{0,2},{2,0},{4,6},{6,4},{8,10},{10,8},{12,14},{14,12},{1,3},{3,1},... | collective-permute-start | bytes 786440 | tf_op jit(solution)/shard_map/ppermute | solution.py:390
  19.6 0.7 copy-start.5
  20.3 1.2 copy-start.3
  21.5 0.9 copy-start.6
  24.0 4.3 %copy-start.7 = (bf16[1,1,128,256]{3,2,1,0:T(8,128)(2,1)}, bf16[1,1,128,256]{3,2,1,0:T(8,128)(2,1)S(1)}, u32[]{:S(2)}) copy-start(bf16[1,1,128,256]{3,2,1,0:T(8,128)(2,1)S(1)} %get-tuple-element.23) | copy-start | bytes 196612
  24.0 5.2 %collective-permute-start.1 = (bf16[1,1,128,256]{3,2,1,0:T(8,128)(2,1)S(1)}, bf16[1,1,128,256]{3,2,1,0:T(8,128)(2,1)S(1)}, u32[]{:S(2)}, u32[]{:S(2)}) collective-permute-start(bf16[1,1,128,256]{3,2,1,0:T(8,128)(2,1)S(1)} %get-tuple-element.23), channel_id=1, source_target_pairs={{0,8},{2,10},{4,12},{6,14},{8,0},{10,2},{12,4},{14,6},{1,9},{3,11}... | collective-permute-start | bytes 196616 | tf_op jit(solution)/shard_map/ppermute | solution.py:390
  26.4 8.0 %copy-start.12 = (s32[8,1]{0,1:T(1,128)S(1)}, s32[8,1]{0,1:T(1,128)}, u32[]{:S(2)}) copy-start(s32[8,1]{0,1:T(1,128)} %get-tuple-element.35) | copy-start | bytes 100
  26.4 8.3 %copy-start.10 = (bf16[4,1,128,256]{3,2,1,0:T(8,128)(2,1)S(1)}, bf16[4,1,128,256]{3,2,1,0:T(8,128)(2,1)}, u32[]{:S(2)}) copy-start(bf16[4,1,128,256]{3,2,1,0:T(8,128)(2,1)} %copy-done.9) | copy-start | bytes 786436
  28.2 6.4 %copy-start.8 = (bf16[1,1,128,256]{3,2,1,0:T(8,128)(2,1)S(1)}, bf16[1,1,128,256]{3,2,1,0:T(8,128)(2,1)}, u32[]{:S(2)}) copy-start(bf16[1,1,128,256]{3,2,1,0:T(8,128)(2,1)} %copy-done.7) | copy-start | bytes 196612
  29.2 36.6 %all-to-all-start.1 = ((bf16[8,2,128,256]{3,2,1,0:T(8,128)(2,1)}), bf16[8,2,128,256]{3,2,1,0:T(8,128)(2,1)S(1)}, u32[]{:S(2)}, u32[]{:S(2)}) async-start(bf16[8,2,128,256]{3,2,1,0:T(8,128)(2,1)} %shard_map.40), calls=%async_computation.1 | async-start | bytes 2097152 | tf_op jit(solution)/shard_map/all_to_all | solution.py:396
  35.8 18.5 %collective-permute-start.2 = (bf16[2,1,128,256]{3,2,1,0:T(8,128)(2,1)S(1)}, bf16[2,1,128,256]{3,2,1,0:T(8,128)(2,1)S(1)}, u32[]{:S(2)}, u32[]{:S(2)}) collective-permute-start(bf16[2,1,128,256]{3,2,1,0:T(8,128)(2,1)S(1)} %slice.89), channel_id=1, source_target_pairs={{0,4},{2,6},{4,0},{6,2},{8,12},{10,14},{12,8},{14,10},{1,5},{3,7},... | collective-permute-start | bytes 393224 | tf_op jit(solution)/shard_map/ppermute | solution.py:390
  37.9 21.5 %collective-permute-start.4 = (bf16[2,1,128,256]{3,2,1,0:T(8,128)(2,1)S(1)}, bf16[2,1,128,256]{3,2,1,0:T(8,128)(2,1)S(1)}, u32[]{:S(2)}, u32[]{:S(2)}) collective-permute-start(bf16[2,1,128,256]{3,2,1,0:T(8,128)(2,1)S(1)} %pad_maximum_fusion), channel_id=1, source_target_pairs={{0,4},{2,6},{4,0},{6,2},{8,12},{10,14},{12,8},{14,10},{1,5},{3,7},... | collective-permute-start | bytes 393224 | tf_op jit(solution)/shard_map/ppermute | solution.py:390
  54.3 7.8 %collective-permute-start.3 = (bf16[1,1,128,256]{3,2,1,0:T(8,128)(2,1)S(1)}, bf16[1,1,128,256]{3,2,1,0:T(8,128)(2,1)S(1)}, u32[]{:S(2)}, u32[]{:S(2)}) collective-permute-start(bf16[1,1,128,256]{3,2,1,0:T(8,128)(2,1)S(1)} %slice.99), channel_id=1, source_target_pairs={{0,8},{2,10},{4,12},{6,14},{8,0},{10,2},{12,4},{14,6},{1,9},{3,11}... | collective-permute-start | bytes 196616 | tf_op jit(solution)/shard_map/ppermute | solution.py:390
  59.4 6.4 %collective-permute-start.5 = (bf16[4,1,128,256]{3,2,1,0:T(8,128)(2,1)S(1)}, bf16[4,1,128,256]{3,2,1,0:T(8,128)(2,1)S(1)}, u32[]{:S(2)}, u32[]{:S(2)}) collective-permute-start(bf16[4,1,128,256]{3,2,1,0:T(8,128)(2,1)S(1)} %constant_dynamic-update-slice_fusion.hot_a), channel_id=1, source_target_pairs={{0,2},{2,0},{4,6},{6,4},{8,10},{10,8},{12,14},{14,12},{1,3},{3,1},... | collective-permute-start | bytes 786440 | tf_op jit(solution)/shard_map/ppermute | solution.py:390
  67.1 4.2 %collective-permute-start.6 = (f32[16,128,256]{2,1,0:T(8,128)S(1)}, f32[16,128,256]{2,1,0:T(8,128)S(1)}, u32[]{:S(2)}, u32[]{:S(2)}) collective-permute-start(f32[16,128,256]{2,1,0:T(8,128)S(1)} %shard_map.41.own.mine_hbm), channel_id=1, source_target_pairs={{0,1},{1,0},{2,3},{3,2},{4,5},{5,4},{6,7},{7,6},{8,9},{9,8},{10,11... | collective-permute-start | bytes 6291464 | tf_op jit(solution)/shard_map/ppermute | solution.py:393
  73.3 4.9 %collective-permute-start.7 = (f32[192,128]{1,0:T(8,128)S(1)}, f32[192,128]{1,0:T(8,128)S(1)}, u32[]{:S(2)}, u32[]{:S(2)}) collective-permute-start(f32[192,128]{1,0:T(8,128)S(1)} %shard_map.43), channel_id=1, source_target_pairs={{0,2},{2,0},{4,6},{6,4},{8,10},{10,8},{12,14},{14,12},{1,3},{3,1},... | collective-permute-start | bytes 294920 | tf_op jit(solution)/shard_map/ppermute | solution.py:390
  78.2 4.7 %collective-permute-start.8 = (f32[192,128]{1,0:T(8,128)S(1)}, f32[192,128]{1,0:T(8,128)S(1)}, u32[]{:S(2)}, u32[]{:S(2)}) collective-permute-start(f32[192,128]{1,0:T(8,128)S(1)} %add.60), channel_id=1, source_target_pairs={{0,4},{2,6},{4,0},{6,2},{8,12},{10,14},{12,8},{14,10},{1,5},{3,7},... | collective-permute-start | bytes 294920 | tf_op jit(solution)/shard_map/ppermute | solution.py:390
  82.9 6.1 %collective-permute-start.9 = (f32[192,128]{1,0:T(8,128)S(1)}, f32[192,128]{1,0:T(8,128)S(1)}, u32[]{:S(2)}, u32[]{:S(2)}) collective-permute-start(f32[192,128]{1,0:T(8,128)S(1)} %add.61), channel_id=1, source_target_pairs={{0,8},{2,10},{4,12},{6,14},{8,0},{10,2},{12,4},{14,6},{1,9},{3,11}... | collective-permute-start | bytes 294920 | tf_op jit(solution)/shard_map/ppermute | solution.py:390
  89.0 1.4 collective-permute-start.10
  104.8 8.4 %collective-permute-start.11 = (bf16[4,1,128,256]{3,2,1,0:T(8,128)(2,1)S(1)}, bf16[4,1,128,256]{3,2,1,0:T(8,128)(2,1)S(1)}, u32[]{:S(2)}, u32[]{:S(2)}) collective-permute-start(bf16[4,1,128,256]{3,2,1,0:T(8,128)(2,1)S(1)} %get-tuple-element.29), channel_id=1, source_target_pairs={{0,2},{2,0},{4,6},{6,4},{8,10},{10,8},{12,14},{14,12},{1,3},{3,1},... | collective-permute-start | bytes 786440 | tf_op jit(solution)/shard_map/ppermute | solution.py:390
  106.3 5.5 %collective-permute-start.12 = (bf16[1,1,128,256]{3,2,1,0:T(8,128)(2,1)S(1)}, bf16[1,1,128,256]{3,2,1,0:T(8,128)(2,1)S(1)}, u32[]{:S(2)}, u32[]{:S(2)}) collective-permute-start(bf16[1,1,128,256]{3,2,1,0:T(8,128)(2,1)S(1)} %get-tuple-element.30), channel_id=1, source_target_pairs={{0,8},{2,10},{4,12},{6,14},{8,0},{10,2},{12,4},{14,6},{1,9},{3,11}... | collective-permute-start | bytes 196616 | tf_op jit(solution)/shard_map/ppermute | solution.py:390
  113.3 36.0 %all-to-all-start.2 = ((bf16[8,2,128,256]{3,2,1,0:T(8,128)(2,1)}), bf16[8,2,128,256]{3,2,1,0:T(8,128)(2,1)S(1)}, u32[]{:S(2)}, u32[]{:S(2)}) async-start(bf16[8,2,128,256]{3,2,1,0:T(8,128)(2,1)} %shard_map.45), calls=%async_computation.2 | async-start | bytes 2097152 | tf_op jit(solution)/shard_map/all_to_all | solution.py:396
  117.0 20.8 %collective-permute-start.13 = (bf16[2,1,128,256]{3,2,1,0:T(8,128)(2,1)S(1)}, bf16[2,1,128,256]{3,2,1,0:T(8,128)(2,1)S(1)}, u32[]{:S(2)}, u32[]{:S(2)}) collective-permute-start(bf16[2,1,128,256]{3,2,1,0:T(8,128)(2,1)S(1)} %slice.93), channel_id=1, source_target_pairs={{0,4},{2,6},{4,0},{6,2},{8,12},{10,14},{12,8},{14,10},{1,5},{3,7},... | collective-permute-start | bytes 393224 | tf_op jit(solution)/shard_map/ppermute | solution.py:390
  119.0 23.8 %collective-permute-start.15 = (bf16[2,1,128,256]{3,2,1,0:T(8,128)(2,1)S(1)}, bf16[2,1,128,256]{3,2,1,0:T(8,128)(2,1)S(1)}, u32[]{:S(2)}, u32[]{:S(2)}) collective-permute-start(bf16[2,1,128,256]{3,2,1,0:T(8,128)(2,1)S(1)} %pad_maximum_fusion.1), channel_id=1, source_target_pairs={{0,4},{2,6},{4,0},{6,2},{8,12},{10,14},{12,8},{14,10},{1,5},{3,7},... | collective-permute-start | bytes 393224 | tf_op jit(solution)/shard_map/ppermute | solution.py:390
  137.9 7.8 %collective-permute-start.14 = (bf16[1,1,128,256]{3,2,1,0:T(8,128)(2,1)S(1)}, bf16[1,1,128,256]{3,2,1,0:T(8,128)(2,1)S(1)}, u32[]{:S(2)}, u32[]{:S(2)}) collective-permute-start(bf16[1,1,128,256]{3,2,1,0:T(8,128)(2,1)S(1)} %slice.101), channel_id=1, source_target_pairs={{0,8},{2,10},{4,12},{6,14},{8,0},{10,2},{12,4},{14,6},{1,9},{3,11}... | collective-permute-start | bytes 196616 | tf_op jit(solution)/shard_map/ppermute | solution.py:390
  142.8 6.4 %collective-permute-start.16 = (bf16[4,1,128,256]{3,2,1,0:T(8,128)(2,1)S(1)}, bf16[4,1,128,256]{3,2,1,0:T(8,128)(2,1)S(1)}, u32[]{:S(2)}, u32[]{:S(2)}) collective-permute-start(bf16[4,1,128,256]{3,2,1,0:T(8,128)(2,1)S(1)} %constant_dynamic-update-slice_fusion.3.hot_a), channel_id=1, source_target_pairs={{0,2},{2,0},{4,6},{6,4},{8,10},{10,8},{12,14},{14,12},{1,3},{3,1},... | collective-permute-start | bytes 786440 | tf_op jit(solution)/shard_map/ppermute | solution.py:390
  150.5 4.2 %collective-permute-start.17 = (f32[16,128,256]{2,1,0:T(8,128)S(1)}, f32[16,128,256]{2,1,0:T(8,128)S(1)}, u32[]{:S(2)}, u32[]{:S(2)}) collective-permute-start(f32[16,128,256]{2,1,0:T(8,128)S(1)} %shard_map.46.own.mine_hbm), channel_id=1, source_target_pairs={{0,1},{1,0},{2,3},{3,2},{4,5},{5,4},{6,7},{7,6},{8,9},{9,8},{10,11... | collective-permute-start | bytes 6291464 | tf_op jit(solution)/shard_map/ppermute | solution.py:393
  156.7 4.9 %collective-permute-start.18 = (f32[192,128]{1,0:T(8,128)S(1)}, f32[192,128]{1,0:T(8,128)S(1)}, u32[]{:S(2)}, u32[]{:S(2)}) collective-permute-start(f32[192,128]{1,0:T(8,128)S(1)} %shard_map.48), channel_id=1, source_target_pairs={{0,2},{2,0},{4,6},{6,4},{8,10},{10,8},{12,14},{14,12},{1,3},{3,1},... | collective-permute-start | bytes 294920 | tf_op jit(solution)/shard_map/ppermute | solution.py:390
  161.7 4.7 %collective-permute-start.19 = (f32[192,128]{1,0:T(8,128)S(1)}, f32[192,128]{1,0:T(8,128)S(1)}, u32[]{:S(2)}, u32[]{:S(2)}) collective-permute-start(f32[192,128]{1,0:T(8,128)S(1)} %add.63), channel_id=1, source_target_pairs={{0,4},{2,6},{4,0},{6,2},{8,12},{10,14},{12,8},{14,10},{1,5},{3,7},... | collective-permute-start | bytes 294920 | tf_op jit(solution)/shard_map/ppermute | solution.py:390
  166.3 6.1 %collective-permute-start.20 = (f32[192,128]{1,0:T(8,128)S(1)}, f32[192,128]{1,0:T(8,128)S(1)}, u32[]{:S(2)}, u32[]{:S(2)}) collective-permute-start(f32[192,128]{1,0:T(8,128)S(1)} %add.64), channel_id=1, source_target_pairs={{0,8},{2,10},{4,12},{6,14},{8,0},{10,2},{12,4},{14,6},{1,9},{3,11}... | collective-permute-start | bytes 294920 | tf_op jit(solution)/shard_map/ppermute | solution.py:390
  172.4 1.4 collective-permute-start.21

commit v5 on v4

--- a/solution.py
+++ b/solution.py
@@ -24,7 +24,7 @@
     )
 
 
-def call(kernel, out_shape, in_specs, out_specs=None, scratch=(), flops=0, vmem=32):
+def call(kernel, out_shape, in_specs, out_specs=None, scratch=(), flops=0, vmem=20):
     if out_specs is None:
         out_specs = jax.tree.map(lambda _: VMEM, out_shape)
     return pl.pallas_call(
@@ -41,6 +41,9 @@
 class Table:
     def __init__(self, groups, nnz):
         self.groups, self.nnz, self.hot = groups, nnz, nnz - groups
+        bits = [1 << b for b in range(groups.bit_length() - 1)]
+        self.bits = bits
+        self.steps = bits[1:-1] + bits[:1] + bits[-1:]
         self.main_j = 0
         self.hot_j = self.main_j + groups
         self.row_i = self.hot_j + groups * self.hot
@@ -71,13 +74,15 @@
 
 
 def gather_hot(t, tab, blocks, near, far):
+    bit = t.steps[0]
     for k in range(t.groups):
+        place = (k // (2 * bit)) * bit + k % bit
         for m in range(t.hot):
             j = tab[t.hot_j + k * t.hot + m]
 
             @pl.when(j >= 0)
             def _():
-                (far if k % 2 else near)[k // 2, m] = blocks[j]
+                (far if k & bit else near)[place, m] = blocks[j]
 
 
 def product(t, tab, blocks, ppmi, s):
@@ -89,10 +94,15 @@
         hot[0, m] = product(t, tab, blocks, ppmi, t.groups + m)
 
 
-def make_main_kernel(t):
+def gather_main(t, tab, blocks, send, slot):
+    for r in range(t.groups):
+        send[r, slot] = blocks[tab[t.main_j + r]]
+
+
+def make_main_kernel(t, with_blocks):
     def kernel(tab, blocks, ppmi, send):
-        for r in range(t.groups):
-            send[r, 1] = blocks[tab[t.main_j + r]]
+        if with_blocks:
+            gather_main(t, tab, blocks, send, 1)
         for s in range(t.groups):
             send[tab[t.dest + s], 0] = product(t, tab, blocks, ppmi, s)
 
@@ -100,11 +110,12 @@
 
 
 def make_source_kernel(t):
-    def kernel(tab, sketch_ref, turned, near, far):
+    def kernel(tab, sketch_ref, turned, send, near, far):
         @pl.loop(0, sketch_ref.shape[0])
         def _(i):
             turned[i] = sketch_ref[i].T
 
+        gather_main(t, tab, turned, send, 0)
         gather_hot(t, tab, turned, near, far)
 
     return kernel
@@ -141,14 +152,17 @@
 
 
 def make_result_kernel(t, order):
-    def kernel(tab, ppmi_ref, got, hot_x, hot_a, hot_b, result):
+    def kernel(tab, ppmi_ref, *refs):
+        got_t, got_x = refs[0], refs[-5]
+        hot_x, hot_a, hot_b, result = refs[-4:]
+        slot = got_x.shape[1] - 1
         result[...] = jnp.zeros_like(result)
         for s in range(t.nnz):
-            block = got[tab[t.dest + s], 1] if s < t.groups else hot_x[0, s - t.groups]
+            block = got_x[tab[t.dest + s], slot] if s < t.groups else hot_x[0, s - t.groups]
             forward = contract(block, ppmi_ref[s], 1, 1).astype(bf16)
             result[tab[t.row_i + s]] += forward.astype(f32)
         for r in range(t.groups):
-            result[tab[t.main_j + r]] += got[r, 0].astype(f32)
+            result[tab[t.main_j + r]] += got_t[r, 0].astype(f32)
         for n, k in enumerate(order):
             ref, place = (hot_a, n) if n < t.groups // 2 else (hot_b, n - t.groups // 2)
             for m in range(t.hot):
@@ -384,7 +398,6 @@
     t = Table(groups, nnz)
     hot = t.hot
     depth = -(-2 * nnz // 8) * 8
-    bits = [1 << b for b in range(groups.bit_length() - 1)]
 
     def peer(x, k):
         return lax.ppermute(x, "row", [(r, r ^ k) for r in range(groups)])
@@ -396,44 +409,56 @@
         return lax.all_to_all(x, "row", split_axis=0, concat_axis=0, tiled=True)
 
     def add_up(x):
-        for bit in bits:
+        for bit in t.bits:
             x = x + peer(x, bit)
         return x
 
     def spread_hot(part, got):
         part = jnp.concatenate([part, got], axis=0)
-        for bit in bits[-2:0:-1]:
+        for bit in t.steps[-2:0:-1]:
             part = jnp.concatenate([part, peer(part, bit)], axis=0)
-        return part, peer(part, bits[0])
+        return part, peer(part, t.steps[0])
 
     hot_order = [0]
-    for bit in bits[::-1]:
+    for bit in t.steps[::-1]:
         hot_order += [k ^ bit for k in hot_order]
 
+    def halve(x, kept, bit):
+        low = sum(1 for k in kept if k < bit)
+        x = x.reshape(-1, 2, low, *x.shape[1:])
+        return [x[:, n].reshape(-1, *x.shape[3:]) for n in range(2)]
+
     def scatter_hot(near, far, got, towards):
-        for bit in bits:
-            if bit > 1:
+        kept = list(range(groups))
+        for bit in t.steps:
+            if bit != t.steps[0]:
+                near, far = halve(part, kept, bit)
                 got = peer(far, bit)
-            towards = towards[::2]
+            towards = halve(towards, kept, bit)[0]
+            kept = [k for k in kept if not k & bit]
             stay = (towards & bit) == 0
             part = jnp.where(stay[:, :, None, None], near, got)
-            near, far = part[::2], part[1::2]
         return part
 
     send_shape = shape((groups, 2, half, rows), bf16)
+    one_shape = shape((groups, 1, half, rows), bf16)
     hot_shape = shape((1, hot, half, rows), bf16)
     side_shape = shape((groups // 2, hot, half, rows), bf16)
     ppmi_shape = shape((nnz, rows, rows), bf16)
     result_shape = shape((blocks, half, rows), f32)
 
-    sums = call(sums_kernel, shape((groups, depth, rows), f32), [VMEM])(counts)
+    sums = call(sums_kernel, shape((groups, depth, rows), f32), [VMEM], vmem=8)(counts)
     sums_all = exchange(sums)
     tab, towards = t.build(block_pairs, me, my_col)
-    turned, near, far = call(
+    turned, send_x, near, far = call(
         make_source_kernel(t),
-        [shape((blocks, half, rows), bf16), side_shape, side_shape],
+        [shape((blocks, half, rows), bf16), one_shape, side_shape, side_shape],
         [SMEM, VMEM],
+        vmem=8,
     )(tab, sketch)
+    send_x, sums_all = lax.optimization_barrier((send_x, sums_all))
+    got_x = exchange(send_x)
+    x_step = peer(far, t.steps[0])
 
     row_ids = block_pairs[:, :, 0] * groups + jnp.arange(groups)[:, None]
     col_ids = block_pairs[:, :, 2] * groups + block_pairs[:, :, 1]
@@ -447,27 +472,39 @@
         [ppmi_shape, hot_shape],
         [SMEM] + [VMEM] * 4,
         scratch=[pltpu.VMEM((depth, rows), f32)],
+        vmem=12,
     )(tab, match, counts, turned, sums_all)
 
-    def finish(source, near, far, hot_t):
-        send = call(make_main_kernel(t), send_shape, [SMEM, VMEM, VMEM])(tab, source, ppmi)
-        send, x_step, t_step = lax.optimization_barrier(
-            (send, peer(far, bits[0]), peer(hot_t, bits[-1]))
-        )
-        got = exchange(send)
+    def finish(source, got_x, near, far, x_step, hot_t):
+        t_step = peer(hot_t, t.steps[-1])
+        if x_step is None:
+            x_step = peer(far, t.steps[0])
+        send = call(
+            make_main_kernel(t, got_x is None),
+            one_shape if got_x is not None else send_shape,
+            [SMEM, VMEM, VMEM],
+            vmem=8,
+        )(tab, source, ppmi)
+        if got_x is None:
+            send, x_step, t_step = lax.optimization_barrier((send, x_step, t_step))
+        else:
+            send, t_step = lax.optimization_barrier((send, t_step))
+        got = [exchange(send)] + ([] if got_x is None else [got_x])
         hot_x = scatter_hot(near, far, x_step, towards)
         hot_a, hot_b = spread_hot(hot_t, t_step)
         result = call(
             make_result_kernel(t, hot_order),
             result_shape,
-            [SMEM] + [VMEM] * 5,
-        )(tab, ppmi, got, hot_x, hot_a, hot_b)
+            [SMEM] + [VMEM] * (4 + len(got)),
+            vmem=12,
+        )(tab, ppmi, *got, hot_x, hot_a, hot_b)
         other = swap(result)
-        square = call(own_gram_kernel, shape((half, half), f32), [VMEM])(result)
+        square = call(own_gram_kernel, shape((half, half), f32), [VMEM], vmem=12)(result)
         gram = call(
             make_cross_gram_kernel(t),
             shape((half + half // 2, half), f32),
             [SMEM] + [VMEM] * 3,
+            vmem=16,
         )(tab, result, other, square)
         gram = add_up(gram)
         return result, other, gram, swap(gram)
@@ -477,7 +514,9 @@
         pltpu.VMEM((2, 2, half, half), f32),
     ]
     result_scratch = [pltpu.VMEM((blocks, half, rows), f32)] * 2
-    result, other, gram, other_gram = finish(turned, near, far, hot_t)
+    result, other, gram, other_gram = finish(
+        turned, got_x, near, far, x_step, hot_t
+    )
     normal, near, far, hot_t = call(
         make_second_kernel(t, 1.0 / vocab),
         [shape((blocks, half, rows), bf16), side_shape, side_shape, hot_shape],
@@ -486,7 +525,9 @@
         + result_scratch
         + [pltpu.VMEM((nnz, rows, rows), bf16), pltpu.SemaphoreType.DMA((3,))],
     )(tab, gram, other_gram, result, other, ppmi)
-    result, other, gram, other_gram = finish(normal, near, far, hot_t)
+    result, other, gram, other_gram = finish(
+        normal, None, near, far, None, hot_t
+    )
     return call(
         make_final_kernel(t, 1.0 / vocab),
         shape((blocks, rows, half), f32),

time: 191 us -> 190 us (level)
  waiting for transfers between devices: 83.3 us -> 74.6 us
  starting transfers between devices: 46.5 us -> 53.1 us
    ppermute x18, waiting for transfers between devices: 75.1 us -> 66.4 us  [peer(): return lax.ppermute(x, 'row', [(r, r ^ k) for r in range(groups)])]
    all_to_all x3 -> x4, starting transfers between devices: 16.1 us -> 21.7 us  [exchange(): return lax.all_to_all(x, 'row', split_axis=0, concat_axis=0, tiled=True)]
    unnamed x31 -> x29, local copies, waits for them, and re-layouts: 7.42 us -> 6.09 us
  transfers between devices with their start and end apart: 25 -> 26, of which waited for: 19 -> 21; matrix products, arithmetic and copies ran while one was open for 2% -> 3% of each run, Pallas kernels for 5% -> 6%
where the time goes in v5:
time: 190 us; the launch traced here: 189 us
  waiting for transfers between devices  74.6 us (39%)
  starting transfers between devices  53.1 us (28%)
  Pallas kernels  48.9 us (26%)
  local copies, waits for them, and re-layouts  8.21 us (4%)
  other arithmetic  3.64 us (2%)
    ppermute x18, waiting for transfers between devices, peer(): return lax.ppermute(x, 'row', [(r, r ^ k) for r in range(groups)])  66.4 us
    ppermute x18, starting transfers between devices, peer(): return lax.ppermute(x, 'row', [(r, r ^ k) for r in range(groups)])  31.1 us
    all_to_all x4, starting transfers between devices, exchange(): return lax.all_to_all(x, 'row', split_axis=0, concat_axis=0, tiled=True)  21.7 us
    pallas_call x1, Pallas kernels, body(): call(make_final_kernel(t, 1.0 / vocab), shape((blocks, rows, half), f32),...  16.4 us
    pallas_call x1, Pallas kernels, body(): call(make_second_kernel(t, 1.0 / vocab), [shape((blocks, half, rows), bf1...  14.4 us
    ppermute x4, waiting for transfers between devices, swap(): return lax.ppermute(x, 'col', [(0, 1), (1, 0)])  8.19 us
    unnamed x29, local copies, waits for them, and re-layouts  6.09 us
    pallas_call x2, Pallas kernels, finish(): call(make_cross_gram_kernel(t), shape((half + half // 2, half), f32), [SM...  3.88 us
  transfers between devices with their start and end apart: 26, of which 21 were waited for; matrix products, arithmetic and copies ran while one was open for 3% of the time, Pallas kernels for 6%

profile of v5, /device:TPU:0, one launch (start us, length us, event | category | flops | bytes accessed | tf_op | source)
XLA Modules:
  0.0 189.1 jit_solution(9261317714853489505)
XLA Ops:
  0.0 1.7 copy-done
  3.0 7.4 %all-to-all-start = ((f32[8,24,256]{2,1,0:T(8,128)}), f32[8,24,256]{2,1,0:T(8,128)}, u32[]{:S(2)}, u32[]{:S(2)}) async-start(f32[8,24,256]{2,1,0:T(8,128)} %copy-done.5), calls=%async_computation | async-start | bytes 393216 | tf_op jit(solution)/shard_map/all_to_all | solution.py:409
  11.5 2.5 %shard_map.37 = (bf16[16,128,256]{2,1,0:T(8,128)(2,1)S(1)}, bf16[8,1,128,256]{3,2,1,0:T(8,128)(2,1)S(1)}, bf16[4,1,128,256]{3,2,1,0:T(8,128)(2,1)S(1)}, bf16[4,1,128,256]{3,2,1,0:T(8,128)(2,1)}) custom-call(s32[35]{0:T(128)S(1)} %concatenate.20.tab, bf16[16,256,128]{2,1,0:T(8,128)(2,1)S(1)} %copy-done.4), custom_call_target="tpu_custom_call" | custom-call | bytes 4194304 | tf_op jit(solution)/shard_map/pallas_call | solution.py:453
  16.5 2.0 %collective-permute-start.1 = (bf16[4,1,128,256]{3,2,1,0:T(8,128)(2,1)}, bf16[4,1,128,256]{3,2,1,0:T(8,128)(2,1)S(1)}, u32[]{:S(2)}, u32[]{:S(2)}) collective-permute-start(bf16[4,1,128,256]{3,2,1,0:T(8,128)(2,1)} %get-tuple-element.30), channel_id=1, source_target_pairs={{0,4},{2,6},{4,0},{6,2},{8,12},{10,14},{12,8},{14,10},{1,5},{3,7},... | collective-permute-start | bytes 786440 | tf_op jit(solution)/shard_map/ppermute | solution.py:403
  18.9 4.5 %all-to-all-start.2 = ((bf16[8,1,128,256]{3,2,1,0:T(8,128)(2,1)}), bf16[8,1,128,256]{3,2,1,0:T(8,128)(2,1)}, u32[]{:S(2)}, u32[]{:S(2)}) async-start(bf16[8,1,128,256]{3,2,1,0:T(8,128)(2,1)} %copy-done.6), calls=%async_computation.2 | async-start | bytes 1048576 | tf_op jit(solution)/shard_map/all_to_all | solution.py:409
  26.4 1.5 collective-permute-start.2
  29.3 1.9 %shard_map.39 = (bf16[9,256,256]{2,1,0:T(8,128)(2,1)S(1)}, bf16[1,1,128,256]{3,2,1,0:T(8,128)(2,1)S(1)}) custom-call(s32[35]{0:T(128)S(1)} %concatenate.20.tab, bf16[24,192]{1,0:T(8,128)(2,1)S(1)} %compare_convert_fusion.match_ref, s32[9,256,256]{2,1,0:T(8,128)S(1)} %copy-done.1, bf16[16,128,256]{2,1,0:T(8,128)(2,1)S(1)} %copy-done.3, ...), custom_call_target="tpu_custom_call" | custom-call | bytes 4194304 | tf_op jit(solution)/shard_map/pallas_call | solution.py:470
  31.3 1.6 shard_map.40
  32.9 3.3 %collective-permute-start = (bf16[1,1,128,256]{3,2,1,0:T(8,128)(2,1)S(1)}, bf16[1,1,128,256]{3,2,1,0:T(8,128)(2,1)S(1)}, u32[]{:S(2)}, u32[]{:S(2)}) collective-permute-start(bf16[1,1,128,256]{3,2,1,0:T(8,128)(2,1)S(1)} %get-tuple-element.26), channel_id=1, source_target_pairs={{0,8},{2,10},{4,12},{6,14},{8,0},{10,2},{12,4},{14,6},{1,9},{3,11}... | collective-permute-start | bytes 196616 | tf_op jit(solution)/shard_map/ppermute | solution.py:403
  36.2 3.1 %collective-permute-done = bf16[1,1,128,256]{3,2,1,0:T(8,128)(2,1)S(1)} collective-permute-done((bf16[1,1,128,256]{3,2,1,0:T(8,128)(2,1)S(1)}, bf16[1,1,128,256]{3,2,1,0:T(8,128)(2,1)S(1)}, u32[]{:S(2)}, u32[]{:S(2)}) %collective-permute-start) | collective-permute-done | bytes 65568 | tf_op jit(solution)/shard_map/ppermute | solution.py:403
  39.3 5.4 %all-to-all-start.1 = ((bf16[8,1,128,256]{3,2,1,0:T(8,128)(2,1)}), bf16[8,1,128,256]{3,2,1,0:T(8,128)(2,1)S(1)}, u32[]{:S(2)}, u32[]{:S(2)}) async-start(bf16[8,1,128,256]{3,2,1,0:T(8,128)(2,1)} %shard_map.40), calls=%async_computation.1 | async-start | bytes 1048576 | tf_op jit(solution)/shard_map/all_to_all | solution.py:409
  46.6 2.1 %collective-permute-start.4 = (bf16[2,1,128,256]{3,2,1,0:T(8,128)(2,1)S(1)}, bf16[2,1,128,256]{3,2,1,0:T(8,128)(2,1)S(1)}, u32[]{:S(2)}, u32[]{:S(2)}) collective-permute-start(bf16[2,1,128,256]{3,2,1,0:T(8,128)(2,1)S(1)} %pad_maximum_fusion), channel_id=1, source_target_pairs={{0,2},{2,0},{4,6},{6,4},{8,10},{10,8},{12,14},{14,12},{1,3},{3,1},... | collective-permute-start | bytes 393224 | tf_op jit(solution)/shard_map/ppermute | solution.py:403
  48.6 2.4 %collective-permute-start.3 = (bf16[1,1,128,256]{3,2,1,0:T(8,128)(2,1)S(1)}, bf16[1,1,128,256]{3,2,1,0:T(8,128)(2,1)S(1)}, u32[]{:S(2)}, u32[]{:S(2)}) collective-permute-start(bf16[1,1,128,256]{3,2,1,0:T(8,128)(2,1)S(1)} %slice_bitcast_fusion.6), channel_id=1, source_target_pairs={{0,8},{2,10},{4,12},{6,14},{8,0},{10,2},{12,4},{14,6},{1,9},{3,11}... | collective-permute-start | bytes 196616 | tf_op jit(solution)/shard_map/ppermute | solution.py:403
  51.0 2.1 %collective-permute-done.4 = bf16[2,1,128,256]{3,2,1,0:T(8,128)(2,1)S(1)} collective-permute-done((bf16[2,1,128,256]{3,2,1,0:T(8,128)(2,1)S(1)}, bf16[2,1,128,256]{3,2,1,0:T(8,128)(2,1)S(1)}, u32[]{:S(2)}, u32[]{:S(2)}) %collective-permute-start.4) | collective-permute-done | bytes 131104 | tf_op jit(solution)/shard_map/ppermute | solution.py:403
  53.1 2.1 %collective-permute-start.5 = (bf16[4,1,128,256]{3,2,1,0:T(8,128)(2,1)S(1)}, bf16[4,1,128,256]{3,2,1,0:T(8,128)(2,1)S(1)}, u32[]{:S(2)}, u32[]{:S(2)}) collective-permute-start(bf16[4,1,128,256]{3,2,1,0:T(8,128)(2,1)S(1)} %constant_dynamic-update-slice_fusion.refs_3_), channel_id=1, source_target_pairs={{0,4},{2,6},{4,0},{6,2},{8,12},{10,14},{12,8},{14,10},{1,5},{3,7},... | collective-permute-start | bytes 786440 | tf_op jit(solution)/shard_map/ppermute | solution.py:403
  55.3 4.4 %collective-permute-done.3 = bf16[1,1,128,256]{3,2,1,0:T(8,128)(2,1)S(1)} collective-permute-done((bf16[1,1,128,256]{3,2,1,0:T(8,128)(2,1)S(1)}, bf16[1,1,128,256]{3,2,1,0:T(8,128)(2,1)S(1)}, u32[]{:S(2)}, u32[]{:S(2)}) %collective-permute-start.3) | collective-permute-done | bytes 65568 | tf_op jit(solution)/shard_map/ppermute | solution.py:403
  59.8 2.7 %collective-permute-done.5.refs_4_ = bf16[4,1,128,256]{3,2,1,0:T(8,128)(2,1)S(1)} collective-permute-done((bf16[4,1,128,256]{3,2,1,0:T(8,128)(2,1)S(1)}, bf16[4,1,128,256]{3,2,1,0:T(8,128)(2,1)S(1)}, u32[]{:S(2)}, u32[]{:S(2)}) %collective-permute-start.5) | collective-permute-done | bytes 262176 | tf_op jit(solution)/shard_map/ppermute | solution.py:403
  62.4 1.8 shard_map.41.own.mine_hbm
  64.3 1.3 shard_map.42.square
  65.7 2.8 %collective-permute-done.6.other.other_hbm = f32[16,128,256]{2,1,0:T(8,128)S(1)} collective-permute-done((f32[16,128,256]{2,1,0:T(8,128)S(1)}, f32[16,128,256]{2,1,0:T(8,128)S(1)}, u32[]{:S(2)}, u32[]{:S(2)}) %collective-permute-start.6) | collective-permute-done | bytes 2097184 | tf_op jit(solution)/shard_map/ppermute | solution.py:406
  68.5 1.9 %shard_map.43 = f32[192,128]{1,0:T(8,128)S(1)} custom-call(s32[35]{0:T(128)S(1)} %concatenate.20.tab, f32[16,128,256]{2,1,0:T(8,128)S(1)} %shard_map.41.own.mine_hbm, f32[16,128,256]{2,1,0:T(8,128)S(1)} %collective-permute-done.6.other.other_hbm, f32[128,128]{1,0:T(8,128)S(1)} %shard_map.42.square), custom_call_target="tpu_custom_call" | custom-call | bytes 4194304 | tf_op jit(solution)/shard_map/pallas_call | solution.py:503
  70.4 1.5 collective-permute-start.7
  71.9 3.4 %collective-permute-done.7 = f32[192,128]{1,0:T(8,128)S(1)} collective-permute-done((f32[192,128]{1,0:T(8,128)S(1)}, f32[192,128]{1,0:T(8,128)S(1)}, u32[]{:S(2)}, u32[]{:S(2)}) %collective-permute-start.7) | collective-permute-done | bytes 98336 | tf_op jit(solution)/shard_map/ppermute | solution.py:403
  75.4 4.6 %collective-permute-done.8 = f32[192,128]{1,0:T(8,128)S(1)} collective-permute-done((f32[192,128]{1,0:T(8,128)S(1)}, f32[192,128]{1,0:T(8,128)S(1)}, u32[]{:S(2)}, u32[]{:S(2)}) %collective-permute-start.8) | collective-permute-done | bytes 98336 | tf_op jit(solution)/shard_map/ppermute | solution.py:403
  80.0 2.3 %collective-permute-start.9 = (f32[192,128]{1,0:T(8,128)S(1)}, f32[192,128]{1,0:T(8,128)S(1)}, u32[]{:S(2)}, u32[]{:S(2)}) collective-permute-start(f32[192,128]{1,0:T(8,128)S(1)} %add.61), channel_id=1, source_target_pairs={{0,8},{2,10},{4,12},{6,14},{8,0},{10,2},{12,4},{14,6},{1,9},{3,11}... | collective-permute-start | bytes 294920 | tf_op jit(solution)/shard_map/ppermute | solution.py:403
  82.3 4.4 %collective-permute-done.9 = f32[192,128]{1,0:T(8,128)S(1)} collective-permute-done((f32[192,128]{1,0:T(8,128)S(1)}, f32[192,128]{1,0:T(8,128)S(1)}, u32[]{:S(2)}, u32[]{:S(2)}) %collective-permute-start.9) | collective-permute-done | bytes 98336 | tf_op jit(solution)/shard_map/ppermute | solution.py:403
  86.7 1.3 collective-permute-done.10.other_g
  88.0 14.4 %shard_map.44 = (bf16[16,128,256]{2,1,0:T(8,128)(2,1)S(1)}, bf16[4,1,128,256]{3,2,1,0:T(8,128)(2,1)S(1)}, bf16[4,1,128,256]{3,2,1,0:T(8,128)(2,1)S(1)}, bf16[1,1,128,256]{3,2,1,0:T(8,128)(2,1)S(1)}) custom-call(s32[35]{0:T(128)S(1)} %concatenate.20.tab, f32[192,128]{1,0:T(8,128)S(1)} %add.62.own_g, f32[192,128]{1,0:T(8,128)S(1)} %collective-permute-done.10.other_g, ...), custom_call_target="tpu_custom_call" | custom-call | bytes 4194304 | tf_op jit(solution)/shard_map/pallas_call | solution.py:520
  102.9 3.3 %collective-permute-start.12 = (bf16[1,1,128,256]{3,2,1,0:T(8,128)(2,1)S(1)}, bf16[1,1,128,256]{3,2,1,0:T(8,128)(2,1)S(1)}, u32[]{:S(2)}, u32[]{:S(2)}) collective-permute-start(bf16[1,1,128,256]{3,2,1,0:T(8,128)(2,1)S(1)} %get-tuple-element.34), channel_id=1, source_target_pairs={{0,8},{2,10},{4,12},{6,14},{8,0},{10,2},{12,4},{14,6},{1,9},{3,11}... | collective-permute-start | bytes 196616 | tf_op jit(solution)/shard_map/ppermute | solution.py:403
  106.2 1.8 shard_map.45
  108.0 2.1 %collective-permute-done.12 = bf16[1,1,128,256]{3,2,1,0:T(8,128)(2,1)S(1)} collective-permute-done((bf16[1,1,128,256]{3,2,1,0:T(8,128)(2,1)S(1)}, bf16[1,1,128,256]{3,2,1,0:T(8,128)(2,1)S(1)}, u32[]{:S(2)}, u32[]{:S(2)}) %collective-permute-start.12) | collective-permute-done | bytes 65568 | tf_op jit(solution)/shard_map/ppermute | solution.py:403
  110.2 2.1 %collective-permute-done.11 = bf16[4,1,128,256]{3,2,1,0:T(8,128)(2,1)S(1)} collective-permute-done((bf16[4,1,128,256]{3,2,1,0:T(8,128)(2,1)S(1)}, bf16[4,1,128,256]{3,2,1,0:T(8,128)(2,1)S(1)}, u32[]{:S(2)}, u32[]{:S(2)}) %collective-permute-start.11) | collective-permute-done | bytes 262176 | tf_op jit(solution)/shard_map/ppermute | solution.py:403
  112.3 4.4 %all-to-all-start.3 = ((bf16[8,2,128,256]{3,2,1,0:T(8,128)(2,1)}), bf16[8,2,128,256]{3,2,1,0:T(8,128)(2,1)S(1)}, u32[]{:S(2)}, u32[]{:S(2)}) async-start(bf16[8,2,128,256]{3,2,1,0:T(8,128)(2,1)} %shard_map.45), calls=%async_computation.3 | async-start | bytes 2097152 | tf_op jit(solution)/shard_map/all_to_all | solution.py:409
  116.8 2.1 %collective-permute-start.13 = (bf16[2,1,128,256]{3,2,0,1:T(8,128)(2,1)S(1)}, bf16[2,1,128,256]{3,2,0,1:T(8,128)(2,1)S(1)}, u32[]{:S(2)}, u32[]{:S(2)}) collective-permute-start(bf16[2,1,128,256]{3,2,0,1:T(8,128)(2,1)S(1)} %slice_bitcast_fusion), channel_id=1, source_target_pairs={{0,2},{2,0},{4,6},{6,4},{8,10},{10,8},{12,14},{14,12},{1,3},{3,1},... | collective-permute-start | bytes 393224 | tf_op jit(solution)/shard_map/ppermute | solution.py:403
  119.0 12.6 %collective-permute-done.13 = bf16[2,1,128,256]{3,2,0,1:T(8,128)(2,1)S(1)} collective-permute-done((bf16[2,1,128,256]{3,2,0,1:T(8,128)(2,1)S(1)}, bf16[2,1,128,256]{3,2,0,1:T(8,128)(2,1)S(1)}, u32[]{:S(2)}, u32[]{:S(2)}) %collective-permute-start.13) | collective-permute-done | bytes 131104 | tf_op jit(solution)/shard_map/ppermute | solution.py:403
  131.7 1.5 collective-permute-start.14
  134.0 4.1 %collective-permute-start.16 = (bf16[4,1,128,256]{3,2,1,0:T(8,128)(2,1)S(1)}, bf16[4,1,128,256]{3,2,1,0:T(8,128)(2,1)S(1)}, u32[]{:S(2)}, u32[]{:S(2)}) collective-permute-start(bf16[4,1,128,256]{3,2,1,0:T(8,128)(2,1)S(1)} %constant_dynamic-update-slice_fusion.3.refs_2_), channel_id=1, source_target_pairs={{0,4},{2,6},{4,0},{6,2},{8,12},{10,14},{12,8},{14,10},{1,5},{3,7},... | collective-permute-start | bytes 786440 | tf_op jit(solution)/shard_map/ppermute | solution.py:403
  138.0 7.0 %collective-permute-done.14 = bf16[1,1,128,256]{3,2,1,0:T(8,128)(2,1)S(1)} collective-permute-done((bf16[1,1,128,256]{3,2,1,0:T(8,128)(2,1)S(1)}, bf16[1,1,128,256]{3,2,1,0:T(8,128)(2,1)S(1)}, u32[]{:S(2)}, u32[]{:S(2)}) %collective-permute-start.14) | collective-permute-done | bytes 65568 | tf_op jit(solution)/shard_map/ppermute | solution.py:403
  145.1 2.3 %collective-permute-done.16.refs_3_ = bf16[4,1,128,256]{3,2,1,0:T(8,128)(2,1)S(1)} collective-permute-done((bf16[4,1,128,256]{3,2,1,0:T(8,128)(2,1)S(1)}, bf16[4,1,128,256]{3,2,1,0:T(8,128)(2,1)S(1)}, u32[]{:S(2)}, u32[]{:S(2)}) %collective-permute-start.16) | collective-permute-done | bytes 262176 | tf_op jit(solution)/shard_map/ppermute | solution.py:403
  148.8 1.3 shard_map.47.square
  150.1 2.8 %collective-permute-done.17.other.other_hbm = f32[16,128,256]{2,1,0:T(8,128)S(1)} collective-permute-done((f32[16,128,256]{2,1,0:T(8,128)S(1)}, f32[16,128,256]{2,1,0:T(8,128)S(1)}, u32[]{:S(2)}, u32[]{:S(2)}) %collective-permute-start.17) | collective-permute-done | bytes 2097184 | tf_op jit(solution)/shard_map/ppermute | solution.py:406
  152.9 2.0 %shard_map.48 = f32[192,128]{1,0:T(8,128)S(1)} custom-call(s32[35]{0:T(128)S(1)} %concatenate.20.tab, f32[16,128,256]{2,1,0:T(8,128)S(1)} %shard_map.46.own.mine_hbm, f32[16,128,256]{2,1,0:T(8,128)S(1)} %collective-permute-done.17.other.other_hbm, f32[128,128]{1,0:T(8,128)S(1)} %shard_map.47.square), custom_call_target="tpu_custom_call" | custom-call | bytes 4194304 | tf_op jit(solution)/shard_map/pallas_call | solution.py:503
  155.0 4.8 %collective-permute-done.18 = f32[192,128]{1,0:T(8,128)S(1)} collective-permute-done((f32[192,128]{1,0:T(8,128)S(1)}, f32[192,128]{1,0:T(8,128)S(1)}, u32[]{:S(2)}, u32[]{:S(2)}) %collective-permute-start.18) | collective-permute-done | bytes 98336 | tf_op jit(solution)/shard_map/ppermute | solution.py:403
  159.9 4.6 %collective-permute-done.19 = f32[192,128]{1,0:T(8,128)S(1)} collective-permute-done((f32[192,128]{1,0:T(8,128)S(1)}, f32[192,128]{1,0:T(8,128)S(1)}, u32[]{:S(2)}, u32[]{:S(2)}) %collective-permute-start.19) | collective-permute-done | bytes 98336 | tf_op jit(solution)/shard_map/ppermute | solution.py:403
  164.5 2.3 %collective-permute-start.20 = (f32[192,128]{1,0:T(8,128)S(1)}, f32[192,128]{1,0:T(8,128)S(1)}, u32[]{:S(2)}, u32[]{:S(2)}) collective-permute-start(f32[192,128]{1,0:T(8,128)S(1)} %add.64), channel_id=1, source_target_pairs={{0,8},{2,10},{4,12},{6,14},{8,0},{10,2},{12,4},{14,6},{1,9},{3,11}... | collective-permute-start | bytes 294920 | tf_op jit(solution)/shard_map/ppermute | solution.py:403
  166.8 4.3 %collective-permute-done.20 = f32[192,128]{1,0:T(8,128)S(1)} collective-permute-done((f32[192,128]{1,0:T(8,128)S(1)}, f32[192,128]{1,0:T(8,128)S(1)}, u32[]{:S(2)}, u32[]{:S(2)}) %collective-permute-start.20) | collective-permute-done | bytes 98336 | tf_op jit(solution)/shard_map/ppermute | solution.py:403
  171.2 1.3 collective-permute-done.21.other_g
  172.5 16.4 %shard_map.49 = f32[16,256,128]{2,1,0:T(8,128)} custom-call(s32[35]{0:T(128)S(1)} %concatenate.20.tab, f32[192,128]{1,0:T(8,128)S(1)} %add.65.own_g, f32[192,128]{1,0:T(8,128)S(1)} %collective-permute-done.21.other_g, f32[16,128,256]{2,1,0:T(8,128)S(1)} %shard_map.46.own.mine_hbm, f32[16,128,256]{2,1,0:T(8,128)S(1)} %collective-permute-done.17.other.other_hbm), custom_call_target="tpu_custom_call" | custom-call | bytes 4194304 | tf_op jit(solution)/shard_map/pallas_call | solution.py:531
  (93 shorter events, 14.9 us)
Async XLA Ops:
  0.0 1.7 copy-start
  1.7 8.7 %copy-start.11 = (s32[8,9,3]{1,0,2:T(8,128)S(1)}, s32[8,9,3]{1,0,2:T(8,128)}, u32[]{:S(2)}) copy-start(s32[8,9,3]{1,0,2:T(8,128)} %param.4) | copy-start | bytes 2596
  1.7 9.9 %copy-start.4 = (bf16[16,256,128]{2,1,0:T(8,128)(2,1)S(1)}, bf16[16,256,128]{2,1,0:T(8,128)(2,1)}, u32[]{:S(2)}) copy-start(bf16[16,256,128]{2,1,0:T(8,128)(2,1)} %sketch_ref.1) | copy-start | bytes 3145732
  2.3 0.7 copy-start.5
  3.0 25.1 %copy-start.1 = (s32[9,256,256]{2,1,0:T(8,128)S(1)}, s32[9,256,256]{2,1,0:T(8,128)}, u32[]{:S(2)}) copy-start(s32[9,256,256]{2,1,0:T(8,128)} %counts_ref.3) | copy-start | bytes 7077892
  3.0 16.0 %all-to-all-start = ((f32[8,24,256]{2,1,0:T(8,128)}), f32[8,24,256]{2,1,0:T(8,128)}, u32[]{:S(2)}, u32[]{:S(2)}) async-start(f32[8,24,256]{2,1,0:T(8,128)} %copy-done.5), calls=%async_computation | async-start | bytes 393216 | tf_op jit(solution)/shard_map/all_to_all | solution.py:409
  14.0 1.0 copy-start.2
  15.0 0.8 copy-start.6
  15.8 0.7 copy-start.8
  16.5 8.2 %collective-permute-start.1 = (bf16[4,1,128,256]{3,2,1,0:T(8,128)(2,1)}, bf16[4,1,128,256]{3,2,1,0:T(8,128)(2,1)S(1)}, u32[]{:S(2)}, u32[]{:S(2)}) collective-permute-start(bf16[4,1,128,256]{3,2,1,0:T(8,128)(2,1)} %get-tuple-element.30), channel_id=1, source_target_pairs={{0,4},{2,6},{4,0},{6,2},{8,12},{10,14},{12,8},{14,10},{1,5},{3,7},... | collective-permute-start | bytes 786440 | tf_op jit(solution)/shard_map/ppermute | solution.py:403
  18.9 20.3 %all-to-all-start.2 = ((bf16[8,1,128,256]{3,2,1,0:T(8,128)(2,1)}), bf16[8,1,128,256]{3,2,1,0:T(8,128)(2,1)}, u32[]{:S(2)}, u32[]{:S(2)}) async-start(bf16[8,1,128,256]{3,2,1,0:T(8,128)(2,1)} %copy-done.6), calls=%async_computation.2 | async-start | bytes 1048576 | tf_op jit(solution)/shard_map/all_to_all | solution.py:409
  25.7 2.4 %copy-start.9 = (bf16[4,1,128,256]{3,2,1,0:T(8,128)(2,1)}, bf16[4,1,128,256]{3,2,1,0:T(8,128)(2,1)S(1)}, u32[]{:S(2)}) copy-start(bf16[4,1,128,256]{3,2,1,0:T(8,128)(2,1)S(1)} %broadcast_select_fusion.1) | copy-start | bytes 786436
  26.4 18.3 %collective-permute-start.2 = (bf16[2,1,128,256]{3,2,0,1:T(8,128)(2,1)}, bf16[2,1,128,256]{3,2,0,1:T(8,128)(2,1)}, u32[]{:S(2)}, u32[]{:S(2)}) collective-permute-start(bf16[2,1,128,256]{3,2,0,1:T(8,128)(2,1)} %slice_bitcast_fusion.2), channel_id=1, source_target_pairs={{0,2},{2,0},{4,6},{6,4},{8,10},{10,8},{12,14},{14,12},{1,3},{3,1},... | collective-permute-start | bytes 393224 | tf_op jit(solution)/shard_map/ppermute | solution.py:403
  28.1 1.2 copy-start.3
  31.3 4.9 %copy-start.7 = (bf16[1,1,128,256]{3,2,1,0:T(8,128)(2,1)}, bf16[1,1,128,256]{3,2,1,0:T(8,128)(2,1)S(1)}, u32[]{:S(2)}) copy-start(bf16[1,1,128,256]{3,2,1,0:T(8,128)(2,1)S(1)} %get-tuple-element.26) | copy-start | bytes 196612
  31.3 13.4 %copy-start.10 = (bf16[4,1,128,256]{3,2,1,0:T(8,128)(2,1)S(1)}, bf16[4,1,128,256]{3,2,1,0:T(8,128)(2,1)}, u32[]{:S(2)}) copy-start(bf16[4,1,128,256]{3,2,1,0:T(8,128)(2,1)} %copy-done.9) | copy-start | bytes 786436
  32.9 6.4 %collective-permute-start = (bf16[1,1,128,256]{3,2,1,0:T(8,128)(2,1)S(1)}, bf16[1,1,128,256]{3,2,1,0:T(8,128)(2,1)S(1)}, u32[]{:S(2)}, u32[]{:S(2)}) collective-permute-start(bf16[1,1,128,256]{3,2,1,0:T(8,128)(2,1)S(1)} %get-tuple-element.26), channel_id=1, source_target_pairs={{0,8},{2,10},{4,12},{6,14},{8,0},{10,2},{12,4},{14,6},{1,9},{3,11}... | collective-permute-start | bytes 196616 | tf_op jit(solution)/shard_map/ppermute | solution.py:403
  39.3 23.2 %all-to-all-start.1 = ((bf16[8,1,128,256]{3,2,1,0:T(8,128)(2,1)}), bf16[8,1,128,256]{3,2,1,0:T(8,128)(2,1)S(1)}, u32[]{:S(2)}, u32[]{:S(2)}) async-start(bf16[8,1,128,256]{3,2,1,0:T(8,128)(2,1)} %shard_map.40), calls=%async_computation.1 | async-start | bytes 1048576 | tf_op jit(solution)/shard_map/all_to_all | solution.py:409
  46.6 6.5 %collective-permute-start.4 = (bf16[2,1,128,256]{3,2,1,0:T(8,128)(2,1)S(1)}, bf16[2,1,128,256]{3,2,1,0:T(8,128)(2,1)S(1)}, u32[]{:S(2)}, u32[]{:S(2)}) collective-permute-start(bf16[2,1,128,256]{3,2,1,0:T(8,128)(2,1)S(1)} %pad_maximum_fusion), channel_id=1, source_target_pairs={{0,2},{2,0},{4,6},{6,4},{8,10},{10,8},{12,14},{14,12},{1,3},{3,1},... | collective-permute-start | bytes 393224 | tf_op jit(solution)/shard_map/ppermute | solution.py:403
  48.6 11.1 %collective-permute-start.3 = (bf16[1,1,128,256]{3,2,1,0:T(8,128)(2,1)S(1)}, bf16[1,1,128,256]{3,2,1,0:T(8,128)(2,1)S(1)}, u32[]{:S(2)}, u32[]{:S(2)}) collective-permute-start(bf16[1,1,128,256]{3,2,1,0:T(8,128)(2,1)S(1)} %slice_bitcast_fusion.6), channel_id=1, source_target_pairs={{0,8},{2,10},{4,12},{6,14},{8,0},{10,2},{12,4},{14,6},{1,9},{3,11}... | collective-permute-start | bytes 196616 | tf_op jit(solution)/shard_map/ppermute | solution.py:403
  53.1 9.4 %collective-permute-start.5 = (bf16[4,1,128,256]{3,2,1,0:T(8,128)(2,1)S(1)}, bf16[4,1,128,256]{3,2,1,0:T(8,128)(2,1)S(1)}, u32[]{:S(2)}, u32[]{:S(2)}) collective-permute-start(bf16[4,1,128,256]{3,2,1,0:T(8,128)(2,1)S(1)} %constant_dynamic-update-slice_fusion.refs_3_), channel_id=1, source_target_pairs={{0,4},{2,6},{4,0},{6,2},{8,12},{10,14},{12,8},{14,10},{1,5},{3,7},... | collective-permute-start | bytes 786440 | tf_op jit(solution)/shard_map/ppermute | solution.py:403
  64.2 4.2 %collective-permute-start.6 = (f32[16,128,256]{2,1,0:T(8,128)S(1)}, f32[16,128,256]{2,1,0:T(8,128)S(1)}, u32[]{:S(2)}, u32[]{:S(2)}) collective-permute-start(f32[16,128,256]{2,1,0:T(8,128)S(1)} %shard_map.41.own.mine_hbm), channel_id=1, source_target_pairs={{0,1},{1,0},{2,3},{3,2},{4,5},{5,4},{6,7},{7,6},{8,9},{9,8},{10,11... | collective-permute-start | bytes 6291464 | tf_op jit(solution)/shard_map/ppermute | solution.py:406
  70.4 4.9 %collective-permute-start.7 = (f32[192,128]{1,0:T(8,128)S(1)}, f32[192,128]{1,0:T(8,128)S(1)}, u32[]{:S(2)}, u32[]{:S(2)}) collective-permute-start(f32[192,128]{1,0:T(8,128)S(1)} %shard_map.43), channel_id=1, source_target_pairs={{0,2},{2,0},{4,6},{6,4},{8,10},{10,8},{12,14},{14,12},{1,3},{3,1},... | collective-permute-start | bytes 294920 | tf_op jit(solution)/shard_map/ppermute | solution.py:403
  75.3 4.7 %collective-permute-start.8 = (f32[192,128]{1,0:T(8,128)S(1)}, f32[192,128]{1,0:T(8,128)S(1)}, u32[]{:S(2)}, u32[]{:S(2)}) collective-permute-start(f32[192,128]{1,0:T(8,128)S(1)} %add.60), channel_id=1, source_target_pairs={{0,4},{2,6},{4,0},{6,2},{8,12},{10,14},{12,8},{14,10},{1,5},{3,7},... | collective-permute-start | bytes 294920 | tf_op jit(solution)/shard_map/ppermute | solution.py:403
  80.0 6.6 %collective-permute-start.9 = (f32[192,128]{1,0:T(8,128)S(1)}, f32[192,128]{1,0:T(8,128)S(1)}, u32[]{:S(2)}, u32[]{:S(2)}) collective-permute-start(f32[192,128]{1,0:T(8,128)S(1)} %add.61), channel_id=1, source_target_pairs={{0,8},{2,10},{4,12},{6,14},{8,0},{10,2},{12,4},{14,6},{1,9},{3,11}... | collective-permute-start | bytes 294920 | tf_op jit(solution)/shard_map/ppermute | solution.py:403
  86.7 1.4 collective-permute-start.10
  102.5 9.8 %collective-permute-start.11 = (bf16[4,1,128,256]{3,2,1,0:T(8,128)(2,1)S(1)}, bf16[4,1,128,256]{3,2,1,0:T(8,128)(2,1)S(1)}, u32[]{:S(2)}, u32[]{:S(2)}) collective-permute-start(bf16[4,1,128,256]{3,2,1,0:T(8,128)(2,1)S(1)} %get-tuple-element.33), channel_id=1, source_target_pairs={{0,4},{2,6},{4,0},{6,2},{8,12},{10,14},{12,8},{14,10},{1,5},{3,7},... | collective-permute-start | bytes 786440 | tf_op jit(solution)/shard_map/ppermute | solution.py:403
  102.9 7.3 %collective-permute-start.12 = (bf16[1,1,128,256]{3,2,1,0:T(8,128)(2,1)S(1)}, bf16[1,1,128,256]{3,2,1,0:T(8,128)(2,1)S(1)}, u32[]{:S(2)}, u32[]{:S(2)}) collective-permute-start(bf16[1,1,128,256]{3,2,1,0:T(8,128)(2,1)S(1)} %get-tuple-element.34), channel_id=1, source_target_pairs={{0,8},{2,10},{4,12},{6,14},{8,0},{10,2},{12,4},{14,6},{1,9},{3,11}... | collective-permute-start | bytes 196616 | tf_op jit(solution)/shard_map/ppermute | solution.py:403
  112.3 35.1 %all-to-all-start.3 = ((bf16[8,2,128,256]{3,2,1,0:T(8,128)(2,1)}), bf16[8,2,128,256]{3,2,1,0:T(8,128)(2,1)S(1)}, u32[]{:S(2)}, u32[]{:S(2)}) async-start(bf16[8,2,128,256]{3,2,1,0:T(8,128)(2,1)} %shard_map.45), calls=%async_computation.3 | async-start | bytes 2097152 | tf_op jit(solution)/shard_map/all_to_all | solution.py:409
  116.8 14.8 %collective-permute-start.13 = (bf16[2,1,128,256]{3,2,0,1:T(8,128)(2,1)S(1)}, bf16[2,1,128,256]{3,2,0,1:T(8,128)(2,1)S(1)}, u32[]{:S(2)}, u32[]{:S(2)}) collective-permute-start(bf16[2,1,128,256]{3,2,0,1:T(8,128)(2,1)S(1)} %slice_bitcast_fusion), channel_id=1, source_target_pairs={{0,2},{2,0},{4,6},{6,4},{8,10},{10,8},{12,14},{14,12},{1,3},{3,1},... | collective-permute-start | bytes 393224 | tf_op jit(solution)/shard_map/ppermute | solution.py:403
  118.9 15.1 %collective-permute-start.15 = (bf16[2,1,128,256]{3,2,1,0:T(8,128)(2,1)S(1)}, bf16[2,1,128,256]{3,2,1,0:T(8,128)(2,1)S(1)}, u32[]{:S(2)}, u32[]{:S(2)}) collective-permute-start(bf16[2,1,128,256]{3,2,1,0:T(8,128)(2,1)S(1)} %pad_maximum_fusion.1), channel_id=1, source_target_pairs={{0,2},{2,0},{4,6},{6,4},{8,10},{10,8},{12,14},{14,12},{1,3},{3,1},... | collective-permute-start | bytes 393224 | tf_op jit(solution)/shard_map/ppermute | solution.py:403
  131.7 13.4 %collective-permute-start.14 = (bf16[1,1,128,256]{3,2,1,0:T(8,128)(2,1)S(1)}, bf16[1,1,128,256]{3,2,1,0:T(8,128)(2,1)S(1)}, u32[]{:S(2)}, u32[]{:S(2)}) collective-permute-start(bf16[1,1,128,256]{3,2,1,0:T(8,128)(2,1)S(1)} %slice_bitcast_fusion.4), channel_id=1, source_target_pairs={{0,8},{2,10},{4,12},{6,14},{8,0},{10,2},{12,4},{14,6},{1,9},{3,11}... | collective-permute-start | bytes 196616 | tf_op jit(solution)/shard_map/ppermute | solution.py:403
  134.0 13.4 %collective-permute-start.16 = (bf16[4,1,128,256]{3,2,1,0:T(8,128)(2,1)S(1)}, bf16[4,1,128,256]{3,2,1,0:T(8,128)(2,1)S(1)}, u32[]{:S(2)}, u32[]{:S(2)}) collective-permute-start(bf16[4,1,128,256]{3,2,1,0:T(8,128)(2,1)S(1)} %constant_dynamic-update-slice_fusion.3.refs_2_), channel_id=1, source_target_pairs={{0,4},{2,6},{4,0},{6,2},{8,12},{10,14},{12,8},{14,10},{1,5},{3,7},... | collective-permute-start | bytes 786440 | tf_op jit(solution)/shard_map/ppermute | solution.py:403
  148.7 4.2 %collective-permute-start.17 = (f32[16,128,256]{2,1,0:T(8,128)S(1)}, f32[16,128,256]{2,1,0:T(8,128)S(1)}, u32[]{:S(2)}, u32[]{:S(2)}) collective-permute-start(f32[16,128,256]{2,1,0:T(8,128)S(1)} %shard_map.46.own.mine_hbm), channel_id=1, source_target_pairs={{0,1},{1,0},{2,3},{3,2},{4,5},{5,4},{6,7},{7,6},{8,9},{9,8},{10,11... | collective-permute-start | bytes 6291464 | tf_op jit(solution)/shard_map/ppermute | solution.py:406
  154.9 4.9 %collective-permute-start.18 = (f32[192,128]{1,0:T(8,128)S(1)}, f32[192,128]{1,0:T(8,128)S(1)}, u32[]{:S(2)}, u32[]{:S(2)}) collective-permute-start(f32[192,128]{1,0:T(8,128)S(1)} %shard_map.48), channel_id=1, source_target_pairs={{0,2},{2,0},{4,6},{6,4},{8,10},{10,8},{12,14},{14,12},{1,3},{3,1},... | collective-permute-start | bytes 294920 | tf_op jit(solution)/shard_map/ppermute | solution.py:403
  159.8 4.7 %collective-permute-start.19 = (f32[192,128]{1,0:T(8,128)S(1)}, f32[192,128]{1,0:T(8,128)S(1)}, u32[]{:S(2)}, u32[]{:S(2)}) collective-permute-start(f32[192,128]{1,0:T(8,128)S(1)} %add.63), channel_id=1, source_target_pairs={{0,4},{2,6},{4,0},{6,2},{8,12},{10,14},{12,8},{14,10},{1,5},{3,7},... | collective-permute-start | bytes 294920 | tf_op jit(solution)/shard_map/ppermute | solution.py:403
  164.5 6.6 %collective-permute-start.20 = (f32[192,128]{1,0:T(8,128)S(1)}, f32[192,128]{1,0:T(8,128)S(1)}, u32[]{:S(2)}, u32[]{:S(2)}) collective-permute-start(f32[192,128]{1,0:T(8,128)S(1)} %add.64), channel_id=1, source_target_pairs={{0,8},{2,10},{4,12},{6,14},{8,0},{10,2},{12,4},{14,6},{1,9},{3,11}... | collective-permute-start | bytes 294920 | tf_op jit(solution)/shard_map/ppermute | solution.py:403
  171.1 1.4 collective-permute-start.21

commit v6 on v5

--- a/solution.py
+++ b/solution.py
@@ -94,17 +94,15 @@
         hot[0, m] = product(t, tab, blocks, ppmi, t.groups + m)
 
 
-def gather_main(t, tab, blocks, send, slot):
+def gather_main(t, tab, blocks, send):
     for r in range(t.groups):
-        send[r, slot] = blocks[tab[t.main_j + r]]
-
-
-def make_main_kernel(t, with_blocks):
+        send[r] = blocks[tab[t.main_j + r]]
+
+
+def make_main_kernel(t):
     def kernel(tab, blocks, ppmi, send):
-        if with_blocks:
-            gather_main(t, tab, blocks, send, 1)
         for s in range(t.groups):
-            send[tab[t.dest + s], 0] = product(t, tab, blocks, ppmi, s)
+            send[tab[t.dest + s]] = product(t, tab, blocks, ppmi, s)
 
     return kernel
 
@@ -115,7 +113,7 @@
         def _(i):
             turned[i] = sketch_ref[i].T
 
-        gather_main(t, tab, turned, send, 0)
+        gather_main(t, tab, turned, send)
         gather_hot(t, tab, turned, near, far)
 
     return kernel
@@ -152,17 +150,14 @@
 
 
 def make_result_kernel(t, order):
-    def kernel(tab, ppmi_ref, *refs):
-        got_t, got_x = refs[0], refs[-5]
-        hot_x, hot_a, hot_b, result = refs[-4:]
-        slot = got_x.shape[1] - 1
+    def kernel(tab, ppmi_ref, got_t, got_x, hot_x, hot_a, hot_b, result):
         result[...] = jnp.zeros_like(result)
         for s in range(t.nnz):
-            block = got_x[tab[t.dest + s], slot] if s < t.groups else hot_x[0, s - t.groups]
+            block = got_x[tab[t.dest + s]] if s < t.groups else hot_x[0, s - t.groups]
             forward = contract(block, ppmi_ref[s], 1, 1).astype(bf16)
             result[tab[t.row_i + s]] += forward.astype(f32)
         for r in range(t.groups):
-            result[tab[t.main_j + r]] += got_t[r, 0].astype(f32)
+            result[tab[t.main_j + r]] += got_t[r].astype(f32)
         for n, k in enumerate(order):
             ref, place = (hot_a, n) if n < t.groups // 2 else (hot_b, n - t.groups // 2)
             for m in range(t.hot):
@@ -236,14 +231,17 @@
     rows = [
         [jnp.broadcast_to(side[i : i + 1, :], full) for side in (left, right)] for i in range(8)
     ]
-    scale = []
+    zero = jnp.zeros(full, f32)
+    inv = [[None] * 8 for _ in range(8)]
+    done = []
+    solved = [[zero, zero] for _ in range(8)]
     for k in range(0, 8, 2):
         a, b, c = piv[k][k], piv[k + 1][k], piv[k + 1][k + 1]
         det = a * c - b * b
         root, det_root = lax.rsqrt(a), lax.rsqrt(det)
         both = det_root * root
-        scale += [root, det_root * (a * root)]
-        piv[k + 1][k] = b * root
+        scale = det_root * (a * root)
+        across = b * root
         for i in range(k + 2, 8):
             p, q = piv[i][k], piv[i][k + 1]
             piv[i][k] = p * root
@@ -253,19 +251,31 @@
                 piv[i][m] = piv[i][m] - (
                     piv[i][k] * piv[m][k] + piv[i][k + 1] * piv[m][k + 1]
                 )
+        pair = []
         for side in range(2):
             first = rows[k][side] * root
-            second = (rows[k + 1][side] - piv[k + 1][k] * first) * scale[k + 1]
-            rows[k][side], rows[k + 1][side] = first, second
+            second = (rows[k + 1][side] - across * first) * scale
+            pair.append((first, second))
             for i in range(k + 2, 8):
                 rows[i][side] = rows[i][side] - (piv[i][k] * first + piv[i][k + 1] * second)
-    solved = [list(row) for row in rows]
-    for k in range(7, -1, -1):
-        for side in range(2):
-            solved[k][side] = solved[k][side] * scale[k]
-            for i in range(k):
-                solved[i][side] = solved[i][side] - piv[k][i] * solved[k][side]
-    return rows, solved
+        done += [[pair[0][0], pair[1][0]], [pair[0][1], pair[1][1]]]
+        for i in range(k):
+            inv[k][i] = inv[k][i] * root
+            inv[k + 1][i] = (inv[k + 1][i] - across * inv[k][i]) * scale
+        inv[k][k] = root
+        inv[k + 1][k] = -across * root * scale
+        inv[k + 1][k + 1] = scale
+        for i in range(k + 2, 8):
+            for m in range(k + 2):
+                part = piv[i][k + 1] * inv[k + 1][m]
+                if m <= k:
+                    part = part + piv[i][k] * inv[k][m]
+                inv[i][m] = -part if inv[i][m] is None else inv[i][m] - part
+        for n in (k, k + 1):
+            for i in range(n + 1):
+                for side in range(2):
+                    solved[i][side] = solved[i][side] + inv[n][i] * done[n][side]
+    return done, solved
 
 
 def inverse_factor(block):
@@ -333,17 +343,14 @@
     my_col = tab[t.col]
     half = mine.shape[1]
     factor = jnp.concatenate([inverse[my_col, my_col], inverse[my_col, 1 - my_col]], axis=1)
-    high, mid, low = split(factor)
-    three = jnp.concatenate([high, mid, low], axis=0)
+    high, mid, _ = split(factor)
     two = jnp.concatenate([high, mid], axis=0)
 
     @pl.loop(0, mine.shape[0])
     def _(i):
-        y_high, y_mid, y_low = split(jnp.concatenate([mine[i], other[i]], axis=0))
-        by_high = contract(three, y_high, 1, 0)
-        by_mid = contract(two, y_mid, 1, 0)
-        small = by_high[2 * half :] + by_mid[half:] + contract(high, y_low, 1, 0)
-        store(i, by_high[:half] + (by_high[half : 2 * half] + by_mid[:half] + small))
+        y_high, y_mid, _ = split(jnp.concatenate([mine[i], other[i]], axis=0))
+        by_high = contract(two, y_high, 1, 0)
+        store(i, by_high[:half] + (by_high[half:] + contract(high, y_mid, 1, 0)))
 
 
 def start_copies(pairs, sems):
@@ -355,7 +362,7 @@
 
 def make_second_kernel(t, scale):
     def kernel(
-        tab, own_g, other_g, mine_hbm, other_hbm, ppmi_hbm, normal, near, far, hot,
+        tab, own_g, other_g, mine_hbm, other_hbm, ppmi_hbm, normal, send, near, far, hot,
         gram, inverse, mine, other, ppmi, sems,
     ):
         copies = start_copies([(mine_hbm, mine), (other_hbm, other), (ppmi_hbm, ppmi)], sems)
@@ -367,6 +374,7 @@
             normal[i] = value.astype(bf16)
 
         normal_blocks(t, tab, inverse, mine, other, store)
+        gather_main(t, tab, normal, send)
         gather_hot(t, tab, normal, near, far)
         hot_products(t, tab, normal, ppmi, hot)
 
@@ -374,16 +382,26 @@
 
 
 def make_final_kernel(t, scale):
-    def kernel(tab, own_g, other_g, mine_hbm, other_hbm, out, gram, inverse, mine, other, sems):
+    def kernel(
+        tab, own_g, other_g, mine_hbm, other_hbm, out, gram, inverse, mine, other, held, sems
+    ):
         copies = start_copies([(mine_hbm, mine), (other_hbm, other)], sems)
         invert(t, tab, own_g, other_g, gram, inverse, scale)
         for copy in copies:
             copy.wait()
 
+        def leave(i):
+            return pltpu.make_async_copy(held.at[i], out.at[i], sems.at[2])
+
         def store(i, value):
-            out[i] = value.T
+            held[i] = value.T
+            leave(i).start()
 
         normal_blocks(t, tab, inverse, mine, other, store)
+
+        @pl.loop(0, held.shape[0])
+        def _(i):
+            leave(i).wait()
 
     return kernel
 
@@ -407,6 +425,9 @@
 
     def exchange(x):
         return lax.all_to_all(x, "row", split_axis=0, concat_axis=0, tiled=True)
+
+    def send_blocks(send, far):
+        return exchange(send), peer(far, t.steps[0])
 
     def add_up(x):
         for bit in t.bits:
@@ -440,25 +461,22 @@
             part = jnp.where(stay[:, :, None, None], near, got)
         return part
 
-    send_shape = shape((groups, 2, half, rows), bf16)
-    one_shape = shape((groups, 1, half, rows), bf16)
+    send_shape = shape((groups, half, rows), bf16)
     hot_shape = shape((1, hot, half, rows), bf16)
     side_shape = shape((groups // 2, hot, half, rows), bf16)
     ppmi_shape = shape((nnz, rows, rows), bf16)
     result_shape = shape((blocks, half, rows), f32)
 
     sums = call(sums_kernel, shape((groups, depth, rows), f32), [VMEM], vmem=8)(counts)
+    sums, sketch = lax.optimization_barrier((sums, sketch))
     sums_all = exchange(sums)
     tab, towards = t.build(block_pairs, me, my_col)
     turned, send_x, near, far = call(
         make_source_kernel(t),
-        [shape((blocks, half, rows), bf16), one_shape, side_shape, side_shape],
+        [shape((blocks, half, rows), bf16), send_shape, side_shape, side_shape],
         [SMEM, VMEM],
         vmem=8,
     )(tab, sketch)
-    send_x, sums_all = lax.optimization_barrier((send_x, sums_all))
-    got_x = exchange(send_x)
-    x_step = peer(far, t.steps[0])
 
     row_ids = block_pairs[:, :, 0] * groups + jnp.arange(groups)[:, None]
     col_ids = block_pairs[:, :, 2] * groups + block_pairs[:, :, 1]
@@ -467,6 +485,7 @@
     my_ids = lax.dynamic_index_in_dim(ids, me, 0, keepdims=False)
     match = (my_ids[:, None] == ids.reshape(-1)[None, :]).astype(bf16)
 
+    got_x, x_step = send_blocks(send_x, far)
     ppmi, hot_t = call(
         make_ppmi_kernel(t),
         [ppmi_shape, hot_shape],
@@ -477,27 +496,19 @@
 
     def finish(source, got_x, near, far, x_step, hot_t):
         t_step = peer(hot_t, t.steps[-1])
-        if x_step is None:
-            x_step = peer(far, t.steps[0])
-        send = call(
-            make_main_kernel(t, got_x is None),
-            one_shape if got_x is not None else send_shape,
-            [SMEM, VMEM, VMEM],
-            vmem=8,
-        )(tab, source, ppmi)
-        if got_x is None:
-            send, x_step, t_step = lax.optimization_barrier((send, x_step, t_step))
-        else:
-            send, t_step = lax.optimization_barrier((send, t_step))
-        got = [exchange(send)] + ([] if got_x is None else [got_x])
+        send = call(make_main_kernel(t), send_shape, [SMEM, VMEM, VMEM], vmem=8)(
+            tab, source, ppmi
+        )
+        send, t_step = lax.optimization_barrier((send, t_step))
+        got_t = exchange(send)
         hot_x = scatter_hot(near, far, x_step, towards)
         hot_a, hot_b = spread_hot(hot_t, t_step)
         result = call(
             make_result_kernel(t, hot_order),
             result_shape,
-            [SMEM] + [VMEM] * (4 + len(got)),
+            [SMEM] + [VMEM] * 6,
             vmem=12,
-        )(tab, ppmi, *got, hot_x, hot_a, hot_b)
+        )(tab, ppmi, got_t, got_x, hot_x, hot_a, hot_b)
         other = swap(result)
         square = call(own_gram_kernel, shape((half, half), f32), [VMEM], vmem=12)(result)
         gram = call(
@@ -517,22 +528,26 @@
     result, other, gram, other_gram = finish(
         turned, got_x, near, far, x_step, hot_t
     )
-    normal, near, far, hot_t = call(
+    normal, send_x, near, far, hot_t = call(
         make_second_kernel(t, 1.0 / vocab),
-        [shape((blocks, half, rows), bf16), side_shape, side_shape, hot_shape],
+        [shape((blocks, half, rows), bf16), send_shape, side_shape, side_shape, hot_shape],
         [SMEM] + [VMEM] * 2 + [ANY] * 3,
         scratch=gram_scratch
         + result_scratch
         + [pltpu.VMEM((nnz, rows, rows), bf16), pltpu.SemaphoreType.DMA((3,))],
     )(tab, gram, other_gram, result, other, ppmi)
+    got_x, x_step = send_blocks(send_x, far)
     result, other, gram, other_gram = finish(
-        normal, None, near, far, None, hot_t
+        normal, got_x, near, far, x_step, hot_t
     )
     return call(
         make_final_kernel(t, 1.0 / vocab),
         shape((blocks, rows, half), f32),
         [SMEM] + [VMEM] * 2 + [ANY] * 2,
-        scratch=gram_scratch + result_scratch + [pltpu.SemaphoreType.DMA((2,))],
+        ANY,
+        scratch=gram_scratch
+        + result_scratch
+        + [pltpu.VMEM((blocks, rows, half), f32), pltpu.SemaphoreType.DMA((3,))],
     )(tab, gram, other_gram, result, other)
 
 

time: 190 us -> 191 us (level)
  starting transfers between devices: 53.1 us -> 57.5 us
  waiting for transfers between devices: 74.6 us -> 72 us
    all_to_all x4 -> x5, starting transfers between devices: 21.7 us -> 26.4 us  [exchange(): return lax.all_to_all(x, 'row', split_axis=0, concat_axis=0, tiled=True)]
    ppermute x18, waiting for transfers between devices: 66.4 us -> 63.8 us  [peer(): return lax.ppermute(x, 'row', [(r, r ^ k) for r in range(groups)])]
    unnamed x29 -> x35, local copies, waits for them, and re-layouts: 6.09 us -> 7.48 us
  transfers between devices with their start and end apart: 26 -> 27, of which waited for: 21 -> 19; matrix products, arithmetic and copies ran while one was open for 3% -> 3% of each run, Pallas kernels for 6% -> 5%
where the time goes in v6:
time: 191 us
  waiting for transfers between devices  72 us (38%)
  starting transfers between devices  57.5 us (30%)
  Pallas kernels  47.3 us (25%)
  local copies, waits for them, and re-layouts  9.64 us (5%)
  other arithmetic  3.66 us (2%)
    ppermute x18, waiting for transfers between devices, peer(): return lax.ppermute(x, 'row', [(r, r ^ k) for r in range(groups)])  63.8 us
    ppermute x18, starting transfers between devices, peer(): return lax.ppermute(x, 'row', [(r, r ^ k) for r in range(groups)])  30.8 us
    all_to_all x5, starting transfers between devices, exchange(): return lax.all_to_all(x, 'row', split_axis=0, concat_axis=0, tiled=True)  26.4 us
    pallas_call x1, Pallas kernels, body(): call(make_final_kernel(t, 1.0 / vocab), shape((blocks, rows, half), f32),...  15 us
    pallas_call x1, Pallas kernels, body(): call(make_second_kernel(t, 1.0 / vocab), [shape((blocks, half, rows), bf1...  14.4 us
    ppermute x4, waiting for transfers between devices, swap(): return lax.ppermute(x, 'col', [(0, 1), (1, 0)])  8.19 us
    unnamed x35, local copies, waits for them, and re-layouts  7.48 us
    pallas_call x2, Pallas kernels, finish(): call(make_cross_gram_kernel(t), shape((half + half // 2, half), f32), [SM...  3.87 us
  transfers between devices with their start and end apart: 27, of which 19 were waited for; matrix products, arithmetic and copies ran while one was open for 3% of the time, Pallas kernels for 5%

profile of v6, /device:TPU:0, one launch (start us, length us, event | category | flops | bytes accessed | tf_op | source)
XLA Modules:
  0.0 190.7 jit_solution(7368223741129351011)
XLA Ops:
  0.0 1.7 copy-done
  3.0 7.4 %all-to-all-start = ((f32[8,24,256]{2,1,0:T(8,128)}), f32[8,24,256]{2,1,0:T(8,128)}, u32[]{:S(2)}, u32[]{:S(2)}) async-start(f32[8,24,256]{2,1,0:T(8,128)} %copy-done.5), calls=%async_computation | async-start | bytes 393216 | tf_op jit(solution)/shard_map/all_to_all | solution.py:427
  11.5 2.5 %shard_map.38 = (bf16[16,128,256]{2,1,0:T(8,128)(2,1)S(1)}, bf16[8,128,256]{2,1,0:T(8,128)(2,1)S(1)}, bf16[4,1,128,256]{3,2,1,0:T(8,128)(2,1)S(1)}, bf16[4,1,128,256]{3,2,1,0:T(8,128)(2,1)}) custom-call(s32[35]{0:T(128)S(1)} %concatenate.20.tab, bf16[16,256,128]{2,1,0:T(8,128)(2,1)S(1)} %copy-done.4), custom_call_target="tpu_custom_call" | custom-call | bytes 4194304 | tf_op jit(solution)/shard_map/pallas_call | solution.py:474
  16.5 2.0 %collective-permute-start.1 = (bf16[4,1,128,256]{3,2,1,0:T(8,128)(2,1)}, bf16[4,1,128,256]{3,2,1,0:T(8,128)(2,1)S(1)}, u32[]{:S(2)}, u32[]{:S(2)}) collective-permute-start(bf16[4,1,128,256]{3,2,1,0:T(8,128)(2,1)} %get-tuple-element.30), channel_id=1, source_target_pairs={{0,4},{2,6},{4,0},{6,2},{8,12},{10,14},{12,8},{14,10},{1,5},{3,7},... | collective-permute-start | bytes 786440 | tf_op jit(solution)/shard_map/ppermute | solution.py:421
  18.9 4.5 %all-to-all-start.2 = ((bf16[8,128,256]{2,1,0:T(8,128)(2,1)}), bf16[8,128,256]{2,1,0:T(8,128)(2,1)}, u32[]{:S(2)}, u32[]{:S(2)}) async-start(bf16[8,128,256]{2,1,0:T(8,128)(2,1)} %copy-done.6), calls=%async_computation.2 | async-start | bytes 1048576 | tf_op jit(solution)/shard_map/all_to_all | solution.py:427
  26.4 1.5 collective-permute-start.2
  29.3 1.9 %shard_map.39 = (bf16[9,256,256]{2,1,0:T(8,128)(2,1)S(1)}, bf16[1,1,128,256]{3,2,1,0:T(8,128)(2,1)S(1)}) custom-call(s32[35]{0:T(128)S(1)} %concatenate.20.tab, bf16[24,192]{1,0:T(8,128)(2,1)S(1)} %compare_convert_fusion.match_ref, s32[9,256,256]{2,1,0:T(8,128)S(1)} %copy-done.1, bf16[16,128,256]{2,1,0:T(8,128)(2,1)S(1)} %copy-done.3, ...), custom_call_target="tpu_custom_call" | custom-call | bytes 4194304 | tf_op jit(solution)/shard_map/pallas_call | solution.py:489
  31.3 1.6 shard_map.40
  32.9 3.3 %collective-permute-start = (bf16[1,1,128,256]{3,2,1,0:T(8,128)(2,1)S(1)}, bf16[1,1,128,256]{3,2,1,0:T(8,128)(2,1)S(1)}, u32[]{:S(2)}, u32[]{:S(2)}) collective-permute-start(bf16[1,1,128,256]{3,2,1,0:T(8,128)(2,1)S(1)} %get-tuple-element.26), channel_id=1, source_target_pairs={{0,8},{2,10},{4,12},{6,14},{8,0},{10,2},{12,4},{14,6},{1,9},{3,11}... | collective-permute-start | bytes 196616 | tf_op jit(solution)/shard_map/ppermute | solution.py:421
  36.2 3.0 %collective-permute-done = bf16[1,1,128,256]{3,2,1,0:T(8,128)(2,1)S(1)} collective-permute-done((bf16[1,1,128,256]{3,2,1,0:T(8,128)(2,1)S(1)}, bf16[1,1,128,256]{3,2,1,0:T(8,128)(2,1)S(1)}, u32[]{:S(2)}, u32[]{:S(2)}) %collective-permute-start) | collective-permute-done | bytes 65568 | tf_op jit(solution)/shard_map/ppermute | solution.py:421
  39.3 5.4 %all-to-all-start.1 = ((bf16[8,128,256]{2,1,0:T(8,128)(2,1)}), bf16[8,128,256]{2,1,0:T(8,128)(2,1)S(1)}, u32[]{:S(2)}, u32[]{:S(2)}) async-start(bf16[8,128,256]{2,1,0:T(8,128)(2,1)} %shard_map.40), calls=%async_computation.1 | async-start | bytes 1048576 | tf_op jit(solution)/shard_map/all_to_all | solution.py:427
  46.6 2.1 %collective-permute-start.4 = (bf16[2,1,128,256]{3,2,1,0:T(8,128)(2,1)S(1)}, bf16[2,1,128,256]{3,2,1,0:T(8,128)(2,1)S(1)}, u32[]{:S(2)}, u32[]{:S(2)}) collective-permute-start(bf16[2,1,128,256]{3,2,1,0:T(8,128)(2,1)S(1)} %pad_maximum_fusion), channel_id=1, source_target_pairs={{0,2},{2,0},{4,6},{6,4},{8,10},{10,8},{12,14},{14,12},{1,3},{3,1},... | collective-permute-start | bytes 393224 | tf_op jit(solution)/shard_map/ppermute | solution.py:421
  48.7 2.4 %collective-permute-start.3 = (bf16[1,1,128,256]{3,2,1,0:T(8,128)(2,1)S(1)}, bf16[1,1,128,256]{3,2,1,0:T(8,128)(2,1)S(1)}, u32[]{:S(2)}, u32[]{:S(2)}) collective-permute-start(bf16[1,1,128,256]{3,2,1,0:T(8,128)(2,1)S(1)} %slice_bitcast_fusion.6), channel_id=1, source_target_pairs={{0,8},{2,10},{4,12},{6,14},{8,0},{10,2},{12,4},{14,6},{1,9},{3,11}... | collective-permute-start | bytes 196616 | tf_op jit(solution)/shard_map/ppermute | solution.py:421
  51.0 2.0 %collective-permute-done.4 = bf16[2,1,128,256]{3,2,1,0:T(8,128)(2,1)S(1)} collective-permute-done((bf16[2,1,128,256]{3,2,1,0:T(8,128)(2,1)S(1)}, bf16[2,1,128,256]{3,2,1,0:T(8,128)(2,1)S(1)}, u32[]{:S(2)}, u32[]{:S(2)}) %collective-permute-start.4) | collective-permute-done | bytes 131104 | tf_op jit(solution)/shard_map/ppermute | solution.py:421
  53.1 2.1 %collective-permute-start.5 = (bf16[4,1,128,256]{3,2,1,0:T(8,128)(2,1)S(1)}, bf16[4,1,128,256]{3,2,1,0:T(8,128)(2,1)S(1)}, u32[]{:S(2)}, u32[]{:S(2)}) collective-permute-start(bf16[4,1,128,256]{3,2,1,0:T(8,128)(2,1)S(1)} %constant_dynamic-update-slice_fusion.hot_a), channel_id=1, source_target_pairs={{0,4},{2,6},{4,0},{6,2},{8,12},{10,14},{12,8},{14,10},{1,5},{3,7},... | collective-permute-start | bytes 786440 | tf_op jit(solution)/shard_map/ppermute | solution.py:421
  55.3 4.4 %collective-permute-done.3 = bf16[1,1,128,256]{3,2,1,0:T(8,128)(2,1)S(1)} collective-permute-done((bf16[1,1,128,256]{3,2,1,0:T(8,128)(2,1)S(1)}, bf16[1,1,128,256]{3,2,1,0:T(8,128)(2,1)S(1)}, u32[]{:S(2)}, u32[]{:S(2)}) %collective-permute-start.3) | collective-permute-done | bytes 65568 | tf_op jit(solution)/shard_map/ppermute | solution.py:421
  59.7 2.7 %collective-permute-done.5.hot_b = bf16[4,1,128,256]{3,2,1,0:T(8,128)(2,1)S(1)} collective-permute-done((bf16[4,1,128,256]{3,2,1,0:T(8,128)(2,1)S(1)}, bf16[4,1,128,256]{3,2,1,0:T(8,128)(2,1)S(1)}, u32[]{:S(2)}, u32[]{:S(2)}) %collective-permute-start.5) | collective-permute-done | bytes 262176 | tf_op jit(solution)/shard_map/ppermute | solution.py:421
  62.4 1.8 shard_map.41.own.mine_hbm
  64.3 1.3 shard_map.42.square
  65.6 2.8 %collective-permute-done.6.other.other_hbm = f32[16,128,256]{2,1,0:T(8,128)S(1)} collective-permute-done((f32[16,128,256]{2,1,0:T(8,128)S(1)}, f32[16,128,256]{2,1,0:T(8,128)S(1)}, u32[]{:S(2)}, u32[]{:S(2)}) %collective-permute-start.6) | collective-permute-done | bytes 2097184 | tf_op jit(solution)/shard_map/ppermute | solution.py:424
  68.4 1.9 shard_map.43
  70.4 1.5 collective-permute-start.7
  71.9 3.4 %collective-permute-done.7 = f32[192,128]{1,0:T(8,128)S(1)} collective-permute-done((f32[192,128]{1,0:T(8,128)S(1)}, f32[192,128]{1,0:T(8,128)S(1)}, u32[]{:S(2)}, u32[]{:S(2)}) %collective-permute-start.7) | collective-permute-done | bytes 98336 | tf_op jit(solution)/shard_map/ppermute | solution.py:421
  75.4 4.6 %collective-permute-done.8 = f32[192,128]{1,0:T(8,128)S(1)} collective-permute-done((f32[192,128]{1,0:T(8,128)S(1)}, f32[192,128]{1,0:T(8,128)S(1)}, u32[]{:S(2)}, u32[]{:S(2)}) %collective-permute-start.8) | collective-permute-done | bytes 98336 | tf_op jit(solution)/shard_map/ppermute | solution.py:421
  80.0 2.2 %collective-permute-start.9 = (f32[192,128]{1,0:T(8,128)S(1)}, f32[192,128]{1,0:T(8,128)S(1)}, u32[]{:S(2)}, u32[]{:S(2)}) collective-permute-start(f32[192,128]{1,0:T(8,128)S(1)} %add.61), channel_id=1, source_target_pairs={{0,8},{2,10},{4,12},{6,14},{8,0},{10,2},{12,4},{14,6},{1,9},{3,11}... | collective-permute-start | bytes 294920 | tf_op jit(solution)/shard_map/ppermute | solution.py:421
  82.2 4.4 %collective-permute-done.9 = f32[192,128]{1,0:T(8,128)S(1)} collective-permute-done((f32[192,128]{1,0:T(8,128)S(1)}, f32[192,128]{1,0:T(8,128)S(1)}, u32[]{:S(2)}, u32[]{:S(2)}) %collective-permute-start.9) | collective-permute-done | bytes 98336 | tf_op jit(solution)/shard_map/ppermute | solution.py:421
  86.7 1.3 collective-permute-done.10.other_g
  88.0 14.4 %shard_map.44 = (bf16[16,128,256]{2,1,0:T(8,128)(2,1)S(1)}, bf16[8,128,256]{2,1,0:T(8,128)(2,1)}, bf16[4,1,128,256]{3,2,1,0:T(8,128)(2,1)S(1)}, bf16[4,1,128,256...) custom-call(s32[35]{0:T(128)S(1)} %concatenate.20.tab, f32[192,128]{1,0:T(8,128)S(1)} %add.62.own_g, ...), custom_call_target="tpu_custom_call" | custom-call | bytes 4194304 | tf_op jit(solution)/shard_map/pallas_call | solution.py:531
  103.8 4.5 %all-to-all-start.4 = ((bf16[8,128,256]{2,1,0:T(8,128)(2,1)}), bf16[8,128,256]{2,1,0:T(8,128)(2,1)S(1)}, u32[]{:S(2)}, u32[]{:S(2)}) async-start(bf16[8,128,256]{2,1,0:T(8,128)(2,1)} %get-tuple-element.35), calls=%async_computation.4 | async-start | bytes 1048576 | tf_op jit(solution)/shard_map/all_to_all | solution.py:427
  108.3 2.0 %collective-permute-start.12 = (bf16[4,1,128,256]{3,2,1,0:T(8,128)(2,1)}, bf16[4,1,128,256]{3,2,1,0:T(8,128)(2,1)S(1)}, u32[]{:S(2)}, u32[]{:S(2)}) collective-permute-start(bf16[4,1,128,256]{3,2,1,0:T(8,128)(2,1)} %copy-done.11), channel_id=1, source_target_pairs={{0,4},{2,6},{4,0},{6,2},{8,12},{10,14},{12,8},{14,10},{1,5},{3,7},... | collective-permute-start | bytes 786440 | tf_op jit(solution)/shard_map/ppermute | solution.py:421
  110.3 1.6 shard_map.45
  112.0 2.4 %collective-permute-start.11 = (bf16[1,1,128,256]{3,2,1,0:T(8,128)(2,1)S(1)}, bf16[1,1,128,256]{3,2,1,0:T(8,128)(2,1)S(1)}, u32[]{:S(2)}, u32[]{:S(2)}) collective-permute-start(bf16[1,1,128,256]{3,2,1,0:T(8,128)(2,1)S(1)} %get-tuple-element.33), channel_id=1, source_target_pairs={{0,8},{2,10},{4,12},{6,14},{8,0},{10,2},{12,4},{14,6},{1,9},{3,11}... | collective-permute-start | bytes 196616 | tf_op jit(solution)/shard_map/ppermute | solution.py:421
  114.3 10.3 %collective-permute-done.11 = bf16[1,1,128,256]{3,2,1,0:T(8,128)(2,1)S(1)} collective-permute-done((bf16[1,1,128,256]{3,2,1,0:T(8,128)(2,1)S(1)}, bf16[1,1,128,256]{3,2,1,0:T(8,128)(2,1)S(1)}, u32[]{:S(2)}, u32[]{:S(2)}) %collective-permute-start.11) | collective-permute-done | bytes 65568 | tf_op jit(solution)/shard_map/ppermute | solution.py:421
  124.6 1.8 collective-permute-done.12
  126.5 1.6 collective-permute-start.13
  128.7 4.5 %all-to-all-start.3 = ((bf16[8,128,256]{2,1,0:T(8,128)(2,1)}), bf16[8,128,256]{2,1,0:T(8,128)(2,1)S(1)}, u32[]{:S(2)}, u32[]{:S(2)}) async-start(bf16[8,128,256]{2,1,0:T(8,128)(2,1)} %shard_map.45), calls=%async_computation.3 | async-start | bytes 1048576 | tf_op jit(solution)/shard_map/all_to_all | solution.py:427
  133.4 3.0 %collective-permute-start.14 = (bf16[1,1,128,256]{3,2,1,0:T(8,128)(2,1)S(1)}, bf16[1,1,128,256]{3,2,1,0:T(8,128)(2,1)S(1)}, u32[]{:S(2)}, u32[]{:S(2)}) collective-permute-start(bf16[1,1,128,256]{3,2,1,0:T(8,128)(2,1)S(1)} %slice_bitcast_fusion.4), channel_id=1, source_target_pairs={{0,8},{2,10},{4,12},{6,14},{8,0},{10,2},{12,4},{14,6},{1,9},{3,11}... | collective-permute-start | bytes 196616 | tf_op jit(solution)/shard_map/ppermute | solution.py:421
  136.4 1.5 collective-permute-start.16
  137.9 11.6 %collective-permute-done.14 = bf16[1,1,128,256]{3,2,1,0:T(8,128)(2,1)S(1)} collective-permute-done((bf16[1,1,128,256]{3,2,1,0:T(8,128)(2,1)S(1)}, bf16[1,1,128,256]{3,2,1,0:T(8,128)(2,1)S(1)}, u32[]{:S(2)}, u32[]{:S(2)}) %collective-permute-start.14) | collective-permute-done | bytes 65568 | tf_op jit(solution)/shard_map/ppermute | solution.py:421
  149.5 1.3 collective-permute-done.16.hot_b
  152.2 1.3 shard_map.47.square
  153.6 2.8 %collective-permute-done.17.other.other_hbm = f32[16,128,256]{2,1,0:T(8,128)S(1)} collective-permute-done((f32[16,128,256]{2,1,0:T(8,128)S(1)}, f32[16,128,256]{2,1,0:T(8,128)S(1)}, u32[]{:S(2)}, u32[]{:S(2)}) %collective-permute-start.17) | collective-permute-done | bytes 2097184 | tf_op jit(solution)/shard_map/ppermute | solution.py:424
  156.4 2.0 %shard_map.48 = f32[192,128]{1,0:T(8,128)S(1)} custom-call(s32[35]{0:T(128)S(1)} %concatenate.20.tab, f32[16,128,256]{2,1,0:T(8,128)S(1)} %shard_map.46.own.mine_hbm, f32[16,128,256]{2,1,0:T(8,128)S(1)} %collective-permute-done.17.other.other_hbm, f32[128,128]{1,0:T(8,128)S(1)} %shard_map.47.square), custom_call_target="tpu_custom_call" | custom-call | bytes 4194304 | tf_op jit(solution)/shard_map/pallas_call | solution.py:514
  159.3 4.0 %collective-permute-done.18 = f32[192,128]{1,0:T(8,128)S(1)} collective-permute-done((f32[192,128]{1,0:T(8,128)S(1)}, f32[192,128]{1,0:T(8,128)S(1)}, u32[]{:S(2)}, u32[]{:S(2)}) %collective-permute-start.18) | collective-permute-done | bytes 98336 | tf_op jit(solution)/shard_map/ppermute | solution.py:421
  163.4 4.6 %collective-permute-done.19 = f32[192,128]{1,0:T(8,128)S(1)} collective-permute-done((f32[192,128]{1,0:T(8,128)S(1)}, f32[192,128]{1,0:T(8,128)S(1)}, u32[]{:S(2)}, u32[]{:S(2)}) %collective-permute-start.19) | collective-permute-done | bytes 98336 | tf_op jit(solution)/shard_map/ppermute | solution.py:421
  168.0 1.5 collective-permute-start.20
  169.5 4.5 %collective-permute-done.20 = f32[192,128]{1,0:T(8,128)S(1)} collective-permute-done((f32[192,128]{1,0:T(8,128)S(1)}, f32[192,128]{1,0:T(8,128)S(1)}, u32[]{:S(2)}, u32[]{:S(2)}) %collective-permute-start.20) | collective-permute-done | bytes 98336 | tf_op jit(solution)/shard_map/ppermute | solution.py:421
  175.4 15.0 %shard_map.49 = f32[16,256,128]{2,1,0:T(8,128)} custom-call(s32[35]{0:T(128)S(1)} %concatenate.20.tab, f32[192,128]{1,0:T(8,128)S(1)} %add.65.own_g, f32[192,128]{1,0:T(8,128)S(1)} %collective-permute-done.21.other_g, f32[16,128,256]{2,1,0:T(8,128)S(1)} %shard_map.46.own.mine_hbm, f32[16,128,256]{2,1,0:T(8,128)S(1)} %collective-permute-done.17.other.other_hbm), custom_call_target="tpu_custom_call" | custom-call | bytes 4194304 | tf_op jit(solution)/shard_map/pallas_call | solution.py:543
  (101 shorter events, 17.8 us)
Async XLA Ops:
  0.0 1.7 copy-start
  1.7 8.7 %copy-start.14 = (s32[8,9,3]{1,0,2:T(8,128)S(1)}, s32[8,9,3]{1,0,2:T(8,128)}, u32[]{:S(2)}) copy-start(s32[8,9,3]{1,0,2:T(8,128)} %param.4) | copy-start | bytes 2596
  1.7 9.9 %copy-start.4 = (bf16[16,256,128]{2,1,0:T(8,128)(2,1)S(1)}, bf16[16,256,128]{2,1,0:T(8,128)(2,1)}, u32[]{:S(2)}) copy-start(bf16[16,256,128]{2,1,0:T(8,128)(2,1)} %sketch_ref) | copy-start | bytes 3145732
  2.3 0.7 copy-start.5
  3.0 25.1 %copy-start.1 = (s32[9,256,256]{2,1,0:T(8,128)S(1)}, s32[9,256,256]{2,1,0:T(8,128)}, u32[]{:S(2)}) copy-start(s32[9,256,256]{2,1,0:T(8,128)} %counts_ref.3) | copy-start | bytes 7077892
  3.0 16.0 %all-to-all-start = ((f32[8,24,256]{2,1,0:T(8,128)}), f32[8,24,256]{2,1,0:T(8,128)}, u32[]{:S(2)}, u32[]{:S(2)}) async-start(f32[8,24,256]{2,1,0:T(8,128)} %copy-done.5), calls=%async_computation | async-start | bytes 393216 | tf_op jit(solution)/shard_map/all_to_all | solution.py:427
  14.0 1.0 copy-start.2
  15.0 0.8 copy-start.6
  15.8 0.7 copy-start.8
  16.5 8.2 %collective-permute-start.1 = (bf16[4,1,128,256]{3,2,1,0:T(8,128)(2,1)}, bf16[4,1,128,256]{3,2,1,0:T(8,128)(2,1)S(1)}, u32[]{:S(2)}, u32[]{:S(2)}) collective-permute-start(bf16[4,1,128,256]{3,2,1,0:T(8,128)(2,1)} %get-tuple-element.30), channel_id=1, source_target_pairs={{0,4},{2,6},{4,0},{6,2},{8,12},{10,14},{12,8},{14,10},{1,5},{3,7},... | collective-permute-start | bytes 786440 | tf_op jit(solution)/shard_map/ppermute | solution.py:421
  18.9 20.3 %all-to-all-start.2 = ((bf16[8,128,256]{2,1,0:T(8,128)(2,1)}), bf16[8,128,256]{2,1,0:T(8,128)(2,1)}, u32[]{:S(2)}, u32[]{:S(2)}) async-start(bf16[8,128,256]{2,1,0:T(8,128)(2,1)} %copy-done.6), calls=%async_computation.2 | async-start | bytes 1048576 | tf_op jit(solution)/shard_map/all_to_all | solution.py:427
  25.7 2.4 %copy-start.12 = (bf16[4,1,128,256]{3,2,1,0:T(8,128)(2,1)}, bf16[4,1,128,256]{3,2,1,0:T(8,128)(2,1)S(1)}, u32[]{:S(2)}) copy-start(bf16[4,1,128,256]{3,2,1,0:T(8,128)(2,1)S(1)} %broadcast_select_fusion.1) | copy-start | bytes 786436
  26.4 18.3 %collective-permute-start.2 = (bf16[2,1,128,256]{3,2,0,1:T(8,128)(2,1)}, bf16[2,1,128,256]{3,2,0,1:T(8,128)(2,1)}, u32[]{:S(2)}, u32[]{:S(2)}) collective-permute-start(bf16[2,1,128,256]{3,2,0,1:T(8,128)(2,1)} %slice_bitcast_fusion.2), channel_id=1, source_target_pairs={{0,2},{2,0},{4,6},{6,4},{8,10},{10,8},{12,14},{14,12},{1,3},{3,1},... | collective-permute-start | bytes 393224 | tf_op jit(solution)/shard_map/ppermute | solution.py:421
  28.1 1.2 copy-start.3
  31.3 4.9 %copy-start.7 = (bf16[1,1,128,256]{3,2,1,0:T(8,128)(2,1)}, bf16[1,1,128,256]{3,2,1,0:T(8,128)(2,1)S(1)}, u32[]{:S(2)}) copy-start(bf16[1,1,128,256]{3,2,1,0:T(8,128)(2,1)S(1)} %get-tuple-element.26) | copy-start | bytes 196612
  31.3 13.4 %copy-start.13 = (bf16[4,1,128,256]{3,2,1,0:T(8,128)(2,1)S(1)}, bf16[4,1,128,256]{3,2,1,0:T(8,128)(2,1)}, u32[]{:S(2)}) copy-start(bf16[4,1,128,256]{3,2,1,0:T(8,128)(2,1)} %copy-done.12) | copy-start | bytes 786436
  32.9 6.3 %collective-permute-start = (bf16[1,1,128,256]{3,2,1,0:T(8,128)(2,1)S(1)}, bf16[1,1,128,256]{3,2,1,0:T(8,128)(2,1)S(1)}, u32[]{:S(2)}, u32[]{:S(2)}) collective-permute-start(bf16[1,1,128,256]{3,2,1,0:T(8,128)(2,1)S(1)} %get-tuple-element.26), channel_id=1, source_target_pairs={{0,8},{2,10},{4,12},{6,14},{8,0},{10,2},{12,4},{14,6},{1,9},{3,11}... | collective-permute-start | bytes 196616 | tf_op jit(solution)/shard_map/ppermute | solution.py:421
  39.3 23.2 %all-to-all-start.1 = ((bf16[8,128,256]{2,1,0:T(8,128)(2,1)}), bf16[8,128,256]{2,1,0:T(8,128)(2,1)S(1)}, u32[]{:S(2)}, u32[]{:S(2)}) async-start(bf16[8,128,256]{2,1,0:T(8,128)(2,1)} %shard_map.40), calls=%async_computation.1 | async-start | bytes 1048576 | tf_op jit(solution)/shard_map/all_to_all | solution.py:427
  46.6 6.5 %collective-permute-start.4 = (bf16[2,1,128,256]{3,2,1,0:T(8,128)(2,1)S(1)}, bf16[2,1,128,256]{3,2,1,0:T(8,128)(2,1)S(1)}, u32[]{:S(2)}, u32[]{:S(2)}) collective-permute-start(bf16[2,1,128,256]{3,2,1,0:T(8,128)(2,1)S(1)} %pad_maximum_fusion), channel_id=1, source_target_pairs={{0,2},{2,0},{4,6},{6,4},{8,10},{10,8},{12,14},{14,12},{1,3},{3,1},... | collective-permute-start | bytes 393224 | tf_op jit(solution)/shard_map/ppermute | solution.py:421
  48.7 11.1 %collective-permute-start.3 = (bf16[1,1,128,256]{3,2,1,0:T(8,128)(2,1)S(1)}, bf16[1,1,128,256]{3,2,1,0:T(8,128)(2,1)S(1)}, u32[]{:S(2)}, u32[]{:S(2)}) collective-permute-start(bf16[1,1,128,256]{3,2,1,0:T(8,128)(2,1)S(1)} %slice_bitcast_fusion.6), channel_id=1, source_target_pairs={{0,8},{2,10},{4,12},{6,14},{8,0},{10,2},{12,4},{14,6},{1,9},{3,11}... | collective-permute-start | bytes 196616 | tf_op jit(solution)/shard_map/ppermute | solution.py:421
  53.1 9.3 %collective-permute-start.5 = (bf16[4,1,128,256]{3,2,1,0:T(8,128)(2,1)S(1)}, bf16[4,1,128,256]{3,2,1,0:T(8,128)(2,1)S(1)}, u32[]{:S(2)}, u32[]{:S(2)}) collective-permute-start(bf16[4,1,128,256]{3,2,1,0:T(8,128)(2,1)S(1)} %constant_dynamic-update-slice_fusion.hot_a), channel_id=1, source_target_pairs={{0,4},{2,6},{4,0},{6,2},{8,12},{10,14},{12,8},{14,10},{1,5},{3,7},... | collective-permute-start | bytes 786440 | tf_op jit(solution)/shard_map/ppermute | solution.py:421
  64.2 4.2 %collective-permute-start.6 = (f32[16,128,256]{2,1,0:T(8,128)S(1)}, f32[16,128,256]{2,1,0:T(8,128)S(1)}, u32[]{:S(2)}, u32[]{:S(2)}) collective-permute-start(f32[16,128,256]{2,1,0:T(8,128)S(1)} %shard_map.41.own.mine_hbm), channel_id=1, source_target_pairs={{0,1},{1,0},{2,3},{3,2},{4,5},{5,4},{6,7},{7,6},{8,9},{9,8},{10,11... | collective-permute-start | bytes 6291464 | tf_op jit(solution)/shard_map/ppermute | solution.py:424
  70.4 4.9 %collective-permute-start.7 = (f32[192,128]{1,0:T(8,128)S(1)}, f32[192,128]{1,0:T(8,128)S(1)}, u32[]{:S(2)}, u32[]{:S(2)}) collective-permute-start(f32[192,128]{1,0:T(8,128)S(1)} %shard_map.43), channel_id=1, source_target_pairs={{0,2},{2,0},{4,6},{6,4},{8,10},{10,8},{12,14},{14,12},{1,3},{3,1},... | collective-permute-start | bytes 294920 | tf_op jit(solution)/shard_map/ppermute | solution.py:421
  75.3 4.7 %collective-permute-start.8 = (f32[192,128]{1,0:T(8,128)S(1)}, f32[192,128]{1,0:T(8,128)S(1)}, u32[]{:S(2)}, u32[]{:S(2)}) collective-permute-start(f32[192,128]{1,0:T(8,128)S(1)} %add.60), channel_id=1, source_target_pairs={{0,4},{2,6},{4,0},{6,2},{8,12},{10,14},{12,8},{14,10},{1,5},{3,7},... | collective-permute-start | bytes 294920 | tf_op jit(solution)/shard_map/ppermute | solution.py:421
  80.0 6.6 %collective-permute-start.9 = (f32[192,128]{1,0:T(8,128)S(1)}, f32[192,128]{1,0:T(8,128)S(1)}, u32[]{:S(2)}, u32[]{:S(2)}) collective-permute-start(f32[192,128]{1,0:T(8,128)S(1)} %add.61), channel_id=1, source_target_pairs={{0,8},{2,10},{4,12},{6,14},{8,0},{10,2},{12,4},{14,6},{1,9},{3,11}... | collective-permute-start | bytes 294920 | tf_op jit(solution)/shard_map/ppermute | solution.py:421
  86.6 1.4 collective-permute-start.10
  102.4 0.7 copy-start.9
  103.1 0.7 copy-start.11
  103.8 22.6 %copy-start.10 = (bf16[4,1,128,256]{3,2,1,0:T(8,128)(2,1)S(1)}, bf16[4,1,128,256]{3,2,1,0:T(8,128)(2,1)}, u32[]{:S(2)}) copy-start(bf16[4,1,128,256]{3,2,1,0:T(8,128)(2,1)} %copy-done.9) | copy-start | bytes 786436
  103.8 24.9 %all-to-all-start.4 = ((bf16[8,128,256]{2,1,0:T(8,128)(2,1)}), bf16[8,128,256]{2,1,0:T(8,128)(2,1)S(1)}, u32[]{:S(2)}, u32[]{:S(2)}) async-start(bf16[8,128,256]{2,1,0:T(8,128)(2,1)} %get-tuple-element.35), calls=%async_computation.4 | async-start | bytes 1048576 | tf_op jit(solution)/shard_map/all_to_all | solution.py:427
  108.3 18.1 %collective-permute-start.12 = (bf16[4,1,128,256]{3,2,1,0:T(8,128)(2,1)}, bf16[4,1,128,256]{3,2,1,0:T(8,128)(2,1)S(1)}, u32[]{:S(2)}, u32[]{:S(2)}) collective-permute-start(bf16[4,1,128,256]{3,2,1,0:T(8,128)(2,1)} %copy-done.11), channel_id=1, source_target_pairs={{0,4},{2,6},{4,0},{6,2},{8,12},{10,14},{12,8},{14,10},{1,5},{3,7},... | collective-permute-start | bytes 786440 | tf_op jit(solution)/shard_map/ppermute | solution.py:421
  112.0 12.6 %collective-permute-start.11 = (bf16[1,1,128,256]{3,2,1,0:T(8,128)(2,1)S(1)}, bf16[1,1,128,256]{3,2,1,0:T(8,128)(2,1)S(1)}, u32[]{:S(2)}, u32[]{:S(2)}) collective-permute-start(bf16[1,1,128,256]{3,2,1,0:T(8,128)(2,1)S(1)} %get-tuple-element.33), channel_id=1, source_target_pairs={{0,8},{2,10},{4,12},{6,14},{8,0},{10,2},{12,4},{14,6},{1,9},{3,11}... | collective-permute-start | bytes 196616 | tf_op jit(solution)/shard_map/ppermute | solution.py:421
  126.5 6.7 %collective-permute-start.13 = (bf16[2,1,128,256]{3,2,0,1:T(8,128)(2,1)S(1)}, bf16[2,1,128,256]{3,2,0,1:T(8,128)(2,1)S(1)}, u32[]{:S(2)}, u32[]{:S(2)}) collective-permute-start(bf16[2,1,128,256]{3,2,0,1:T(8,128)(2,1)S(1)} %slice_bitcast_fusion), channel_id=1, source_target_pairs={{0,2},{2,0},{4,6},{6,4},{8,10},{10,8},{12,14},{14,12},{1,3},{3,1},... | collective-permute-start | bytes 393224 | tf_op jit(solution)/shard_map/ppermute | solution.py:421
  128.1 8.2 %collective-permute-start.15 = (bf16[2,1,128,256]{3,2,1,0:T(8,128)(2,1)S(1)}, bf16[2,1,128,256]{3,2,1,0:T(8,128)(2,1)S(1)}, u32[]{:S(2)}, u32[]{:S(2)}) collective-permute-start(bf16[2,1,128,256]{3,2,1,0:T(8,128)(2,1)S(1)} %pad_maximum_fusion.1), channel_id=1, source_target_pairs={{0,2},{2,0},{4,6},{6,4},{8,10},{10,8},{12,14},{14,12},{1,3},{3,1},... | collective-permute-start | bytes 393224 | tf_op jit(solution)/shard_map/ppermute | solution.py:421
  128.7 22.2 %all-to-all-start.3 = ((bf16[8,128,256]{2,1,0:T(8,128)(2,1)}), bf16[8,128,256]{2,1,0:T(8,128)(2,1)S(1)}, u32[]{:S(2)}, u32[]{:S(2)}) async-start(bf16[8,128,256]{2,1,0:T(8,128)(2,1)} %shard_map.45), calls=%async_computation.3 | async-start | bytes 1048576 | tf_op jit(solution)/shard_map/all_to_all | solution.py:427
  133.4 16.1 %collective-permute-start.14 = (bf16[1,1,128,256]{3,2,1,0:T(8,128)(2,1)S(1)}, bf16[1,1,128,256]{3,2,1,0:T(8,128)(2,1)S(1)}, u32[]{:S(2)}, u32[]{:S(2)}) collective-permute-start(bf16[1,1,128,256]{3,2,1,0:T(8,128)(2,1)S(1)} %slice_bitcast_fusion.4), channel_id=1, source_target_pairs={{0,8},{2,10},{4,12},{6,14},{8,0},{10,2},{12,4},{14,6},{1,9},{3,11}... | collective-permute-start | bytes 196616 | tf_op jit(solution)/shard_map/ppermute | solution.py:421
  136.4 14.5 %collective-permute-start.16 = (bf16[4,1,128,256]{3,2,1,0:T(8,128)(2,1)S(1)}, bf16[4,1,128,256]{3,2,1,0:T(8,128)(2,1)S(1)}, u32[]{:S(2)}, u32[]{:S(2)}) collective-permute-start(bf16[4,1,128,256]{3,2,1,0:T(8,128)(2,1)S(1)} %constant_dynamic-update-slice_fusion.3.hot_a), channel_id=1, source_target_pairs={{0,4},{2,6},{4,0},{6,2},{8,12},{10,14},{12,8},{14,10},{1,5},{3,7},... | collective-permute-start | bytes 786440 | tf_op jit(solution)/shard_map/ppermute | solution.py:421
  152.2 4.2 %collective-permute-start.17 = (f32[16,128,256]{2,1,0:T(8,128)S(1)}, f32[16,128,256]{2,1,0:T(8,128)S(1)}, u32[]{:S(2)}, u32[]{:S(2)}) collective-permute-start(f32[16,128,256]{2,1,0:T(8,128)S(1)} %shard_map.46.own.mine_hbm), channel_id=1, source_target_pairs={{0,1},{1,0},{2,3},{3,2},{4,5},{5,4},{6,7},{7,6},{8,9},{9,8},{10,11... | collective-permute-start | bytes 6291464 | tf_op jit(solution)/shard_map/ppermute | solution.py:424
  158.4 4.9 %collective-permute-start.18 = (f32[192,128]{1,0:T(8,128)S(1)}, f32[192,128]{1,0:T(8,128)S(1)}, u32[]{:S(2)}, u32[]{:S(2)}) collective-permute-start(f32[192,128]{1,0:T(8,128)S(1)} %shard_map.48), channel_id=1, source_target_pairs={{0,2},{2,0},{4,6},{6,4},{8,10},{10,8},{12,14},{14,12},{1,3},{3,1},... | collective-permute-start | bytes 294920 | tf_op jit(solution)/shard_map/ppermute | solution.py:421
  163.3 4.7 %collective-permute-start.19 = (f32[192,128]{1,0:T(8,128)S(1)}, f32[192,128]{1,0:T(8,128)S(1)}, u32[]{:S(2)}, u32[]{:S(2)}) collective-permute-start(f32[192,128]{1,0:T(8,128)S(1)} %add.63), channel_id=1, source_target_pairs={{0,4},{2,6},{4,0},{6,2},{8,12},{10,14},{12,8},{14,10},{1,5},{3,7},... | collective-permute-start | bytes 294920 | tf_op jit(solution)/shard_map/ppermute | solution.py:421
  168.0 6.1 %collective-permute-start.20 = (f32[192,128]{1,0:T(8,128)S(1)}, f32[192,128]{1,0:T(8,128)S(1)}, u32[]{:S(2)}, u32[]{:S(2)}) collective-permute-start(f32[192,128]{1,0:T(8,128)S(1)} %add.64), channel_id=1, source_target_pairs={{0,8},{2,10},{4,12},{6,14},{8,0},{10,2},{12,4},{14,6},{1,9},{3,11}... | collective-permute-start | bytes 294920 | tf_op jit(solution)/shard_map/ppermute | solution.py:421
  174.1 1.4 collective-permute-start.21

commit v7 on v6

--- a/solution.py
+++ b/solution.py
@@ -64,13 +64,11 @@
 def sums_kernel(counts_ref, sums_ref):
     nnz, rows, cols = counts_ref.shape
     ones = jnp.ones((8, cols), bf16)
-    sums_ref[0] = jnp.zeros(sums_ref.shape[1:], f32)
+    sums_ref[...] = jnp.zeros(sums_ref.shape, f32)
     for s in range(nnz):
         block = counts_ref[s].astype(bf16)
         sums_ref[0, pl.ds(s, 1), :] = contract(ones, block, 1, 1)[0:1, :]
         sums_ref[0, pl.ds(nnz + s, 1), :] = contract(ones, block, 1, 0)[0:1, :]
-    for r in range(1, sums_ref.shape[0]):
-        sums_ref[r] = sums_ref[0]
 
 
 def gather_hot(t, tab, blocks, near, far):
@@ -94,15 +92,17 @@
         hot[0, m] = product(t, tab, blocks, ppmi, t.groups + m)
 
 
-def gather_main(t, tab, blocks, send):
+def gather_main(t, tab, blocks, send, slot):
     for r in range(t.groups):
-        send[r] = blocks[tab[t.main_j + r]]
-
-
-def make_main_kernel(t):
+        send[r, slot] = blocks[tab[t.main_j + r]]
+
+
+def make_main_kernel(t, with_blocks):
     def kernel(tab, blocks, ppmi, send):
+        if with_blocks:
+            gather_main(t, tab, blocks, send, 1)
         for s in range(t.groups):
-            send[tab[t.dest + s]] = product(t, tab, blocks, ppmi, s)
+            send[tab[t.dest + s], 0] = product(t, tab, blocks, ppmi, s)
 
     return kernel
 
@@ -113,15 +113,17 @@
         def _(i):
             turned[i] = sketch_ref[i].T
 
-        gather_main(t, tab, turned, send)
+        gather_main(t, tab, turned, send, 0)
         gather_hot(t, tab, turned, near, far)
 
     return kernel
 
 
 def make_ppmi_kernel(t):
-    def kernel(tab, match_ref, counts_ref, turned, sums_ref, ppmi_ref, hot, cols_log):
-        sums = jnp.concatenate([sums_ref[r] for r in range(t.groups)], axis=0)
+    def kernel(tab, match_ref, counts_ref, turned, sums_a, sums_b, ppmi_ref, hot, cols_log):
+        sums = jnp.concatenate(
+            [ref[r] for ref in (sums_a, sums_b) for r in range(t.groups // 2)], axis=0
+        )
         high = jnp.floor(sums * (1.0 / 256.0))
         low = sums - high * 256.0
         match = match_ref[...]
@@ -150,14 +152,17 @@
 
 
 def make_result_kernel(t, order):
-    def kernel(tab, ppmi_ref, got_t, got_x, hot_x, hot_a, hot_b, result):
+    def kernel(tab, ppmi_ref, *refs):
+        got_t, got_x = refs[0], refs[-5]
+        hot_x, hot_a, hot_b, result = refs[-4:]
+        slot = got_x.shape[1] - 1
         result[...] = jnp.zeros_like(result)
         for s in range(t.nnz):
-            block = got_x[tab[t.dest + s]] if s < t.groups else hot_x[0, s - t.groups]
+            block = got_x[tab[t.dest + s], slot] if s < t.groups else hot_x[0, s - t.groups]
             forward = contract(block, ppmi_ref[s], 1, 1).astype(bf16)
             result[tab[t.row_i + s]] += forward.astype(f32)
         for r in range(t.groups):
-            result[tab[t.main_j + r]] += got_t[r].astype(f32)
+            result[tab[t.main_j + r]] += got_t[r, 0].astype(f32)
         for n, k in enumerate(order):
             ref, place = (hot_a, n) if n < t.groups // 2 else (hot_b, n - t.groups // 2)
             for m in range(t.hot):
@@ -200,7 +205,14 @@
         blocks, half, _ = own.shape
         cut = half // 2
         step = 4
-        gram[pl.ds(0, half), :] = square[...]
+        full = square[...]
+        row = lax.broadcasted_iota(i32, (half, half), 0)
+        lane = lax.broadcasted_iota(i32, (half, half), 1)
+        diagonal = jnp.sum(jnp.where(row == lane, full, 0.0), axis=0, keepdims=True)
+        gram[pl.ds(0, cut), :] = jnp.where(
+            lane[:cut] >= row[:cut], full[:cut], pltpu.roll(full[cut:], cut, 1)
+        )
+        gram[pl.ds(cut, 8), :] = jnp.broadcast_to(diagonal, (8, half))
 
         def cross(left, rows, right):
             total = jnp.zeros((cut, half), f32)
@@ -211,7 +223,7 @@
                 by_mid = contract(jnp.concatenate([high, mid], axis=0), r_mid, 1, 1)
                 small = by_high[2 * cut :] + by_mid[cut:] + contract(high, r_low, 1, 1)
                 total += by_high[:cut] + (by_high[cut : 2 * cut] + by_mid[:cut] + small)
-            gram[pl.ds(half, cut), :] = total
+            gram[pl.ds(cut + 8, cut), :] = total
 
         @pl.when(tab[t.col] == 0)
         def _():
@@ -321,18 +333,28 @@
     return jnp.concatenate([side[1] for side in sides], axis=0)
 
 
+def unpack(packed):
+    half = packed.shape[1]
+    cut = half // 2
+    row = lax.broadcasted_iota(i32, (half, half), 0)
+    lane = lax.broadcasted_iota(i32, (half, half), 1)
+    folded = packed[:cut]
+    keep = lane[:cut] >= row[:cut]
+    upper = jnp.where(keep, folded, 0.0)
+    lower = pltpu.roll(jnp.where(keep, 0.0, folded), cut, 1)
+    triangle = jnp.concatenate([upper, lower], axis=0)
+    return jnp.where(row == lane, packed[cut : cut + 1], triangle + triangle.T)
+
+
 def invert(t, tab, own, other, gram, inverse, scale):
-    half = own.shape[1]
-    cut = half // 2
+    cut = own.shape[1] // 2
     my_col = tab[t.col]
     gram[my_col] = own[...] * scale
     gram[1 - my_col] = other[...] * scale
-    low = inverse_factor(gram[0, pl.ds(0, half), :])
-    lower = jnp.concatenate([gram[0, pl.ds(half, cut), :], gram[1, pl.ds(half, cut), :]], axis=0)
+    low = inverse_factor(unpack(gram[0]))
+    lower = jnp.concatenate([gram[n, pl.ds(cut + 8, cut), :] for n in range(2)], axis=0)
     across = contract(lower, low, 1, 1, HIGHEST)
-    high = inverse_factor(
-        gram[1, pl.ds(0, half), :] - contract(across, across, 1, 1, HIGHEST)
-    )
+    high = inverse_factor(unpack(gram[1]) - contract(across, across, 1, 1, HIGHEST))
     inverse[0, 0] = low
     inverse[0, 1] = jnp.zeros_like(low)
     inverse[1, 0] = -contract(high, contract(across, low, 1, 0, HIGHEST), 1, 0, HIGHEST)
@@ -362,7 +384,7 @@
 
 def make_second_kernel(t, scale):
     def kernel(
-        tab, own_g, other_g, mine_hbm, other_hbm, ppmi_hbm, normal, send, near, far, hot,
+        tab, own_g, other_g, mine_hbm, other_hbm, ppmi_hbm, normal, near, far, hot,
         gram, inverse, mine, other, ppmi, sems,
     ):
         copies = start_copies([(mine_hbm, mine), (other_hbm, other), (ppmi_hbm, ppmi)], sems)
@@ -374,7 +396,6 @@
             normal[i] = value.astype(bf16)
 
         normal_blocks(t, tab, inverse, mine, other, store)
-        gather_main(t, tab, normal, send)
         gather_hot(t, tab, normal, near, far)
         hot_products(t, tab, normal, ppmi, hot)
 
@@ -426,23 +447,20 @@
     def exchange(x):
         return lax.all_to_all(x, "row", split_axis=0, concat_axis=0, tiled=True)
 
-    def send_blocks(send, far):
-        return exchange(send), peer(far, t.steps[0])
-
     def add_up(x):
         for bit in t.bits:
             x = x + peer(x, bit)
         return x
 
-    def spread_hot(part, got):
-        part = jnp.concatenate([part, got], axis=0)
-        for bit in t.steps[-2:0:-1]:
-            part = jnp.concatenate([part, peer(part, bit)], axis=0)
-        return part, peer(part, t.steps[0])
-
-    hot_order = [0]
-    for bit in t.steps[::-1]:
-        hot_order += [k ^ bit for k in hot_order]
+    def spread(part, steps, got=None):
+        order = [0]
+        for n, bit in enumerate(steps):
+            if n or got is None:
+                got = peer(part, bit)
+            order += [k ^ bit for k in order]
+            if n < len(steps) - 1:
+                part = jnp.concatenate([part, got], axis=0)
+        return part, got, order
 
     def halve(x, kept, bit):
         low = sum(1 for k in kept if k < bit)
@@ -461,19 +479,19 @@
             part = jnp.where(stay[:, :, None, None], near, got)
         return part
 
-    send_shape = shape((groups, half, rows), bf16)
+    def send_shape(slots):
+        return shape((groups, slots, half, rows), bf16)
+
     hot_shape = shape((1, hot, half, rows), bf16)
     side_shape = shape((groups // 2, hot, half, rows), bf16)
     ppmi_shape = shape((nnz, rows, rows), bf16)
     result_shape = shape((blocks, half, rows), f32)
 
-    sums = call(sums_kernel, shape((groups, depth, rows), f32), [VMEM], vmem=8)(counts)
-    sums, sketch = lax.optimization_barrier((sums, sketch))
-    sums_all = exchange(sums)
+    sums = call(sums_kernel, shape((1, depth, rows), f32), [VMEM], vmem=8)(counts)
     tab, towards = t.build(block_pairs, me, my_col)
     turned, send_x, near, far = call(
         make_source_kernel(t),
-        [shape((blocks, half, rows), bf16), send_shape, side_shape, side_shape],
+        [shape((blocks, half, rows), bf16), send_shape(1), side_shape, side_shape],
         [SMEM, VMEM],
         vmem=8,
     )(tab, sketch)
@@ -482,38 +500,43 @@
     col_ids = block_pairs[:, :, 2] * groups + block_pairs[:, :, 1]
     no_id = jnp.full((groups, depth - 2 * nnz), -1, i32)
     ids = jnp.concatenate([row_ids, col_ids, no_id], axis=1)
-    my_ids = lax.dynamic_index_in_dim(ids, me, 0, keepdims=False)
+    sums_a, sums_b, order = spread(sums, t.bits[::-1])
+    ids = jnp.take(ids, me ^ jnp.array(order), axis=0)
+    my_ids = ids[0]
     match = (my_ids[:, None] == ids.reshape(-1)[None, :]).astype(bf16)
 
-    got_x, x_step = send_blocks(send_x, far)
+    got_x, x_step = exchange(send_x), peer(far, t.steps[0])
     ppmi, hot_t = call(
         make_ppmi_kernel(t),
         [ppmi_shape, hot_shape],
-        [SMEM] + [VMEM] * 4,
+        [SMEM] + [VMEM] * 5,
         scratch=[pltpu.VMEM((depth, rows), f32)],
         vmem=12,
-    )(tab, match, counts, turned, sums_all)
+    )(tab, match, counts, turned, sums_a, sums_b)
 
     def finish(source, got_x, near, far, x_step, hot_t):
         t_step = peer(hot_t, t.steps[-1])
-        send = call(make_main_kernel(t), send_shape, [SMEM, VMEM, VMEM], vmem=8)(
-            tab, source, ppmi
-        )
+        if x_step is None:
+            x_step = peer(far, t.steps[0])
+        merged = got_x is None
+        send = call(
+            make_main_kernel(t, merged), send_shape(1 + merged), [SMEM, VMEM, VMEM], vmem=8
+        )(tab, source, ppmi)
         send, t_step = lax.optimization_barrier((send, t_step))
-        got_t = exchange(send)
+        got = [exchange(send)] + ([] if merged else [got_x])
         hot_x = scatter_hot(near, far, x_step, towards)
-        hot_a, hot_b = spread_hot(hot_t, t_step)
+        hot_a, hot_b, order = spread(hot_t, t.steps[::-1], t_step)
         result = call(
-            make_result_kernel(t, hot_order),
+            make_result_kernel(t, order),
             result_shape,
-            [SMEM] + [VMEM] * 6,
+            [SMEM] + [VMEM] * (4 + len(got)),
             vmem=12,
-        )(tab, ppmi, got_t, got_x, hot_x, hot_a, hot_b)
+        )(tab, ppmi, *got, hot_x, hot_a, hot_b)
         other = swap(result)
         square = call(own_gram_kernel, shape((half, half), f32), [VMEM], vmem=12)(result)
         gram = call(
             make_cross_gram_kernel(t),
-            shape((half + half // 2, half), f32),
+            shape((half + 8, half), f32),
             [SMEM] + [VMEM] * 3,
             vmem=16,
         )(tab, result, other, square)
@@ -521,25 +544,22 @@
         return result, other, gram, swap(gram)
 
     gram_scratch = [
-        pltpu.VMEM((2, half + half // 2, half), f32),
+        pltpu.VMEM((2, half + 8, half), f32),
         pltpu.VMEM((2, 2, half, half), f32),
     ]
     result_scratch = [pltpu.VMEM((blocks, half, rows), f32)] * 2
     result, other, gram, other_gram = finish(
         turned, got_x, near, far, x_step, hot_t
     )
-    normal, send_x, near, far, hot_t = call(
+    normal, near, far, hot_t = call(
         make_second_kernel(t, 1.0 / vocab),
-        [shape((blocks, half, rows), bf16), send_shape, side_shape, side_shape, hot_shape],
+        [shape((blocks, half, rows), bf16), side_shape, side_shape, hot_shape],
         [SMEM] + [VMEM] * 2 + [ANY] * 3,
         scratch=gram_scratch
         + result_scratch
         + [pltpu.VMEM((nnz, rows, rows), bf16), pltpu.SemaphoreType.DMA((3,))],
     )(tab, gram, other_gram, result, other, ppmi)
-    got_x, x_step = send_blocks(send_x, far)
-    result, other, gram, other_gram = finish(
-        normal, got_x, near, far, x_step, hot_t
-    )
+    result, other, gram, other_gram = finish(normal, None, near, far, None, hot_t)
     return call(
         make_final_kernel(t, 1.0 / vocab),
         shape((blocks, rows, half), f32),

time: 191 us -> 203 us (1.063)
  waiting for transfers between devices: 72 us -> 90.2 us
  starting transfers between devices: 57.5 us -> 50 us
    ppermute x18 -> x21, waiting for transfers between devices: 63.8 us -> 82.1 us  [peer(): return lax.ppermute(x, 'row', [(r, r ^ k) for r in range(groups)])]
    all_to_all x5 -> x3, starting transfers between devices: 26.4 us -> 14.1 us  [exchange(): return lax.all_to_all(x, 'row', split_axis=0, concat_axis=0, tiled=True)]
    ppermute x18 -> x21, starting transfers between devices: 30.8 us -> 35.6 us  [peer(): return lax.ppermute(x, 'row', [(r, r ^ k) for r in range(groups)])]
    unnamed x35 -> x39, local copies, waits for them, and re-layouts: 7.48 us -> 8.93 us
  transfers between devices with their start and end apart: 27 -> 28, of which waited for: 19 -> 20; matrix products, arithmetic and copies ran while one was open for 3% -> 3% of each run, Pallas kernels for 5% -> 5%
where the time goes in v7:
time: 203 us; the launch traced here: 202 us
  waiting for transfers between devices  90.2 us (44%)
  starting transfers between devices  50 us (25%)
  Pallas kernels  47.5 us (23%)
  local copies, waits for them, and re-layouts  11.5 us (6%)
  other arithmetic  2.54 us (1%)
    ppermute x21, waiting for transfers between devices, peer(): return lax.ppermute(x, 'row', [(r, r ^ k) for r in range(groups)])  82.1 us
    ppermute x21, starting transfers between devices, peer(): return lax.ppermute(x, 'row', [(r, r ^ k) for r in range(groups)])  35.6 us
    pallas_call x1, Pallas kernels, body(): call(make_final_kernel(t, 1.0 / vocab), shape((blocks, rows, half), f32),...  15.2 us
    all_to_all x3, starting transfers between devices, exchange(): return lax.all_to_all(x, 'row', split_axis=0, concat_axis=0, tiled=True)  14.1 us
    pallas_call x1, Pallas kernels, body(): call(make_second_kernel(t, 1.0 / vocab), [shape((blocks, half, rows), bf1...  14 us
    unnamed x39, local copies, waits for them, and re-layouts  8.93 us
    ppermute x4, waiting for transfers between devices, swap(): return lax.ppermute(x, 'col', [(0, 1), (1, 0)])  8.07 us
  transfers between devices with their start and end apart: 28, of which 20 were waited for; matrix products, arithmetic and copies ran while one was open for 3% of the time, Pallas kernels for 5%

profile of v7, /device:TPU:0, one launch (start us, length us, event | category | flops | bytes accessed | tf_op | source)
XLA Modules:
  0.0 202.2 jit_solution(9239436002012846154)
XLA Ops:
  0.0 1.7 copy-done
  2.3 4.1 %collective-permute-start = (f32[1,24,256]{2,1,0:T(8,128)S(1)}, f32[1,24,256]{2,1,0:T(8,128)S(1)}, u32[]{:S(2)}, u32[]{:S(2)}) collective-permute-start(f32[1,24,256]{2,1,0:T(8,128)S(1)} %shard_map.47), channel_id=1, source_target_pairs={{0,8},{2,10},{4,12},{6,14},{8,0},{10,2},{12,4},{14,6},{1,9},{3,11}... | collective-permute-start | bytes 73736 | tf_op jit(solution)/shard_map/ppermute | solution.py:442
  8.7 2.7 %shard_map.46 = (bf16[16,128,256]{2,1,0:T(8,128)(2,1)S(1)}, bf16[8,1,128,256]{3,2,1,0:T(8,128)(2,1)}, bf16[4,1,128,256]{3,2,1,0:T(8,128)(2,1)S(1)}, bf16[4,1,128,256]{3,2,1,0:T(8,128)(2,1)}) custom-call(s32[35]{0:T(128)S(1)} %concatenate.27.tab, bf16[16,256,128]{2,1,0:T(8,128)(2,1)S(1)} %copy-done.4), custom_call_target="tpu_custom_call" | custom-call | bytes 4194304 | tf_op jit(solution)/shard_map/pallas_call | solution.py:492
  13.1 4.1 %all-to-all-start.1 = ((bf16[8,1,128,256]{3,2,1,0:T(8,128)(2,1)}), bf16[8,1,128,256]{3,2,1,0:T(8,128)(2,1)}, u32[]{:S(2)}, u32[]{:S(2)}) async-start(bf16[8,1,128,256]{3,2,1,0:T(8,128)(2,1)} %get-tuple-element.23), calls=%async_computation.1 | async-start | bytes 1048576 | tf_op jit(solution)/shard_map/all_to_all | solution.py:448
  17.2 1.9 collective-permute-start.4
  20.5 14.1 %collective-permute-done.1 = f32[2,24,256]{2,1,0:T(8,128)S(1)} collective-permute-done((f32[2,24,256]{2,1,0:T(8,128)S(1)}, f32[2,24,256]{2,1,0:T(8,128)S(1)}, u32[]{:S(2)}, u32[]{:S(2)}) %collective-permute-start.1) | collective-permute-done | bytes 49184 | tf_op jit(solution)/shard_map/ppermute | solution.py:442
  34.6 1.6 collective-permute-start.2
  42.9 1.6 shard_map.48
  44.5 1.6 shard_map.49
  46.1 2.4 %collective-permute-start.3 = (bf16[1,1,128,256]{3,2,1,0:T(8,128)(2,1)S(1)}, bf16[1,1,128,256]{3,2,1,0:T(8,128)(2,1)S(1)}, u32[]{:S(2)}, u32[]{:S(2)}) collective-permute-start(bf16[1,1,128,256]{3,2,1,0:T(8,128)(2,1)S(1)} %get-tuple-element.21), channel_id=1, source_target_pairs={{0,8},{2,10},{4,12},{6,14},{8,0},{10,2},{12,4},{14,6},{1,9},{3,11}... | collective-permute-start | bytes 196616 | tf_op jit(solution)/shard_map/ppermute | solution.py:442
  48.6 3.2 %collective-permute-done.3 = bf16[1,1,128,256]{3,2,1,0:T(8,128)(2,1)S(1)} collective-permute-done((bf16[1,1,128,256]{3,2,1,0:T(8,128)(2,1)S(1)}, bf16[1,1,128,256]{3,2,1,0:T(8,128)(2,1)S(1)}, u32[]{:S(2)}, u32[]{:S(2)}) %collective-permute-start.3) | collective-permute-done | bytes 65568 | tf_op jit(solution)/shard_map/ppermute | solution.py:442
  51.8 1.8 collective-permute-start.7
  55.0 4.2 %all-to-all-start = ((bf16[8,1,128,256]{3,2,1,0:T(8,128)(2,1)}), bf16[8,1,128,256]{3,2,1,0:T(8,128)(2,1)S(1)}, u32[]{:S(2)}, u32[]{:S(2)}) async-start(bf16[8,1,128,256]{3,2,1,0:T(8,128)(2,1)} %shard_map.49), calls=%async_computation | async-start | bytes 1048576 | tf_op jit(solution)/shard_map/all_to_all | solution.py:448
  59.3 2.1 %collective-permute-start.8 = (bf16[4,1,128,256]{3,2,1,0:T(8,128)(2,1)S(1)}, bf16[4,1,128,256]{3,2,1,0:T(8,128)(2,1)S(1)}, u32[]{:S(2)}, u32[]{:S(2)}) collective-permute-start(bf16[4,1,128,256]{3,2,1,0:T(8,128)(2,1)S(1)} %constant_dynamic-update-slice_fusion.refs_3_), channel_id=1, source_target_pairs={{0,4},{2,6},{4,0},{6,2},{8,12},{10,14},{12,8},{14,10},{1,5},{3,7},... | collective-permute-start | bytes 786440 | tf_op jit(solution)/shard_map/ppermute | solution.py:442
  61.5 2.4 %collective-permute-start.6 = (bf16[1,1,128,256]{3,2,1,0:T(8,128)(2,1)S(1)}, bf16[1,1,128,256]{3,2,1,0:T(8,128)(2,1)S(1)}, u32[]{:S(2)}, u32[]{:S(2)}) collective-permute-start(bf16[1,1,128,256]{3,2,1,0:T(8,128)(2,1)S(1)} %slice_bitcast_fusion.6), channel_id=1, source_target_pairs={{0,8},{2,10},{4,12},{6,14},{8,0},{10,2},{12,4},{14,6},{1,9},{3,11}... | collective-permute-start | bytes 196616 | tf_op jit(solution)/shard_map/ppermute | solution.py:442
  64.1 9.2 %collective-permute-done.6 = bf16[1,1,128,256]{3,2,1,0:T(8,128)(2,1)S(1)} collective-permute-done((bf16[1,1,128,256]{3,2,1,0:T(8,128)(2,1)S(1)}, bf16[1,1,128,256]{3,2,1,0:T(8,128)(2,1)S(1)}, u32[]{:S(2)}, u32[]{:S(2)}) %collective-permute-start.6) | collective-permute-done | bytes 65568 | tf_op jit(solution)/shard_map/ppermute | solution.py:442
  74.4 1.9 shard_map.50.own.mine_hbm
  76.3 1.4 shard_map.51.square
  77.7 2.8 %collective-permute-done.9.other.other_hbm = f32[16,128,256]{2,1,0:T(8,128)S(1)} collective-permute-done((f32[16,128,256]{2,1,0:T(8,128)S(1)}, f32[16,128,256]{2,1,0:T(8,128)S(1)}, u32[]{:S(2)}, u32[]{:S(2)}) %collective-permute-start.9) | collective-permute-done | bytes 2097184 | tf_op jit(solution)/shard_map/ppermute | solution.py:445
  80.5 2.0 shard_map.52
  82.5 1.5 collective-permute-start.10
  83.9 2.9 %collective-permute-done.10 = f32[136,128]{1,0:T(8,128)S(1)} collective-permute-done((f32[136,128]{1,0:T(8,128)S(1)}, f32[136,128]{1,0:T(8,128)S(1)}, u32[]{:S(2)}, u32[]{:S(2)}) %collective-permute-start.10) | collective-permute-done | bytes 69664 | tf_op jit(solution)/shard_map/ppermute | solution.py:442
  86.9 2.5 %collective-permute-start.11 = (f32[136,128]{1,0:T(8,128)S(1)}, f32[136,128]{1,0:T(8,128)S(1)}, u32[]{:S(2)}, u32[]{:S(2)}) collective-permute-start(f32[136,128]{1,0:T(8,128)S(1)} %add.63), channel_id=1, source_target_pairs={{0,4},{2,6},{4,0},{6,2},{8,12},{10,14},{12,8},{14,10},{1,5},{3,7},... | collective-permute-start | bytes 208904 | tf_op jit(solution)/shard_map/ppermute | solution.py:442
  89.3 2.3 %collective-permute-done.11 = f32[136,128]{1,0:T(8,128)S(1)} collective-permute-done((f32[136,128]{1,0:T(8,128)S(1)}, f32[136,128]{1,0:T(8,128)S(1)}, u32[]{:S(2)}, u32[]{:S(2)}) %collective-permute-start.11) | collective-permute-done | bytes 69664 | tf_op jit(solution)/shard_map/ppermute | solution.py:442
  91.6 1.4 collective-permute-start.12
  93.0 3.9 %collective-permute-done.12 = f32[136,128]{1,0:T(8,128)S(1)} collective-permute-done((f32[136,128]{1,0:T(8,128)S(1)}, f32[136,128]{1,0:T(8,128)S(1)}, u32[]{:S(2)}, u32[]{:S(2)}) %collective-permute-start.12) | collective-permute-done | bytes 69664 | tf_op jit(solution)/shard_map/ppermute | solution.py:442
  98.3 14.0 %shard_map.53 = (bf16[16,128,256]{2,1,0:T(8,128)(2,1)S(1)}, bf16[4,1,128,256]{3,2,1,0:T(8,128)(2,1)S(1)}, bf16[4,1,128,256]{3,2,1,0:T(8,128)(2,1)S(1)}, bf16[1,1,128,256]{3,2,1,0:T(8,128)(2,1)S(1)}) custom-call(s32[35]{0:T(128)S(1)} %concatenate.27.tab, f32[136,128]{1,0:T(8,128)S(1)} %add.65.own_g, f32[136,128]{1,0:T(8,128)S(1)} %collective-permute-done.13.other_g, ...), custom_call_target="tpu_custom_call" | custom-call | bytes 4194304 | tf_op jit(solution)/shard_map/pallas_call | solution.py:554
  112.2 1.4 collective-permute-start.14
  113.7 1.8 shard_map.54
  115.5 2.0 collective-permute-done.14
  117.5 5.8 %all-to-all-start.2 = ((bf16[8,2,128,256]{3,2,1,0:T(8,128)(2,1)}), bf16[8,2,128,256]{3,2,1,0:T(8,128)(2,1)S(1)}, u32[]{:S(2)}, u32[]{:S(2)}) async-start(bf16[8,2,128,256]{3,2,1,0:T(8,128)(2,1)} %shard_map.54), calls=%async_computation.2 | async-start | bytes 2097152 | tf_op jit(solution)/shard_map/all_to_all | solution.py:448
  123.2 2.0 collective-permute-start.15
  125.2 21.2 %collective-permute-done.15 = bf16[4,1,128,256]{3,2,1,0:T(8,128)(2,1)S(1)} collective-permute-done((bf16[4,1,128,256]{3,2,1,0:T(8,128)(2,1)S(1)}, bf16[4,1,128,256]{3,2,1,0:T(8,128)(2,1)S(1)}, u32[]{:S(2)}, u32[]{:S(2)}) %collective-permute-start.15) | collective-permute-done | bytes 262176 | tf_op jit(solution)/shard_map/ppermute | solution.py:442
  146.6 1.4 collective-permute-start.16
  148.7 3.8 %collective-permute-done.16 = bf16[2,1,128,256]{3,2,0,1:T(8,128)(2,1)S(1)} collective-permute-done((bf16[2,1,128,256]{3,2,0,1:T(8,128)(2,1)S(1)}, bf16[2,1,128,256]{3,2,0,1:T(8,128)(2,1)S(1)}, u32[]{:S(2)}, u32[]{:S(2)}) %collective-permute-start.16) | collective-permute-done | bytes 131104 | tf_op jit(solution)/shard_map/ppermute | solution.py:442
  152.7 4.0 %collective-permute-start.17 = (bf16[1,1,128,256]{3,2,1,0:T(8,128)(2,1)S(1)}, bf16[1,1,128,256]{3,2,1,0:T(8,128)(2,1)S(1)}, u32[]{:S(2)}, u32[]{:S(2)}) collective-permute-start(bf16[1,1,128,256]{3,2,1,0:T(8,128)(2,1)S(1)} %slice_bitcast_fusion.4), channel_id=1, source_target_pairs={{0,8},{2,10},{4,12},{6,14},{8,0},{10,2},{12,4},{14,6},{1,9},{3,11}... | collective-permute-start | bytes 196616 | tf_op jit(solution)/shard_map/ppermute | solution.py:442
  156.8 2.3 %collective-permute-done.17 = bf16[1,1,128,256]{3,2,1,0:T(8,128)(2,1)S(1)} collective-permute-done((bf16[1,1,128,256]{3,2,1,0:T(8,128)(2,1)S(1)}, bf16[1,1,128,256]{3,2,1,0:T(8,128)(2,1)S(1)}, u32[]{:S(2)}, u32[]{:S(2)}) %collective-permute-start.17) | collective-permute-done | bytes 65568 | tf_op jit(solution)/shard_map/ppermute | solution.py:442
  159.0 4.1 %collective-permute-done.19.refs_3_ = bf16[4,1,128,256]{3,2,1,0:T(8,128)(2,1)S(1)} collective-permute-done((bf16[4,1,128,256]{3,2,1,0:T(8,128)(2,1)S(1)}, bf16[4,1,128,256]{3,2,1,0:T(8,128)(2,1)S(1)}, u32[]{:S(2)}, u32[]{:S(2)}) %collective-permute-start.19) | collective-permute-done | bytes 262176 | tf_op jit(solution)/shard_map/ppermute | solution.py:442
  163.1 1.4 shard_map.55.own.mine_hbm
  164.6 1.4 shard_map.56.square
  165.9 2.8 %collective-permute-done.20.other.other_hbm = f32[16,128,256]{2,1,0:T(8,128)S(1)} collective-permute-done((f32[16,128,256]{2,1,0:T(8,128)S(1)}, f32[16,128,256]{2,1,0:T(8,128)S(1)}, u32[]{:S(2)}, u32[]{:S(2)}) %collective-permute-start.20) | collective-permute-done | bytes 2097184 | tf_op jit(solution)/shard_map/ppermute | solution.py:445
  168.7 2.0 %shard_map.57 = f32[136,128]{1,0:T(8,128)S(1)} custom-call(s32[35]{0:T(128)S(1)} %concatenate.27.tab, f32[16,128,256]{2,1,0:T(8,128)S(1)} %shard_map.55.own.mine_hbm, f32[16,128,256]{2,1,0:T(8,128)S(1)} %collective-permute-done.20.other.other_hbm, f32[128,128]{1,0:T(8,128)S(1)} %shard_map.56.square), custom_call_target="tpu_custom_call" | custom-call | bytes 4194304 | tf_op jit(solution)/shard_map/pallas_call | solution.py:537
  170.7 1.4 collective-permute-start.21
  172.2 2.9 %collective-permute-done.21 = f32[136,128]{1,0:T(8,128)S(1)} collective-permute-done((f32[136,128]{1,0:T(8,128)S(1)}, f32[136,128]{1,0:T(8,128)S(1)}, u32[]{:S(2)}, u32[]{:S(2)}) %collective-permute-start.21) | collective-permute-done | bytes 69664 | tf_op jit(solution)/shard_map/ppermute | solution.py:442
  175.7 3.8 %collective-permute-done.22 = f32[136,128]{1,0:T(8,128)S(1)} collective-permute-done((f32[136,128]{1,0:T(8,128)S(1)}, f32[136,128]{1,0:T(8,128)S(1)}, u32[]{:S(2)}, u32[]{:S(2)}) %collective-permute-start.22) | collective-permute-done | bytes 69664 | tf_op jit(solution)/shard_map/ppermute | solution.py:442
  179.5 1.7 collective-permute-start.23
  181.3 4.3 %collective-permute-done.23 = f32[136,128]{1,0:T(8,128)S(1)} collective-permute-done((f32[136,128]{1,0:T(8,128)S(1)}, f32[136,128]{1,0:T(8,128)S(1)}, u32[]{:S(2)}, u32[]{:S(2)}) %collective-permute-start.23) | collective-permute-done | bytes 69664 | tf_op jit(solution)/shard_map/ppermute | solution.py:442
  186.9 15.2 %shard_map.58 = f32[16,256,128]{2,1,0:T(8,128)} custom-call(s32[35]{0:T(128)S(1)} %concatenate.27.tab, f32[136,128]{1,0:T(8,128)S(1)} %add.68.own_g, f32[136,128]{1,0:T(8,128)S(1)} %collective-permute-done.24.other_g, f32[16,128,256]{2,1,0:T(8,128)S(1)} %shard_map.55.own.mine_hbm, f32[16,128,256]{2,1,0:T(8,128)S(1)} %collective-permute-done.20.other.other_hbm), custom_call_target="tpu_custom_call" | custom-call | bytes 4194304 | tf_op jit(solution)/shard_map/pallas_call | solution.py:563
  (112 shorter events, 19.9 us)
Async XLA Ops:
  0.0 6.6 %copy-start.16 = (s32[8]{0:T(128)S(1)}, s32[8]{0:T(128)}, u32[]{:S(2)}) copy-start(s32[8]{0:T(128)} %constant.59.clone) | copy-start | bytes 100
  0.0 1.7 copy-start
  1.7 4.7 %copy-start.11 = (s32[8,9,3]{1,0,2:T(8,128)S(1)}, s32[8,9,3]{1,0,2:T(8,128)}, u32[]{:S(2)}) copy-start(s32[8,9,3]{1,0,2:T(8,128)} %param.5) | copy-start | bytes 2596
  1.7 38.2 %copy-start.1 = (s32[9,256,256]{2,1,0:T(8,128)S(1)}, s32[9,256,256]{2,1,0:T(8,128)}, u32[]{:S(2)}) copy-start(s32[9,256,256]{2,1,0:T(8,128)} %counts_ref.3) | copy-start | bytes 7077892
  2.3 17.9 %collective-permute-start = (f32[1,24,256]{2,1,0:T(8,128)S(1)}, f32[1,24,256]{2,1,0:T(8,128)S(1)}, u32[]{:S(2)}, u32[]{:S(2)}) collective-permute-start(f32[1,24,256]{2,1,0:T(8,128)S(1)} %shard_map.47), channel_id=1, source_target_pairs={{0,8},{2,10},{4,12},{6,14},{8,0},{10,2},{12,4},{14,6},{1,9},{3,11}... | collective-permute-start | bytes 73736 | tf_op jit(solution)/shard_map/ppermute | solution.py:442
  7.5 1.2 copy-start.4
  11.4 1.0 copy-start.2
  12.4 0.7 copy-start.7
  13.1 41.9 %all-to-all-start.1 = ((bf16[8,1,128,256]{3,2,1,0:T(8,128)(2,1)}), bf16[8,1,128,256]{3,2,1,0:T(8,128)(2,1)}, u32[]{:S(2)}, u32[]{:S(2)}) async-start(bf16[8,1,128,256]{3,2,1,0:T(8,128)(2,1)} %get-tuple-element.23), calls=%async_computation.1 | async-start | bytes 1048576 | tf_op jit(solution)/shard_map/all_to_all | solution.py:448
  17.2 36.4 %collective-permute-start.4 = (bf16[4,1,128,256]{3,2,1,0:T(8,128)(2,1)}, bf16[4,1,128,256]{3,2,1,0:T(8,128)(2,1)}, u32[]{:S(2)}, u32[]{:S(2)}) collective-permute-start(bf16[4,1,128,256]{3,2,1,0:T(8,128)(2,1)} %get-tuple-element.25), channel_id=1, source_target_pairs={{0,4},{2,6},{4,0},{6,2},{8,12},{10,14},{12,8},{14,10},{1,5},{3,7},... | collective-permute-start | bytes 786440 | tf_op jit(solution)/shard_map/ppermute | solution.py:442
  20.2 14.4 %collective-permute-start.1 = (f32[2,24,256]{2,1,0:T(8,128)S(1)}, f32[2,24,256]{2,1,0:T(8,128)S(1)}, u32[]{:S(2)}, u32[]{:S(2)}) collective-permute-start(f32[2,24,256]{2,1,0:T(8,128)S(1)} %pad_maximum_fusion.3), channel_id=1, source_target_pairs={{0,4},{2,6},{4,0},{6,2},{8,12},{10,14},{12,8},{14,10},{1,5},{3,7},... | collective-permute-start | bytes 147464 | tf_op jit(solution)/shard_map/ppermute | solution.py:442
  20.5 18.8 %copy-start.14 = (s32[2,1,2,1]{2,1,0,3:T(1,128)}, s32[2,1,2,1]{2,1,0,3:T(1,128)S(1)}, u32[]{:S(2)}) copy-start(s32[2,1,2,1]{2,1,0,3:T(1,128)S(1)} %slice.99) | copy-start | bytes 52
  34.6 4.7 %collective-permute-start.2 = (f32[4,24,256]{2,1,0:T(8,128)S(1)}, f32[4,24,256]{2,1,0:T(8,128)S(1)}, u32[]{:S(2)}, u32[]{:S(2)}) collective-permute-start(f32[4,24,256]{2,1,0:T(8,128)S(1)} %pad_maximum_fusion.2.sums_a), channel_id=1, source_target_pairs={{0,2},{2,0},{4,6},{6,4},{8,10},{10,8},{12,14},{14,12},{1,3},{3,1},... | collective-permute-start | bytes 294920 | tf_op jit(solution)/shard_map/ppermute | solution.py:442
  36.2 0.6 copy-start.5
  39.3 0.6 copy-start.9
  39.9 1.2 copy-start.3
  41.1 0.9 copy-start.6
  42.0 0.9 copy-start.10
  44.5 9.1 %copy-start.8 = (bf16[4,1,128,256]{3,2,1,0:T(8,128)(2,1)S(1)}, bf16[4,1,128,256]{3,2,1,0:T(8,128)(2,1)}, u32[]{:S(2)}) copy-start(bf16[4,1,128,256]{3,2,1,0:T(8,128)(2,1)} %copy-done.7) | copy-start | bytes 786436
  44.5 9.1 %copy-start.13 = (pred[4]{0:T(512)(128)(4,1)S(1)}, pred[4]{0:T(512)(128)(4,1)}, u32[]{:S(2)}) copy-start(pred[4]{0:T(512)(128)(4,1)} %eq.65) | copy-start | bytes 16
  46.1 15.2 %copy-start.12 = (pred[2]{0:T(512)(128)(4,1)S(1)}, pred[2]{0:T(512)(128)(4,1)}, u32[]{:S(2)}) copy-start(pred[2]{0:T(512)(128)(4,1)} %compare_reduce_fusion.1) | copy-start | bytes 10
  46.1 17.8 %copy-start.15 = (s32[2,1,2,1]{2,1,0,3:T(1,128)S(1)}, s32[2,1,2,1]{2,1,0,3:T(1,128)}, u32[]{:S(2)}) copy-start(s32[2,1,2,1]{2,1,0,3:T(1,128)} %copy-done.14) | copy-start | bytes 52
  46.1 5.6 %collective-permute-start.3 = (bf16[1,1,128,256]{3,2,1,0:T(8,128)(2,1)S(1)}, bf16[1,1,128,256]{3,2,1,0:T(8,128)(2,1)S(1)}, u32[]{:S(2)}, u32[]{:S(2)}) collective-permute-start(bf16[1,1,128,256]{3,2,1,0:T(8,128)(2,1)S(1)} %get-tuple-element.21), channel_id=1, source_target_pairs={{0,8},{2,10},{4,12},{6,14},{8,0},{10,2},{12,4},{14,6},{1,9},{3,11}... | collective-permute-start | bytes 196616 | tf_op jit(solution)/shard_map/ppermute | solution.py:442
  51.8 7.5 %collective-permute-start.7 = (bf16[2,1,128,256]{3,2,1,0:T(8,128)(2,1)S(1)}, bf16[2,1,128,256]{3,2,1,0:T(8,128)(2,1)S(1)}, u32[]{:S(2)}, u32[]{:S(2)}) collective-permute-start(bf16[2,1,128,256]{3,2,1,0:T(8,128)(2,1)S(1)} %pad_maximum_fusion), channel_id=1, source_target_pairs={{0,2},{2,0},{4,6},{6,4},{8,10},{10,8},{12,14},{14,12},{1,3},{3,1},... | collective-permute-start | bytes 393224 | tf_op jit(solution)/shard_map/ppermute | solution.py:442
  54.7 6.7 %collective-permute-start.5 = (bf16[2,1,128,256]{3,2,0,1:T(8,128)(2,1)S(1)}, bf16[2,1,128,256]{3,2,0,1:T(8,128)(2,1)S(1)}, u32[]{:S(2)}, u32[]{:S(2)}) collective-permute-start(bf16[2,1,128,256]{3,2,0,1:T(8,128)(2,1)S(1)} %slice_bitcast_fusion.2), channel_id=1, source_target_pairs={{0,2},{2,0},{4,6},{6,4},{8,10},{10,8},{12,14},{14,12},{1,3},{3,1},... | collective-permute-start | bytes 393224 | tf_op jit(solution)/shard_map/ppermute | solution.py:442
  55.0 19.3 %all-to-all-start = ((bf16[8,1,128,256]{3,2,1,0:T(8,128)(2,1)}), bf16[8,1,128,256]{3,2,1,0:T(8,128)(2,1)S(1)}, u32[]{:S(2)}, u32[]{:S(2)}) async-start(bf16[8,1,128,256]{3,2,1,0:T(8,128)(2,1)} %shard_map.49), calls=%async_computation | async-start | bytes 1048576 | tf_op jit(solution)/shard_map/all_to_all | solution.py:448
  59.3 15.1 %collective-permute-start.8 = (bf16[4,1,128,256]{3,2,1,0:T(8,128)(2,1)S(1)}, bf16[4,1,128,256]{3,2,1,0:T(8,128)(2,1)S(1)}, u32[]{:S(2)}, u32[]{:S(2)}) collective-permute-start(bf16[4,1,128,256]{3,2,1,0:T(8,128)(2,1)S(1)} %constant_dynamic-update-slice_fusion.refs_3_), channel_id=1, source_target_pairs={{0,4},{2,6},{4,0},{6,2},{8,12},{10,14},{12,8},{14,10},{1,5},{3,7},... | collective-permute-start | bytes 786440 | tf_op jit(solution)/shard_map/ppermute | solution.py:442
  61.5 11.8 %collective-permute-start.6 = (bf16[1,1,128,256]{3,2,1,0:T(8,128)(2,1)S(1)}, bf16[1,1,128,256]{3,2,1,0:T(8,128)(2,1)S(1)}, u32[]{:S(2)}, u32[]{:S(2)}) collective-permute-start(bf16[1,1,128,256]{3,2,1,0:T(8,128)(2,1)S(1)} %slice_bitcast_fusion.6), channel_id=1, source_target_pairs={{0,8},{2,10},{4,12},{6,14},{8,0},{10,2},{12,4},{14,6},{1,9},{3,11}... | collective-permute-start | bytes 196616 | tf_op jit(solution)/shard_map/ppermute | solution.py:442
  76.2 4.2 %collective-permute-start.9 = (f32[16,128,256]{2,1,0:T(8,128)S(1)}, f32[16,128,256]{2,1,0:T(8,128)S(1)}, u32[]{:S(2)}, u32[]{:S(2)}) collective-permute-start(f32[16,128,256]{2,1,0:T(8,128)S(1)} %shard_map.50.own.mine_hbm), channel_id=1, source_target_pairs={{0,1},{1,0},{2,3},{3,2},{4,5},{5,4},{6,7},{7,6},{8,9},{9,8},{10,11... | collective-permute-start | bytes 6291464 | tf_op jit(solution)/shard_map/ppermute | solution.py:445
  82.5 4.4 %collective-permute-start.10 = (f32[136,128]{1,0:T(8,128)S(1)}, f32[136,128]{1,0:T(8,128)S(1)}, u32[]{:S(2)}, u32[]{:S(2)}) collective-permute-start(f32[136,128]{1,0:T(8,128)S(1)} %shard_map.52), channel_id=1, source_target_pairs={{0,2},{2,0},{4,6},{6,4},{8,10},{10,8},{12,14},{14,12},{1,3},{3,1},... | collective-permute-start | bytes 208904 | tf_op jit(solution)/shard_map/ppermute | solution.py:442
  86.9 4.8 %collective-permute-start.11 = (f32[136,128]{1,0:T(8,128)S(1)}, f32[136,128]{1,0:T(8,128)S(1)}, u32[]{:S(2)}, u32[]{:S(2)}) collective-permute-start(f32[136,128]{1,0:T(8,128)S(1)} %add.63), channel_id=1, source_target_pairs={{0,4},{2,6},{4,0},{6,2},{8,12},{10,14},{12,8},{14,10},{1,5},{3,7},... | collective-permute-start | bytes 208904 | tf_op jit(solution)/shard_map/ppermute | solution.py:442
  91.6 5.3 %collective-permute-start.12 = (f32[136,128]{1,0:T(8,128)S(1)}, f32[136,128]{1,0:T(8,128)S(1)}, u32[]{:S(2)}, u32[]{:S(2)}) collective-permute-start(f32[136,128]{1,0:T(8,128)S(1)} %add.64), channel_id=1, source_target_pairs={{0,8},{2,10},{4,12},{6,14},{8,0},{10,2},{12,4},{14,6},{1,9},{3,11}... | collective-permute-start | bytes 208904 | tf_op jit(solution)/shard_map/ppermute | solution.py:442
  96.9 1.3 collective-permute-start.13
  112.2 5.2 %collective-permute-start.14 = (bf16[1,1,128,256]{3,2,1,0:T(8,128)(2,1)S(1)}, bf16[1,1,128,256]{3,2,1,0:T(8,128)(2,1)S(1)}, u32[]{:S(2)}, u32[]{:S(2)}) collective-permute-start(bf16[1,1,128,256]{3,2,1,0:T(8,128)(2,1)S(1)} %get-tuple-element.28), channel_id=1, source_target_pairs={{0,8},{2,10},{4,12},{6,14},{8,0},{10,2},{12,4},{14,6},{1,9},{3,11}... | collective-permute-start | bytes 196616 | tf_op jit(solution)/shard_map/ppermute | solution.py:442
  117.5 45.7 %all-to-all-start.2 = ((bf16[8,2,128,256]{3,2,1,0:T(8,128)(2,1)}), bf16[8,2,128,256]{3,2,1,0:T(8,128)(2,1)S(1)}, u32[]{:S(2)}, u32[]{:S(2)}) async-start(bf16[8,2,128,256]{3,2,1,0:T(8,128)(2,1)} %shard_map.54), calls=%async_computation.2 | async-start | bytes 2097152 | tf_op jit(solution)/shard_map/all_to_all | solution.py:448
  123.2 23.2 %collective-permute-start.15 = (bf16[4,1,128,256]{3,2,1,0:T(8,128)(2,1)S(1)}, bf16[4,1,128,256]{3,2,1,0:T(8,128)(2,1)S(1)}, u32[]{:S(2)}, u32[]{:S(2)}) collective-permute-start(bf16[4,1,128,256]{3,2,1,0:T(8,128)(2,1)S(1)} %get-tuple-element.31), channel_id=1, source_target_pairs={{0,4},{2,6},{4,0},{6,2},{8,12},{10,14},{12,8},{14,10},{1,5},{3,7},... | collective-permute-start | bytes 786440 | tf_op jit(solution)/shard_map/ppermute | solution.py:442
  146.6 6.0 %collective-permute-start.16 = (bf16[2,1,128,256]{3,2,0,1:T(8,128)(2,1)S(1)}, bf16[2,1,128,256]{3,2,0,1:T(8,128)(2,1)S(1)}, u32[]{:S(2)}, u32[]{:S(2)}) collective-permute-start(bf16[2,1,128,256]{3,2,0,1:T(8,128)(2,1)S(1)} %slice_bitcast_fusion), channel_id=1, source_target_pairs={{0,2},{2,0},{4,6},{6,4},{8,10},{10,8},{12,14},{14,12},{1,3},{3,1},... | collective-permute-start | bytes 393224 | tf_op jit(solution)/shard_map/ppermute | solution.py:442
  148.0 8.7 %collective-permute-start.18 = (bf16[2,1,128,256]{3,2,1,0:T(8,128)(2,1)S(1)}, bf16[2,1,128,256]{3,2,1,0:T(8,128)(2,1)S(1)}, u32[]{:S(2)}, u32[]{:S(2)}) collective-permute-start(bf16[2,1,128,256]{3,2,1,0:T(8,128)(2,1)S(1)} %pad_maximum_fusion.1), channel_id=1, source_target_pairs={{0,2},{2,0},{4,6},{6,4},{8,10},{10,8},{12,14},{14,12},{1,3},{3,1},... | collective-permute-start | bytes 393224 | tf_op jit(solution)/shard_map/ppermute | solution.py:442
  152.7 6.3 %collective-permute-start.17 = (bf16[1,1,128,256]{3,2,1,0:T(8,128)(2,1)S(1)}, bf16[1,1,128,256]{3,2,1,0:T(8,128)(2,1)S(1)}, u32[]{:S(2)}, u32[]{:S(2)}) collective-permute-start(bf16[1,1,128,256]{3,2,1,0:T(8,128)(2,1)S(1)} %slice_bitcast_fusion.4), channel_id=1, source_target_pairs={{0,8},{2,10},{4,12},{6,14},{8,0},{10,2},{12,4},{14,6},{1,9},{3,11}... | collective-permute-start | bytes 196616 | tf_op jit(solution)/shard_map/ppermute | solution.py:442
  156.7 6.4 %collective-permute-start.19 = (bf16[4,1,128,256]{3,2,1,0:T(8,128)(2,1)S(1)}, bf16[4,1,128,256]{3,2,1,0:T(8,128)(2,1)S(1)}, u32[]{:S(2)}, u32[]{:S(2)}) collective-permute-start(bf16[4,1,128,256]{3,2,1,0:T(8,128)(2,1)S(1)} %constant_dynamic-update-slice_fusion.3.refs_2_), channel_id=1, source_target_pairs={{0,4},{2,6},{4,0},{6,2},{8,12},{10,14},{12,8},{14,10},{1,5},{3,7},... | collective-permute-start | bytes 786440 | tf_op jit(solution)/shard_map/ppermute | solution.py:442
  164.5 4.2 %collective-permute-start.20 = (f32[16,128,256]{2,1,0:T(8,128)S(1)}, f32[16,128,256]{2,1,0:T(8,128)S(1)}, u32[]{:S(2)}, u32[]{:S(2)}) collective-permute-start(f32[16,128,256]{2,1,0:T(8,128)S(1)} %shard_map.55.own.mine_hbm), channel_id=1, source_target_pairs={{0,1},{1,0},{2,3},{3,2},{4,5},{5,4},{6,7},{7,6},{8,9},{9,8},{10,11... | collective-permute-start | bytes 6291464 | tf_op jit(solution)/shard_map/ppermute | solution.py:445
  170.7 4.4 %collective-permute-start.21 = (f32[136,128]{1,0:T(8,128)S(1)}, f32[136,128]{1,0:T(8,128)S(1)}, u32[]{:S(2)}, u32[]{:S(2)}) collective-permute-start(f32[136,128]{1,0:T(8,128)S(1)} %shard_map.57), channel_id=1, source_target_pairs={{0,2},{2,0},{4,6},{6,4},{8,10},{10,8},{12,14},{14,12},{1,3},{3,1},... | collective-permute-start | bytes 208904 | tf_op jit(solution)/shard_map/ppermute | solution.py:442
  175.1 4.4 %collective-permute-start.22 = (f32[136,128]{1,0:T(8,128)S(1)}, f32[136,128]{1,0:T(8,128)S(1)}, u32[]{:S(2)}, u32[]{:S(2)}) collective-permute-start(f32[136,128]{1,0:T(8,128)S(1)} %add.66), channel_id=1, source_target_pairs={{0,4},{2,6},{4,0},{6,2},{8,12},{10,14},{12,8},{14,10},{1,5},{3,7},... | collective-permute-start | bytes 208904 | tf_op jit(solution)/shard_map/ppermute | solution.py:442
  179.5 6.0 %collective-permute-start.23 = (f32[136,128]{1,0:T(8,128)S(1)}, f32[136,128]{1,0:T(8,128)S(1)}, u32[]{:S(2)}, u32[]{:S(2)}) collective-permute-start(f32[136,128]{1,0:T(8,128)S(1)} %add.67), channel_id=1, source_target_pairs={{0,8},{2,10},{4,12},{6,14},{8,0},{10,2},{12,4},{14,6},{1,9},{3,11}... | collective-permute-start | bytes 208904 | tf_op jit(solution)/shard_map/ppermute | solution.py:442
  185.5 1.3 collective-permute-start.24

commit v8 on v7

--- a/solution.py
+++ b/solution.py
@@ -10,6 +10,7 @@
 VMEM = pl.BlockSpec(memory_space=pltpu.VMEM)
 SMEM = pl.BlockSpec(memory_space=pltpu.SMEM)
 ANY = pl.BlockSpec(memory_space=pl.ANY)
+HBM = pl.BlockSpec(memory_space=pltpu.HBM)
 shape = jax.ShapeDtypeStruct
 f32, bf16, i32 = jnp.float32, jnp.bfloat16, jnp.int32
 
@@ -61,14 +62,19 @@
         return jnp.concatenate([p.astype(i32) for p in parts]), late[:, :, 1] ^ me
 
 
-def sums_kernel(counts_ref, sums_ref):
-    nnz, rows, cols = counts_ref.shape
+def sums_kernel(counts_hbm, sums_hbm, counts, sums, sems):
+    nnz, rows, cols = counts.shape
+    groups = sums_hbm.shape[0]
+    loads = start_copies([(counts_hbm.at[s], counts.at[s]) for s in range(nnz)], sems)
     ones = jnp.ones((8, cols), bf16)
-    sums_ref[...] = jnp.zeros(sums_ref.shape, f32)
+    sums[...] = jnp.zeros(sums.shape, f32)
     for s in range(nnz):
-        block = counts_ref[s].astype(bf16)
-        sums_ref[0, pl.ds(s, 1), :] = contract(ones, block, 1, 1)[0:1, :]
-        sums_ref[0, pl.ds(nnz + s, 1), :] = contract(ones, block, 1, 0)[0:1, :]
+        loads[s].wait()
+        block = counts[s].astype(bf16)
+        sums[pl.ds(s, 1), :] = contract(ones, block, 1, 1)[0:1, :]
+        sums[pl.ds(nnz + s, 1), :] = contract(ones, block, 1, 0)[0:1, :]
+    for copy in start_copies([(sums, sums_hbm.at[r]) for r in range(groups)], sems.at[nnz:]):
+        copy.wait()
 
 
 def gather_hot(t, tab, blocks, near, far):
@@ -108,22 +114,26 @@
 
 
 def make_source_kernel(t):
-    def kernel(tab, sketch_ref, turned, send, near, far):
+    def kernel(tab, sketch_ref, turned_hbm, send, near, far, turned, sems):
         @pl.loop(0, sketch_ref.shape[0])
         def _(i):
             turned[i] = sketch_ref[i].T
 
-        gather_main(t, tab, turned, send, 0)
+        copies = start_copies(
+            [(turned.at[tab[t.main_j + r]], send.at[r, 0]) for r in range(t.groups)]
+            + [(turned, turned_hbm)],
+            sems,
+        )
         gather_hot(t, tab, turned, near, far)
+        for copy in copies:
+            copy.wait()
 
     return kernel
 
 
 def make_ppmi_kernel(t):
-    def kernel(tab, match_ref, counts_ref, turned, sums_a, sums_b, ppmi_ref, hot, cols_log):
-        sums = jnp.concatenate(
-            [ref[r] for ref in (sums_a, sums_b) for r in range(t.groups // 2)], axis=0
-        )
+    def kernel(tab, match_ref, counts_ref, turned, sums_ref, ppmi_ref, hot, cols_log):
+        sums = jnp.concatenate([sums_ref[r] for r in range(t.groups)], axis=0)
         high = jnp.floor(sums * (1.0 / 256.0))
         low = sums - high * 256.0
         match = match_ref[...]
@@ -487,12 +497,28 @@
     ppmi_shape = shape((nnz, rows, rows), bf16)
     result_shape = shape((blocks, half, rows), f32)
 
-    sums = call(sums_kernel, shape((1, depth, rows), f32), [VMEM], vmem=8)(counts)
+    sums = call(
+        sums_kernel,
+        shape((groups, depth, rows), f32),
+        [HBM],
+        HBM,
+        scratch=[
+            pltpu.VMEM((nnz, rows, rows), i32),
+            pltpu.VMEM((depth, rows), f32),
+            pltpu.SemaphoreType.DMA((nnz + groups,)),
+        ],
+    )(counts)
+    sums_all = exchange(sums)
     tab, towards = t.build(block_pairs, me, my_col)
     turned, send_x, near, far = call(
         make_source_kernel(t),
         [shape((blocks, half, rows), bf16), send_shape(1), side_shape, side_shape],
         [SMEM, VMEM],
+        [HBM, HBM, VMEM, VMEM],
+        scratch=[
+            pltpu.VMEM((blocks, half, rows), bf16),
+            pltpu.SemaphoreType.DMA((groups + 1,)),
+        ],
         vmem=8,
     )(tab, sketch)
 
@@ -500,19 +526,18 @@
     col_ids = block_pairs[:, :, 2] * groups + block_pairs[:, :, 1]
     no_id = jnp.full((groups, depth - 2 * nnz), -1, i32)
     ids = jnp.concatenate([row_ids, col_ids, no_id], axis=1)
-    sums_a, sums_b, order = spread(sums, t.bits[::-1])
-    ids = jnp.take(ids, me ^ jnp.array(order), axis=0)
-    my_ids = ids[0]
+    my_ids = lax.dynamic_index_in_dim(ids, me, 0, keepdims=False)
     match = (my_ids[:, None] == ids.reshape(-1)[None, :]).astype(bf16)
 
+    send_x, sums_all = lax.optimization_barrier((send_x, sums_all))
     got_x, x_step = exchange(send_x), peer(far, t.steps[0])
     ppmi, hot_t = call(
         make_ppmi_kernel(t),
         [ppmi_shape, hot_shape],
-        [SMEM] + [VMEM] * 5,
+        [SMEM] + [VMEM] * 4,
         scratch=[pltpu.VMEM((depth, rows), f32)],
         vmem=12,
-    )(tab, match, counts, turned, sums_a, sums_b)
+    )(tab, match, counts, turned, sums_all)
 
     def finish(source, got_x, near, far, x_step, hot_t):
         t_step = peer(hot_t, t.steps[-1])
@@ -522,7 +547,10 @@
         send = call(
             make_main_kernel(t, merged), send_shape(1 + merged), [SMEM, VMEM, VMEM], vmem=8
         )(tab, source, ppmi)
-        send, t_step = lax.optimization_barrier((send, t_step))
+        if merged:
+            send, x_step, t_step = lax.optimization_barrier((send, x_step, t_step))
+        else:
+            send, t_step = lax.optimization_barrier((send, t_step))
         got = [exchange(send)] + ([] if merged else [got_x])
         hot_x = scatter_hot(near, far, x_step, towards)
         hot_a, hot_b, order = spread(hot_t, t.steps[::-1], t_step)

time: 203 us -> 187 us (0.921)
  waiting for transfers between devices: 90.2 us -> 69.6 us
  starting transfers between devices: 50 us -> 54.3 us
  local copies, waits for them, and re-layouts: 11.5 us -> 8.19 us
  Pallas kernels: 47.5 us -> 49.9 us
    ppermute x21 -> x18, waiting for transfers between devices: 82.1 us -> 61.5 us  [peer(): return lax.ppermute(x, 'row', [(r, r ^ k) for r in range(groups)])]
    all_to_all x3 -> x4, starting transfers between devices: 14.1 us -> 22.4 us  [exchange(): return lax.all_to_all(x, 'row', split_axis=0, concat_axis=0, tiled=True)]
    ppermute x21 -> x18, starting transfers between devices: 35.6 us -> 31.6 us  [peer(): return lax.ppermute(x, 'row', [(r, r ^ k) for r in range(groups)])]
    unnamed x39 -> x29, local copies, waits for them, and re-layouts: 8.93 us -> 6.07 us
    pallas_call x2, Pallas kernels: 2.13 us -> 4.2 us  [the longest x1 2.25 us: body(): call(sums_kernel, shape((groups, depth, rows), f32), [HBM], HBM, scratch=...]
  transfers between devices with their start and end apart: 28 -> 26, of which waited for: 20 -> 21; matrix products, arithmetic and copies ran while one was open for 3% -> 3% of each run, Pallas kernels for 5% -> 6%
where the time goes in v8:
time: 187 us; the launch traced here: 186 us
  waiting for transfers between devices  69.6 us (37%)
  starting transfers between devices  54.3 us (29%)
  Pallas kernels  49.9 us (27%)
  local copies, waits for them, and re-layouts  8.19 us (4%)
  other arithmetic  3.63 us (2%)
    ppermute x18, waiting for transfers between devices, peer(): return lax.ppermute(x, 'row', [(r, r ^ k) for r in range(groups)])  61.5 us
    ppermute x18, starting transfers between devices, peer(): return lax.ppermute(x, 'row', [(r, r ^ k) for r in range(groups)])  31.6 us
    all_to_all x4, starting transfers between devices, exchange(): return lax.all_to_all(x, 'row', split_axis=0, concat_axis=0, tiled=True)  22.4 us
    pallas_call x1, Pallas kernels, body(): call(make_final_kernel(t, 1.0 / vocab), shape((blocks, rows, half), f32),...  15.2 us
    pallas_call x1, Pallas kernels, body(): call(make_second_kernel(t, 1.0 / vocab), [shape((blocks, half, rows), bf1...  13.9 us
    ppermute x4, waiting for transfers between devices, swap(): return lax.ppermute(x, 'col', [(0, 1), (1, 0)])  8.1 us
    unnamed x29, local copies, waits for them, and re-layouts  6.07 us
    pallas_call x2, Pallas kernels, finish(): call(make_cross_gram_kernel(t), shape((half + 8, half), f32), [SMEM] + [V...  4.02 us
  transfers between devices with their start and end apart: 26, of which 21 were waited for; matrix products, arithmetic and copies ran while one was open for 3% of the time, Pallas kernels for 6%

profile of v8, /device:TPU:0, one launch (start us, length us, event | category | flops | bytes accessed | tf_op | source)
XLA Modules:
  0.0 186.2 jit_solution(6804343280882491766)
XLA Ops:
  0.0 1.7 copy-done
  1.7 2.2 %shard_map.38 = f32[8,24,256]{2,1,0:T(8,128)S(1)} custom-call(s32[9,256,256]{2,1,0:T(8,128)S(1)} %copy-done), custom_call_target="tpu_custom_call" | custom-call | bytes 4194304 | tf_op jit(solution)/shard_map/pallas_call | solution.py:500
  4.6 7.4 %all-to-all-start = ((f32[8,24,256]{2,1,0:T(8,128)}), f32[8,24,256]{2,1,0:T(8,128)}, u32[]{:S(2)}, u32[]{:S(2)}) async-start(f32[8,24,256]{2,1,0:T(8,128)} %copy-done.5), calls=%async_computation | async-start | bytes 393216 | tf_op jit(solution)/shard_map/all_to_all | solution.py:458
  13.2 3.3 %shard_map.37 = (bf16[16,128,256]{2,1,0:T(8,128)(2,1)S(1)}, bf16[8,1,128,256]{3,2,1,0:T(8,128)(2,1)S(1)}, bf16[4,1,128,256]{3,2,1,0:T(8,128)(2,1)S(1)}, bf16[4,1,128,256]{3,2,1,0:T(8,128)(2,1)}) custom-call(s32[35]{0:T(128)S(1)} %concatenate.20.tab, bf16[16,256,128]{2,1,0:T(8,128)(2,1)S(1)} %copy-done.4), custom_call_target="tpu_custom_call" | custom-call | bytes 4194304 | tf_op jit(solution)/shard_map/pallas_call | solution.py:513
  18.9 2.0 %collective-permute-start.1 = (bf16[4,1,128,256]{3,2,1,0:T(8,128)(2,1)}, bf16[4,1,128,256]{3,2,1,0:T(8,128)(2,1)S(1)}, u32[]{:S(2)}, u32[]{:S(2)}) collective-permute-start(bf16[4,1,128,256]{3,2,1,0:T(8,128)(2,1)} %get-tuple-element.30), channel_id=1, source_target_pairs={{0,4},{2,6},{4,0},{6,2},{8,12},{10,14},{12,8},{14,10},{1,5},{3,7},... | collective-permute-start | bytes 786440 | tf_op jit(solution)/shard_map/ppermute | solution.py:452
  21.4 4.5 %all-to-all-start.2 = ((bf16[8,1,128,256]{3,2,1,0:T(8,128)(2,1)}), bf16[8,1,128,256]{3,2,1,0:T(8,128)(2,1)}, u32[]{:S(2)}, u32[]{:S(2)}) async-start(bf16[8,1,128,256]{3,2,1,0:T(8,128)(2,1)} %copy-done.6), calls=%async_computation.2 | async-start | bytes 1048576 | tf_op jit(solution)/shard_map/all_to_all | solution.py:458
  28.9 1.5 collective-permute-start.2
  31.8 1.9 %shard_map.39 = (bf16[9,256,256]{2,1,0:T(8,128)(2,1)S(1)}, bf16[1,1,128,256]{3,2,1,0:T(8,128)(2,1)S(1)}) custom-call(s32[35]{0:T(128)S(1)} %concatenate.20.tab, bf16[24,192]{1,0:T(8,128)(2,1)S(1)} %compare_convert_fusion.match_ref, s32[9,256,256]{2,1,0:T(8,128)S(1)} %copy-done.1, bf16[16,128,256]{2,1,0:T(8,128)(2,1)S(1)} %copy-done.3, ...), custom_call_target="tpu_custom_call" | custom-call | bytes 4194304 | tf_op jit(solution)/shard_map/pallas_call | solution.py:534
  33.7 1.6 shard_map.40
  35.4 3.3 %collective-permute-start = (bf16[1,1,128,256]{3,2,1,0:T(8,128)(2,1)S(1)}, bf16[1,1,128,256]{3,2,1,0:T(8,128)(2,1)S(1)}, u32[]{:S(2)}, u32[]{:S(2)}) collective-permute-start(bf16[1,1,128,256]{3,2,1,0:T(8,128)(2,1)S(1)} %get-tuple-element.26), channel_id=1, source_target_pairs={{0,8},{2,10},{4,12},{6,14},{8,0},{10,2},{12,4},{14,6},{1,9},{3,11}... | collective-permute-start | bytes 196616 | tf_op jit(solution)/shard_map/ppermute | solution.py:452
  38.7 3.1 %collective-permute-done = bf16[1,1,128,256]{3,2,1,0:T(8,128)(2,1)S(1)} collective-permute-done((bf16[1,1,128,256]{3,2,1,0:T(8,128)(2,1)S(1)}, bf16[1,1,128,256]{3,2,1,0:T(8,128)(2,1)S(1)}, u32[]{:S(2)}, u32[]{:S(2)}) %collective-permute-start) | collective-permute-done | bytes 65568 | tf_op jit(solution)/shard_map/ppermute | solution.py:452
  41.8 5.4 %all-to-all-start.1 = ((bf16[8,1,128,256]{3,2,1,0:T(8,128)(2,1)}), bf16[8,1,128,256]{3,2,1,0:T(8,128)(2,1)S(1)}, u32[]{:S(2)}, u32[]{:S(2)}) async-start(bf16[8,1,128,256]{3,2,1,0:T(8,128)(2,1)} %shard_map.40), calls=%async_computation.1 | async-start | bytes 1048576 | tf_op jit(solution)/shard_map/all_to_all | solution.py:458
  49.0 2.1 %collective-permute-start.4 = (bf16[2,1,128,256]{3,2,1,0:T(8,128)(2,1)S(1)}, bf16[2,1,128,256]{3,2,1,0:T(8,128)(2,1)S(1)}, u32[]{:S(2)}, u32[]{:S(2)}) collective-permute-start(bf16[2,1,128,256]{3,2,1,0:T(8,128)(2,1)S(1)} %pad_maximum_fusion), channel_id=1, source_target_pairs={{0,2},{2,0},{4,6},{6,4},{8,10},{10,8},{12,14},{14,12},{1,3},{3,1},... | collective-permute-start | bytes 393224 | tf_op jit(solution)/shard_map/ppermute | solution.py:452
  51.1 2.4 %collective-permute-start.3 = (bf16[1,1,128,256]{3,2,1,0:T(8,128)(2,1)S(1)}, bf16[1,1,128,256]{3,2,1,0:T(8,128)(2,1)S(1)}, u32[]{:S(2)}, u32[]{:S(2)}) collective-permute-start(bf16[1,1,128,256]{3,2,1,0:T(8,128)(2,1)S(1)} %slice_bitcast_fusion.6), channel_id=1, source_target_pairs={{0,8},{2,10},{4,12},{6,14},{8,0},{10,2},{12,4},{14,6},{1,9},{3,11}... | collective-permute-start | bytes 196616 | tf_op jit(solution)/shard_map/ppermute | solution.py:452
  53.5 2.1 %collective-permute-done.4 = bf16[2,1,128,256]{3,2,1,0:T(8,128)(2,1)S(1)} collective-permute-done((bf16[2,1,128,256]{3,2,1,0:T(8,128)(2,1)S(1)}, bf16[2,1,128,256]{3,2,1,0:T(8,128)(2,1)S(1)}, u32[]{:S(2)}, u32[]{:S(2)}) %collective-permute-start.4) | collective-permute-done | bytes 131104 | tf_op jit(solution)/shard_map/ppermute | solution.py:452
  55.5 2.1 %collective-permute-start.5 = (bf16[4,1,128,256]{3,2,1,0:T(8,128)(2,1)S(1)}, bf16[4,1,128,256]{3,2,1,0:T(8,128)(2,1)S(1)}, u32[]{:S(2)}, u32[]{:S(2)}) collective-permute-start(bf16[4,1,128,256]{3,2,1,0:T(8,128)(2,1)S(1)} %constant_dynamic-update-slice_fusion.refs_3_), channel_id=1, source_target_pairs={{0,4},{2,6},{4,0},{6,2},{8,12},{10,14},{12,8},{14,10},{1,5},{3,7},... | collective-permute-start | bytes 786440 | tf_op jit(solution)/shard_map/ppermute | solution.py:452
  57.8 4.4 %collective-permute-done.3 = bf16[1,1,128,256]{3,2,1,0:T(8,128)(2,1)S(1)} collective-permute-done((bf16[1,1,128,256]{3,2,1,0:T(8,128)(2,1)S(1)}, bf16[1,1,128,256]{3,2,1,0:T(8,128)(2,1)S(1)}, u32[]{:S(2)}, u32[]{:S(2)}) %collective-permute-start.3) | collective-permute-done | bytes 65568 | tf_op jit(solution)/shard_map/ppermute | solution.py:452
  62.2 2.7 %collective-permute-done.5.refs_4_ = bf16[4,1,128,256]{3,2,1,0:T(8,128)(2,1)S(1)} collective-permute-done((bf16[4,1,128,256]{3,2,1,0:T(8,128)(2,1)S(1)}, bf16[4,1,128,256]{3,2,1,0:T(8,128)(2,1)S(1)}, u32[]{:S(2)}, u32[]{:S(2)}) %collective-permute-start.5) | collective-permute-done | bytes 262176 | tf_op jit(solution)/shard_map/ppermute | solution.py:452
  64.9 1.8 shard_map.41.own.mine_hbm
  66.8 1.3 shard_map.42.square
  68.1 2.8 %collective-permute-done.6.other.other_hbm = f32[16,128,256]{2,1,0:T(8,128)S(1)} collective-permute-done((f32[16,128,256]{2,1,0:T(8,128)S(1)}, f32[16,128,256]{2,1,0:T(8,128)S(1)}, u32[]{:S(2)}, u32[]{:S(2)}) %collective-permute-start.6) | collective-permute-done | bytes 2097184 | tf_op jit(solution)/shard_map/ppermute | solution.py:455
  70.9 2.0 %shard_map.43 = f32[136,128]{1,0:T(8,128)S(1)} custom-call(s32[35]{0:T(128)S(1)} %concatenate.20.tab, f32[16,128,256]{2,1,0:T(8,128)S(1)} %shard_map.41.own.mine_hbm, f32[16,128,256]{2,1,0:T(8,128)S(1)} %collective-permute-done.6.other.other_hbm, f32[128,128]{1,0:T(8,128)S(1)} %shard_map.42.square), custom_call_target="tpu_custom_call" | custom-call | bytes 4194304 | tf_op jit(solution)/shard_map/pallas_call | solution.py:565
  72.9 1.5 collective-permute-start.7
  74.5 2.8 %collective-permute-done.7 = f32[136,128]{1,0:T(8,128)S(1)} collective-permute-done((f32[136,128]{1,0:T(8,128)S(1)}, f32[136,128]{1,0:T(8,128)S(1)}, u32[]{:S(2)}, u32[]{:S(2)}) %collective-permute-start.7) | collective-permute-done | bytes 69664 | tf_op jit(solution)/shard_map/ppermute | solution.py:452
  77.4 4.3 %collective-permute-done.8 = f32[136,128]{1,0:T(8,128)S(1)} collective-permute-done((f32[136,128]{1,0:T(8,128)S(1)}, f32[136,128]{1,0:T(8,128)S(1)}, u32[]{:S(2)}, u32[]{:S(2)}) %collective-permute-start.8) | collective-permute-done | bytes 69664 | tf_op jit(solution)/shard_map/ppermute | solution.py:452
  81.7 2.2 %collective-permute-start.9 = (f32[136,128]{1,0:T(8,128)S(1)}, f32[136,128]{1,0:T(8,128)S(1)}, u32[]{:S(2)}, u32[]{:S(2)}) collective-permute-start(f32[136,128]{1,0:T(8,128)S(1)} %add.61), channel_id=1, source_target_pairs={{0,8},{2,10},{4,12},{6,14},{8,0},{10,2},{12,4},{14,6},{1,9},{3,11}... | collective-permute-start | bytes 208904 | tf_op jit(solution)/shard_map/ppermute | solution.py:452
  83.9 3.1 %collective-permute-done.9 = f32[136,128]{1,0:T(8,128)S(1)} collective-permute-done((f32[136,128]{1,0:T(8,128)S(1)}, f32[136,128]{1,0:T(8,128)S(1)}, u32[]{:S(2)}, u32[]{:S(2)}) %collective-permute-start.9) | collective-permute-done | bytes 69664 | tf_op jit(solution)/shard_map/ppermute | solution.py:452
  88.3 13.9 %shard_map.44 = (bf16[16,128,256]{2,1,0:T(8,128)(2,1)S(1)}, bf16[4,1,128,256]{3,2,1,0:T(8,128)(2,1)S(1)}, bf16[4,1,128,256]{3,2,1,0:T(8,128)(2,1)S(1)}, bf16[1,1,128,256]{3,2,1,0:T(8,128)(2,1)S(1)}) custom-call(s32[35]{0:T(128)S(1)} %concatenate.20.tab, f32[136,128]{1,0:T(8,128)S(1)} %add.62.own_g, f32[136,128]{1,0:T(8,128)S(1)} %collective-permute-done.10.other_g, ...), custom_call_target="tpu_custom_call" | custom-call | bytes 4194304 | tf_op jit(solution)/shard_map/pallas_call | solution.py:582
  102.3 1.4 collective-permute-start.11
  103.6 3.0 %collective-permute-start.12 = (bf16[1,1,128,256]{3,2,1,0:T(8,128)(2,1)S(1)}, bf16[1,1,128,256]{3,2,1,0:T(8,128)(2,1)S(1)}, u32[]{:S(2)}, u32[]{:S(2)}) collective-permute-start(bf16[1,1,128,256]{3,2,1,0:T(8,128)(2,1)S(1)} %get-tuple-element.34), channel_id=1, source_target_pairs={{0,8},{2,10},{4,12},{6,14},{8,0},{10,2},{12,4},{14,6},{1,9},{3,11}... | collective-permute-start | bytes 196616 | tf_op jit(solution)/shard_map/ppermute | solution.py:452
  106.7 1.8 shard_map.45
  108.5 2.5 %collective-permute-done.12 = bf16[1,1,128,256]{3,2,1,0:T(8,128)(2,1)S(1)} collective-permute-done((bf16[1,1,128,256]{3,2,1,0:T(8,128)(2,1)S(1)}, bf16[1,1,128,256]{3,2,1,0:T(8,128)(2,1)S(1)}, u32[]{:S(2)}, u32[]{:S(2)}) %collective-permute-start.12) | collective-permute-done | bytes 65568 | tf_op jit(solution)/shard_map/ppermute | solution.py:452
  112.1 5.0 %all-to-all-start.3 = ((bf16[8,2,128,256]{3,2,1,0:T(8,128)(2,1)}), bf16[8,2,128,256]{3,2,1,0:T(8,128)(2,1)S(1)}, u32[]{:S(2)}, u32[]{:S(2)}) async-start(bf16[8,2,128,256]{3,2,1,0:T(8,128)(2,1)} %shard_map.45), calls=%async_computation.3 | async-start | bytes 2097152 | tf_op jit(solution)/shard_map/all_to_all | solution.py:458
  117.3 2.1 %collective-permute-start.13 = (bf16[2,1,128,256]{3,2,0,1:T(8,128)(2,1)S(1)}, bf16[2,1,128,256]{3,2,0,1:T(8,128)(2,1)S(1)}, u32[]{:S(2)}, u32[]{:S(2)}) collective-permute-start(bf16[2,1,128,256]{3,2,0,1:T(8,128)(2,1)S(1)} %slice_bitcast_fusion), channel_id=1, source_target_pairs={{0,2},{2,0},{4,6},{6,4},{8,10},{10,8},{12,14},{14,12},{1,3},{3,1},... | collective-permute-start | bytes 393224 | tf_op jit(solution)/shard_map/ppermute | solution.py:452
  119.5 12.6 %collective-permute-done.13 = bf16[2,1,128,256]{3,2,0,1:T(8,128)(2,1)S(1)} collective-permute-done((bf16[2,1,128,256]{3,2,0,1:T(8,128)(2,1)S(1)}, bf16[2,1,128,256]{3,2,0,1:T(8,128)(2,1)S(1)}, u32[]{:S(2)}, u32[]{:S(2)}) %collective-permute-start.13) | collective-permute-done | bytes 131104 | tf_op jit(solution)/shard_map/ppermute | solution.py:452
  132.2 1.5 collective-permute-start.14
  134.4 4.1 %collective-permute-start.16 = (bf16[4,1,128,256]{3,2,1,0:T(8,128)(2,1)S(1)}, bf16[4,1,128,256]{3,2,1,0:T(8,128)(2,1)S(1)}, u32[]{:S(2)}, u32[]{:S(2)}) collective-permute-start(bf16[4,1,128,256]{3,2,1,0:T(8,128)(2,1)S(1)} %constant_dynamic-update-slice_fusion.3.refs_2_), channel_id=1, source_target_pairs={{0,4},{2,6},{4,0},{6,2},{8,12},{10,14},{12,8},{14,10},{1,5},{3,7},... | collective-permute-start | bytes 786440 | tf_op jit(solution)/shard_map/ppermute | solution.py:452
  138.5 7.0 %collective-permute-done.14 = bf16[1,1,128,256]{3,2,1,0:T(8,128)(2,1)S(1)} collective-permute-done((bf16[1,1,128,256]{3,2,1,0:T(8,128)(2,1)S(1)}, bf16[1,1,128,256]{3,2,1,0:T(8,128)(2,1)S(1)}, u32[]{:S(2)}, u32[]{:S(2)}) %collective-permute-start.14) | collective-permute-done | bytes 65568 | tf_op jit(solution)/shard_map/ppermute | solution.py:452
  145.5 2.3 %collective-permute-done.16.refs_3_ = bf16[4,1,128,256]{3,2,1,0:T(8,128)(2,1)S(1)} collective-permute-done((bf16[4,1,128,256]{3,2,1,0:T(8,128)(2,1)S(1)}, bf16[4,1,128,256]{3,2,1,0:T(8,128)(2,1)S(1)}, u32[]{:S(2)}, u32[]{:S(2)}) %collective-permute-start.16) | collective-permute-done | bytes 262176 | tf_op jit(solution)/shard_map/ppermute | solution.py:452
  147.9 1.3 shard_map.46.own.mine_hbm
  149.2 1.3 shard_map.47.square
  150.6 2.8 %collective-permute-done.17.other.other_hbm = f32[16,128,256]{2,1,0:T(8,128)S(1)} collective-permute-done((f32[16,128,256]{2,1,0:T(8,128)S(1)}, f32[16,128,256]{2,1,0:T(8,128)S(1)}, u32[]{:S(2)}, u32[]{:S(2)}) %collective-permute-start.17) | collective-permute-done | bytes 2097184 | tf_op jit(solution)/shard_map/ppermute | solution.py:455
  153.4 2.0 %shard_map.48 = f32[136,128]{1,0:T(8,128)S(1)} custom-call(s32[35]{0:T(128)S(1)} %concatenate.20.tab, f32[16,128,256]{2,1,0:T(8,128)S(1)} %shard_map.46.own.mine_hbm, f32[16,128,256]{2,1,0:T(8,128)S(1)} %collective-permute-done.17.other.other_hbm, f32[128,128]{1,0:T(8,128)S(1)} %shard_map.47.square), custom_call_target="tpu_custom_call" | custom-call | bytes 4194304 | tf_op jit(solution)/shard_map/pallas_call | solution.py:565
  155.5 4.3 %collective-permute-done.18 = f32[136,128]{1,0:T(8,128)S(1)} collective-permute-done((f32[136,128]{1,0:T(8,128)S(1)}, f32[136,128]{1,0:T(8,128)S(1)}, u32[]{:S(2)}, u32[]{:S(2)}) %collective-permute-start.18) | collective-permute-done | bytes 69664 | tf_op jit(solution)/shard_map/ppermute | solution.py:452
  159.9 4.3 %collective-permute-done.19 = f32[136,128]{1,0:T(8,128)S(1)} collective-permute-done((f32[136,128]{1,0:T(8,128)S(1)}, f32[136,128]{1,0:T(8,128)S(1)}, u32[]{:S(2)}, u32[]{:S(2)}) %collective-permute-start.19) | collective-permute-done | bytes 69664 | tf_op jit(solution)/shard_map/ppermute | solution.py:452
  164.2 2.3 %collective-permute-start.20 = (f32[136,128]{1,0:T(8,128)S(1)}, f32[136,128]{1,0:T(8,128)S(1)}, u32[]{:S(2)}, u32[]{:S(2)}) collective-permute-start(f32[136,128]{1,0:T(8,128)S(1)} %add.64), channel_id=1, source_target_pairs={{0,8},{2,10},{4,12},{6,14},{8,0},{10,2},{12,4},{14,6},{1,9},{3,11}... | collective-permute-start | bytes 208904 | tf_op jit(solution)/shard_map/ppermute | solution.py:452
  166.4 3.0 %collective-permute-done.20 = f32[136,128]{1,0:T(8,128)S(1)} collective-permute-done((f32[136,128]{1,0:T(8,128)S(1)}, f32[136,128]{1,0:T(8,128)S(1)}, u32[]{:S(2)}, u32[]{:S(2)}) %collective-permute-start.20) | collective-permute-done | bytes 69664 | tf_op jit(solution)/shard_map/ppermute | solution.py:452
  170.8 15.2 %shard_map.49 = f32[16,256,128]{2,1,0:T(8,128)} custom-call(s32[35]{0:T(128)S(1)} %concatenate.20.tab, f32[136,128]{1,0:T(8,128)S(1)} %add.65.own_g, f32[136,128]{1,0:T(8,128)S(1)} %collective-permute-done.21.other_g, f32[16,128,256]{2,1,0:T(8,128)S(1)} %shard_map.46.own.mine_hbm, f32[16,128,256]{2,1,0:T(8,128)S(1)} %collective-permute-done.17.other.other_hbm), custom_call_target="tpu_custom_call" | custom-call | bytes 4194304 | tf_op jit(solution)/shard_map/pallas_call | solution.py:591
  (93 shorter events, 16.3 us)
Async XLA Ops:
  0.0 1.7 copy-start
  1.7 10.4 %copy-start.11 = (s32[8,9,3]{1,0,2:T(8,128)S(1)}, s32[8,9,3]{1,0,2:T(8,128)}, u32[]{:S(2)}) copy-start(s32[8,9,3]{1,0,2:T(8,128)} %param.4) | copy-start | bytes 2596
  1.7 11.5 %copy-start.4 = (bf16[16,256,128]{2,1,0:T(8,128)(2,1)S(1)}, bf16[16,256,128]{2,1,0:T(8,128)(2,1)}, u32[]{:S(2)}) copy-start(bf16[16,256,128]{2,1,0:T(8,128)(2,1)} %sketch_ref.1) | copy-start | bytes 3145732
  3.9 0.7 copy-start.5
  4.6 25.9 %copy-start.1 = (s32[9,256,256]{2,1,0:T(8,128)S(1)}, s32[9,256,256]{2,1,0:T(8,128)}, u32[]{:S(2)}) copy-start(s32[9,256,256]{2,1,0:T(8,128)} %counts_ref.1) | copy-start | bytes 7077892
  4.6 16.8 %all-to-all-start = ((f32[8,24,256]{2,1,0:T(8,128)}), f32[8,24,256]{2,1,0:T(8,128)}, u32[]{:S(2)}, u32[]{:S(2)}) async-start(f32[8,24,256]{2,1,0:T(8,128)} %copy-done.5), calls=%async_computation | async-start | bytes 393216 | tf_op jit(solution)/shard_map/all_to_all | solution.py:458
  16.5 1.0 copy-start.2
  17.4 0.8 copy-start.6
  18.2 0.7 copy-start.8
  18.9 8.2 %collective-permute-start.1 = (bf16[4,1,128,256]{3,2,1,0:T(8,128)(2,1)}, bf16[4,1,128,256]{3,2,1,0:T(8,128)(2,1)S(1)}, u32[]{:S(2)}, u32[]{:S(2)}) collective-permute-start(bf16[4,1,128,256]{3,2,1,0:T(8,128)(2,1)} %get-tuple-element.30), channel_id=1, source_target_pairs={{0,4},{2,6},{4,0},{6,2},{8,12},{10,14},{12,8},{14,10},{1,5},{3,7},... | collective-permute-start | bytes 786440 | tf_op jit(solution)/shard_map/ppermute | solution.py:452
  21.4 20.3 %all-to-all-start.2 = ((bf16[8,1,128,256]{3,2,1,0:T(8,128)(2,1)}), bf16[8,1,128,256]{3,2,1,0:T(8,128)(2,1)}, u32[]{:S(2)}, u32[]{:S(2)}) async-start(bf16[8,1,128,256]{3,2,1,0:T(8,128)(2,1)} %copy-done.6), calls=%async_computation.2 | async-start | bytes 1048576 | tf_op jit(solution)/shard_map/all_to_all | solution.py:458
  28.2 2.4 %copy-start.9 = (bf16[4,1,128,256]{3,2,1,0:T(8,128)(2,1)}, bf16[4,1,128,256]{3,2,1,0:T(8,128)(2,1)S(1)}, u32[]{:S(2)}) copy-start(bf16[4,1,128,256]{3,2,1,0:T(8,128)(2,1)S(1)} %broadcast_select_fusion.1) | copy-start | bytes 786436
  28.9 18.3 %collective-permute-start.2 = (bf16[2,1,128,256]{3,2,0,1:T(8,128)(2,1)}, bf16[2,1,128,256]{3,2,0,1:T(8,128)(2,1)}, u32[]{:S(2)}, u32[]{:S(2)}) collective-permute-start(bf16[2,1,128,256]{3,2,0,1:T(8,128)(2,1)} %slice_bitcast_fusion.2), channel_id=1, source_target_pairs={{0,2},{2,0},{4,6},{6,4},{8,10},{10,8},{12,14},{14,12},{1,3},{3,1},... | collective-permute-start | bytes 393224 | tf_op jit(solution)/shard_map/ppermute | solution.py:452
  30.5 1.2 copy-start.3
  33.7 4.9 %copy-start.7 = (bf16[1,1,128,256]{3,2,1,0:T(8,128)(2,1)}, bf16[1,1,128,256]{3,2,1,0:T(8,128)(2,1)S(1)}, u32[]{:S(2)}) copy-start(bf16[1,1,128,256]{3,2,1,0:T(8,128)(2,1)S(1)} %get-tuple-element.26) | copy-start | bytes 196612
  33.7 13.4 %copy-start.10 = (bf16[4,1,128,256]{3,2,1,0:T(8,128)(2,1)S(1)}, bf16[4,1,128,256]{3,2,1,0:T(8,128)(2,1)}, u32[]{:S(2)}) copy-start(bf16[4,1,128,256]{3,2,1,0:T(8,128)(2,1)} %copy-done.9) | copy-start | bytes 786436
  35.4 6.4 %collective-permute-start = (bf16[1,1,128,256]{3,2,1,0:T(8,128)(2,1)S(1)}, bf16[1,1,128,256]{3,2,1,0:T(8,128)(2,1)S(1)}, u32[]{:S(2)}, u32[]{:S(2)}) collective-permute-start(bf16[1,1,128,256]{3,2,1,0:T(8,128)(2,1)S(1)} %get-tuple-element.26), channel_id=1, source_target_pairs={{0,8},{2,10},{4,12},{6,14},{8,0},{10,2},{12,4},{14,6},{1,9},{3,11}... | collective-permute-start | bytes 196616 | tf_op jit(solution)/shard_map/ppermute | solution.py:452
  41.8 23.2 %all-to-all-start.1 = ((bf16[8,1,128,256]{3,2,1,0:T(8,128)(2,1)}), bf16[8,1,128,256]{3,2,1,0:T(8,128)(2,1)S(1)}, u32[]{:S(2)}, u32[]{:S(2)}) async-start(bf16[8,1,128,256]{3,2,1,0:T(8,128)(2,1)} %shard_map.40), calls=%async_computation.1 | async-start | bytes 1048576 | tf_op jit(solution)/shard_map/all_to_all | solution.py:458
  49.0 6.5 %collective-permute-start.4 = (bf16[2,1,128,256]{3,2,1,0:T(8,128)(2,1)S(1)}, bf16[2,1,128,256]{3,2,1,0:T(8,128)(2,1)S(1)}, u32[]{:S(2)}, u32[]{:S(2)}) collective-permute-start(bf16[2,1,128,256]{3,2,1,0:T(8,128)(2,1)S(1)} %pad_maximum_fusion), channel_id=1, source_target_pairs={{0,2},{2,0},{4,6},{6,4},{8,10},{10,8},{12,14},{14,12},{1,3},{3,1},... | collective-permute-start | bytes 393224 | tf_op jit(solution)/shard_map/ppermute | solution.py:452
  51.1 11.1 %collective-permute-start.3 = (bf16[1,1,128,256]{3,2,1,0:T(8,128)(2,1)S(1)}, bf16[1,1,128,256]{3,2,1,0:T(8,128)(2,1)S(1)}, u32[]{:S(2)}, u32[]{:S(2)}) collective-permute-start(bf16[1,1,128,256]{3,2,1,0:T(8,128)(2,1)S(1)} %slice_bitcast_fusion.6), channel_id=1, source_target_pairs={{0,8},{2,10},{4,12},{6,14},{8,0},{10,2},{12,4},{14,6},{1,9},{3,11}... | collective-permute-start | bytes 196616 | tf_op jit(solution)/shard_map/ppermute | solution.py:452
  55.5 9.4 %collective-permute-start.5 = (bf16[4,1,128,256]{3,2,1,0:T(8,128)(2,1)S(1)}, bf16[4,1,128,256]{3,2,1,0:T(8,128)(2,1)S(1)}, u32[]{:S(2)}, u32[]{:S(2)}) collective-permute-start(bf16[4,1,128,256]{3,2,1,0:T(8,128)(2,1)S(1)} %constant_dynamic-update-slice_fusion.refs_3_), channel_id=1, source_target_pairs={{0,4},{2,6},{4,0},{6,2},{8,12},{10,14},{12,8},{14,10},{1,5},{3,7},... | collective-permute-start | bytes 786440 | tf_op jit(solution)/shard_map/ppermute | solution.py:452
  66.7 4.2 %collective-permute-start.6 = (f32[16,128,256]{2,1,0:T(8,128)S(1)}, f32[16,128,256]{2,1,0:T(8,128)S(1)}, u32[]{:S(2)}, u32[]{:S(2)}) collective-permute-start(f32[16,128,256]{2,1,0:T(8,128)S(1)} %shard_map.41.own.mine_hbm), channel_id=1, source_target_pairs={{0,1},{1,0},{2,3},{3,2},{4,5},{5,4},{6,7},{7,6},{8,9},{9,8},{10,11... | collective-permute-start | bytes 6291464 | tf_op jit(solution)/shard_map/ppermute | solution.py:455
  72.9 4.4 %collective-permute-start.7 = (f32[136,128]{1,0:T(8,128)S(1)}, f32[136,128]{1,0:T(8,128)S(1)}, u32[]{:S(2)}, u32[]{:S(2)}) collective-permute-start(f32[136,128]{1,0:T(8,128)S(1)} %shard_map.43), channel_id=1, source_target_pairs={{0,2},{2,0},{4,6},{6,4},{8,10},{10,8},{12,14},{14,12},{1,3},{3,1},... | collective-permute-start | bytes 208904 | tf_op jit(solution)/shard_map/ppermute | solution.py:452
  77.3 4.4 %collective-permute-start.8 = (f32[136,128]{1,0:T(8,128)S(1)}, f32[136,128]{1,0:T(8,128)S(1)}, u32[]{:S(2)}, u32[]{:S(2)}) collective-permute-start(f32[136,128]{1,0:T(8,128)S(1)} %add.60), channel_id=1, source_target_pairs={{0,4},{2,6},{4,0},{6,2},{8,12},{10,14},{12,8},{14,10},{1,5},{3,7},... | collective-permute-start | bytes 208904 | tf_op jit(solution)/shard_map/ppermute | solution.py:452
  81.7 5.3 %collective-permute-start.9 = (f32[136,128]{1,0:T(8,128)S(1)}, f32[136,128]{1,0:T(8,128)S(1)}, u32[]{:S(2)}, u32[]{:S(2)}) collective-permute-start(f32[136,128]{1,0:T(8,128)S(1)} %add.61), channel_id=1, source_target_pairs={{0,8},{2,10},{4,12},{6,14},{8,0},{10,2},{12,4},{14,6},{1,9},{3,11}... | collective-permute-start | bytes 208904 | tf_op jit(solution)/shard_map/ppermute | solution.py:452
  87.0 1.3 collective-permute-start.10
  102.3 9.8 %collective-permute-start.11 = (bf16[4,1,128,256]{3,2,1,0:T(8,128)(2,1)S(1)}, bf16[4,1,128,256]{3,2,1,0:T(8,128)(2,1)S(1)}, u32[]{:S(2)}, u32[]{:S(2)}) collective-permute-start(bf16[4,1,128,256]{3,2,1,0:T(8,128)(2,1)S(1)} %get-tuple-element.33), channel_id=1, source_target_pairs={{0,4},{2,6},{4,0},{6,2},{8,12},{10,14},{12,8},{14,10},{1,5},{3,7},... | collective-permute-start | bytes 786440 | tf_op jit(solution)/shard_map/ppermute | solution.py:452
  103.6 7.3 %collective-permute-start.12 = (bf16[1,1,128,256]{3,2,1,0:T(8,128)(2,1)S(1)}, bf16[1,1,128,256]{3,2,1,0:T(8,128)(2,1)S(1)}, u32[]{:S(2)}, u32[]{:S(2)}) collective-permute-start(bf16[1,1,128,256]{3,2,1,0:T(8,128)(2,1)S(1)} %get-tuple-element.34), channel_id=1, source_target_pairs={{0,8},{2,10},{4,12},{6,14},{8,0},{10,2},{12,4},{14,6},{1,9},{3,11}... | collective-permute-start | bytes 196616 | tf_op jit(solution)/shard_map/ppermute | solution.py:452
  112.1 35.7 %all-to-all-start.3 = ((bf16[8,2,128,256]{3,2,1,0:T(8,128)(2,1)}), bf16[8,2,128,256]{3,2,1,0:T(8,128)(2,1)S(1)}, u32[]{:S(2)}, u32[]{:S(2)}) async-start(bf16[8,2,128,256]{3,2,1,0:T(8,128)(2,1)} %shard_map.45), calls=%async_computation.3 | async-start | bytes 2097152 | tf_op jit(solution)/shard_map/all_to_all | solution.py:458
  117.3 14.8 %collective-permute-start.13 = (bf16[2,1,128,256]{3,2,0,1:T(8,128)(2,1)S(1)}, bf16[2,1,128,256]{3,2,0,1:T(8,128)(2,1)S(1)}, u32[]{:S(2)}, u32[]{:S(2)}) collective-permute-start(bf16[2,1,128,256]{3,2,0,1:T(8,128)(2,1)S(1)} %slice_bitcast_fusion), channel_id=1, source_target_pairs={{0,2},{2,0},{4,6},{6,4},{8,10},{10,8},{12,14},{14,12},{1,3},{3,1},... | collective-permute-start | bytes 393224 | tf_op jit(solution)/shard_map/ppermute | solution.py:452
  119.4 15.1 %collective-permute-start.15 = (bf16[2,1,128,256]{3,2,1,0:T(8,128)(2,1)S(1)}, bf16[2,1,128,256]{3,2,1,0:T(8,128)(2,1)S(1)}, u32[]{:S(2)}, u32[]{:S(2)}) collective-permute-start(bf16[2,1,128,256]{3,2,1,0:T(8,128)(2,1)S(1)} %pad_maximum_fusion.1), channel_id=1, source_target_pairs={{0,2},{2,0},{4,6},{6,4},{8,10},{10,8},{12,14},{14,12},{1,3},{3,1},... | collective-permute-start | bytes 393224 | tf_op jit(solution)/shard_map/ppermute | solution.py:452
  132.2 13.4 %collective-permute-start.14 = (bf16[1,1,128,256]{3,2,1,0:T(8,128)(2,1)S(1)}, bf16[1,1,128,256]{3,2,1,0:T(8,128)(2,1)S(1)}, u32[]{:S(2)}, u32[]{:S(2)}) collective-permute-start(bf16[1,1,128,256]{3,2,1,0:T(8,128)(2,1)S(1)} %slice_bitcast_fusion.4), channel_id=1, source_target_pairs={{0,8},{2,10},{4,12},{6,14},{8,0},{10,2},{12,4},{14,6},{1,9},{3,11}... | collective-permute-start | bytes 196616 | tf_op jit(solution)/shard_map/ppermute | solution.py:452
  134.4 13.4 %collective-permute-start.16 = (bf16[4,1,128,256]{3,2,1,0:T(8,128)(2,1)S(1)}, bf16[4,1,128,256]{3,2,1,0:T(8,128)(2,1)S(1)}, u32[]{:S(2)}, u32[]{:S(2)}) collective-permute-start(bf16[4,1,128,256]{3,2,1,0:T(8,128)(2,1)S(1)} %constant_dynamic-update-slice_fusion.3.refs_2_), channel_id=1, source_target_pairs={{0,4},{2,6},{4,0},{6,2},{8,12},{10,14},{12,8},{14,10},{1,5},{3,7},... | collective-permute-start | bytes 786440 | tf_op jit(solution)/shard_map/ppermute | solution.py:452
  149.1 4.2 %collective-permute-start.17 = (f32[16,128,256]{2,1,0:T(8,128)S(1)}, f32[16,128,256]{2,1,0:T(8,128)S(1)}, u32[]{:S(2)}, u32[]{:S(2)}) collective-permute-start(f32[16,128,256]{2,1,0:T(8,128)S(1)} %shard_map.46.own.mine_hbm), channel_id=1, source_target_pairs={{0,1},{1,0},{2,3},{3,2},{4,5},{5,4},{6,7},{7,6},{8,9},{9,8},{10,11... | collective-permute-start | bytes 6291464 | tf_op jit(solution)/shard_map/ppermute | solution.py:455
  155.4 4.4 %collective-permute-start.18 = (f32[136,128]{1,0:T(8,128)S(1)}, f32[136,128]{1,0:T(8,128)S(1)}, u32[]{:S(2)}, u32[]{:S(2)}) collective-permute-start(f32[136,128]{1,0:T(8,128)S(1)} %shard_map.48), channel_id=1, source_target_pairs={{0,2},{2,0},{4,6},{6,4},{8,10},{10,8},{12,14},{14,12},{1,3},{3,1},... | collective-permute-start | bytes 208904 | tf_op jit(solution)/shard_map/ppermute | solution.py:452
  159.8 4.4 %collective-permute-start.19 = (f32[136,128]{1,0:T(8,128)S(1)}, f32[136,128]{1,0:T(8,128)S(1)}, u32[]{:S(2)}, u32[]{:S(2)}) collective-permute-start(f32[136,128]{1,0:T(8,128)S(1)} %add.63), channel_id=1, source_target_pairs={{0,4},{2,6},{4,0},{6,2},{8,12},{10,14},{12,8},{14,10},{1,5},{3,7},... | collective-permute-start | bytes 208904 | tf_op jit(solution)/shard_map/ppermute | solution.py:452
  164.2 5.3 %collective-permute-start.20 = (f32[136,128]{1,0:T(8,128)S(1)}, f32[136,128]{1,0:T(8,128)S(1)}, u32[]{:S(2)}, u32[]{:S(2)}) collective-permute-start(f32[136,128]{1,0:T(8,128)S(1)} %add.64), channel_id=1, source_target_pairs={{0,8},{2,10},{4,12},{6,14},{8,0},{10,2},{12,4},{14,6},{1,9},{3,11}... | collective-permute-start | bytes 208904 | tf_op jit(solution)/shard_map/ppermute | solution.py:452
  169.5 1.3 collective-permute-start.21

commit v9 on v7

--- a/solution.py
+++ b/solution.py
@@ -64,11 +64,13 @@
 def sums_kernel(counts_ref, sums_ref):
     nnz, rows, cols = counts_ref.shape
     ones = jnp.ones((8, cols), bf16)
-    sums_ref[...] = jnp.zeros(sums_ref.shape, f32)
+    sums_ref[0] = jnp.zeros(sums_ref.shape[1:], f32)
     for s in range(nnz):
         block = counts_ref[s].astype(bf16)
         sums_ref[0, pl.ds(s, 1), :] = contract(ones, block, 1, 1)[0:1, :]
         sums_ref[0, pl.ds(nnz + s, 1), :] = contract(ones, block, 1, 0)[0:1, :]
+    for r in range(1, sums_ref.shape[0]):
+        sums_ref[r] = sums_ref[0]
 
 
 def gather_hot(t, tab, blocks, near, far):
@@ -120,10 +122,8 @@
 
 
 def make_ppmi_kernel(t):
-    def kernel(tab, match_ref, counts_ref, turned, sums_a, sums_b, ppmi_ref, hot, cols_log):
-        sums = jnp.concatenate(
-            [ref[r] for ref in (sums_a, sums_b) for r in range(t.groups // 2)], axis=0
-        )
+    def kernel(tab, match_ref, counts_ref, turned, sums_ref, ppmi_ref, hot, cols_log):
+        sums = jnp.concatenate([sums_ref[r] for r in range(t.groups)], axis=0)
         high = jnp.floor(sums * (1.0 / 256.0))
         low = sums - high * 256.0
         match = match_ref[...]
@@ -487,7 +487,8 @@
     ppmi_shape = shape((nnz, rows, rows), bf16)
     result_shape = shape((blocks, half, rows), f32)
 
-    sums = call(sums_kernel, shape((1, depth, rows), f32), [VMEM], vmem=8)(counts)
+    sums = call(sums_kernel, shape((groups, depth, rows), f32), [VMEM], vmem=8)(counts)
+    sums_all = exchange(sums)
     tab, towards = t.build(block_pairs, me, my_col)
     turned, send_x, near, far = call(
         make_source_kernel(t),
@@ -500,19 +501,18 @@
     col_ids = block_pairs[:, :, 2] * groups + block_pairs[:, :, 1]
     no_id = jnp.full((groups, depth - 2 * nnz), -1, i32)
     ids = jnp.concatenate([row_ids, col_ids, no_id], axis=1)
-    sums_a, sums_b, order = spread(sums, t.bits[::-1])
-    ids = jnp.take(ids, me ^ jnp.array(order), axis=0)
-    my_ids = ids[0]
+    my_ids = lax.dynamic_index_in_dim(ids, me, 0, keepdims=False)
     match = (my_ids[:, None] == ids.reshape(-1)[None, :]).astype(bf16)
 
+    send_x, sums_all = lax.optimization_barrier((send_x, sums_all))
     got_x, x_step = exchange(send_x), peer(far, t.steps[0])
     ppmi, hot_t = call(
         make_ppmi_kernel(t),
         [ppmi_shape, hot_shape],
-        [SMEM] + [VMEM] * 5,
+        [SMEM] + [VMEM] * 4,
         scratch=[pltpu.VMEM((depth, rows), f32)],
         vmem=12,
-    )(tab, match, counts, turned, sums_a, sums_b)
+    )(tab, match, counts, turned, sums_all)
 
     def finish(source, got_x, near, far, x_step, hot_t):
         t_step = peer(hot_t, t.steps[-1])
@@ -522,7 +522,10 @@
         send = call(
             make_main_kernel(t, merged), send_shape(1 + merged), [SMEM, VMEM, VMEM], vmem=8
         )(tab, source, ppmi)
-        send, t_step = lax.optimization_barrier((send, t_step))
+        if merged:
+            send, x_step, t_step = lax.optimization_barrier((send, x_step, t_step))
+        else:
+            send, t_step = lax.optimization_barrier((send, t_step))
         got = [exchange(send)] + ([] if merged else [got_x])
         hot_x = scatter_hot(near, far, x_step, towards)
         hot_a, hot_b, order = spread(hot_t, t.steps[::-1], t_step)

time: 203 us -> 184 us (0.906)
  waiting for transfers between devices: 90.2 us -> 69.6 us
  starting transfers between devices: 50 us -> 54.4 us
  local copies, waits for them, and re-layouts: 11.5 us -> 8.21 us
    ppermute x21 -> x18, waiting for transfers between devices: 82.1 us -> 61.4 us  [peer(): return lax.ppermute(x, 'row', [(r, r ^ k) for r in range(groups)])]
    all_to_all x3 -> x4, starting transfers between devices: 14.1 us -> 22.4 us  [exchange(): return lax.all_to_all(x, 'row', split_axis=0, concat_axis=0, tiled=True)]
    ppermute x21 -> x18, starting transfers between devices: 35.6 us -> 31.8 us  [peer(): return lax.ppermute(x, 'row', [(r, r ^ k) for r in range(groups)])]
    unnamed x39 -> x29, local copies, waits for them, and re-layouts: 8.93 us -> 6.09 us
  transfers between devices with their start and end apart: 28 -> 26, of which waited for: 20 -> 21; matrix products, arithmetic and copies ran while one was open for 3% -> 3% of each run, Pallas kernels for 5% -> 6%
where the time goes in v9:
time: 184 us
  waiting for transfers between devices  69.6 us (38%)
  starting transfers between devices  54.4 us (30%)
  Pallas kernels  47.4 us (26%)
  local copies, waits for them, and re-layouts  8.21 us (4%)
  other arithmetic  3.63 us (2%)
    ppermute x18, waiting for transfers between devices, peer(): return lax.ppermute(x, 'row', [(r, r ^ k) for r in range(groups)])  61.4 us
    ppermute x18, starting transfers between devices, peer(): return lax.ppermute(x, 'row', [(r, r ^ k) for r in range(groups)])  31.8 us
    all_to_all x4, starting transfers between devices, exchange(): return lax.all_to_all(x, 'row', split_axis=0, concat_axis=0, tiled=True)  22.4 us
    pallas_call x1, Pallas kernels, body(): call(make_final_kernel(t, 1.0 / vocab), shape((blocks, rows, half), f32),...  15.2 us
    pallas_call x1, Pallas kernels, body(): call(make_second_kernel(t, 1.0 / vocab), [shape((blocks, half, rows), bf1...  13.9 us
    ppermute x4, waiting for transfers between devices, swap(): return lax.ppermute(x, 'col', [(0, 1), (1, 0)])  8.11 us
    unnamed x29, local copies, waits for them, and re-layouts  6.09 us
    pallas_call x2, Pallas kernels, finish(): call(make_cross_gram_kernel(t), shape((half + 8, half), f32), [SMEM] + [V...  4.02 us
  transfers between devices with their start and end apart: 26, of which 21 were waited for; matrix products, arithmetic and copies ran while one was open for 3% of the time, Pallas kernels for 6%

profile of v9, /device:TPU:0, one launch (start us, length us, event | category | flops | bytes accessed | tf_op | source)
XLA Modules:
  0.0 183.8 jit_solution(9744573255372849365)
XLA Ops:
  0.0 1.7 copy-done
  3.0 7.4 %all-to-all-start = ((f32[8,24,256]{2,1,0:T(8,128)}), f32[8,24,256]{2,1,0:T(8,128)}, u32[]{:S(2)}, u32[]{:S(2)}) async-start(f32[8,24,256]{2,1,0:T(8,128)} %copy-done.5), calls=%async_computation | async-start | bytes 393216 | tf_op jit(solution)/shard_map/all_to_all | solution.py:448
  11.5 2.5 %shard_map.37 = (bf16[16,128,256]{2,1,0:T(8,128)(2,1)S(1)}, bf16[8,1,128,256]{3,2,1,0:T(8,128)(2,1)S(1)}, bf16[4,1,128,256]{3,2,1,0:T(8,128)(2,1)S(1)}, bf16[4,1,128,256]{3,2,1,0:T(8,128)(2,1)}) custom-call(s32[35]{0:T(128)S(1)} %concatenate.20.tab, bf16[16,256,128]{2,1,0:T(8,128)(2,1)S(1)} %copy-done.4), custom_call_target="tpu_custom_call" | custom-call | bytes 4194304 | tf_op jit(solution)/shard_map/pallas_call | solution.py:493
  16.5 2.0 %collective-permute-start.1 = (bf16[4,1,128,256]{3,2,1,0:T(8,128)(2,1)}, bf16[4,1,128,256]{3,2,1,0:T(8,128)(2,1)S(1)}, u32[]{:S(2)}, u32[]{:S(2)}) collective-permute-start(bf16[4,1,128,256]{3,2,1,0:T(8,128)(2,1)} %get-tuple-element.30), channel_id=1, source_target_pairs={{0,4},{2,6},{4,0},{6,2},{8,12},{10,14},{12,8},{14,10},{1,5},{3,7},... | collective-permute-start | bytes 786440 | tf_op jit(solution)/shard_map/ppermute | solution.py:442
  18.9 4.6 %all-to-all-start.2 = ((bf16[8,1,128,256]{3,2,1,0:T(8,128)(2,1)}), bf16[8,1,128,256]{3,2,1,0:T(8,128)(2,1)}, u32[]{:S(2)}, u32[]{:S(2)}) async-start(bf16[8,1,128,256]{3,2,1,0:T(8,128)(2,1)} %copy-done.6), calls=%async_computation.2 | async-start | bytes 1048576 | tf_op jit(solution)/shard_map/all_to_all | solution.py:448
  26.4 1.6 collective-permute-start.2
  29.3 1.9 %shard_map.39 = (bf16[9,256,256]{2,1,0:T(8,128)(2,1)S(1)}, bf16[1,1,128,256]{3,2,1,0:T(8,128)(2,1)S(1)}) custom-call(s32[35]{0:T(128)S(1)} %concatenate.20.tab, bf16[24,192]{1,0:T(8,128)(2,1)S(1)} %compare_convert_fusion.match_ref, s32[9,256,256]{2,1,0:T(8,128)S(1)} %copy-done.1, bf16[16,128,256]{2,1,0:T(8,128)(2,1)S(1)} %copy-done.3, ...), custom_call_target="tpu_custom_call" | custom-call | bytes 4194304 | tf_op jit(solution)/shard_map/pallas_call | solution.py:509
  31.3 1.6 shard_map.40
  32.9 3.3 %collective-permute-start = (bf16[1,1,128,256]{3,2,1,0:T(8,128)(2,1)S(1)}, bf16[1,1,128,256]{3,2,1,0:T(8,128)(2,1)S(1)}, u32[]{:S(2)}, u32[]{:S(2)}) collective-permute-start(bf16[1,1,128,256]{3,2,1,0:T(8,128)(2,1)S(1)} %get-tuple-element.26), channel_id=1, source_target_pairs={{0,8},{2,10},{4,12},{6,14},{8,0},{10,2},{12,4},{14,6},{1,9},{3,11}... | collective-permute-start | bytes 196616 | tf_op jit(solution)/shard_map/ppermute | solution.py:442
  36.2 3.1 %collective-permute-done = bf16[1,1,128,256]{3,2,1,0:T(8,128)(2,1)S(1)} collective-permute-done((bf16[1,1,128,256]{3,2,1,0:T(8,128)(2,1)S(1)}, bf16[1,1,128,256]{3,2,1,0:T(8,128)(2,1)S(1)}, u32[]{:S(2)}, u32[]{:S(2)}) %collective-permute-start) | collective-permute-done | bytes 65568 | tf_op jit(solution)/shard_map/ppermute | solution.py:442
  39.3 5.4 %all-to-all-start.1 = ((bf16[8,1,128,256]{3,2,1,0:T(8,128)(2,1)}), bf16[8,1,128,256]{3,2,1,0:T(8,128)(2,1)S(1)}, u32[]{:S(2)}, u32[]{:S(2)}) async-start(bf16[8,1,128,256]{3,2,1,0:T(8,128)(2,1)} %shard_map.40), calls=%async_computation.1 | async-start | bytes 1048576 | tf_op jit(solution)/shard_map/all_to_all | solution.py:448
  46.5 2.1 %collective-permute-start.4 = (bf16[2,1,128,256]{3,2,1,0:T(8,128)(2,1)S(1)}, bf16[2,1,128,256]{3,2,1,0:T(8,128)(2,1)S(1)}, u32[]{:S(2)}, u32[]{:S(2)}) collective-permute-start(bf16[2,1,128,256]{3,2,1,0:T(8,128)(2,1)S(1)} %pad_maximum_fusion), channel_id=1, source_target_pairs={{0,2},{2,0},{4,6},{6,4},{8,10},{10,8},{12,14},{14,12},{1,3},{3,1},... | collective-permute-start | bytes 393224 | tf_op jit(solution)/shard_map/ppermute | solution.py:442
  48.6 2.4 %collective-permute-start.3 = (bf16[1,1,128,256]{3,2,1,0:T(8,128)(2,1)S(1)}, bf16[1,1,128,256]{3,2,1,0:T(8,128)(2,1)S(1)}, u32[]{:S(2)}, u32[]{:S(2)}) collective-permute-start(bf16[1,1,128,256]{3,2,1,0:T(8,128)(2,1)S(1)} %slice_bitcast_fusion.6), channel_id=1, source_target_pairs={{0,8},{2,10},{4,12},{6,14},{8,0},{10,2},{12,4},{14,6},{1,9},{3,11}... | collective-permute-start | bytes 196616 | tf_op jit(solution)/shard_map/ppermute | solution.py:442
  51.0 2.1 %collective-permute-done.4 = bf16[2,1,128,256]{3,2,1,0:T(8,128)(2,1)S(1)} collective-permute-done((bf16[2,1,128,256]{3,2,1,0:T(8,128)(2,1)S(1)}, bf16[2,1,128,256]{3,2,1,0:T(8,128)(2,1)S(1)}, u32[]{:S(2)}, u32[]{:S(2)}) %collective-permute-start.4) | collective-permute-done | bytes 131104 | tf_op jit(solution)/shard_map/ppermute | solution.py:442
  53.1 2.1 %collective-permute-start.5 = (bf16[4,1,128,256]{3,2,1,0:T(8,128)(2,1)S(1)}, bf16[4,1,128,256]{3,2,1,0:T(8,128)(2,1)S(1)}, u32[]{:S(2)}, u32[]{:S(2)}) collective-permute-start(bf16[4,1,128,256]{3,2,1,0:T(8,128)(2,1)S(1)} %constant_dynamic-update-slice_fusion.refs_3_), channel_id=1, source_target_pairs={{0,4},{2,6},{4,0},{6,2},{8,12},{10,14},{12,8},{14,10},{1,5},{3,7},... | collective-permute-start | bytes 786440 | tf_op jit(solution)/shard_map/ppermute | solution.py:442
  55.3 4.4 %collective-permute-done.3 = bf16[1,1,128,256]{3,2,1,0:T(8,128)(2,1)S(1)} collective-permute-done((bf16[1,1,128,256]{3,2,1,0:T(8,128)(2,1)S(1)}, bf16[1,1,128,256]{3,2,1,0:T(8,128)(2,1)S(1)}, u32[]{:S(2)}, u32[]{:S(2)}) %collective-permute-start.3) | collective-permute-done | bytes 65568 | tf_op jit(solution)/shard_map/ppermute | solution.py:442
  59.8 2.7 %collective-permute-done.5.refs_4_ = bf16[4,1,128,256]{3,2,1,0:T(8,128)(2,1)S(1)} collective-permute-done((bf16[4,1,128,256]{3,2,1,0:T(8,128)(2,1)S(1)}, bf16[4,1,128,256]{3,2,1,0:T(8,128)(2,1)S(1)}, u32[]{:S(2)}, u32[]{:S(2)}) %collective-permute-start.5) | collective-permute-done | bytes 262176 | tf_op jit(solution)/shard_map/ppermute | solution.py:442
  62.5 1.8 shard_map.41.own.mine_hbm
  64.3 1.3 shard_map.42.square
  65.7 2.8 %collective-permute-done.6.other.other_hbm = f32[16,128,256]{2,1,0:T(8,128)S(1)} collective-permute-done((f32[16,128,256]{2,1,0:T(8,128)S(1)}, f32[16,128,256]{2,1,0:T(8,128)S(1)}, u32[]{:S(2)}, u32[]{:S(2)}) %collective-permute-start.6) | collective-permute-done | bytes 2097184 | tf_op jit(solution)/shard_map/ppermute | solution.py:445
  68.5 2.0 %shard_map.43 = f32[136,128]{1,0:T(8,128)S(1)} custom-call(s32[35]{0:T(128)S(1)} %concatenate.20.tab, f32[16,128,256]{2,1,0:T(8,128)S(1)} %shard_map.41.own.mine_hbm, f32[16,128,256]{2,1,0:T(8,128)S(1)} %collective-permute-done.6.other.other_hbm, f32[128,128]{1,0:T(8,128)S(1)} %shard_map.42.square), custom_call_target="tpu_custom_call" | custom-call | bytes 4194304 | tf_op jit(solution)/shard_map/pallas_call | solution.py:540
  70.5 1.5 collective-permute-start.7
  72.0 2.8 %collective-permute-done.7 = f32[136,128]{1,0:T(8,128)S(1)} collective-permute-done((f32[136,128]{1,0:T(8,128)S(1)}, f32[136,128]{1,0:T(8,128)S(1)}, u32[]{:S(2)}, u32[]{:S(2)}) %collective-permute-start.7) | collective-permute-done | bytes 69664 | tf_op jit(solution)/shard_map/ppermute | solution.py:442
  74.9 4.3 %collective-permute-done.8 = f32[136,128]{1,0:T(8,128)S(1)} collective-permute-done((f32[136,128]{1,0:T(8,128)S(1)}, f32[136,128]{1,0:T(8,128)S(1)}, u32[]{:S(2)}, u32[]{:S(2)}) %collective-permute-start.8) | collective-permute-done | bytes 69664 | tf_op jit(solution)/shard_map/ppermute | solution.py:442
  79.2 2.2 %collective-permute-start.9 = (f32[136,128]{1,0:T(8,128)S(1)}, f32[136,128]{1,0:T(8,128)S(1)}, u32[]{:S(2)}, u32[]{:S(2)}) collective-permute-start(f32[136,128]{1,0:T(8,128)S(1)} %add.61), channel_id=1, source_target_pairs={{0,8},{2,10},{4,12},{6,14},{8,0},{10,2},{12,4},{14,6},{1,9},{3,11}... | collective-permute-start | bytes 208904 | tf_op jit(solution)/shard_map/ppermute | solution.py:442
  81.5 3.1 %collective-permute-done.9 = f32[136,128]{1,0:T(8,128)S(1)} collective-permute-done((f32[136,128]{1,0:T(8,128)S(1)}, f32[136,128]{1,0:T(8,128)S(1)}, u32[]{:S(2)}, u32[]{:S(2)}) %collective-permute-start.9) | collective-permute-done | bytes 69664 | tf_op jit(solution)/shard_map/ppermute | solution.py:442
  84.6 1.2 collective-permute-done.10.other_g
  85.9 13.9 %shard_map.44 = (bf16[16,128,256]{2,1,0:T(8,128)(2,1)S(1)}, bf16[4,1,128,256]{3,2,1,0:T(8,128)(2,1)S(1)}, bf16[4,1,128,256]{3,2,1,0:T(8,128)(2,1)S(1)}, bf16[1,1,128,256]{3,2,1,0:T(8,128)(2,1)S(1)}) custom-call(s32[35]{0:T(128)S(1)} %concatenate.20.tab, f32[136,128]{1,0:T(8,128)S(1)} %add.62.own_g, f32[136,128]{1,0:T(8,128)S(1)} %collective-permute-done.10.other_g, ...), custom_call_target="tpu_custom_call" | custom-call | bytes 4194304 | tf_op jit(solution)/shard_map/pallas_call | solution.py:557
  99.8 1.4 collective-permute-start.11
  101.2 3.1 %collective-permute-start.12 = (bf16[1,1,128,256]{3,2,1,0:T(8,128)(2,1)S(1)}, bf16[1,1,128,256]{3,2,1,0:T(8,128)(2,1)S(1)}, u32[]{:S(2)}, u32[]{:S(2)}) collective-permute-start(bf16[1,1,128,256]{3,2,1,0:T(8,128)(2,1)S(1)} %get-tuple-element.34), channel_id=1, source_target_pairs={{0,8},{2,10},{4,12},{6,14},{8,0},{10,2},{12,4},{14,6},{1,9},{3,11}... | collective-permute-start | bytes 196616 | tf_op jit(solution)/shard_map/ppermute | solution.py:442
  104.3 1.8 shard_map.45
  106.1 2.4 %collective-permute-done.12 = bf16[1,1,128,256]{3,2,1,0:T(8,128)(2,1)S(1)} collective-permute-done((bf16[1,1,128,256]{3,2,1,0:T(8,128)(2,1)S(1)}, bf16[1,1,128,256]{3,2,1,0:T(8,128)(2,1)S(1)}, u32[]{:S(2)}, u32[]{:S(2)}) %collective-permute-start.12) | collective-permute-done | bytes 65568 | tf_op jit(solution)/shard_map/ppermute | solution.py:442
  109.7 5.1 %all-to-all-start.3 = ((bf16[8,2,128,256]{3,2,1,0:T(8,128)(2,1)}), bf16[8,2,128,256]{3,2,1,0:T(8,128)(2,1)S(1)}, u32[]{:S(2)}, u32[]{:S(2)}) async-start(bf16[8,2,128,256]{3,2,1,0:T(8,128)(2,1)} %shard_map.45), calls=%async_computation.3 | async-start | bytes 2097152 | tf_op jit(solution)/shard_map/all_to_all | solution.py:448
  114.9 2.1 %collective-permute-start.13 = (bf16[2,1,128,256]{3,2,0,1:T(8,128)(2,1)S(1)}, bf16[2,1,128,256]{3,2,0,1:T(8,128)(2,1)S(1)}, u32[]{:S(2)}, u32[]{:S(2)}) collective-permute-start(bf16[2,1,128,256]{3,2,0,1:T(8,128)(2,1)S(1)} %slice_bitcast_fusion), channel_id=1, source_target_pairs={{0,2},{2,0},{4,6},{6,4},{8,10},{10,8},{12,14},{14,12},{1,3},{3,1},... | collective-permute-start | bytes 393224 | tf_op jit(solution)/shard_map/ppermute | solution.py:442
  117.1 12.6 %collective-permute-done.13 = bf16[2,1,128,256]{3,2,0,1:T(8,128)(2,1)S(1)} collective-permute-done((bf16[2,1,128,256]{3,2,0,1:T(8,128)(2,1)S(1)}, bf16[2,1,128,256]{3,2,0,1:T(8,128)(2,1)S(1)}, u32[]{:S(2)}, u32[]{:S(2)}) %collective-permute-start.13) | collective-permute-done | bytes 131104 | tf_op jit(solution)/shard_map/ppermute | solution.py:442
  129.8 1.5 collective-permute-start.14
  132.0 4.1 %collective-permute-start.16 = (bf16[4,1,128,256]{3,2,1,0:T(8,128)(2,1)S(1)}, bf16[4,1,128,256]{3,2,1,0:T(8,128)(2,1)S(1)}, u32[]{:S(2)}, u32[]{:S(2)}) collective-permute-start(bf16[4,1,128,256]{3,2,1,0:T(8,128)(2,1)S(1)} %constant_dynamic-update-slice_fusion.3.refs_2_), channel_id=1, source_target_pairs={{0,4},{2,6},{4,0},{6,2},{8,12},{10,14},{12,8},{14,10},{1,5},{3,7},... | collective-permute-start | bytes 786440 | tf_op jit(solution)/shard_map/ppermute | solution.py:442
  136.1 7.0 %collective-permute-done.14 = bf16[1,1,128,256]{3,2,1,0:T(8,128)(2,1)S(1)} collective-permute-done((bf16[1,1,128,256]{3,2,1,0:T(8,128)(2,1)S(1)}, bf16[1,1,128,256]{3,2,1,0:T(8,128)(2,1)S(1)}, u32[]{:S(2)}, u32[]{:S(2)}) %collective-permute-start.14) | collective-permute-done | bytes 65568 | tf_op jit(solution)/shard_map/ppermute | solution.py:442
  143.1 2.3 %collective-permute-done.16.refs_3_ = bf16[4,1,128,256]{3,2,1,0:T(8,128)(2,1)S(1)} collective-permute-done((bf16[4,1,128,256]{3,2,1,0:T(8,128)(2,1)S(1)}, bf16[4,1,128,256]{3,2,1,0:T(8,128)(2,1)S(1)}, u32[]{:S(2)}, u32[]{:S(2)}) %collective-permute-start.16) | collective-permute-done | bytes 262176 | tf_op jit(solution)/shard_map/ppermute | solution.py:442
  145.5 1.3 shard_map.46.own.mine_hbm
  146.8 1.3 shard_map.47.square
  148.2 2.8 %collective-permute-done.17.other.other_hbm = f32[16,128,256]{2,1,0:T(8,128)S(1)} collective-permute-done((f32[16,128,256]{2,1,0:T(8,128)S(1)}, f32[16,128,256]{2,1,0:T(8,128)S(1)}, u32[]{:S(2)}, u32[]{:S(2)}) %collective-permute-start.17) | collective-permute-done | bytes 2097184 | tf_op jit(solution)/shard_map/ppermute | solution.py:445
  151.0 2.0 %shard_map.48 = f32[136,128]{1,0:T(8,128)S(1)} custom-call(s32[35]{0:T(128)S(1)} %concatenate.20.tab, f32[16,128,256]{2,1,0:T(8,128)S(1)} %shard_map.46.own.mine_hbm, f32[16,128,256]{2,1,0:T(8,128)S(1)} %collective-permute-done.17.other.other_hbm, f32[128,128]{1,0:T(8,128)S(1)} %shard_map.47.square), custom_call_target="tpu_custom_call" | custom-call | bytes 4194304 | tf_op jit(solution)/shard_map/pallas_call | solution.py:540
  153.1 4.3 %collective-permute-done.18 = f32[136,128]{1,0:T(8,128)S(1)} collective-permute-done((f32[136,128]{1,0:T(8,128)S(1)}, f32[136,128]{1,0:T(8,128)S(1)}, u32[]{:S(2)}, u32[]{:S(2)}) %collective-permute-start.18) | collective-permute-done | bytes 69664 | tf_op jit(solution)/shard_map/ppermute | solution.py:442
  157.5 4.3 %collective-permute-done.19 = f32[136,128]{1,0:T(8,128)S(1)} collective-permute-done((f32[136,128]{1,0:T(8,128)S(1)}, f32[136,128]{1,0:T(8,128)S(1)}, u32[]{:S(2)}, u32[]{:S(2)}) %collective-permute-start.19) | collective-permute-done | bytes 69664 | tf_op jit(solution)/shard_map/ppermute | solution.py:442
  161.8 2.3 %collective-permute-start.20 = (f32[136,128]{1,0:T(8,128)S(1)}, f32[136,128]{1,0:T(8,128)S(1)}, u32[]{:S(2)}, u32[]{:S(2)}) collective-permute-start(f32[136,128]{1,0:T(8,128)S(1)} %add.64), channel_id=1, source_target_pairs={{0,8},{2,10},{4,12},{6,14},{8,0},{10,2},{12,4},{14,6},{1,9},{3,11}... | collective-permute-start | bytes 208904 | tf_op jit(solution)/shard_map/ppermute | solution.py:442
  164.0 3.0 %collective-permute-done.20 = f32[136,128]{1,0:T(8,128)S(1)} collective-permute-done((f32[136,128]{1,0:T(8,128)S(1)}, f32[136,128]{1,0:T(8,128)S(1)}, u32[]{:S(2)}, u32[]{:S(2)}) %collective-permute-start.20) | collective-permute-done | bytes 69664 | tf_op jit(solution)/shard_map/ppermute | solution.py:442
  168.4 15.2 %shard_map.49 = f32[16,256,128]{2,1,0:T(8,128)} custom-call(s32[35]{0:T(128)S(1)} %concatenate.20.tab, f32[136,128]{1,0:T(8,128)S(1)} %add.65.own_g, f32[136,128]{1,0:T(8,128)S(1)} %collective-permute-done.21.other_g, f32[16,128,256]{2,1,0:T(8,128)S(1)} %shard_map.46.own.mine_hbm, f32[16,128,256]{2,1,0:T(8,128)S(1)} %collective-permute-done.17.other.other_hbm), custom_call_target="tpu_custom_call" | custom-call | bytes 4194304 | tf_op jit(solution)/shard_map/pallas_call | solution.py:566
  (93 shorter events, 15.6 us)
Async XLA Ops:
  0.0 1.7 copy-start
  1.7 8.7 %copy-start.11 = (s32[8,9,3]{1,0,2:T(8,128)S(1)}, s32[8,9,3]{1,0,2:T(8,128)}, u32[]{:S(2)}) copy-start(s32[8,9,3]{1,0,2:T(8,128)} %param.4) | copy-start | bytes 2596
  1.7 9.9 %copy-start.4 = (bf16[16,256,128]{2,1,0:T(8,128)(2,1)S(1)}, bf16[16,256,128]{2,1,0:T(8,128)(2,1)}, u32[]{:S(2)}) copy-start(bf16[16,256,128]{2,1,0:T(8,128)(2,1)} %sketch_ref.1) | copy-start | bytes 3145732
  2.3 0.7 copy-start.5
  3.0 25.1 %copy-start.1 = (s32[9,256,256]{2,1,0:T(8,128)S(1)}, s32[9,256,256]{2,1,0:T(8,128)}, u32[]{:S(2)}) copy-start(s32[9,256,256]{2,1,0:T(8,128)} %counts_ref.3) | copy-start | bytes 7077892
  3.0 16.0 %all-to-all-start = ((f32[8,24,256]{2,1,0:T(8,128)}), f32[8,24,256]{2,1,0:T(8,128)}, u32[]{:S(2)}, u32[]{:S(2)}) async-start(f32[8,24,256]{2,1,0:T(8,128)} %copy-done.5), calls=%async_computation | async-start | bytes 393216 | tf_op jit(solution)/shard_map/all_to_all | solution.py:448
  14.0 1.0 copy-start.2
  15.0 0.8 copy-start.6
  15.8 0.7 copy-start.8
  16.5 8.2 %collective-permute-start.1 = (bf16[4,1,128,256]{3,2,1,0:T(8,128)(2,1)}, bf16[4,1,128,256]{3,2,1,0:T(8,128)(2,1)S(1)}, u32[]{:S(2)}, u32[]{:S(2)}) collective-permute-start(bf16[4,1,128,256]{3,2,1,0:T(8,128)(2,1)} %get-tuple-element.30), channel_id=1, source_target_pairs={{0,4},{2,6},{4,0},{6,2},{8,12},{10,14},{12,8},{14,10},{1,5},{3,7},... | collective-permute-start | bytes 786440 | tf_op jit(solution)/shard_map/ppermute | solution.py:442
  18.9 20.4 %all-to-all-start.2 = ((bf16[8,1,128,256]{3,2,1,0:T(8,128)(2,1)}), bf16[8,1,128,256]{3,2,1,0:T(8,128)(2,1)}, u32[]{:S(2)}, u32[]{:S(2)}) async-start(bf16[8,1,128,256]{3,2,1,0:T(8,128)(2,1)} %copy-done.6), calls=%async_computation.2 | async-start | bytes 1048576 | tf_op jit(solution)/shard_map/all_to_all | solution.py:448
  25.7 2.4 %copy-start.9 = (bf16[4,1,128,256]{3,2,1,0:T(8,128)(2,1)}, bf16[4,1,128,256]{3,2,1,0:T(8,128)(2,1)S(1)}, u32[]{:S(2)}) copy-start(bf16[4,1,128,256]{3,2,1,0:T(8,128)(2,1)S(1)} %broadcast_select_fusion.1) | copy-start | bytes 786436
  26.4 18.3 %collective-permute-start.2 = (bf16[2,1,128,256]{3,2,0,1:T(8,128)(2,1)}, bf16[2,1,128,256]{3,2,0,1:T(8,128)(2,1)}, u32[]{:S(2)}, u32[]{:S(2)}) collective-permute-start(bf16[2,1,128,256]{3,2,0,1:T(8,128)(2,1)} %slice_bitcast_fusion.2), channel_id=1, source_target_pairs={{0,2},{2,0},{4,6},{6,4},{8,10},{10,8},{12,14},{14,12},{1,3},{3,1},... | collective-permute-start | bytes 393224 | tf_op jit(solution)/shard_map/ppermute | solution.py:442
  28.1 1.2 copy-start.3
  31.3 4.9 %copy-start.7 = (bf16[1,1,128,256]{3,2,1,0:T(8,128)(2,1)}, bf16[1,1,128,256]{3,2,1,0:T(8,128)(2,1)S(1)}, u32[]{:S(2)}) copy-start(bf16[1,1,128,256]{3,2,1,0:T(8,128)(2,1)S(1)} %get-tuple-element.26) | copy-start | bytes 196612
  31.3 13.4 %copy-start.10 = (bf16[4,1,128,256]{3,2,1,0:T(8,128)(2,1)S(1)}, bf16[4,1,128,256]{3,2,1,0:T(8,128)(2,1)}, u32[]{:S(2)}) copy-start(bf16[4,1,128,256]{3,2,1,0:T(8,128)(2,1)} %copy-done.9) | copy-start | bytes 786436
  32.9 6.4 %collective-permute-start = (bf16[1,1,128,256]{3,2,1,0:T(8,128)(2,1)S(1)}, bf16[1,1,128,256]{3,2,1,0:T(8,128)(2,1)S(1)}, u32[]{:S(2)}, u32[]{:S(2)}) collective-permute-start(bf16[1,1,128,256]{3,2,1,0:T(8,128)(2,1)S(1)} %get-tuple-element.26), channel_id=1, source_target_pairs={{0,8},{2,10},{4,12},{6,14},{8,0},{10,2},{12,4},{14,6},{1,9},{3,11}... | collective-permute-start | bytes 196616 | tf_op jit(solution)/shard_map/ppermute | solution.py:442
  39.3 23.2 %all-to-all-start.1 = ((bf16[8,1,128,256]{3,2,1,0:T(8,128)(2,1)}), bf16[8,1,128,256]{3,2,1,0:T(8,128)(2,1)S(1)}, u32[]{:S(2)}, u32[]{:S(2)}) async-start(bf16[8,1,128,256]{3,2,1,0:T(8,128)(2,1)} %shard_map.40), calls=%async_computation.1 | async-start | bytes 1048576 | tf_op jit(solution)/shard_map/all_to_all | solution.py:448
  46.5 6.5 %collective-permute-start.4 = (bf16[2,1,128,256]{3,2,1,0:T(8,128)(2,1)S(1)}, bf16[2,1,128,256]{3,2,1,0:T(8,128)(2,1)S(1)}, u32[]{:S(2)}, u32[]{:S(2)}) collective-permute-start(bf16[2,1,128,256]{3,2,1,0:T(8,128)(2,1)S(1)} %pad_maximum_fusion), channel_id=1, source_target_pairs={{0,2},{2,0},{4,6},{6,4},{8,10},{10,8},{12,14},{14,12},{1,3},{3,1},... | collective-permute-start | bytes 393224 | tf_op jit(solution)/shard_map/ppermute | solution.py:442
  48.6 11.1 %collective-permute-start.3 = (bf16[1,1,128,256]{3,2,1,0:T(8,128)(2,1)S(1)}, bf16[1,1,128,256]{3,2,1,0:T(8,128)(2,1)S(1)}, u32[]{:S(2)}, u32[]{:S(2)}) collective-permute-start(bf16[1,1,128,256]{3,2,1,0:T(8,128)(2,1)S(1)} %slice_bitcast_fusion.6), channel_id=1, source_target_pairs={{0,8},{2,10},{4,12},{6,14},{8,0},{10,2},{12,4},{14,6},{1,9},{3,11}... | collective-permute-start | bytes 196616 | tf_op jit(solution)/shard_map/ppermute | solution.py:442
  53.1 9.4 %collective-permute-start.5 = (bf16[4,1,128,256]{3,2,1,0:T(8,128)(2,1)S(1)}, bf16[4,1,128,256]{3,2,1,0:T(8,128)(2,1)S(1)}, u32[]{:S(2)}, u32[]{:S(2)}) collective-permute-start(bf16[4,1,128,256]{3,2,1,0:T(8,128)(2,1)S(1)} %constant_dynamic-update-slice_fusion.refs_3_), channel_id=1, source_target_pairs={{0,4},{2,6},{4,0},{6,2},{8,12},{10,14},{12,8},{14,10},{1,5},{3,7},... | collective-permute-start | bytes 786440 | tf_op jit(solution)/shard_map/ppermute | solution.py:442
  64.2 4.2 %collective-permute-start.6 = (f32[16,128,256]{2,1,0:T(8,128)S(1)}, f32[16,128,256]{2,1,0:T(8,128)S(1)}, u32[]{:S(2)}, u32[]{:S(2)}) collective-permute-start(f32[16,128,256]{2,1,0:T(8,128)S(1)} %shard_map.41.own.mine_hbm), channel_id=1, source_target_pairs={{0,1},{1,0},{2,3},{3,2},{4,5},{5,4},{6,7},{7,6},{8,9},{9,8},{10,11... | collective-permute-start | bytes 6291464 | tf_op jit(solution)/shard_map/ppermute | solution.py:445
  70.5 4.4 %collective-permute-start.7 = (f32[136,128]{1,0:T(8,128)S(1)}, f32[136,128]{1,0:T(8,128)S(1)}, u32[]{:S(2)}, u32[]{:S(2)}) collective-permute-start(f32[136,128]{1,0:T(8,128)S(1)} %shard_map.43), channel_id=1, source_target_pairs={{0,2},{2,0},{4,6},{6,4},{8,10},{10,8},{12,14},{14,12},{1,3},{3,1},... | collective-permute-start | bytes 208904 | tf_op jit(solution)/shard_map/ppermute | solution.py:442
  74.9 4.4 %collective-permute-start.8 = (f32[136,128]{1,0:T(8,128)S(1)}, f32[136,128]{1,0:T(8,128)S(1)}, u32[]{:S(2)}, u32[]{:S(2)}) collective-permute-start(f32[136,128]{1,0:T(8,128)S(1)} %add.60), channel_id=1, source_target_pairs={{0,4},{2,6},{4,0},{6,2},{8,12},{10,14},{12,8},{14,10},{1,5},{3,7},... | collective-permute-start | bytes 208904 | tf_op jit(solution)/shard_map/ppermute | solution.py:442
  79.2 5.3 %collective-permute-start.9 = (f32[136,128]{1,0:T(8,128)S(1)}, f32[136,128]{1,0:T(8,128)S(1)}, u32[]{:S(2)}, u32[]{:S(2)}) collective-permute-start(f32[136,128]{1,0:T(8,128)S(1)} %add.61), channel_id=1, source_target_pairs={{0,8},{2,10},{4,12},{6,14},{8,0},{10,2},{12,4},{14,6},{1,9},{3,11}... | collective-permute-start | bytes 208904 | tf_op jit(solution)/shard_map/ppermute | solution.py:442
  84.5 1.3 collective-permute-start.10
  99.8 9.8 %collective-permute-start.11 = (bf16[4,1,128,256]{3,2,1,0:T(8,128)(2,1)S(1)}, bf16[4,1,128,256]{3,2,1,0:T(8,128)(2,1)S(1)}, u32[]{:S(2)}, u32[]{:S(2)}) collective-permute-start(bf16[4,1,128,256]{3,2,1,0:T(8,128)(2,1)S(1)} %get-tuple-element.33), channel_id=1, source_target_pairs={{0,4},{2,6},{4,0},{6,2},{8,12},{10,14},{12,8},{14,10},{1,5},{3,7},... | collective-permute-start | bytes 786440 | tf_op jit(solution)/shard_map/ppermute | solution.py:442
  101.2 7.3 %collective-permute-start.12 = (bf16[1,1,128,256]{3,2,1,0:T(8,128)(2,1)S(1)}, bf16[1,1,128,256]{3,2,1,0:T(8,128)(2,1)S(1)}, u32[]{:S(2)}, u32[]{:S(2)}) collective-permute-start(bf16[1,1,128,256]{3,2,1,0:T(8,128)(2,1)S(1)} %get-tuple-element.34), channel_id=1, source_target_pairs={{0,8},{2,10},{4,12},{6,14},{8,0},{10,2},{12,4},{14,6},{1,9},{3,11}... | collective-permute-start | bytes 196616 | tf_op jit(solution)/shard_map/ppermute | solution.py:442
  109.7 35.8 %all-to-all-start.3 = ((bf16[8,2,128,256]{3,2,1,0:T(8,128)(2,1)}), bf16[8,2,128,256]{3,2,1,0:T(8,128)(2,1)S(1)}, u32[]{:S(2)}, u32[]{:S(2)}) async-start(bf16[8,2,128,256]{3,2,1,0:T(8,128)(2,1)} %shard_map.45), calls=%async_computation.3 | async-start | bytes 2097152 | tf_op jit(solution)/shard_map/all_to_all | solution.py:448
  114.9 14.8 %collective-permute-start.13 = (bf16[2,1,128,256]{3,2,0,1:T(8,128)(2,1)S(1)}, bf16[2,1,128,256]{3,2,0,1:T(8,128)(2,1)S(1)}, u32[]{:S(2)}, u32[]{:S(2)}) collective-permute-start(bf16[2,1,128,256]{3,2,0,1:T(8,128)(2,1)S(1)} %slice_bitcast_fusion), channel_id=1, source_target_pairs={{0,2},{2,0},{4,6},{6,4},{8,10},{10,8},{12,14},{14,12},{1,3},{3,1},... | collective-permute-start | bytes 393224 | tf_op jit(solution)/shard_map/ppermute | solution.py:442
  117.0 15.1 %collective-permute-start.15 = (bf16[2,1,128,256]{3,2,1,0:T(8,128)(2,1)S(1)}, bf16[2,1,128,256]{3,2,1,0:T(8,128)(2,1)S(1)}, u32[]{:S(2)}, u32[]{:S(2)}) collective-permute-start(bf16[2,1,128,256]{3,2,1,0:T(8,128)(2,1)S(1)} %pad_maximum_fusion.1), channel_id=1, source_target_pairs={{0,2},{2,0},{4,6},{6,4},{8,10},{10,8},{12,14},{14,12},{1,3},{3,1},... | collective-permute-start | bytes 393224 | tf_op jit(solution)/shard_map/ppermute | solution.py:442
  129.8 13.4 %collective-permute-start.14 = (bf16[1,1,128,256]{3,2,1,0:T(8,128)(2,1)S(1)}, bf16[1,1,128,256]{3,2,1,0:T(8,128)(2,1)S(1)}, u32[]{:S(2)}, u32[]{:S(2)}) collective-permute-start(bf16[1,1,128,256]{3,2,1,0:T(8,128)(2,1)S(1)} %slice_bitcast_fusion.4), channel_id=1, source_target_pairs={{0,8},{2,10},{4,12},{6,14},{8,0},{10,2},{12,4},{14,6},{1,9},{3,11}... | collective-permute-start | bytes 196616 | tf_op jit(solution)/shard_map/ppermute | solution.py:442
  132.0 13.4 %collective-permute-start.16 = (bf16[4,1,128,256]{3,2,1,0:T(8,128)(2,1)S(1)}, bf16[4,1,128,256]{3,2,1,0:T(8,128)(2,1)S(1)}, u32[]{:S(2)}, u32[]{:S(2)}) collective-permute-start(bf16[4,1,128,256]{3,2,1,0:T(8,128)(2,1)S(1)} %constant_dynamic-update-slice_fusion.3.refs_2_), channel_id=1, source_target_pairs={{0,4},{2,6},{4,0},{6,2},{8,12},{10,14},{12,8},{14,10},{1,5},{3,7},... | collective-permute-start | bytes 786440 | tf_op jit(solution)/shard_map/ppermute | solution.py:442
  146.7 4.2 %collective-permute-start.17 = (f32[16,128,256]{2,1,0:T(8,128)S(1)}, f32[16,128,256]{2,1,0:T(8,128)S(1)}, u32[]{:S(2)}, u32[]{:S(2)}) collective-permute-start(f32[16,128,256]{2,1,0:T(8,128)S(1)} %shard_map.46.own.mine_hbm), channel_id=1, source_target_pairs={{0,1},{1,0},{2,3},{3,2},{4,5},{5,4},{6,7},{7,6},{8,9},{9,8},{10,11... | collective-permute-start | bytes 6291464 | tf_op jit(solution)/shard_map/ppermute | solution.py:445
  153.0 4.4 %collective-permute-start.18 = (f32[136,128]{1,0:T(8,128)S(1)}, f32[136,128]{1,0:T(8,128)S(1)}, u32[]{:S(2)}, u32[]{:S(2)}) collective-permute-start(f32[136,128]{1,0:T(8,128)S(1)} %shard_map.48), channel_id=1, source_target_pairs={{0,2},{2,0},{4,6},{6,4},{8,10},{10,8},{12,14},{14,12},{1,3},{3,1},... | collective-permute-start | bytes 208904 | tf_op jit(solution)/shard_map/ppermute | solution.py:442
  157.4 4.4 %collective-permute-start.19 = (f32[136,128]{1,0:T(8,128)S(1)}, f32[136,128]{1,0:T(8,128)S(1)}, u32[]{:S(2)}, u32[]{:S(2)}) collective-permute-start(f32[136,128]{1,0:T(8,128)S(1)} %add.63), channel_id=1, source_target_pairs={{0,4},{2,6},{4,0},{6,2},{8,12},{10,14},{12,8},{14,10},{1,5},{3,7},... | collective-permute-start | bytes 208904 | tf_op jit(solution)/shard_map/ppermute | solution.py:442
  161.8 5.3 %collective-permute-start.20 = (f32[136,128]{1,0:T(8,128)S(1)}, f32[136,128]{1,0:T(8,128)S(1)}, u32[]{:S(2)}, u32[]{:S(2)}) collective-permute-start(f32[136,128]{1,0:T(8,128)S(1)} %add.64), channel_id=1, source_target_pairs={{0,8},{2,10},{4,12},{6,14},{8,0},{10,2},{12,4},{14,6},{1,9},{3,11}... | collective-permute-start | bytes 208904 | tf_op jit(solution)/shard_map/ppermute | solution.py:442
  167.1 1.3 collective-permute-start.21

commit v10 on v9

--- a/solution.py
+++ b/solution.py
@@ -368,7 +368,7 @@
     high, mid, _ = split(factor)
     two = jnp.concatenate([high, mid], axis=0)
 
-    @pl.loop(0, mine.shape[0])
+    @pl.loop(0, mine.shape[0], unroll=4)
     def _(i):
         y_high, y_mid, _ = split(jnp.concatenate([mine[i], other[i]], axis=0))
         by_high = contract(two, y_high, 1, 0)

time: 184 us -> 180 us (0.978)
  Pallas kernels: 47.4 us -> 42.5 us
    pallas_call x1, Pallas kernels: 15.2 us -> 12.4 us  [body(): call(make_final_kernel(t, 1.0 / vocab), shape((blocks, rows, half), f32),...]
    pallas_call x1, Pallas kernels: 13.9 us -> 11.8 us  [body(): call(make_second_kernel(t, 1.0 / vocab), [shape((blocks, half, rows), bf1...]
where the time goes in v10:
time: 180 us; the launch traced here: 179 us
  waiting for transfers between devices  69.6 us (39%)
  starting transfers between devices  54.3 us (30%)
  Pallas kernels  42.5 us (24%)
  local copies, waits for them, and re-layouts  8.21 us (5%)
  other arithmetic  3.63 us (2%)
    ppermute x18, waiting for transfers between devices, peer(): return lax.ppermute(x, 'row', [(r, r ^ k) for r in range(groups)])  61.5 us
    ppermute x18, starting transfers between devices, peer(): return lax.ppermute(x, 'row', [(r, r ^ k) for r in range(groups)])  31.7 us
    all_to_all x4, starting transfers between devices, exchange(): return lax.all_to_all(x, 'row', split_axis=0, concat_axis=0, tiled=True)  22.4 us
    pallas_call x1, Pallas kernels, body(): call(make_final_kernel(t, 1.0 / vocab), shape((blocks, rows, half), f32),...  12.4 us
    pallas_call x1, Pallas kernels, body(): call(make_second_kernel(t, 1.0 / vocab), [shape((blocks, half, rows), bf1...  11.8 us
    ppermute x4, waiting for transfers between devices, swap(): return lax.ppermute(x, 'col', [(0, 1), (1, 0)])  8.11 us
    unnamed x29, local copies, waits for them, and re-layouts  6.09 us
    pallas_call x2, Pallas kernels, finish(): call(make_cross_gram_kernel(t), shape((half + 8, half), f32), [SMEM] + [V...  4.02 us
  transfers between devices with their start and end apart: 26, of which 21 were waited for; matrix products, arithmetic and copies ran while one was open for 3% of the time, Pallas kernels for 6%

profile of v10, /device:TPU:0, one launch (start us, length us, event | category | flops | bytes accessed | tf_op | source)
XLA Modules:
  0.0 178.8 jit_solution(15158580080725703381)
XLA Ops:
  0.0 1.7 copy-done
  3.0 7.4 %all-to-all-start = ((f32[8,24,256]{2,1,0:T(8,128)}), f32[8,24,256]{2,1,0:T(8,128)}, u32[]{:S(2)}, u32[]{:S(2)}) async-start(f32[8,24,256]{2,1,0:T(8,128)} %copy-done.5), calls=%async_computation | async-start | bytes 393216 | tf_op jit(solution)/shard_map/all_to_all | solution.py:448
  11.5 2.5 %shard_map.37 = (bf16[16,128,256]{2,1,0:T(8,128)(2,1)S(1)}, bf16[8,1,128,256]{3,2,1,0:T(8,128)(2,1)S(1)}, bf16[4,1,128,256]{3,2,1,0:T(8,128)(2,1)S(1)}, bf16[4,1,128,256]{3,2,1,0:T(8,128)(2,1)}) custom-call(s32[35]{0:T(128)S(1)} %concatenate.20.tab, bf16[16,256,128]{2,1,0:T(8,128)(2,1)S(1)} %copy-done.4), custom_call_target="tpu_custom_call" | custom-call | bytes 4194304 | tf_op jit(solution)/shard_map/pallas_call | solution.py:493
  16.5 2.0 %collective-permute-start.1 = (bf16[4,1,128,256]{3,2,1,0:T(8,128)(2,1)}, bf16[4,1,128,256]{3,2,1,0:T(8,128)(2,1)S(1)}, u32[]{:S(2)}, u32[]{:S(2)}) collective-permute-start(bf16[4,1,128,256]{3,2,1,0:T(8,128)(2,1)} %get-tuple-element.30), channel_id=1, source_target_pairs={{0,4},{2,6},{4,0},{6,2},{8,12},{10,14},{12,8},{14,10},{1,5},{3,7},... | collective-permute-start | bytes 786440 | tf_op jit(solution)/shard_map/ppermute | solution.py:442
  18.9 4.5 %all-to-all-start.2 = ((bf16[8,1,128,256]{3,2,1,0:T(8,128)(2,1)}), bf16[8,1,128,256]{3,2,1,0:T(8,128)(2,1)}, u32[]{:S(2)}, u32[]{:S(2)}) async-start(bf16[8,1,128,256]{3,2,1,0:T(8,128)(2,1)} %copy-done.6), calls=%async_computation.2 | async-start | bytes 1048576 | tf_op jit(solution)/shard_map/all_to_all | solution.py:448
  26.4 1.5 collective-permute-start.2
  29.3 1.9 %shard_map.39 = (bf16[9,256,256]{2,1,0:T(8,128)(2,1)S(1)}, bf16[1,1,128,256]{3,2,1,0:T(8,128)(2,1)S(1)}) custom-call(s32[35]{0:T(128)S(1)} %concatenate.20.tab, bf16[24,192]{1,0:T(8,128)(2,1)S(1)} %compare_convert_fusion.match_ref, s32[9,256,256]{2,1,0:T(8,128)S(1)} %copy-done.1, bf16[16,128,256]{2,1,0:T(8,128)(2,1)S(1)} %copy-done.3, ...), custom_call_target="tpu_custom_call" | custom-call | bytes 4194304 | tf_op jit(solution)/shard_map/pallas_call | solution.py:509
  31.3 1.6 shard_map.40
  32.9 3.3 %collective-permute-start = (bf16[1,1,128,256]{3,2,1,0:T(8,128)(2,1)S(1)}, bf16[1,1,128,256]{3,2,1,0:T(8,128)(2,1)S(1)}, u32[]{:S(2)}, u32[]{:S(2)}) collective-permute-start(bf16[1,1,128,256]{3,2,1,0:T(8,128)(2,1)S(1)} %get-tuple-element.26), channel_id=1, source_target_pairs={{0,8},{2,10},{4,12},{6,14},{8,0},{10,2},{12,4},{14,6},{1,9},{3,11}... | collective-permute-start | bytes 196616 | tf_op jit(solution)/shard_map/ppermute | solution.py:442
  36.2 3.1 %collective-permute-done = bf16[1,1,128,256]{3,2,1,0:T(8,128)(2,1)S(1)} collective-permute-done((bf16[1,1,128,256]{3,2,1,0:T(8,128)(2,1)S(1)}, bf16[1,1,128,256]{3,2,1,0:T(8,128)(2,1)S(1)}, u32[]{:S(2)}, u32[]{:S(2)}) %collective-permute-start) | collective-permute-done | bytes 65568 | tf_op jit(solution)/shard_map/ppermute | solution.py:442
  39.3 5.4 %all-to-all-start.1 = ((bf16[8,1,128,256]{3,2,1,0:T(8,128)(2,1)}), bf16[8,1,128,256]{3,2,1,0:T(8,128)(2,1)S(1)}, u32[]{:S(2)}, u32[]{:S(2)}) async-start(bf16[8,1,128,256]{3,2,1,0:T(8,128)(2,1)} %shard_map.40), calls=%async_computation.1 | async-start | bytes 1048576 | tf_op jit(solution)/shard_map/all_to_all | solution.py:448
  46.6 2.1 %collective-permute-start.4 = (bf16[2,1,128,256]{3,2,1,0:T(8,128)(2,1)S(1)}, bf16[2,1,128,256]{3,2,1,0:T(8,128)(2,1)S(1)}, u32[]{:S(2)}, u32[]{:S(2)}) collective-permute-start(bf16[2,1,128,256]{3,2,1,0:T(8,128)(2,1)S(1)} %pad_maximum_fusion), channel_id=1, source_target_pairs={{0,2},{2,0},{4,6},{6,4},{8,10},{10,8},{12,14},{14,12},{1,3},{3,1},... | collective-permute-start | bytes 393224 | tf_op jit(solution)/shard_map/ppermute | solution.py:442
  48.6 2.4 %collective-permute-start.3 = (bf16[1,1,128,256]{3,2,1,0:T(8,128)(2,1)S(1)}, bf16[1,1,128,256]{3,2,1,0:T(8,128)(2,1)S(1)}, u32[]{:S(2)}, u32[]{:S(2)}) collective-permute-start(bf16[1,1,128,256]{3,2,1,0:T(8,128)(2,1)S(1)} %slice_bitcast_fusion.6), channel_id=1, source_target_pairs={{0,8},{2,10},{4,12},{6,14},{8,0},{10,2},{12,4},{14,6},{1,9},{3,11}... | collective-permute-start | bytes 196616 | tf_op jit(solution)/shard_map/ppermute | solution.py:442
  51.0 2.1 %collective-permute-done.4 = bf16[2,1,128,256]{3,2,1,0:T(8,128)(2,1)S(1)} collective-permute-done((bf16[2,1,128,256]{3,2,1,0:T(8,128)(2,1)S(1)}, bf16[2,1,128,256]{3,2,1,0:T(8,128)(2,1)S(1)}, u32[]{:S(2)}, u32[]{:S(2)}) %collective-permute-start.4) | collective-permute-done | bytes 131104 | tf_op jit(solution)/shard_map/ppermute | solution.py:442
  53.1 2.1 %collective-permute-start.5 = (bf16[4,1,128,256]{3,2,1,0:T(8,128)(2,1)S(1)}, bf16[4,1,128,256]{3,2,1,0:T(8,128)(2,1)S(1)}, u32[]{:S(2)}, u32[]{:S(2)}) collective-permute-start(bf16[4,1,128,256]{3,2,1,0:T(8,128)(2,1)S(1)} %constant_dynamic-update-slice_fusion.refs_3_), channel_id=1, source_target_pairs={{0,4},{2,6},{4,0},{6,2},{8,12},{10,14},{12,8},{14,10},{1,5},{3,7},... | collective-permute-start | bytes 786440 | tf_op jit(solution)/shard_map/ppermute | solution.py:442
  55.3 4.4 %collective-permute-done.3 = bf16[1,1,128,256]{3,2,1,0:T(8,128)(2,1)S(1)} collective-permute-done((bf16[1,1,128,256]{3,2,1,0:T(8,128)(2,1)S(1)}, bf16[1,1,128,256]{3,2,1,0:T(8,128)(2,1)S(1)}, u32[]{:S(2)}, u32[]{:S(2)}) %collective-permute-start.3) | collective-permute-done | bytes 65568 | tf_op jit(solution)/shard_map/ppermute | solution.py:442
  59.8 2.7 %collective-permute-done.5.refs_4_ = bf16[4,1,128,256]{3,2,1,0:T(8,128)(2,1)S(1)} collective-permute-done((bf16[4,1,128,256]{3,2,1,0:T(8,128)(2,1)S(1)}, bf16[4,1,128,256]{3,2,1,0:T(8,128)(2,1)S(1)}, u32[]{:S(2)}, u32[]{:S(2)}) %collective-permute-start.5) | collective-permute-done | bytes 262176 | tf_op jit(solution)/shard_map/ppermute | solution.py:442
  62.4 1.8 %shard_map.41.own.mine_hbm = f32[16,128,256]{2,1,0:T(8,128)S(1)} custom-call(s32[35]{0:T(128)S(1)} %concatenate.20.tab, bf16[9,256,256]{2,1,0:T(8,128)(2,1)S(1)} %get-tuple-element.25.ppmi.ppmi_ref.ppmi_hbm, bf16[8,1,128,256]{3,2,1,0:T(8,128)(2,1)S(1)} %all-to-all-done.1.refs_0_, bf16[8,1,128,256]{3,2,1,0:T(8,128)(2,1)} %all-to-all-done.2.refs_1_, ...), custom_call_target="tpu_custom_call" | custom-call | bytes 4194304 | tf_op jit(solution)/shard_map/pallas_call | solution.py:532
  64.3 1.3 shard_map.42.square
  65.7 2.8 %collective-permute-done.6.other.other_hbm = f32[16,128,256]{2,1,0:T(8,128)S(1)} collective-permute-done((f32[16,128,256]{2,1,0:T(8,128)S(1)}, f32[16,128,256]{2,1,0:T(8,128)S(1)}, u32[]{:S(2)}, u32[]{:S(2)}) %collective-permute-start.6) | collective-permute-done | bytes 2097184 | tf_op jit(solution)/shard_map/ppermute | solution.py:445
  68.5 2.0 %shard_map.43 = f32[136,128]{1,0:T(8,128)S(1)} custom-call(s32[35]{0:T(128)S(1)} %concatenate.20.tab, f32[16,128,256]{2,1,0:T(8,128)S(1)} %shard_map.41.own.mine_hbm, f32[16,128,256]{2,1,0:T(8,128)S(1)} %collective-permute-done.6.other.other_hbm, f32[128,128]{1,0:T(8,128)S(1)} %shard_map.42.square), custom_call_target="tpu_custom_call" | custom-call | bytes 4194304 | tf_op jit(solution)/shard_map/pallas_call | solution.py:540
  70.5 1.5 collective-permute-start.7
  72.0 2.8 %collective-permute-done.7 = f32[136,128]{1,0:T(8,128)S(1)} collective-permute-done((f32[136,128]{1,0:T(8,128)S(1)}, f32[136,128]{1,0:T(8,128)S(1)}, u32[]{:S(2)}, u32[]{:S(2)}) %collective-permute-start.7) | collective-permute-done | bytes 69664 | tf_op jit(solution)/shard_map/ppermute | solution.py:442
  74.9 4.3 %collective-permute-done.8 = f32[136,128]{1,0:T(8,128)S(1)} collective-permute-done((f32[136,128]{1,0:T(8,128)S(1)}, f32[136,128]{1,0:T(8,128)S(1)}, u32[]{:S(2)}, u32[]{:S(2)}) %collective-permute-start.8) | collective-permute-done | bytes 69664 | tf_op jit(solution)/shard_map/ppermute | solution.py:442
  79.2 2.2 %collective-permute-start.9 = (f32[136,128]{1,0:T(8,128)S(1)}, f32[136,128]{1,0:T(8,128)S(1)}, u32[]{:S(2)}, u32[]{:S(2)}) collective-permute-start(f32[136,128]{1,0:T(8,128)S(1)} %add.61), channel_id=1, source_target_pairs={{0,8},{2,10},{4,12},{6,14},{8,0},{10,2},{12,4},{14,6},{1,9},{3,11}... | collective-permute-start | bytes 208904 | tf_op jit(solution)/shard_map/ppermute | solution.py:442
  81.4 3.1 %collective-permute-done.9 = f32[136,128]{1,0:T(8,128)S(1)} collective-permute-done((f32[136,128]{1,0:T(8,128)S(1)}, f32[136,128]{1,0:T(8,128)S(1)}, u32[]{:S(2)}, u32[]{:S(2)}) %collective-permute-start.9) | collective-permute-done | bytes 69664 | tf_op jit(solution)/shard_map/ppermute | solution.py:442
  84.6 1.2 collective-permute-done.10.other_g
  85.9 11.8 %shard_map.44 = (bf16[16,128,256]{2,1,0:T(8,128)(2,1)S(1)}, bf16[4,1,128,256]{3,2,1,0:T(8,128)(2,1)S(1)}, bf16[4,1,128,256]{3,2,1,0:T(8,128)(2,1)S(1)}, bf16[1,1,128,256]{3,2,1,0:T(8,128)(2,1)S(1)}) custom-call(s32[35]{0:T(128)S(1)} %concatenate.20.tab, f32[136,128]{1,0:T(8,128)S(1)} %add.62.own_g, f32[136,128]{1,0:T(8,128)S(1)} %collective-permute-done.10.other_g, ...), custom_call_target="tpu_custom_call" | custom-call | bytes 4194304 | tf_op jit(solution)/shard_map/pallas_call | solution.py:557
  97.7 1.4 collective-permute-start.11
  99.1 3.0 %collective-permute-start.12 = (bf16[1,1,128,256]{3,2,1,0:T(8,128)(2,1)S(1)}, bf16[1,1,128,256]{3,2,1,0:T(8,128)(2,1)S(1)}, u32[]{:S(2)}, u32[]{:S(2)}) collective-permute-start(bf16[1,1,128,256]{3,2,1,0:T(8,128)(2,1)S(1)} %get-tuple-element.34), channel_id=1, source_target_pairs={{0,8},{2,10},{4,12},{6,14},{8,0},{10,2},{12,4},{14,6},{1,9},{3,11}... | collective-permute-start | bytes 196616 | tf_op jit(solution)/shard_map/ppermute | solution.py:442
  102.1 1.8 %shard_map.45 = bf16[8,2,128,256]{3,2,1,0:T(8,128)(2,1)} custom-call(s32[35]{0:T(128)S(1)} %concatenate.20.tab, bf16[16,128,256]{2,1,0:T(8,128)(2,1)S(1)} %get-tuple-element.32.blocks, bf16[9,256,256]{2,1,0:T(8,128)(2,1)S(1)} %get-tuple-element.25.ppmi.ppmi_ref.ppmi_hbm), custom_call_target="tpu_custom_call" | custom-call | bytes 4194304 | tf_op jit(solution)/shard_map/pallas_call | solution.py:522
  103.9 2.4 %collective-permute-done.12 = bf16[1,1,128,256]{3,2,1,0:T(8,128)(2,1)S(1)} collective-permute-done((bf16[1,1,128,256]{3,2,1,0:T(8,128)(2,1)S(1)}, bf16[1,1,128,256]{3,2,1,0:T(8,128)(2,1)S(1)}, u32[]{:S(2)}, u32[]{:S(2)}) %collective-permute-start.12) | collective-permute-done | bytes 65568 | tf_op jit(solution)/shard_map/ppermute | solution.py:442
  107.5 5.0 %all-to-all-start.3 = ((bf16[8,2,128,256]{3,2,1,0:T(8,128)(2,1)}), bf16[8,2,128,256]{3,2,1,0:T(8,128)(2,1)S(1)}, u32[]{:S(2)}, u32[]{:S(2)}) async-start(bf16[8,2,128,256]{3,2,1,0:T(8,128)(2,1)} %shard_map.45), calls=%async_computation.3 | async-start | bytes 2097152 | tf_op jit(solution)/shard_map/all_to_all | solution.py:448
  112.7 2.1 %collective-permute-start.13 = (bf16[2,1,128,256]{3,2,0,1:T(8,128)(2,1)S(1)}, bf16[2,1,128,256]{3,2,0,1:T(8,128)(2,1)S(1)}, u32[]{:S(2)}, u32[]{:S(2)}) collective-permute-start(bf16[2,1,128,256]{3,2,0,1:T(8,128)(2,1)S(1)} %slice_bitcast_fusion), channel_id=1, source_target_pairs={{0,2},{2,0},{4,6},{6,4},{8,10},{10,8},{12,14},{14,12},{1,3},{3,1},... | collective-permute-start | bytes 393224 | tf_op jit(solution)/shard_map/ppermute | solution.py:442
  114.9 12.6 %collective-permute-done.13 = bf16[2,1,128,256]{3,2,0,1:T(8,128)(2,1)S(1)} collective-permute-done((bf16[2,1,128,256]{3,2,0,1:T(8,128)(2,1)S(1)}, bf16[2,1,128,256]{3,2,0,1:T(8,128)(2,1)S(1)}, u32[]{:S(2)}, u32[]{:S(2)}) %collective-permute-start.13) | collective-permute-done | bytes 131104 | tf_op jit(solution)/shard_map/ppermute | solution.py:442
  127.6 1.5 collective-permute-start.14
  129.9 4.1 %collective-permute-start.16 = (bf16[4,1,128,256]{3,2,1,0:T(8,128)(2,1)S(1)}, bf16[4,1,128,256]{3,2,1,0:T(8,128)(2,1)S(1)}, u32[]{:S(2)}, u32[]{:S(2)}) collective-permute-start(bf16[4,1,128,256]{3,2,1,0:T(8,128)(2,1)S(1)} %constant_dynamic-update-slice_fusion.3.refs_2_), channel_id=1, source_target_pairs={{0,4},{2,6},{4,0},{6,2},{8,12},{10,14},{12,8},{14,10},{1,5},{3,7},... | collective-permute-start | bytes 786440 | tf_op jit(solution)/shard_map/ppermute | solution.py:442
  133.9 7.0 %collective-permute-done.14 = bf16[1,1,128,256]{3,2,1,0:T(8,128)(2,1)S(1)} collective-permute-done((bf16[1,1,128,256]{3,2,1,0:T(8,128)(2,1)S(1)}, bf16[1,1,128,256]{3,2,1,0:T(8,128)(2,1)S(1)}, u32[]{:S(2)}, u32[]{:S(2)}) %collective-permute-start.14) | collective-permute-done | bytes 65568 | tf_op jit(solution)/shard_map/ppermute | solution.py:442
  141.0 2.3 %collective-permute-done.16.refs_3_ = bf16[4,1,128,256]{3,2,1,0:T(8,128)(2,1)S(1)} collective-permute-done((bf16[4,1,128,256]{3,2,1,0:T(8,128)(2,1)S(1)}, bf16[4,1,128,256]{3,2,1,0:T(8,128)(2,1)S(1)}, u32[]{:S(2)}, u32[]{:S(2)}) %collective-permute-start.16) | collective-permute-done | bytes 262176 | tf_op jit(solution)/shard_map/ppermute | solution.py:442
  143.3 1.3 shard_map.46.own.mine_hbm
  144.6 1.3 shard_map.47.square
  146.0 2.8 %collective-permute-done.17.other.other_hbm = f32[16,128,256]{2,1,0:T(8,128)S(1)} collective-permute-done((f32[16,128,256]{2,1,0:T(8,128)S(1)}, f32[16,128,256]{2,1,0:T(8,128)S(1)}, u32[]{:S(2)}, u32[]{:S(2)}) %collective-permute-start.17) | collective-permute-done | bytes 2097184 | tf_op jit(solution)/shard_map/ppermute | solution.py:445
  148.8 2.0 %shard_map.48 = f32[136,128]{1,0:T(8,128)S(1)} custom-call(s32[35]{0:T(128)S(1)} %concatenate.20.tab, f32[16,128,256]{2,1,0:T(8,128)S(1)} %shard_map.46.own.mine_hbm, f32[16,128,256]{2,1,0:T(8,128)S(1)} %collective-permute-done.17.other.other_hbm, f32[128,128]{1,0:T(8,128)S(1)} %shard_map.47.square), custom_call_target="tpu_custom_call" | custom-call | bytes 4194304 | tf_op jit(solution)/shard_map/pallas_call | solution.py:540
  150.9 4.3 %collective-permute-done.18 = f32[136,128]{1,0:T(8,128)S(1)} collective-permute-done((f32[136,128]{1,0:T(8,128)S(1)}, f32[136,128]{1,0:T(8,128)S(1)}, u32[]{:S(2)}, u32[]{:S(2)}) %collective-permute-start.18) | collective-permute-done | bytes 69664 | tf_op jit(solution)/shard_map/ppermute | solution.py:442
  155.3 4.3 %collective-permute-done.19 = f32[136,128]{1,0:T(8,128)S(1)} collective-permute-done((f32[136,128]{1,0:T(8,128)S(1)}, f32[136,128]{1,0:T(8,128)S(1)}, u32[]{:S(2)}, u32[]{:S(2)}) %collective-permute-start.19) | collective-permute-done | bytes 69664 | tf_op jit(solution)/shard_map/ppermute | solution.py:442
  159.6 2.3 %collective-permute-start.20 = (f32[136,128]{1,0:T(8,128)S(1)}, f32[136,128]{1,0:T(8,128)S(1)}, u32[]{:S(2)}, u32[]{:S(2)}) collective-permute-start(f32[136,128]{1,0:T(8,128)S(1)} %add.64), channel_id=1, source_target_pairs={{0,8},{2,10},{4,12},{6,14},{8,0},{10,2},{12,4},{14,6},{1,9},{3,11}... | collective-permute-start | bytes 208904 | tf_op jit(solution)/shard_map/ppermute | solution.py:442
  161.9 3.0 %collective-permute-done.20 = f32[136,128]{1,0:T(8,128)S(1)} collective-permute-done((f32[136,128]{1,0:T(8,128)S(1)}, f32[136,128]{1,0:T(8,128)S(1)}, u32[]{:S(2)}, u32[]{:S(2)}) %collective-permute-start.20) | collective-permute-done | bytes 69664 | tf_op jit(solution)/shard_map/ppermute | solution.py:442
  166.2 12.4 %shard_map.49 = f32[16,256,128]{2,1,0:T(8,128)} custom-call(s32[35]{0:T(128)S(1)} %concatenate.20.tab, f32[136,128]{1,0:T(8,128)S(1)} %add.65.own_g, f32[136,128]{1,0:T(8,128)S(1)} %collective-permute-done.21.other_g, f32[16,128,256]{2,1,0:T(8,128)S(1)} %shard_map.46.own.mine_hbm, f32[16,128,256]{2,1,0:T(8,128)S(1)} %collective-permute-done.17.other.other_hbm), custom_call_target="tpu_custom_call" | custom-call | bytes 4194304 | tf_op jit(solution)/shard_map/pallas_call | solution.py:566
  (93 shorter events, 15.7 us)
Async XLA Ops:
  0.0 1.7 copy-start
  1.7 8.7 %copy-start.11 = (s32[8,9,3]{1,0,2:T(8,128)S(1)}, s32[8,9,3]{1,0,2:T(8,128)}, u32[]{:S(2)}) copy-start(s32[8,9,3]{1,0,2:T(8,128)} %param.4) | copy-start | bytes 2596
  1.7 9.9 %copy-start.4 = (bf16[16,256,128]{2,1,0:T(8,128)(2,1)S(1)}, bf16[16,256,128]{2,1,0:T(8,128)(2,1)}, u32[]{:S(2)}) copy-start(bf16[16,256,128]{2,1,0:T(8,128)(2,1)} %sketch_ref.1) | copy-start | bytes 3145732
  2.3 0.7 copy-start.5
  3.0 25.1 %copy-start.1 = (s32[9,256,256]{2,1,0:T(8,128)S(1)}, s32[9,256,256]{2,1,0:T(8,128)}, u32[]{:S(2)}) copy-start(s32[9,256,256]{2,1,0:T(8,128)} %counts_ref.3) | copy-start | bytes 7077892
  3.0 16.0 %all-to-all-start = ((f32[8,24,256]{2,1,0:T(8,128)}), f32[8,24,256]{2,1,0:T(8,128)}, u32[]{:S(2)}, u32[]{:S(2)}) async-start(f32[8,24,256]{2,1,0:T(8,128)} %copy-done.5), calls=%async_computation | async-start | bytes 393216 | tf_op jit(solution)/shard_map/all_to_all | solution.py:448
  14.0 1.0 copy-start.2
  15.0 0.8 copy-start.6
  15.8 0.7 copy-start.8
  16.5 8.2 %collective-permute-start.1 = (bf16[4,1,128,256]{3,2,1,0:T(8,128)(2,1)}, bf16[4,1,128,256]{3,2,1,0:T(8,128)(2,1)S(1)}, u32[]{:S(2)}, u32[]{:S(2)}) collective-permute-start(bf16[4,1,128,256]{3,2,1,0:T(8,128)(2,1)} %get-tuple-element.30), channel_id=1, source_target_pairs={{0,4},{2,6},{4,0},{6,2},{8,12},{10,14},{12,8},{14,10},{1,5},{3,7},... | collective-permute-start | bytes 786440 | tf_op jit(solution)/shard_map/ppermute | solution.py:442
  18.9 20.3 %all-to-all-start.2 = ((bf16[8,1,128,256]{3,2,1,0:T(8,128)(2,1)}), bf16[8,1,128,256]{3,2,1,0:T(8,128)(2,1)}, u32[]{:S(2)}, u32[]{:S(2)}) async-start(bf16[8,1,128,256]{3,2,1,0:T(8,128)(2,1)} %copy-done.6), calls=%async_computation.2 | async-start | bytes 1048576 | tf_op jit(solution)/shard_map/all_to_all | solution.py:448
  25.7 2.4 %copy-start.9 = (bf16[4,1,128,256]{3,2,1,0:T(8,128)(2,1)}, bf16[4,1,128,256]{3,2,1,0:T(8,128)(2,1)S(1)}, u32[]{:S(2)}) copy-start(bf16[4,1,128,256]{3,2,1,0:T(8,128)(2,1)S(1)} %broadcast_select_fusion.1) | copy-start | bytes 786436
  26.4 18.3 %collective-permute-start.2 = (bf16[2,1,128,256]{3,2,0,1:T(8,128)(2,1)}, bf16[2,1,128,256]{3,2,0,1:T(8,128)(2,1)}, u32[]{:S(2)}, u32[]{:S(2)}) collective-permute-start(bf16[2,1,128,256]{3,2,0,1:T(8,128)(2,1)} %slice_bitcast_fusion.2), channel_id=1, source_target_pairs={{0,2},{2,0},{4,6},{6,4},{8,10},{10,8},{12,14},{14,12},{1,3},{3,1},... | collective-permute-start | bytes 393224 | tf_op jit(solution)/shard_map/ppermute | solution.py:442
  28.1 1.2 copy-start.3
  31.3 4.9 %copy-start.7 = (bf16[1,1,128,256]{3,2,1,0:T(8,128)(2,1)}, bf16[1,1,128,256]{3,2,1,0:T(8,128)(2,1)S(1)}, u32[]{:S(2)}) copy-start(bf16[1,1,128,256]{3,2,1,0:T(8,128)(2,1)S(1)} %get-tuple-element.26) | copy-start | bytes 196612
  31.3 13.4 %copy-start.10 = (bf16[4,1,128,256]{3,2,1,0:T(8,128)(2,1)S(1)}, bf16[4,1,128,256]{3,2,1,0:T(8,128)(2,1)}, u32[]{:S(2)}) copy-start(bf16[4,1,128,256]{3,2,1,0:T(8,128)(2,1)} %copy-done.9) | copy-start | bytes 786436
  32.9 6.4 %collective-permute-start = (bf16[1,1,128,256]{3,2,1,0:T(8,128)(2,1)S(1)}, bf16[1,1,128,256]{3,2,1,0:T(8,128)(2,1)S(1)}, u32[]{:S(2)}, u32[]{:S(2)}) collective-permute-start(bf16[1,1,128,256]{3,2,1,0:T(8,128)(2,1)S(1)} %get-tuple-element.26), channel_id=1, source_target_pairs={{0,8},{2,10},{4,12},{6,14},{8,0},{10,2},{12,4},{14,6},{1,9},{3,11}... | collective-permute-start | bytes 196616 | tf_op jit(solution)/shard_map/ppermute | solution.py:442
  39.3 23.2 %all-to-all-start.1 = ((bf16[8,1,128,256]{3,2,1,0:T(8,128)(2,1)}), bf16[8,1,128,256]{3,2,1,0:T(8,128)(2,1)S(1)}, u32[]{:S(2)}, u32[]{:S(2)}) async-start(bf16[8,1,128,256]{3,2,1,0:T(8,128)(2,1)} %shard_map.40), calls=%async_computation.1 | async-start | bytes 1048576 | tf_op jit(solution)/shard_map/all_to_all | solution.py:448
  46.6 6.5 %collective-permute-start.4 = (bf16[2,1,128,256]{3,2,1,0:T(8,128)(2,1)S(1)}, bf16[2,1,128,256]{3,2,1,0:T(8,128)(2,1)S(1)}, u32[]{:S(2)}, u32[]{:S(2)}) collective-permute-start(bf16[2,1,128,256]{3,2,1,0:T(8,128)(2,1)S(1)} %pad_maximum_fusion), channel_id=1, source_target_pairs={{0,2},{2,0},{4,6},{6,4},{8,10},{10,8},{12,14},{14,12},{1,3},{3,1},... | collective-permute-start | bytes 393224 | tf_op jit(solution)/shard_map/ppermute | solution.py:442
  48.6 11.1 %collective-permute-start.3 = (bf16[1,1,128,256]{3,2,1,0:T(8,128)(2,1)S(1)}, bf16[1,1,128,256]{3,2,1,0:T(8,128)(2,1)S(1)}, u32[]{:S(2)}, u32[]{:S(2)}) collective-permute-start(bf16[1,1,128,256]{3,2,1,0:T(8,128)(2,1)S(1)} %slice_bitcast_fusion.6), channel_id=1, source_target_pairs={{0,8},{2,10},{4,12},{6,14},{8,0},{10,2},{12,4},{14,6},{1,9},{3,11}... | collective-permute-start | bytes 196616 | tf_op jit(solution)/shard_map/ppermute | solution.py:442
  53.1 9.4 %collective-permute-start.5 = (bf16[4,1,128,256]{3,2,1,0:T(8,128)(2,1)S(1)}, bf16[4,1,128,256]{3,2,1,0:T(8,128)(2,1)S(1)}, u32[]{:S(2)}, u32[]{:S(2)}) collective-permute-start(bf16[4,1,128,256]{3,2,1,0:T(8,128)(2,1)S(1)} %constant_dynamic-update-slice_fusion.refs_3_), channel_id=1, source_target_pairs={{0,4},{2,6},{4,0},{6,2},{8,12},{10,14},{12,8},{14,10},{1,5},{3,7},... | collective-permute-start | bytes 786440 | tf_op jit(solution)/shard_map/ppermute | solution.py:442
  64.2 4.2 %collective-permute-start.6 = (f32[16,128,256]{2,1,0:T(8,128)S(1)}, f32[16,128,256]{2,1,0:T(8,128)S(1)}, u32[]{:S(2)}, u32[]{:S(2)}) collective-permute-start(f32[16,128,256]{2,1,0:T(8,128)S(1)} %shard_map.41.own.mine_hbm), channel_id=1, source_target_pairs={{0,1},{1,0},{2,3},{3,2},{4,5},{5,4},{6,7},{7,6},{8,9},{9,8},{10,11... | collective-permute-start | bytes 6291464 | tf_op jit(solution)/shard_map/ppermute | solution.py:445
  70.5 4.4 %collective-permute-start.7 = (f32[136,128]{1,0:T(8,128)S(1)}, f32[136,128]{1,0:T(8,128)S(1)}, u32[]{:S(2)}, u32[]{:S(2)}) collective-permute-start(f32[136,128]{1,0:T(8,128)S(1)} %shard_map.43), channel_id=1, source_target_pairs={{0,2},{2,0},{4,6},{6,4},{8,10},{10,8},{12,14},{14,12},{1,3},{3,1},... | collective-permute-start | bytes 208904 | tf_op jit(solution)/shard_map/ppermute | solution.py:442
  74.8 4.4 %collective-permute-start.8 = (f32[136,128]{1,0:T(8,128)S(1)}, f32[136,128]{1,0:T(8,128)S(1)}, u32[]{:S(2)}, u32[]{:S(2)}) collective-permute-start(f32[136,128]{1,0:T(8,128)S(1)} %add.60), channel_id=1, source_target_pairs={{0,4},{2,6},{4,0},{6,2},{8,12},{10,14},{12,8},{14,10},{1,5},{3,7},... | collective-permute-start | bytes 208904 | tf_op jit(solution)/shard_map/ppermute | solution.py:442
  79.2 5.3 %collective-permute-start.9 = (f32[136,128]{1,0:T(8,128)S(1)}, f32[136,128]{1,0:T(8,128)S(1)}, u32[]{:S(2)}, u32[]{:S(2)}) collective-permute-start(f32[136,128]{1,0:T(8,128)S(1)} %add.61), channel_id=1, source_target_pairs={{0,8},{2,10},{4,12},{6,14},{8,0},{10,2},{12,4},{14,6},{1,9},{3,11}... | collective-permute-start | bytes 208904 | tf_op jit(solution)/shard_map/ppermute | solution.py:442
  84.5 1.3 collective-permute-start.10
  97.7 9.8 %collective-permute-start.11 = (bf16[4,1,128,256]{3,2,1,0:T(8,128)(2,1)S(1)}, bf16[4,1,128,256]{3,2,1,0:T(8,128)(2,1)S(1)}, u32[]{:S(2)}, u32[]{:S(2)}) collective-permute-start(bf16[4,1,128,256]{3,2,1,0:T(8,128)(2,1)S(1)} %get-tuple-element.33), channel_id=1, source_target_pairs={{0,4},{2,6},{4,0},{6,2},{8,12},{10,14},{12,8},{14,10},{1,5},{3,7},... | collective-permute-start | bytes 786440 | tf_op jit(solution)/shard_map/ppermute | solution.py:442
  99.1 7.3 %collective-permute-start.12 = (bf16[1,1,128,256]{3,2,1,0:T(8,128)(2,1)S(1)}, bf16[1,1,128,256]{3,2,1,0:T(8,128)(2,1)S(1)}, u32[]{:S(2)}, u32[]{:S(2)}) collective-permute-start(bf16[1,1,128,256]{3,2,1,0:T(8,128)(2,1)S(1)} %get-tuple-element.34), channel_id=1, source_target_pairs={{0,8},{2,10},{4,12},{6,14},{8,0},{10,2},{12,4},{14,6},{1,9},{3,11}... | collective-permute-start | bytes 196616 | tf_op jit(solution)/shard_map/ppermute | solution.py:442
  107.5 35.7 %all-to-all-start.3 = ((bf16[8,2,128,256]{3,2,1,0:T(8,128)(2,1)}), bf16[8,2,128,256]{3,2,1,0:T(8,128)(2,1)S(1)}, u32[]{:S(2)}, u32[]{:S(2)}) async-start(bf16[8,2,128,256]{3,2,1,0:T(8,128)(2,1)} %shard_map.45), calls=%async_computation.3 | async-start | bytes 2097152 | tf_op jit(solution)/shard_map/all_to_all | solution.py:448
  112.7 14.8 %collective-permute-start.13 = (bf16[2,1,128,256]{3,2,0,1:T(8,128)(2,1)S(1)}, bf16[2,1,128,256]{3,2,0,1:T(8,128)(2,1)S(1)}, u32[]{:S(2)}, u32[]{:S(2)}) collective-permute-start(bf16[2,1,128,256]{3,2,0,1:T(8,128)(2,1)S(1)} %slice_bitcast_fusion), channel_id=1, source_target_pairs={{0,2},{2,0},{4,6},{6,4},{8,10},{10,8},{12,14},{14,12},{1,3},{3,1},... | collective-permute-start | bytes 393224 | tf_op jit(solution)/shard_map/ppermute | solution.py:442
  114.8 15.1 %collective-permute-start.15 = (bf16[2,1,128,256]{3,2,1,0:T(8,128)(2,1)S(1)}, bf16[2,1,128,256]{3,2,1,0:T(8,128)(2,1)S(1)}, u32[]{:S(2)}, u32[]{:S(2)}) collective-permute-start(bf16[2,1,128,256]{3,2,1,0:T(8,128)(2,1)S(1)} %pad_maximum_fusion.1), channel_id=1, source_target_pairs={{0,2},{2,0},{4,6},{6,4},{8,10},{10,8},{12,14},{14,12},{1,3},{3,1},... | collective-permute-start | bytes 393224 | tf_op jit(solution)/shard_map/ppermute | solution.py:442
  127.6 13.4 %collective-permute-start.14 = (bf16[1,1,128,256]{3,2,1,0:T(8,128)(2,1)S(1)}, bf16[1,1,128,256]{3,2,1,0:T(8,128)(2,1)S(1)}, u32[]{:S(2)}, u32[]{:S(2)}) collective-permute-start(bf16[1,1,128,256]{3,2,1,0:T(8,128)(2,1)S(1)} %slice_bitcast_fusion.4), channel_id=1, source_target_pairs={{0,8},{2,10},{4,12},{6,14},{8,0},{10,2},{12,4},{14,6},{1,9},{3,11}... | collective-permute-start | bytes 196616 | tf_op jit(solution)/shard_map/ppermute | solution.py:442
  129.9 13.4 %collective-permute-start.16 = (bf16[4,1,128,256]{3,2,1,0:T(8,128)(2,1)S(1)}, bf16[4,1,128,256]{3,2,1,0:T(8,128)(2,1)S(1)}, u32[]{:S(2)}, u32[]{:S(2)}) collective-permute-start(bf16[4,1,128,256]{3,2,1,0:T(8,128)(2,1)S(1)} %constant_dynamic-update-slice_fusion.3.refs_2_), channel_id=1, source_target_pairs={{0,4},{2,6},{4,0},{6,2},{8,12},{10,14},{12,8},{14,10},{1,5},{3,7},... | collective-permute-start | bytes 786440 | tf_op jit(solution)/shard_map/ppermute | solution.py:442
  144.6 4.2 %collective-permute-start.17 = (f32[16,128,256]{2,1,0:T(8,128)S(1)}, f32[16,128,256]{2,1,0:T(8,128)S(1)}, u32[]{:S(2)}, u32[]{:S(2)}) collective-permute-start(f32[16,128,256]{2,1,0:T(8,128)S(1)} %shard_map.46.own.mine_hbm), channel_id=1, source_target_pairs={{0,1},{1,0},{2,3},{3,2},{4,5},{5,4},{6,7},{7,6},{8,9},{9,8},{10,11... | collective-permute-start | bytes 6291464 | tf_op jit(solution)/shard_map/ppermute | solution.py:445
  150.8 4.4 %collective-permute-start.18 = (f32[136,128]{1,0:T(8,128)S(1)}, f32[136,128]{1,0:T(8,128)S(1)}, u32[]{:S(2)}, u32[]{:S(2)}) collective-permute-start(f32[136,128]{1,0:T(8,128)S(1)} %shard_map.48), channel_id=1, source_target_pairs={{0,2},{2,0},{4,6},{6,4},{8,10},{10,8},{12,14},{14,12},{1,3},{3,1},... | collective-permute-start | bytes 208904 | tf_op jit(solution)/shard_map/ppermute | solution.py:442
  155.2 4.4 %collective-permute-start.19 = (f32[136,128]{1,0:T(8,128)S(1)}, f32[136,128]{1,0:T(8,128)S(1)}, u32[]{:S(2)}, u32[]{:S(2)}) collective-permute-start(f32[136,128]{1,0:T(8,128)S(1)} %add.63), channel_id=1, source_target_pairs={{0,4},{2,6},{4,0},{6,2},{8,12},{10,14},{12,8},{14,10},{1,5},{3,7},... | collective-permute-start | bytes 208904 | tf_op jit(solution)/shard_map/ppermute | solution.py:442
  159.6 5.3 %collective-permute-start.20 = (f32[136,128]{1,0:T(8,128)S(1)}, f32[136,128]{1,0:T(8,128)S(1)}, u32[]{:S(2)}, u32[]{:S(2)}) collective-permute-start(f32[136,128]{1,0:T(8,128)S(1)} %add.64), channel_id=1, source_target_pairs={{0,8},{2,10},{4,12},{6,14},{8,0},{10,2},{12,4},{14,6},{1,9},{3,11}... | collective-permute-start | bytes 208904 | tf_op jit(solution)/shard_map/ppermute | solution.py:442
  164.9 1.3 collective-permute-start.21
